TPU v7x, 256 devices: a whole 4x4x8 slice. The times are simulated.
256 devices in a mesh: span: 16 (over z_lo, y, core), seq: 16 (over x, z_hi).
Axes of the slice: x: 4, y: 4, z: 8 (z_hi: 4, z_lo: 2; z = z_hi * 2 + z_lo), core: 2. Of those that a mesh axis runs over, the one named last changes fastest.
Arguments:
- qkv: bfloat16 [3, 16, 1024, 2048], P(None, 'span', 'seq'), may hold values from -6 to 6
- lengths: int32 [16], replicated, may hold values from 512 to 1024, as said below
Outputs:
- attended: bfloat16 [16, 1024, 2048], P('span', 'seq')
Inputs may be any that keep to these rules, and one draw needn't show every extreme that they name: `lengths`: the live tokens of a span are its first ones; some span is full.
All inputs are finite; a program needn't handle non-finite values.
Results may differ from a plain program's by a relative error of at most 0.0065.
Values may be sent and summed in bfloat16 or wider, within the bound.
No kernel may reach another device: no remote copies, remote signals or barrier semaphores. Data moves between devices by JAX's collectives and lax.ppermute only.
A program may use at most 64 MiB of HBM per device.

v0:
```python
import jax
import jax.numpy as jnp
from jax import lax
from jax.sharding import PartitionSpec as P

HD = 128


masked_fill = -1e30


def block_terms(queries, key_rows, values, key_live):
    scores = jnp.einsum(
        "hqe,hke->hqk", queries, key_rows, preferred_element_type=jnp.float32
    ) * key_rows.shape[-1] ** (-0.5)
    scores = jnp.where(key_live[None, None, :], scores, masked_fill)
    row_peak = jnp.max(scores, axis=-1)
    weights = jnp.where(key_live[None, None, :], jnp.exp(scores - row_peak[..., None]), 0.0).astype(
        jnp.bfloat16
    )
    numerator = jnp.einsum("hqk,hke->hqe", weights, values, preferred_element_type=jnp.float32)
    weight_sum = jnp.sum(weights.astype(jnp.float32), axis=-1)
    return (row_peak, numerator, weight_sum)


def combine(first_terms, second_terms):
    row_peak = jnp.maximum(first_terms[0], second_terms[0])
    scale_first = jnp.exp(first_terms[0] - row_peak)
    scale_second = jnp.exp(second_terms[0] - row_peak)
    numerator = first_terms[1] * scale_first[..., None] + second_terms[1] * scale_second[..., None]
    weight_sum = first_terms[2] * scale_first + second_terms[2] * scale_second
    return (row_peak, numerator, weight_sum)


def shards(qkv, lengths):
    span_index = lax.axis_index("span")
    spread = lax.all_to_all(qkv, "seq", split_axis=3, concat_axis=2, tiled=True)
    query_part = spread[0:1]
    pair_part = spread[1:3]
    span_rows = query_part.shape[2]
    heads_here = query_part.shape[3] // HD

    def split_heads(stacked):
        return stacked.reshape(stacked.shape[0], span_rows, heads_here, HD).transpose(0, 2, 1, 3)

    queries = split_heads(query_part)[0]
    pair_heads = split_heads(pair_part)
    positions = jnp.arange(span_rows)
    span_list = jnp.arange(lengths.shape[0])

    def live_keys(other_index):
        live_count = jnp.sum(jnp.where(span_list == other_index, lengths, 0))
        return (other_index <= span_index) & (positions < live_count)

    initial = (
        jnp.full((heads_here, span_rows), masked_fill, jnp.float32),
        jnp.zeros((heads_here, span_rows, HD), jnp.float32),
        jnp.zeros((heads_here, span_rows), jnp.float32),
    )
    arrived_block = lax.all_gather(pair_heads, "span", axis=2, tiled=True)
    blocks = arrived_block.shape[2] // span_rows
    first_span = jnp.int32(0) // span_rows
    lower_block = jnp.clip(-first_span, 0, blocks)
    upper_block = jnp.clip(span_index + 1, 0, blocks)

    def add_single(block_number, current):
        block_part = lax.dynamic_slice_in_dim(arrived_block, block_number * span_rows, span_rows, 2)
        return combine(
            current, block_terms(queries, block_part[0], block_part[1], live_keys(block_number))
        )

    running_state = lax.fori_loop(lower_block, upper_block, add_single, initial)
    attended = running_state[1] / running_state[2][..., None]
    own_count = jnp.sum(jnp.where(span_list == span_index, lengths, 0))
    attended = jnp.where((positions < own_count)[None, :, None], attended, 0.0).astype(jnp.bfloat16)
    merged = attended.transpose(1, 0, 2).reshape(1, span_rows, heads_here * HD)
    return lax.all_to_all(merged, "seq", split_axis=1, concat_axis=2, tiled=True)


def solution(mesh):
    in_specs = (P(None, "span", "seq", None), P())
    out_specs = P("span", "seq", None)
    return jax.shard_map(shards, mesh=mesh, in_specs=in_specs, out_specs=out_specs, check_vma=False)
```

profile of v0, /device:TPU:57, one launch (start us, length us, event | category | flops | bytes accessed | tf_op | source)
XLA Modules:
  0.0 237.0 jit_solution(6266499786171253801)
XLA Ops:
  6.5 2.8 %copy.43 = bf16[3,1,64,2048]{2,0,1,3:T(4,128)(2,1)S(1)} copy(bf16[3,1,64,2048]{3,2,1,0:T(8,128)(2,1)} %param.4) | data formatting | bytes 1572864 | tf_op args[0]
  10.9 32.4 %all_to_all.33 = bf16[16,2,12288]{2,1,0:T(2,128)(2,1)} all-to-all(bf16[16,2,12288]{2,1,0:T(2,128)(2,1)S(1)} %reshape.56), channel_id=1, replica_groups=mesh['span'=16,'seq'=16] {'seq'}, dimensions={0} | all-to-all | bytes 1572864 | tf_op jit(solution)/shard_map/all_to_all | solution.py:37
  43.3 2.9 %reshape.57 = bf16[2048,1,3,64]{3,2,1,0:T(4,128)(2,1)S(1)} reshape(bf16[16,2,12288]{2,1,0:T(2,128)(2,1)} %all_to_all.33) | data formatting | bytes 1572864
  49.8 50.8 %all-gather.2.cloned.1.call-done = bf16[2,1,16384,128]{3,2,0,1:T(8,128)(2,1)} async-done(((bf16[2,1,1024,128]{3,2,0,1:T(8,128)(2,1)}), bf16[2,1,16384,128]{3,2,0,1:T(8,128)(2,1)}) %all-gather.2.cloned.1.call-update) | async-done | bytes 8388624 | tf_op jit(solution)/shard_map/all_gather | solution.py:60
  100.6 105.6 %while.15 = (s32[]{:T(128)}, f32[1,1024]{1,0:T(1,128)S(1)}, f32[1,1024,128]{2,1,0:T(8,128)S(1)}, f32[1,1024]{1,0:T(1,128)S(1)}, s32[]{:T(128)}, /*index=5*/s32[]...) while((s32[]{:T(128)}, f32[1,1024]{1,0:T(1,128)S(1)}, ...), condition=%wide.region_5.6_spmd.clone, body=%wide.region_1.0_spmd.clone.sunk | while | flops 547756096 | bytes 14474529 | solution.py:72
  101.8 1.7 fusion.23
  103.6 1.6 convert_reduce_fusion.2
  105.2 2.0 fusion.24
  108.5 1.7 fusion.23
  111.8 2.0 fusion.24
  115.1 1.7 fusion.23
  116.7 1.6 convert_reduce_fusion.2
  118.4 2.0 fusion.24
  121.7 1.7 fusion.23
  123.4 1.6 convert_reduce_fusion.2
  125.0 2.0 fusion.24
  128.3 1.7 fusion.23
  131.6 2.0 fusion.24
  134.9 1.7 fusion.23
  136.6 1.6 convert_reduce_fusion.2
  138.2 2.0 fusion.24
  141.5 1.7 fusion.23
  143.2 1.6 convert_reduce_fusion.2
  144.8 2.0 fusion.24
  148.1 1.7 fusion.23
  149.8 1.6 convert_reduce_fusion.2
  151.4 2.0 fusion.24
  154.7 1.7 fusion.23
  158.0 2.0 fusion.24
  161.3 1.7 fusion.23
  164.6 2.0 fusion.24
  167.9 1.7 fusion.23
  169.6 1.6 convert_reduce_fusion.2
  171.2 2.0 fusion.24
  174.5 1.7 fusion.23
  176.2 1.6 convert_reduce_fusion.2
  177.8 2.0 fusion.24
  181.1 1.7 fusion.23
  182.8 1.6 convert_reduce_fusion.2
  184.4 2.0 fusion.24
  187.7 1.7 fusion.23
  191.0 2.0 fusion.24
  194.3 1.7 fusion.23
  197.6 2.0 fusion.24
  200.9 1.7 fusion.23
  204.2 2.0 fusion.24
  207.6 2.2 reduce.6
  209.9 19.2 %all_to_all.34 = bf16[16,2,4096]{2,1,0:T(2,128)(2,1)S(1)} all-to-all(bf16[16,2,4096]{2,1,0:T(2,128)(2,1)S(1)} %reshape.58), channel_id=1, replica_groups=mesh['span'=16,'seq'=16] {'seq'}, dimensions={0} | all-to-all | bytes 524288 | tf_op jit(solution)/shard_map/all_to_all | solution.py:77
  (77 shorter events, 38.0 us)
Async XLA Ops:
  6.5 94.0 %all-gather.2.cloned.1.call-start = ((), (), s32[]{:S(2)}) async-start(), calls=%async_computation.2 | async-start | bytes 8912896 | tf_op jit(solution)/shard_map/all_gather | solution.py:60
  43.3 5.2 %copy-start = (s32[16]{0:T(128)S(1)}, s32[16]{0:T(128)}, u32[]{:S(2)}) copy-start(s32[16]{0:T(128)} %param.5) | copy-start | bytes 196
Sparse Core Ops, SparseCore 0:
  48.5 51.9 all-gather.1
where the time goes:
time: 238 us; the launch traced here: 237 us
  matrix products  59.7 us (25%)
  blocking collectives  51.6 us (22%)
  waiting for transfers between devices  50.8 us (21%)
  other arithmetic  48.8 us (21%)
  between operations  13.5 us (6%)
  local copies, waits for them, and re-layouts  11.6 us (5%)
    all_gather x1, waiting for transfers between devices, shards(): arrived_block = lax.all_gather(pair_heads, 'span', axis=2, tiled=True)  50.8 us
    dot_general x16, matrix products, block_terms(): jnp.einsum('hqk,hke->hqe', weights, values, preferred_element_type=jnp.fl...  32.7 us
    all_to_all x1, blocking collectives, shards(): spread = lax.all_to_all(qkv, 'seq', split_axis=3, concat_axis=2, tiled=True)  32.4 us
    dot_general x16, matrix products, block_terms(): jnp.einsum('hqe,hke->hqk', queries, key_rows, preferred_element_type=jnp....  27 us
    reduce_sum x16, other arithmetic, block_terms(): weight_sum = jnp.sum(weights.astype(jnp.float32), axis=-1)  25.7 us
    all_to_all x1, blocking collectives, shards(): lax.all_to_all(merged, 'seq', split_axis=1, concat_axis=2, tiled=True)  19.2 us
    reduce_sum x16, other arithmetic, live_keys(): live_count = jnp.sum(jnp.where(span_list == other_index, lengths, 0))  9.67 us
    and x16, other arithmetic, live_keys(): return (other_index <= span_index) & (positions < live_count)  9.16 us
  transfers between devices with their start and end apart: 1, of which 1 were waited for; matrix products, arithmetic and copies ran while one was open for 1% of the time, Pallas kernels for 0%

commit v1 on v0

v1 whole, which is shorter than its diff:
```python
import functools
import math

import jax
import jax.numpy as jnp
from jax import lax
from jax.experimental import pallas as pl
from jax.experimental.pallas import tpu as pltpu
from jax.sharding import Mesh
from jax.sharding import PartitionSpec as P

HD = 128
SLICE = 64
ROWS = 256
FILL = -1e30
EXTRA = 16
STATE = HD + EXTRA
SCALE = math.log2(math.e) / math.sqrt(HD)
VMEM = pltpu.VMEM
RING = ("zlo", "zhi")


def pack(qkv_ref, pair_ref, query_ref):
    for head in range(query_ref.shape[0]):
        columns = slice(head * HD, (head + 1) * HD)
        query_ref[head] = qkv_ref[0, :, columns]
        pair_ref[head, :SLICE] = qkv_ref[1, :, columns]
        pair_ref[head, SLICE:] = qkv_ref[2, :, columns]


def unpack(parts_ref, out_ref):
    for head in range(parts_ref.shape[0]):
        out_ref[:, head * HD : (head + 1) * HD] = parts_ref[head]


def attend(sources, first, *refs):
    refs = list(refs)
    lengths_ref, own_ref, other_ref = refs[:3]
    arrivals = refs[3 : 3 + len(sources)]
    before_ref = None if first else refs[3 + len(sources)]
    state_ref, turned_ref = refs[-2:]
    core = lax.axis_index("core")
    zlo = lax.axis_index("zlo")
    zed = lax.axis_index("zhi") * 2 + zlo
    chunks = []
    for number, (distance, begin) in enumerate(sources):
        for place in range(arrivals[number].shape[0] // 4):
            chunks.append((place + begin, number, place))
    chunks.sort()
    per_span = {}
    for span, number, place in chunks:
        per_span.setdefault(span, []).append((number, place))
    spans = sorted(per_span)
    source_zed = [lax.rem(zed + 8 + distance, 8) for distance, _ in sources]
    source_zlo = lax.rem(source_zed[0], 2)

    if first:
        state_ref[:, :, :HD + 8] = jnp.zeros_like(state_ref[:, :, :HD + 8])
        state_ref[:, :, HD + 8:] = jnp.full_like(state_ref[:, :, HD + 8:], FILL)
    else:
        state_ref[...] = before_ref[...]

    @pl.when(source_zlo <= zlo)
    def _():
        column = 0
        starts = []
        extra = jnp.where(lax.broadcasted_iota(jnp.int32, (EXTRA, ROWS), 0) < 8, 1.0, 0.0)
        for span in spans:
            starts.append(column)
            for number, place in per_span[span]:
                values = arrivals[number][4 * place : 4 * place + 4, SLICE:, :].reshape(ROWS, HD)
                turned_ref[:HD, column : column + ROWS] = values.T
                turned_ref[HD:, column : column + ROWS] = extra.astype(jnp.bfloat16)
                column += ROWS
        starts.append(column)

        def add(block_ref, rel, step, count):
            width = starts[count]
            queries = block_ref[step]
            scores = []
            for span in spans[:count]:
                live = lengths_ref[source_zlo * 8 + 2 * span + core]
                for number, place in per_span[span]:
                    keys = arrivals[number][4 * place : 4 * place + 4, :SLICE, :].reshape(ROWS, HD)
                    score = lax.dot_general(
                        keys, queries, (((1,), (1,)), ((), ())), preferred_element_type=jnp.float32
                    )
                    offset = (source_zed[number] // 2) * SLICE
                    row = lax.broadcasted_iota(jnp.int32, (SLICE, ROWS), 0)
                    pieces = [score[: 2 * SLICE]]
                    for piece in (2, 3):
                        bound = live - piece * ROWS - offset
                        part = score[piece * SLICE : (piece + 1) * SLICE]
                        pieces.append(jnp.where(row < bound, part, FILL))
                    scores.append(jnp.concatenate(pieces, axis=0))
            scores = jnp.concatenate(scores, axis=0)
            old_peak = state_ref[rel, step, HD + 8 : HD + 9, :]
            peak = jnp.maximum(old_peak, jnp.max(scores, axis=0, keepdims=True))
            weights = jnp.exp2((scores - peak) * SCALE).astype(jnp.bfloat16)
            fresh = jnp.dot(turned_ref[:, :width], weights, preferred_element_type=jnp.float32)
            keep = jnp.exp2((old_peak - peak) * SCALE)
            state_ref[rel, step, : HD + 8, :] = (
                state_ref[rel, step, : HD + 8, :] * keep + fresh[: HD + 8]
            )
            state_ref[rel, step, HD + 8 :, :] = jnp.broadcast_to(peak, (8, ROWS))

        for rel, block_ref in ((0, own_ref), (1, other_ref)):

            @pl.loop(0, 4)
            def _(step):
                mine = 2 * step + (core if rel == 0 else 1 - core)
                reach = jnp.where(source_zlo < zlo, 4, (mine - core + 2) // 2)
                reach = jnp.clip(reach - spans[0], 0, len(spans))
                for count in range(1, len(spans) + 1):

                    @pl.when(reach == count)
                    def _():
                        add(block_ref, rel, step, count)


def join(lengths_ref, own_ref, other_ref, out_ref):
    core = lax.axis_index("core")
    zlo = lax.axis_index("zlo")
    offset = lax.axis_index("zhi") * SLICE
    for step in range(4):
        live = lengths_ref[zlo * 8 + 2 * step + core]
        first_peak = own_ref[0, step, HD + 8 : HD + 9, :]
        second_peak = other_ref[step, HD + 8 : HD + 9, :]
        peak = jnp.maximum(first_peak, second_peak)
        first = jnp.exp2((first_peak - peak) * SCALE)
        second = jnp.exp2((second_peak - peak) * SCALE)
        total = own_ref[0, step, HD : HD + 1, :] * first + other_ref[step, HD : HD + 1, :] * second
        numerator = own_ref[0, step, :HD, :] * first + other_ref[step, :HD, :] * second
        result = (numerator / total).T
        row = lax.broadcasted_iota(jnp.int32, (SLICE, HD), 0)
        for piece in range(4):
            part = result[piece * SLICE : (piece + 1) * SLICE]
            part = jnp.where(row < live - piece * ROWS - offset, part, 0.0)
            out_ref[4 * step + piece] = part.astype(jnp.bfloat16)


def call(kernel, out_shape, in_specs, scratch=(), flops=0, moved=0, **kw):
    spec = pl.BlockSpec(memory_space=VMEM)
    return pl.pallas_call(
        kernel,
        out_shape=out_shape,
        in_specs=in_specs,
        out_specs=jax.tree.map(lambda _: spec, out_shape),
        scratch_shapes=list(scratch),
        compiler_params=pltpu.CompilerParams(vmem_limit_bytes=40 * 2**20),
        cost_estimate=pl.CostEstimate(flops=flops, bytes_accessed=moved, transcendentals=0),
        **kw,
    )


def shards(qkv, lengths):
    vmem = pl.BlockSpec(memory_space=VMEM)
    smem = pl.BlockSpec(memory_space=pltpu.SMEM)
    heads = 16
    bf16 = jnp.bfloat16
    with jax.named_scope("pack"):
        pairs, queries = call(
            pack,
            [
                jax.ShapeDtypeStruct((heads, 2 * SLICE, HD), bf16),
                jax.ShapeDtypeStruct((heads, SLICE, HD), bf16),
            ],
            [vmem],
        )(qkv[:, 0])
    with jax.named_scope("pairs_to_heads"):
        pairs = lax.all_to_all(pairs, ("y", "x"), 0, 0, tiled=True)
    with jax.named_scope("queries_to_heads"):
        queries = lax.all_to_all(queries, ("y", "x"), 0, 0, tiled=True)

    chips = 8
    place = [z % 2 * 4 + z // 2 for z in range(chips)]
    up = [(place[z], place[(z + 1) % chips]) for z in range(chips)]
    down = [(place[z], place[(z - 1) % chips]) for z in range(chips)]

    def swap(block):
        return lax.ppermute(block, "core", [(0, 1), (1, 0)])

    own = queries.reshape(4, ROWS, HD)
    with jax.named_scope("swap_queries"):
        other = swap(own)
    state_shape = jax.ShapeDtypeStruct((2, 4, STATE, ROWS), jnp.float32)

    def step(arrivals, sources, state):
        first = state is None
        operands = [lengths, own, other] + arrivals + ([] if first else [state])
        count = sum(a.shape[0] // 4 for a in arrivals)
        return call(
            functools.partial(attend, sources, first),
            state_shape,
            [smem] + [vmem] * (len(operands) - 1),
            [pltpu.VMEM((STATE, count * ROWS), bf16)],
            flops=4 * HD * ROWS * ROWS * 8 * count * 4,
            moved=8 * 2**20,
            input_output_aliases={} if first else {len(operands) - 1: 0},
        )(*operands)

    from_below, from_above = pairs, pairs
    state = None
    arrived = [pairs]
    sources = [(0, 0)]
    for distance in range(1, 6):
        if distance < 4:
            with jax.named_scope("ring"):
                from_below = lax.ppermute(from_below, RING, up)
                from_above = lax.ppermute(from_above, RING, down)
        elif distance == 4:
            half = heads // 2
            with jax.named_scope("ring"):
                from_below = lax.ppermute(from_below[:half], RING, up)
                from_above = lax.ppermute(from_above[half:], RING, down)
        with jax.named_scope("attend"):
            state = step(arrived, tuple(sources), state)
        arrived = [from_below, from_above]
        sources = [(-distance, 0), (distance, 0 if distance < 4 else 2)]
    with jax.named_scope("swap_terms"):
        theirs = swap(state[1])
    with jax.named_scope("join"):
        attended = call(
            join,
            jax.ShapeDtypeStruct((heads, SLICE, HD), bf16),
            [smem, vmem, vmem],
        )(lengths, state, theirs)
    with jax.named_scope("heads_to_tokens"):
        attended = lax.all_to_all(attended, ("y", "x"), 0, 0, tiled=True)
    with jax.named_scope("unpack"):
        out = call(unpack, jax.ShapeDtypeStruct((SLICE, heads * HD), bf16), [vmem])(attended)
    return out[None]


def solution(mesh):
    fine = Mesh(mesh.devices.reshape(2, 4, 2, 4, 4), ("zlo", "y", "core", "x", "zhi"))
    span, seq = ("zlo", "y", "core"), ("x", "zhi")
    return jax.shard_map(
        shards,
        mesh=fine,
        in_specs=(P(None, span, seq, None), P()),
        out_specs=P(span, seq, None),
        check_vma=False,
    )
```

time: 238 us -> 103 us (0.43)
  the two profiles are of different devices: /device:TPU:57 before, /device:TPU:96 now
where the time goes in v1:
time: 103 us
  Pallas kernels  41.5 us (40%)
  blocking collectives  27.4 us (27%)
  waiting for transfers between devices  17.9 us (17%)
  starting transfers between devices  15.1 us (15%)
  local copies, waits for them, and re-layouts  1.21 us (1%)
    pallas_call x5, Pallas kernels, step(): call(functools.partial(attend, sources, first), state_shape, [smem] + [vm...  39.1 us
    all_to_all x1, blocking collectives, shards(): queries = lax.all_to_all(queries, ('y', 'x'), 0, 0, tiled=True)  15.5 us
    all_to_all x1, blocking collectives, shards(): attended = lax.all_to_all(attended, ('y', 'x'), 0, 0, tiled=True)  11.9 us
    all_to_all x1, waiting for transfers between devices, shards(): pairs = lax.all_to_all(pairs, ('y', 'x'), 0, 0, tiled=True)  10.3 us
    ppermute x3, starting transfers between devices, shards(): from_below = lax.ppermute(from_below, RING, up)  8.49 us
    ppermute x3, waiting for transfers between devices, shards(): from_below = lax.ppermute(from_below, RING, up)  5.56 us
    all_to_all x1, starting transfers between devices, shards(): pairs = lax.all_to_all(pairs, ('y', 'x'), 0, 0, tiled=True)  3.57 us
  transfers between devices with their start and end apart: 11, of which 4 were waited for; matrix products, arithmetic and copies ran while one was open for 0% of the time, Pallas kernels for 33%

profile of v1, /device:TPU:96, one launch (start us, length us, event | category | flops | bytes accessed | tf_op | source)
XLA Modules:
  0.0 103.1 jit_solution(11059663696844129407)
XLA Ops:
  0.0 0.0 copy-start
  0.0 1.1 %copy-done = bf16[3,1,64,2048]{3,2,1,0:T(8,128)(2,1)S(1)} copy-done((bf16[3,1,64,2048]{3,2,1,0:T(8,128)(2,1)S(1)}, bf16[3,1,64,2048]{3,2,1,0:T(8,128)(2,1)}, u32[]{:S(2)}) %copy-start) | copy-done | bytes 786456
  1.1 0.0 copy-start.1
  1.1 0.9 pack.1
  2.1 15.5 %all_to_all.15 = bf16[16,64,128]{2,1,0:T(8,128)(2,1)S(1)} all-to-all(bf16[16,64,128]{2,1,0:T(8,128)(2,1)S(1)} %get-tuple-element.7), channel_id=1, replica_groups=mesh['zlo'=2,'y'=4,'core'=2,'x'=4,'zhi'=4] {'y','x'}, dimensions={0} | all-to-all | bytes 524288 | tf_op jit(solution)/shard_map/queries_to_heads/all_to_all | solution.py:173
  17.6 3.6 %all-to-all-start.1 = ((bf16[16,128,128]{2,1,0:T(8,128)(2,1)}), bf16[16,128,128]{2,1,0:T(8,128)(2,1)S(1)}, u32[]{:S(2)}, u32[]{:S(2)}) async-start(bf16[16,128,128]{2,1,0:T(8,128)(2,1)} %get-tuple-element.8), calls=%async_computation.1 | async-start | bytes 1048576 | tf_op jit(solution)/shard_map/pairs_to_heads/all_to_all | solution.py:171
  21.2 0.1 collective-permute-start
  21.3 10.3 %all-to-all-done.1.refs_3_ = bf16[16,128,128]{2,1,0:T(8,128)(2,1)S(1)} async-done(((bf16[16,128,128]{2,1,0:T(8,128)(2,1)}), bf16[16,128,128]{2,1,0:T(8,128)(2,1)S(1)}, u32[]{:S(2)}, u32[]{:S(2)}) %all-to-all-start.1) | async-done | bytes 524320 | tf_op jit(solution)/shard_map/pairs_to_heads/all_to_all | solution.py:171
  31.6 3.1 %collective-permute-start.1 = (bf16[16,128,128]{2,1,0:T(8,128)(2,1)S(1)}, bf16[16,128,128]{2,1,0:T(8,128)(2,1)S(1)}, u32[]{:S(2)}, u32[]{:S(2)}) collective-permute-start(bf16[16,128,128]{2,1,0:T(8,128)(2,1)S(1)} %all-to-all-done.1.refs_3_), channel_id=1, source_target_pairs={{0,128},{128,1},{1,129},{129,2},{2,130},{130,3},{3,131},{131,0},{4... | collective-permute-start | bytes 1572872 | tf_op jit(solution)/shard_map/ring/ppermute | solution.py:209
  34.7 0.0 collective-permute-start.5
  34.7 0.0 collective-permute-done.refs_2_
  34.7 0.0 copy-done.1
  34.7 5.3 %attend.5.refs_5_ = f32[2,4,144,256]{3,2,1,0:T(8,128)S(1)} custom-call(s32[16]{0:T(128)S(1)} %copy-done.1, bf16[4,256,128]{2,1,0:T(8,128)(2,1)S(1)} %bitcast.7, bf16[4,256,128]{2,1,0:T(8,128)(2,1)S(1)} %collective-permute-done.refs_2_, bf16[16,128,128]{2,1,0:T(8,128)(2,1)S(1)} %all-to-all-done.1.refs_3_), custom_call_target="tpu_custom_call" | custom-call | flops 4294967296 | bytes 8388608 | tf_op jit(solution)/shard_map/attend/pallas_call | solution.py:192
  40.0 3.5 %collective-permute-done.1.refs_3_ = bf16[16,128,128]{2,1,0:T(8,128)(2,1)S(1)} collective-permute-done((bf16[16,128,128]{2,1,0:T(8,128)(2,1)S(1)}, bf16[16,128,128]{2,1,0:T(8,128)(2,1)S(1)}, u32[]{:S(2)}, u32[]{:S(2)}) %collective-permute-start.1) | collective-permute-done | bytes 524320 | tf_op jit(solution)/shard_map/ring/ppermute | solution.py:209
  43.5 3.7 %collective-permute-start.2 = (bf16[16,128,128]{2,1,0:T(8,128)(2,1)S(1)}, bf16[16,128,128]{2,1,0:T(8,128)(2,1)S(1)}, u32[]{:S(2)}, u32[]{:S(2)}) collective-permute-start(bf16[16,128,128]{2,1,0:T(8,128)(2,1)S(1)} %collective-permute-done.1.refs_3_), channel_id=1, source_target_pairs={{0,128},{128,1},{1,129},{129,2},{2,130},{130,3},{3,131},{131,0},{4... | collective-permute-start | bytes 1572872 | tf_op jit(solution)/shard_map/ring/ppermute | solution.py:209
  47.2 0.0 collective-permute-done.5.refs_4_
  47.2 0.0 collective-permute-start.6
  47.2 10.4 %attend.6.refs_5_ = f32[2,4,144,256]{3,2,1,0:T(8,128)S(1)} custom-call(s32[16]{0:T(128)S(1)} %copy-done.1, bf16[4,256,128]{2,1,0:T(8,128)(2,1)S(1)} %bitcast.8, bf16[4,256,128]{2,1,0:T(8,128)(2,1)S(1)} %collective-permute-done.refs_2_, bf16[16,128,128]{2,1,0:T(8,128)(2,1)S(1)} %collective-permute-done.1.refs_3_, ...), custom_call_target="tpu_custom_call", output_to_operand_aliasing={{}: (5, {})} | custom-call | flops 8589934592 | bytes 8388608 | tf_op jit(solution)/shard_map/attend/pallas_call | solution.py:192
  57.6 0.0 collective-permute-done.2.refs_3_
  57.6 1.7 %collective-permute-start.3 = (bf16[16,128,128]{2,1,0:T(8,128)(2,1)S(1)}, bf16[16,128,128]{2,1,0:T(8,128)(2,1)S(1)}, u32[]{:S(2)}, u32[]{:S(2)}) collective-permute-start(bf16[16,128,128]{2,1,0:T(8,128)(2,1)S(1)} %collective-permute-done.2.refs_3_), channel_id=1, source_target_pairs={{0,128},{128,1},{1,129},{129,2},{2,130},{130,3},{3,131},{131,0},{4... | collective-permute-start | bytes 1572872 | tf_op jit(solution)/shard_map/ring/ppermute | solution.py:209
  59.3 0.0 collective-permute-done.6.refs_4_
  59.3 0.4 collective-permute-start.7
  59.7 7.6 %attend.7.refs_5_ = f32[2,4,144,256]{3,2,1,0:T(8,128)S(1)} custom-call(s32[16]{0:T(128)S(1)} %copy-done.1, bf16[4,256,128]{2,1,0:T(8,128)(2,1)S(1)} %bitcast.9, bf16[4,256,128]{2,1,0:T(8,128)(2,1)S(1)} %collective-permute-done.refs_2_, bf16[16,128,128]{2,1,0:T(8,128)(2,1)S(1)} %collective-permute-done.2.refs_3_, ...), custom_call_target="tpu_custom_call", output_to_operand_aliasing={{}: (5, {})} | custom-call | flops 8589934592 | bytes 8388608 | tf_op jit(solution)/shard_map/attend/pallas_call | solution.py:192
  67.4 2.1 %collective-permute-done.3.refs_3_ = bf16[16,128,128]{2,1,0:T(8,128)(2,1)S(1)} collective-permute-done((bf16[16,128,128]{2,1,0:T(8,128)(2,1)S(1)}, bf16[16,128,128]{2,1,0:T(8,128)(2,1)S(1)}, u32[]{:S(2)}, u32[]{:S(2)}) %collective-permute-start.3) | collective-permute-done | bytes 524320 | tf_op jit(solution)/shard_map/ring/ppermute | solution.py:209
  69.5 1.9 %collective-permute-start.4 = (bf16[8,128,128]{2,1,0:T(8,128)(2,1)S(1)}, bf16[8,128,128]{2,1,0:T(8,128)(2,1)S(1)}, u32[]{:S(2)}, u32[]{:S(2)}) collective-permute-start(bf16[8,128,128]{2,1,0:T(8,128)(2,1)S(1)} %slice.12), channel_id=1, source_target_pairs={{0,128},{128,1},{1,129},{129,2},{2,130},{130,3},{3,131},{131,0},{4... | collective-permute-start | bytes 786440 | tf_op jit(solution)/shard_map/ring/ppermute | solution.py:214
  71.4 0.0 collective-permute-done.7.refs_4_
  71.4 0.5 collective-permute-start.8
  71.9 10.2 %attend.8.refs_5_ = f32[2,4,144,256]{3,2,1,0:T(8,128)S(1)} custom-call(s32[16]{0:T(128)S(1)} %copy-done.1, bf16[4,256,128]{2,1,0:T(8,128)(2,1)S(1)} %bitcast.10, bf16[4,256,128]{2,1,0:T(8,128)(2,1)S(1)} %collective-permute-done.refs_2_, bf16[16,128,128]{2,1,0:T(8,128)(2,1)S(1)} %collective-permute-done.3.refs_3_, ...), custom_call_target="tpu_custom_call", output_to_operand_aliasing={{}: (5, {})} | custom-call | flops 8589934592 | bytes 8388608 | tf_op jit(solution)/shard_map/attend/pallas_call | solution.py:192
  82.1 0.0 collective-permute-done.4.refs_3_
  82.2 0.0 collective-permute-done.8.refs_4_
  82.2 5.5 %attend.9.own_ref = f32[2,4,144,256]{3,2,1,0:T(8,128)S(1)} custom-call(s32[16]{0:T(128)S(1)} %copy-done.1, bf16[4,256,128]{2,1,0:T(8,128)(2,1)S(1)} %bitcast.11, bf16[4,256,128]{2,1,0:T(8,128)(2,1)S(1)} %collective-permute-done.refs_2_, bf16[8,128,128]{2,1,0:T(8,128)(2,1)S(1)} %collective-permute-done.4.refs_3_, ...), custom_call_target="tpu_custom_call", output_to_operand_aliasing={{}: (5, {})} | custom-call | flops 4294967296 | bytes 8388608 | tf_op jit(solution)/shard_map/attend/pallas_call | solution.py:192
  87.7 0.1 collective-permute-start.9
  87.8 2.0 %collective-permute-done.9.other_ref = f32[4,144,256]{2,1,0:T(8,128)S(1)} collective-permute-done((f32[4,144,256]{2,1,0:T(8,128)S(1)}, f32[4,144,256]{2,1,0:T(8,128)S(1)}, u32[]{:S(2)}, u32[]{:S(2)}) %collective-permute-start.9) | collective-permute-done | bytes 589856 | tf_op jit(solution)/shard_map/swap_terms/ppermute | solution.py:181
  89.8 0.7 join.1
  90.5 11.9 %all_to_all.16.parts_ref = bf16[16,64,128]{2,1,0:T(8,128)(2,1)S(1)} all-to-all(bf16[16,64,128]{2,1,0:T(8,128)(2,1)S(1)} %join.1), channel_id=1, replica_groups=mesh['zlo'=2,'y'=4,'core'=2,'x'=4,'zhi'=4] {'y','x'}, dimensions={0} | all-to-all | bytes 524288 | tf_op jit(solution)/shard_map/heads_to_tokens/all_to_all | solution.py:229
  102.4 0.8 unpack.1
  (3 shorter events, 0.1 us)
Async XLA Ops:
  0.0 1.1 %copy-start = (bf16[3,1,64,2048]{3,2,1,0:T(8,128)(2,1)S(1)}, bf16[3,1,64,2048]{3,2,1,0:T(8,128)(2,1)}, u32[]{:S(2)}) copy-start(bf16[3,1,64,2048]{3,2,1,0:T(8,128)(2,1)} %param.2) | copy-start | bytes 2359300
  1.1 33.6 %copy-start.1 = (s32[16]{0:T(128)S(1)}, s32[16]{0:T(128)}, u32[]{:S(2)}) copy-start(s32[16]{0:T(128)} %lengths_ref.1) | copy-start | bytes 196
  17.6 14.0 %all-to-all-start.1 = ((bf16[16,128,128]{2,1,0:T(8,128)(2,1)}), bf16[16,128,128]{2,1,0:T(8,128)(2,1)S(1)}, u32[]{:S(2)}, u32[]{:S(2)}) async-start(bf16[16,128,128]{2,1,0:T(8,128)(2,1)} %get-tuple-element.8), calls=%async_computation.1 | async-start | bytes 1048576 | tf_op jit(solution)/shard_map/pairs_to_heads/all_to_all | solution.py:171
  21.2 13.5 %collective-permute-start = (bf16[4,256,128]{2,1,0:T(8,128)(2,1)S(1)}, bf16[4,256,128]{2,1,0:T(8,128)(2,1)S(1)}, u32[]{:S(2)}, u32[]{:S(2)}) collective-permute-start(bf16[4,256,128]{2,1,0:T(8,128)(2,1)S(1)} %bitcast.6), channel_id=1, source_target_pairs={{0,16},{16,0},{1,17},{17,1},{2,18},{18,2},{3,19},{19,3},{4,20},{20... | collective-permute-start | bytes 786440 | tf_op jit(solution)/shard_map/swap_queries/ppermute | solution.py:181
  31.6 12.0 %collective-permute-start.1 = (bf16[16,128,128]{2,1,0:T(8,128)(2,1)S(1)}, bf16[16,128,128]{2,1,0:T(8,128)(2,1)S(1)}, u32[]{:S(2)}, u32[]{:S(2)}) collective-permute-start(bf16[16,128,128]{2,1,0:T(8,128)(2,1)S(1)} %all-to-all-done.1.refs_3_), channel_id=1, source_target_pairs={{0,128},{128,1},{1,129},{129,2},{2,130},{130,3},{3,131},{131,0},{4... | collective-permute-start | bytes 1572872 | tf_op jit(solution)/shard_map/ring/ppermute | solution.py:209
  34.7 12.5 %collective-permute-start.5 = (bf16[16,128,128]{2,1,0:T(8,128)(2,1)S(1)}, bf16[16,128,128]{2,1,0:T(8,128)(2,1)S(1)}, u32[]{:S(2)}, u32[]{:S(2)}) collective-permute-start(bf16[16,128,128]{2,1,0:T(8,128)(2,1)S(1)} %all-to-all-done.1.refs_3_), channel_id=1, source_target_pairs={{0,131},{128,0},{1,128},{129,1},{2,129},{130,2},{3,130},{131,3},{4... | collective-permute-start | bytes 1572872 | tf_op jit(solution)/shard_map/ring/ppermute | solution.py:210
  43.5 14.1 %collective-permute-start.2 = (bf16[16,128,128]{2,1,0:T(8,128)(2,1)S(1)}, bf16[16,128,128]{2,1,0:T(8,128)(2,1)S(1)}, u32[]{:S(2)}, u32[]{:S(2)}) collective-permute-start(bf16[16,128,128]{2,1,0:T(8,128)(2,1)S(1)} %collective-permute-done.1.refs_3_), channel_id=1, source_target_pairs={{0,128},{128,1},{1,129},{129,2},{2,130},{130,3},{3,131},{131,0},{4... | collective-permute-start | bytes 1572872 | tf_op jit(solution)/shard_map/ring/ppermute | solution.py:209
  47.2 12.1 %collective-permute-start.6 = (bf16[16,128,128]{2,1,0:T(8,128)(2,1)S(1)}, bf16[16,128,128]{2,1,0:T(8,128)(2,1)S(1)}, u32[]{:S(2)}, u32[]{:S(2)}) collective-permute-start(bf16[16,128,128]{2,1,0:T(8,128)(2,1)S(1)} %collective-permute-done.5.refs_4_), channel_id=1, source_target_pairs={{0,131},{128,0},{1,128},{129,1},{2,129},{130,2},{3,130},{131,3},{4... | collective-permute-start | bytes 1572872 | tf_op jit(solution)/shard_map/ring/ppermute | solution.py:210
  57.6 11.8 %collective-permute-start.3 = (bf16[16,128,128]{2,1,0:T(8,128)(2,1)S(1)}, bf16[16,128,128]{2,1,0:T(8,128)(2,1)S(1)}, u32[]{:S(2)}, u32[]{:S(2)}) collective-permute-start(bf16[16,128,128]{2,1,0:T(8,128)(2,1)S(1)} %collective-permute-done.2.refs_3_), channel_id=1, source_target_pairs={{0,128},{128,1},{1,129},{129,2},{2,130},{130,3},{3,131},{131,0},{4... | collective-permute-start | bytes 1572872 | tf_op jit(solution)/shard_map/ring/ppermute | solution.py:209
  59.3 12.1 %collective-permute-start.7 = (bf16[16,128,128]{2,1,0:T(8,128)(2,1)S(1)}, bf16[16,128,128]{2,1,0:T(8,128)(2,1)S(1)}, u32[]{:S(2)}, u32[]{:S(2)}) collective-permute-start(bf16[16,128,128]{2,1,0:T(8,128)(2,1)S(1)} %collective-permute-done.6.refs_4_), channel_id=1, source_target_pairs={{0,131},{128,0},{1,128},{129,1},{2,129},{130,2},{3,130},{131,3},{4... | collective-permute-start | bytes 1572872 | tf_op jit(solution)/shard_map/ring/ppermute | solution.py:210
  69.5 12.7 %collective-permute-start.4 = (bf16[8,128,128]{2,1,0:T(8,128)(2,1)S(1)}, bf16[8,128,128]{2,1,0:T(8,128)(2,1)S(1)}, u32[]{:S(2)}, u32[]{:S(2)}) collective-permute-start(bf16[8,128,128]{2,1,0:T(8,128)(2,1)S(1)} %slice.12), channel_id=1, source_target_pairs={{0,128},{128,1},{1,129},{129,2},{2,130},{130,3},{3,131},{131,0},{4... | collective-permute-start | bytes 786440 | tf_op jit(solution)/shard_map/ring/ppermute | solution.py:214
  71.4 10.8 %collective-permute-start.8 = (bf16[8,128,128]{2,1,0:T(8,128)(2,1)S(1)}, bf16[8,128,128]{2,1,0:T(8,128)(2,1)S(1)}, u32[]{:S(2)}, u32[]{:S(2)}) collective-permute-start(bf16[8,128,128]{2,1,0:T(8,128)(2,1)S(1)} %slice.13), channel_id=1, source_target_pairs={{0,131},{128,0},{1,128},{129,1},{2,129},{130,2},{3,130},{131,3},{4... | collective-permute-start | bytes 786440 | tf_op jit(solution)/shard_map/ring/ppermute | solution.py:215
  87.7 2.1 %collective-permute-start.9 = (f32[4,144,256]{2,1,0:T(8,128)S(1)}, f32[4,144,256]{2,1,0:T(8,128)S(1)}, u32[]{:S(2)}, u32[]{:S(2)}) collective-permute-start(f32[4,144,256]{2,1,0:T(8,128)S(1)} %slice_bitcast_fusion), channel_id=1, source_target_pairs={{0,16},{16,0},{1,17},{17,1},{2,18},{18,2},{3,19},{19,3},{4,20},{20... | collective-permute-start | bytes 1769480 | tf_op jit(solution)/shard_map/swap_terms/ppermute | solution.py:181

commit v2 on v1

v2 whole, which is shorter than its diff:
```python
import functools
import math

import jax
import jax.numpy as jnp
from jax import lax
from jax.experimental import pallas as pl
from jax.experimental.pallas import tpu as pltpu
from jax.sharding import Mesh
from jax.sharding import PartitionSpec as P

HD = 128
SLICE = 64
ROWS = 256
FILL = -1e30
STATE = HD + 16
SCALE = math.log2(math.e) / math.sqrt(HD)
VMEM = pltpu.VMEM
RING = ("zlo", "zhi")


def pack(qkv_ref, out_ref):
    for head in range(out_ref.shape[0]):
        columns = slice(head * HD, (head + 1) * HD)
        for part in range(3):
            out_ref[head, part * SLICE : (part + 1) * SLICE] = qkv_ref[part, :, columns]


def unpack(parts_ref, out_ref):
    for head in range(parts_ref.shape[0]):
        out_ref[:, head * HD : (head + 1) * HD] = parts_ref[head]


def split(parts_ref, query_ref, pair_ref):
    for span in range(4):
        block = parts_ref.at[4 * span : 4 * span + 4]
        query_ref[span] = block[:, :SLICE, :].reshape(ROWS, HD)
        pair_ref[span, :ROWS] = block[:, SLICE : 2 * SLICE, :].reshape(ROWS, HD)
        turned = block[:, 2 * SLICE :, :].reshape(ROWS, HD).T
        pair_ref[span, ROWS : ROWS + HD] = turned[:, :HD]
        pair_ref[span, ROWS + HD :] = turned[:, HD:]


def attend(sources, first, *refs):
    refs = list(refs)
    lengths_ref, own_ref, other_ref = refs[:3]
    arrivals = refs[3 : 3 + len(sources)]
    before_ref = None if first else refs[3 + len(sources)]
    state_ref = refs[-1]
    core = lax.axis_index("core")
    zlo = lax.axis_index("zlo")
    zed = lax.axis_index("zhi") * 2 + zlo
    pieces = []
    for number, (distance, begin) in enumerate(sources):
        for place in range(arrivals[number].shape[0]):
            pieces.append((place + begin, number, place))
    pieces.sort()
    source_zed = [lax.rem(zed + 8 + distance, 8) for distance, _ in sources]
    source_zlo = lax.rem(source_zed[0], 2)
    aligned = sources[0][0] % 2 == 0

    if first:
        state_ref[:, : HD + 8] = jnp.zeros_like(state_ref[:, : HD + 8])
        state_ref[:, HD + 8 :] = jnp.full_like(state_ref[:, HD + 8 :], FILL)
    else:
        state_ref[...] = before_ref[...]

    ones = jnp.where(lax.broadcasted_iota(jnp.int32, (16, ROWS), 0) < 8, 1.0, 0.0)
    ones = ones.astype(jnp.bfloat16)

    def add(step, count, last):
        queries = jnp.concatenate([own_ref[step], other_ref[step]], axis=0)
        scores, values = [], []
        for span, number, place in pieces:
            if span >= count:
                continue
            block = arrivals[number].at[place]
            score = lax.dot_general(
                block[:ROWS, :], queries, (((1,), (1,)), ((), ())), preferred_element_type=jnp.float32
            )
            live = lengths_ref[source_zlo * 8 + 2 * span + core]
            offset = (source_zed[number] // 2) * SLICE
            row = lax.broadcasted_iota(jnp.int32, (SLICE, 2 * ROWS), 0)
            other_half = lax.broadcasted_iota(jnp.int32, (SLICE, 2 * ROWS), 1) >= ROWS
            for part in range(4):
                rows = score[part * SLICE : (part + 1) * SLICE]
                bound = live - part * ROWS - offset
                if span == last:
                    bound = jnp.where(other_half, jnp.where(core == 1, 0, bound), bound)
                    rows = jnp.where(row < bound, rows, FILL)
                elif part >= 2:
                    rows = jnp.where(row < bound, rows, FILL)
                scores.append(rows)
            turned = jnp.concatenate([block[ROWS : ROWS + HD, :], block[ROWS + HD :, :]], axis=1)
            values.append(jnp.concatenate([turned, ones], axis=0))
        scores = jnp.concatenate(scores, axis=0)
        old_peak = state_ref[step, HD + 8 : HD + 9, :]
        peak = jnp.maximum(old_peak, jnp.max(scores, axis=0, keepdims=True))
        shifted = (scores - peak) * SCALE
        weights = jnp.exp2(shifted)
        if last == 0:
            weights = jnp.where(scores > FILL, weights, 0.0)
        weights = weights.astype(jnp.bfloat16)
        fresh = jnp.dot(
            jnp.concatenate(values, axis=1), weights, preferred_element_type=jnp.float32
        )
        keep = jnp.exp2((old_peak - peak) * SCALE)
        state_ref[step, : HD + 8, :] = state_ref[step, : HD + 8, :] * keep + fresh[: HD + 8]
        state_ref[step, HD + 8 :, :] = jnp.broadcast_to(peak, (8, 2 * ROWS))

    if aligned:
        for step in range(4):
            add(step, step + 1, step)
    else:

        @pl.when(source_zlo < zlo)
        def _():
            @pl.loop(0, 4)
            def _(step):
                add(step, 4, -1)


def join(lengths_ref, own_ref, other_ref, out_ref):
    core = lax.axis_index("core")
    zlo = lax.axis_index("zlo")
    offset = lax.axis_index("zhi") * SLICE
    for step in range(4):
        live = lengths_ref[zlo * 8 + 2 * step + core]
        first_peak = own_ref[step, HD + 8 : HD + 9, :ROWS]
        second_peak = other_ref[step, HD + 8 : HD + 9, :]
        peak = jnp.maximum(first_peak, second_peak)
        first = jnp.exp2((first_peak - peak) * SCALE)
        second = jnp.exp2((second_peak - peak) * SCALE)
        total = own_ref[step, HD : HD + 1, :ROWS] * first + other_ref[step, HD : HD + 1, :] * second
        numerator = own_ref[step, :HD, :ROWS] * first + other_ref[step, :HD, :] * second
        result = (numerator / total).T
        row = lax.broadcasted_iota(jnp.int32, (SLICE, HD), 0)
        for piece in range(4):
            part = result[piece * SLICE : (piece + 1) * SLICE]
            part = jnp.where(row < live - piece * ROWS - offset, part, 0.0)
            out_ref[4 * step + piece] = part.astype(jnp.bfloat16)


def call(kernel, out_shape, in_specs, flops=0, moved=0, **kw):
    spec = pl.BlockSpec(memory_space=VMEM)
    return pl.pallas_call(
        kernel,
        out_shape=out_shape,
        in_specs=in_specs,
        out_specs=jax.tree.map(lambda _: spec, out_shape),
        compiler_params=pltpu.CompilerParams(vmem_limit_bytes=40 * 2**20),
        cost_estimate=pl.CostEstimate(flops=flops, bytes_accessed=moved, transcendentals=0),
        **kw,
    )


def shards(qkv, lengths):
    vmem = pl.BlockSpec(memory_space=VMEM)
    smem = pl.BlockSpec(memory_space=pltpu.SMEM)
    heads = 16
    bf16 = jnp.bfloat16
    with jax.named_scope("pack"):
        parts = call(pack, jax.ShapeDtypeStruct((heads, 3 * SLICE, HD), bf16), [vmem])(qkv[:, 0])
    with jax.named_scope("tokens_to_heads"):
        parts = lax.all_to_all(parts, ("y", "x"), 0, 0, tiled=True)
    with jax.named_scope("split"):
        own, pairs = call(
            split,
            [
                jax.ShapeDtypeStruct((4, ROWS, HD), bf16),
                jax.ShapeDtypeStruct((4, 2 * ROWS, HD), bf16),
            ],
            [vmem],
        )(parts)

    chips = 8
    place = [z % 2 * 4 + z // 2 for z in range(chips)]
    up = [(place[z], place[(z + 1) % chips]) for z in range(chips)]
    down = [(place[z], place[(z - 1) % chips]) for z in range(chips)]

    def swap(block):
        return lax.ppermute(block, "core", [(0, 1), (1, 0)])

    with jax.named_scope("swap_queries"):
        other = swap(own)
    state_shape = jax.ShapeDtypeStruct((4, STATE, 2 * ROWS), jnp.float32)

    def step(arrivals, sources, state):
        first = state is None
        operands = [lengths, own, other] + arrivals + ([] if first else [state])
        count = sum(a.shape[0] for a in arrivals)
        return call(
            functools.partial(attend, sources, first),
            state_shape,
            [smem] + [vmem] * (len(operands) - 1),
            flops=4 * HD * ROWS * ROWS * 8 * count * 4,
            moved=8 * 2**20,
            input_output_aliases={} if first else {len(operands) - 1: 0},
        )(*operands)

    from_below, from_above = pairs, pairs
    state = None
    arrived = [pairs]
    sources = [(0, 0)]
    for distance in range(1, 6):
        with jax.named_scope("ring"):
            if distance < 4:
                from_below = lax.ppermute(from_below, RING, up)
                from_above = lax.ppermute(from_above, RING, down)
            elif distance == 4:
                from_below = lax.ppermute(from_below[:2], RING, up)
                from_above = lax.ppermute(from_above[2:], RING, down)
        with jax.named_scope("attend"):
            state = step(arrived, tuple(sources), state)
        arrived = [from_below, from_above]
        sources = [(-distance, 0), (distance, 0 if distance < 4 else 2)]
    with jax.named_scope("swap_terms"):
        theirs = swap(state[:, :, ROWS:])
    with jax.named_scope("join"):
        attended = call(
            join,
            jax.ShapeDtypeStruct((heads, SLICE, HD), bf16),
            [smem, vmem, vmem],
        )(lengths, state, theirs)
    with jax.named_scope("heads_to_tokens"):
        attended = lax.all_to_all(attended, ("y", "x"), 0, 0, tiled=True)
    with jax.named_scope("unpack"):
        out = call(unpack, jax.ShapeDtypeStruct((SLICE, heads * HD), bf16), [vmem])(attended)
    return out[None]


def solution(mesh):
    fine = Mesh(mesh.devices.reshape(2, 4, 2, 4, 4), ("zlo", "y", "core", "x", "zhi"))
    span, seq = ("zlo", "y", "core"), ("x", "zhi")
    return jax.shard_map(
        shards,
        mesh=fine,
        in_specs=(P(None, span, seq, None), P()),
        out_specs=P(span, seq, None),
        check_vma=False,
    )
```

time: 103 us -> 96.5 us (0.937)
  the two profiles are of different devices: /device:TPU:96 before, /device:TPU:1 now
where the time goes in v2:
time: 96.5 us; the launch traced here: 96.3 us
  blocking collectives  31.6 us (33%)
  waiting for transfers between devices  30.1 us (31%)
  starting transfers between devices  19.3 us (20%)
  Pallas kernels  13.9 us (14%)
  local copies, waits for them, and re-layouts  1.22 us (1%)
    ppermute x3, waiting for transfers between devices, shards(): from_below = lax.ppermute(from_below, RING, up)  25.5 us
    all_to_all x1, blocking collectives, shards(): parts = lax.all_to_all(parts, ('y', 'x'), 0, 0, tiled=True)  20.9 us
    pallas_call x5, Pallas kernels, step(): call(functools.partial(attend, sources, first), state_shape, [smem] + [vm...  12.2 us
    all_to_all x1, blocking collectives, shards(): attended = lax.all_to_all(attended, ('y', 'x'), 0, 0, tiled=True)  10.7 us
    ppermute x3, starting transfers between devices, shards(): from_above = lax.ppermute(from_above, RING, down)  9.28 us
    ppermute x2, starting transfers between devices, swap(): return lax.ppermute(block, 'core', [(0, 1), (1, 0)])  5.58 us
    ppermute x1, waiting for transfers between devices, shards(): from_below = lax.ppermute(from_below[:2], RING, up)  2.94 us
    ppermute x1, starting transfers between devices, shards(): from_above = lax.ppermute(from_above[2:], RING, down)  2.73 us
  transfers between devices with their start and end apart: 10, of which 5 were waited for; matrix products, arithmetic and copies ran while one was open for 0% of the time, Pallas kernels for 9%

profile of v2, /device:TPU:1, one launch (start us, length us, event | category | flops | bytes accessed | tf_op | source)
XLA Modules:
  0.0 96.3 jit_solution(4745610306311939928)
XLA Ops:
  0.0 0.0 copy-start
  0.0 1.1 %copy-done = bf16[3,1,64,2048]{3,2,1,0:T(8,128)(2,1)S(1)} copy-done((bf16[3,1,64,2048]{3,2,1,0:T(8,128)(2,1)S(1)}, bf16[3,1,64,2048]{3,2,1,0:T(8,128)(2,1)}, u32[]{:S(2)}) %copy-start) | copy-done | bytes 786456
  1.1 0.1 pack.1
  1.3 0.0 copy-start.1
  1.3 20.9 %all_to_all.10.parts_ref = bf16[16,192,128]{2,1,0:T(8,128)(2,1)S(1)} all-to-all(bf16[16,192,128]{2,1,0:T(8,128)(2,1)S(1)} %pack.1), channel_id=1, replica_groups=mesh['zlo'=2,'y'=4,'core'=2,'x'=4,'zhi'=4] {'y','x'}, dimensions={0} | all-to-all | bytes 1572864 | tf_op jit(solution)/shard_map/tokens_to_heads/all_to_all | solution.py:165
  22.2 0.1 split.1
  22.3 1.9 %collective-permute-start = (bf16[4,256,128]{2,1,0:T(8,128)(2,1)S(1)}, bf16[4,256,128]{2,1,0:T(8,128)(2,1)S(1)}, u32[]{:S(2)}, u32[]{:S(2)}) collective-permute-start(bf16[4,256,128]{2,1,0:T(8,128)(2,1)S(1)} %get-tuple-element.7.refs_1_), channel_id=1, source_target_pairs={{0,16},{16,0},{1,17},{17,1},{2,18},{18,2},{3,19},{19,3},{4,20},{20... | collective-permute-start | bytes 786440 | tf_op jit(solution)/shard_map/swap_queries/ppermute | solution.py:182
  24.2 1.7 %collective-permute-start.1 = (bf16[4,512,128]{2,1,0:T(8,128)(2,1)S(1)}, bf16[4,512,128]{2,1,0:T(8,128)(2,1)S(1)}, u32[]{:S(2)}, u32[]{:S(2)}) collective-permute-start(bf16[4,512,128]{2,1,0:T(8,128)(2,1)S(1)} %get-tuple-element.8.refs_3_), channel_id=1, source_target_pairs={{0,128},{128,1},{1,129},{129,2},{2,130},{130,3},{3,131},{131,0},{4... | collective-permute-start | bytes 1572872 | tf_op jit(solution)/shard_map/ring/ppermute | solution.py:208
  25.8 3.9 %collective-permute-start.5 = (bf16[4,512,128]{2,1,0:T(8,128)(2,1)S(1)}, bf16[4,512,128]{2,1,0:T(8,128)(2,1)S(1)}, u32[]{:S(2)}, u32[]{:S(2)}) collective-permute-start(bf16[4,512,128]{2,1,0:T(8,128)(2,1)S(1)} %get-tuple-element.8.refs_3_), channel_id=1, source_target_pairs={{0,131},{128,0},{1,128},{129,1},{2,129},{130,2},{3,130},{131,3},{4... | collective-permute-start | bytes 1572872 | tf_op jit(solution)/shard_map/ring/ppermute | solution.py:209
  29.8 0.0 collective-permute-done.refs_2_
  29.8 0.0 copy-done.1
  29.8 3.0 %attend.5.refs_5_ = f32[4,144,512]{2,1,0:T(8,128)S(1)} custom-call(s32[16]{0:T(128)S(1)} %copy-done.1, bf16[4,256,128]{2,1,0:T(8,128)(2,1)S(1)} %get-tuple-element.7.refs_1_, bf16[4,256,128]{2,1,0:T(8,128)(2,1)S(1)} %collective-permute-done.refs_2_, bf16[4,512,128]{2,1,0:T(8,128)(2,1)S(1)} %get-tuple-element.8.refs_3_), custom_call_target="tpu_custom_call" | custom-call | flops 4294967296 | bytes 8388608 | tf_op jit(solution)/shard_map/attend/pallas_call | solution.py:192
  32.7 9.2 %collective-permute-done.1.refs_3_ = bf16[4,512,128]{2,1,0:T(8,128)(2,1)S(1)} collective-permute-done((bf16[4,512,128]{2,1,0:T(8,128)(2,1)S(1)}, bf16[4,512,128]{2,1,0:T(8,128)(2,1)S(1)}, u32[]{:S(2)}, u32[]{:S(2)}) %collective-permute-start.1) | collective-permute-done | bytes 524320 | tf_op jit(solution)/shard_map/ring/ppermute | solution.py:208
  42.0 0.0 collective-permute-start.2
  42.0 0.0 collective-permute-done.5.refs_4_
  42.0 2.7 %collective-permute-start.6 = (bf16[4,512,128]{2,1,0:T(8,128)(2,1)S(1)}, bf16[4,512,128]{2,1,0:T(8,128)(2,1)S(1)}, u32[]{:S(2)}, u32[]{:S(2)}) collective-permute-start(bf16[4,512,128]{2,1,0:T(8,128)(2,1)S(1)} %collective-permute-done.5.refs_4_), channel_id=1, source_target_pairs={{0,131},{128,0},{1,128},{129,1},{2,129},{130,2},{3,130},{131,3},{4... | collective-permute-start | bytes 1572872 | tf_op jit(solution)/shard_map/ring/ppermute | solution.py:209
  44.6 0.7 attend.6.refs_5_
  45.4 10.6 %collective-permute-done.2.refs_3_ = bf16[4,512,128]{2,1,0:T(8,128)(2,1)S(1)} collective-permute-done((bf16[4,512,128]{2,1,0:T(8,128)(2,1)S(1)}, bf16[4,512,128]{2,1,0:T(8,128)(2,1)S(1)}, u32[]{:S(2)}, u32[]{:S(2)}) %collective-permute-start.2) | collective-permute-done | bytes 524320 | tf_op jit(solution)/shard_map/ring/ppermute | solution.py:208
  56.0 0.0 collective-permute-start.3
  56.0 0.0 collective-permute-done.6.refs_4_
  56.0 2.7 %collective-permute-start.7 = (bf16[4,512,128]{2,1,0:T(8,128)(2,1)S(1)}, bf16[4,512,128]{2,1,0:T(8,128)(2,1)S(1)}, u32[]{:S(2)}, u32[]{:S(2)}) collective-permute-start(bf16[4,512,128]{2,1,0:T(8,128)(2,1)S(1)} %collective-permute-done.6.refs_4_), channel_id=1, source_target_pairs={{0,131},{128,0},{1,128},{129,1},{2,129},{130,2},{3,130},{131,3},{4... | collective-permute-start | bytes 1572872 | tf_op jit(solution)/shard_map/ring/ppermute | solution.py:209
  58.7 4.7 %attend.7.refs_5_ = f32[4,144,512]{2,1,0:T(8,128)S(1)} custom-call(s32[16]{0:T(128)S(1)} %copy-done.1, bf16[4,256,128]{2,1,0:T(8,128)(2,1)S(1)} %get-tuple-element.7.refs_1_, bf16[4,256,128]{2,1,0:T(8,128)(2,1)S(1)} %collective-permute-done.refs_2_, bf16[4,512,128]{2,1,0:T(8,128)(2,1)S(1)} %collective-permute-done.2.refs_3_, ...), custom_call_target="tpu_custom_call", output_to_operand_aliasing={{}: (5, {})} | custom-call | flops 8589934592 | bytes 8388608 | tf_op jit(solution)/shard_map/attend/pallas_call | solution.py:192
  63.4 5.7 %collective-permute-done.3.refs_3_ = bf16[4,512,128]{2,1,0:T(8,128)(2,1)S(1)} collective-permute-done((bf16[4,512,128]{2,1,0:T(8,128)(2,1)S(1)}, bf16[4,512,128]{2,1,0:T(8,128)(2,1)S(1)}, u32[]{:S(2)}, u32[]{:S(2)}) %collective-permute-start.3) | collective-permute-done | bytes 524320 | tf_op jit(solution)/shard_map/ring/ppermute | solution.py:208
  69.1 0.1 collective-permute-start.4
  69.2 0.0 collective-permute-done.7.refs_4_
  69.2 2.7 %collective-permute-start.8 = (bf16[2,512,128]{2,1,0:T(8,128)(2,1)S(1)}, bf16[2,512,128]{2,1,0:T(8,128)(2,1)S(1)}, u32[]{:S(2)}, u32[]{:S(2)}) collective-permute-start(bf16[2,512,128]{2,1,0:T(8,128)(2,1)S(1)} %slice.13), channel_id=1, source_target_pairs={{0,131},{128,0},{1,128},{129,1},{2,129},{130,2},{3,130},{131,3},{4... | collective-permute-start | bytes 786440 | tf_op jit(solution)/shard_map/ring/ppermute | solution.py:212
  71.9 0.7 attend.8.refs_5_
  72.7 2.9 %collective-permute-done.4.refs_3_ = bf16[2,512,128]{2,1,0:T(8,128)(2,1)S(1)} collective-permute-done((bf16[2,512,128]{2,1,0:T(8,128)(2,1)S(1)}, bf16[2,512,128]{2,1,0:T(8,128)(2,1)S(1)}, u32[]{:S(2)}, u32[]{:S(2)}) %collective-permute-start.4) | collective-permute-done | bytes 262176 | tf_op jit(solution)/shard_map/ring/ppermute | solution.py:211
  75.6 0.0 collective-permute-done.8.refs_4_
  75.6 3.1 %attend.9.own_ref = f32[4,144,512]{2,1,0:T(8,128)S(1)} custom-call(s32[16]{0:T(128)S(1)} %copy-done.1, bf16[4,256,128]{2,1,0:T(8,128)(2,1)S(1)} %get-tuple-element.7.refs_1_, bf16[4,256,128]{2,1,0:T(8,128)(2,1)S(1)} %collective-permute-done.refs_2_, bf16[2,512,128]{2,1,0:T(8,128)(2,1)S(1)} %collective-permute-done.4.refs_3_, ...), custom_call_target="tpu_custom_call", output_to_operand_aliasing={{}: (5, {})} | custom-call | flops 4294967296 | bytes 8388608 | tf_op jit(solution)/shard_map/attend/pallas_call | solution.py:192
  78.7 3.7 %collective-permute-start.9 = (f32[4,144,256]{2,1,0:T(8,128)S(1)}, f32[4,144,256]{2,1,0:T(8,128)S(1)}, u32[]{:S(2)}, u32[]{:S(2)}) collective-permute-start(f32[4,144,256]{2,1,0:T(8,128)S(1)} %slice.14), channel_id=1, source_target_pairs={{0,16},{16,0},{1,17},{17,1},{2,18},{18,2},{3,19},{19,3},{4,20},{20... | collective-permute-start | bytes 1769480 | tf_op jit(solution)/shard_map/swap_terms/ppermute | solution.py:182
  82.4 1.6 %collective-permute-done.9.other_ref = f32[4,144,256]{2,1,0:T(8,128)S(1)} collective-permute-done((f32[4,144,256]{2,1,0:T(8,128)S(1)}, f32[4,144,256]{2,1,0:T(8,128)S(1)}, u32[]{:S(2)}, u32[]{:S(2)}) %collective-permute-start.9) | collective-permute-done | bytes 589856 | tf_op jit(solution)/shard_map/swap_terms/ppermute | solution.py:182
  84.1 0.7 join.1
  84.8 10.7 %all_to_all.11.parts_ref = bf16[16,64,128]{2,1,0:T(8,128)(2,1)S(1)} all-to-all(bf16[16,64,128]{2,1,0:T(8,128)(2,1)S(1)} %join.1), channel_id=1, replica_groups=mesh['zlo'=2,'y'=4,'core'=2,'x'=4,'zhi'=4] {'y','x'}, dimensions={0} | all-to-all | bytes 524288 | tf_op jit(solution)/shard_map/heads_to_tokens/all_to_all | solution.py:226
  95.5 0.8 unpack.1
  (3 shorter events, 0.1 us)
Async XLA Ops:
  0.0 1.1 %copy-start = (bf16[3,1,64,2048]{3,2,1,0:T(8,128)(2,1)S(1)}, bf16[3,1,64,2048]{3,2,1,0:T(8,128)(2,1)}, u32[]{:S(2)}) copy-start(bf16[3,1,64,2048]{3,2,1,0:T(8,128)(2,1)} %param.2) | copy-start | bytes 2359300
  1.3 28.5 %copy-start.1 = (s32[16]{0:T(128)S(1)}, s32[16]{0:T(128)}, u32[]{:S(2)}) copy-start(s32[16]{0:T(128)} %lengths_ref.1) | copy-start | bytes 196
  22.3 7.5 %collective-permute-start = (bf16[4,256,128]{2,1,0:T(8,128)(2,1)S(1)}, bf16[4,256,128]{2,1,0:T(8,128)(2,1)S(1)}, u32[]{:S(2)}, u32[]{:S(2)}) collective-permute-start(bf16[4,256,128]{2,1,0:T(8,128)(2,1)S(1)} %get-tuple-element.7.refs_1_), channel_id=1, source_target_pairs={{0,16},{16,0},{1,17},{17,1},{2,18},{18,2},{3,19},{19,3},{4,20},{20... | collective-permute-start | bytes 786440 | tf_op jit(solution)/shard_map/swap_queries/ppermute | solution.py:182
  24.2 17.8 %collective-permute-start.1 = (bf16[4,512,128]{2,1,0:T(8,128)(2,1)S(1)}, bf16[4,512,128]{2,1,0:T(8,128)(2,1)S(1)}, u32[]{:S(2)}, u32[]{:S(2)}) collective-permute-start(bf16[4,512,128]{2,1,0:T(8,128)(2,1)S(1)} %get-tuple-element.8.refs_3_), channel_id=1, source_target_pairs={{0,128},{128,1},{1,129},{129,2},{2,130},{130,3},{3,131},{131,0},{4... | collective-permute-start | bytes 1572872 | tf_op jit(solution)/shard_map/ring/ppermute | solution.py:208
  25.8 16.1 %collective-permute-start.5 = (bf16[4,512,128]{2,1,0:T(8,128)(2,1)S(1)}, bf16[4,512,128]{2,1,0:T(8,128)(2,1)S(1)}, u32[]{:S(2)}, u32[]{:S(2)}) collective-permute-start(bf16[4,512,128]{2,1,0:T(8,128)(2,1)S(1)} %get-tuple-element.8.refs_3_), channel_id=1, source_target_pairs={{0,131},{128,0},{1,128},{129,1},{2,129},{130,2},{3,130},{131,3},{4... | collective-permute-start | bytes 1572872 | tf_op jit(solution)/shard_map/ring/ppermute | solution.py:209
  42.0 14.0 %collective-permute-start.2 = (bf16[4,512,128]{2,1,0:T(8,128)(2,1)S(1)}, bf16[4,512,128]{2,1,0:T(8,128)(2,1)S(1)}, u32[]{:S(2)}, u32[]{:S(2)}) collective-permute-start(bf16[4,512,128]{2,1,0:T(8,128)(2,1)S(1)} %collective-permute-done.1.refs_3_), channel_id=1, source_target_pairs={{0,128},{128,1},{1,129},{129,2},{2,130},{130,3},{3,131},{131,0},{4... | collective-permute-start | bytes 1572872 | tf_op jit(solution)/shard_map/ring/ppermute | solution.py:208
  42.0 14.0 %collective-permute-start.6 = (bf16[4,512,128]{2,1,0:T(8,128)(2,1)S(1)}, bf16[4,512,128]{2,1,0:T(8,128)(2,1)S(1)}, u32[]{:S(2)}, u32[]{:S(2)}) collective-permute-start(bf16[4,512,128]{2,1,0:T(8,128)(2,1)S(1)} %collective-permute-done.5.refs_4_), channel_id=1, source_target_pairs={{0,131},{128,0},{1,128},{129,1},{2,129},{130,2},{3,130},{131,3},{4... | collective-permute-start | bytes 1572872 | tf_op jit(solution)/shard_map/ring/ppermute | solution.py:209
  56.0 13.1 %collective-permute-start.3 = (bf16[4,512,128]{2,1,0:T(8,128)(2,1)S(1)}, bf16[4,512,128]{2,1,0:T(8,128)(2,1)S(1)}, u32[]{:S(2)}, u32[]{:S(2)}) collective-permute-start(bf16[4,512,128]{2,1,0:T(8,128)(2,1)S(1)} %collective-permute-done.2.refs_3_), channel_id=1, source_target_pairs={{0,128},{128,1},{1,129},{129,2},{2,130},{130,3},{3,131},{131,0},{4... | collective-permute-start | bytes 1572872 | tf_op jit(solution)/shard_map/ring/ppermute | solution.py:208
  56.0 13.2 %collective-permute-start.7 = (bf16[4,512,128]{2,1,0:T(8,128)(2,1)S(1)}, bf16[4,512,128]{2,1,0:T(8,128)(2,1)S(1)}, u32[]{:S(2)}, u32[]{:S(2)}) collective-permute-start(bf16[4,512,128]{2,1,0:T(8,128)(2,1)S(1)} %collective-permute-done.6.refs_4_), channel_id=1, source_target_pairs={{0,131},{128,0},{1,128},{129,1},{2,129},{130,2},{3,130},{131,3},{4... | collective-permute-start | bytes 1572872 | tf_op jit(solution)/shard_map/ring/ppermute | solution.py:209
  69.1 6.5 %collective-permute-start.4 = (bf16[2,512,128]{2,1,0:T(8,128)(2,1)S(1)}, bf16[2,512,128]{2,1,0:T(8,128)(2,1)S(1)}, u32[]{:S(2)}, u32[]{:S(2)}) collective-permute-start(bf16[2,512,128]{2,1,0:T(8,128)(2,1)S(1)} %slice.12), channel_id=1, source_target_pairs={{0,128},{128,1},{1,129},{129,2},{2,130},{130,3},{3,131},{131,0},{4... | collective-permute-start | bytes 786440 | tf_op jit(solution)/shard_map/ring/ppermute | solution.py:211
  69.2 6.4 %collective-permute-start.8 = (bf16[2,512,128]{2,1,0:T(8,128)(2,1)S(1)}, bf16[2,512,128]{2,1,0:T(8,128)(2,1)S(1)}, u32[]{:S(2)}, u32[]{:S(2)}) collective-permute-start(bf16[2,512,128]{2,1,0:T(8,128)(2,1)S(1)} %slice.13), channel_id=1, source_target_pairs={{0,131},{128,0},{1,128},{129,1},{2,129},{130,2},{3,130},{131,3},{4... | collective-permute-start | bytes 786440 | tf_op jit(solution)/shard_map/ring/ppermute | solution.py:212
  78.7 5.3 %collective-permute-start.9 = (f32[4,144,256]{2,1,0:T(8,128)S(1)}, f32[4,144,256]{2,1,0:T(8,128)S(1)}, u32[]{:S(2)}, u32[]{:S(2)}) collective-permute-start(f32[4,144,256]{2,1,0:T(8,128)S(1)} %slice.14), channel_id=1, source_target_pairs={{0,16},{16,0},{1,17},{17,1},{2,18},{18,2},{3,19},{19,3},{4,20},{20... | collective-permute-start | bytes 1769480 | tf_op jit(solution)/shard_map/swap_terms/ppermute | solution.py:182

commit v3 on v2

--- a/solution.py
+++ b/solution.py
@@ -31,39 +31,34 @@
         out_ref[:, head * HD : (head + 1) * HD] = parts_ref[head]
 
 
-def split(parts_ref, query_ref, pair_ref):
+def split(parts_ref, query_ref, key_ref, value_ref):
     for span in range(4):
         block = parts_ref.at[4 * span : 4 * span + 4]
         query_ref[span] = block[:, :SLICE, :].reshape(ROWS, HD)
-        pair_ref[span, :ROWS] = block[:, SLICE : 2 * SLICE, :].reshape(ROWS, HD)
+        key_ref[span] = block[:, SLICE : 2 * SLICE, :].reshape(ROWS, HD)
         turned = block[:, 2 * SLICE :, :].reshape(ROWS, HD).T
-        pair_ref[span, ROWS : ROWS + HD] = turned[:, :HD]
-        pair_ref[span, ROWS + HD :] = turned[:, HD:]
+        value_ref[span, :HD] = turned[:, :HD]
+        value_ref[span, HD:] = turned[:, HD:]
 
 
 def attend(sources, first, *refs):
     refs = list(refs)
     lengths_ref, own_ref, other_ref = refs[:3]
-    arrivals = refs[3 : 3 + len(sources)]
-    before_ref = None if first else refs[3 + len(sources)]
+    key_refs = refs[3 : 3 + len(sources)]
+    value_refs = refs[3 + len(sources) : 3 + 2 * len(sources)]
+    before_ref = None if first else refs[-2]
     state_ref = refs[-1]
     core = lax.axis_index("core")
     zlo = lax.axis_index("zlo")
     zed = lax.axis_index("zhi") * 2 + zlo
     pieces = []
     for number, (distance, begin) in enumerate(sources):
-        for place in range(arrivals[number].shape[0]):
+        for place in range(key_refs[number].shape[0]):
             pieces.append((place + begin, number, place))
     pieces.sort()
     source_zed = [lax.rem(zed + 8 + distance, 8) for distance, _ in sources]
     source_zlo = lax.rem(source_zed[0], 2)
     aligned = sources[0][0] % 2 == 0
-
-    if first:
-        state_ref[:, : HD + 8] = jnp.zeros_like(state_ref[:, : HD + 8])
-        state_ref[:, HD + 8 :] = jnp.full_like(state_ref[:, HD + 8 :], FILL)
-    else:
-        state_ref[...] = before_ref[...]
 
     ones = jnp.where(lax.broadcasted_iota(jnp.int32, (16, ROWS), 0) < 8, 1.0, 0.0)
     ones = ones.astype(jnp.bfloat16)
@@ -74,9 +69,11 @@
         for span, number, place in pieces:
             if span >= count:
                 continue
-            block = arrivals[number].at[place]
             score = lax.dot_general(
-                block[:ROWS, :], queries, (((1,), (1,)), ((), ())), preferred_element_type=jnp.float32
+                key_refs[number][place],
+                queries,
+                (((1,), (1,)), ((), ())),
+                preferred_element_type=jnp.float32,
             )
             live = lengths_ref[source_zlo * 8 + 2 * span + core]
             offset = (source_zed[number] // 2) * SLICE
@@ -91,11 +88,14 @@
                 elif part >= 2:
                     rows = jnp.where(row < bound, rows, FILL)
                 scores.append(rows)
-            turned = jnp.concatenate([block[ROWS : ROWS + HD, :], block[ROWS + HD :, :]], axis=1)
+            block = value_refs[number].at[place]
+            turned = jnp.concatenate([block[:HD, :], block[HD:, :]], axis=1)
             values.append(jnp.concatenate([turned, ones], axis=0))
         scores = jnp.concatenate(scores, axis=0)
-        old_peak = state_ref[step, HD + 8 : HD + 9, :]
-        peak = jnp.maximum(old_peak, jnp.max(scores, axis=0, keepdims=True))
+        peak = jnp.max(scores, axis=0, keepdims=True)
+        if not first:
+            old_peak = before_ref[step, HD + 8 : HD + 9, :]
+            peak = jnp.maximum(old_peak, peak)
         shifted = (scores - peak) * SCALE
         weights = jnp.exp2(shifted)
         if last == 0:
@@ -104,8 +104,11 @@
         fresh = jnp.dot(
             jnp.concatenate(values, axis=1), weights, preferred_element_type=jnp.float32
         )
-        keep = jnp.exp2((old_peak - peak) * SCALE)
-        state_ref[step, : HD + 8, :] = state_ref[step, : HD + 8, :] * keep + fresh[: HD + 8]
+        fresh = fresh[: HD + 8]
+        if not first:
+            keep = jnp.exp2((old_peak - peak) * SCALE)
+            fresh = before_ref[step, : HD + 8, :] * keep + fresh
+        state_ref[step, : HD + 8, :] = fresh
         state_ref[step, HD + 8 :, :] = jnp.broadcast_to(peak, (8, 2 * ROWS))
 
     if aligned:
@@ -118,6 +121,10 @@
             @pl.loop(0, 4)
             def _(step):
                 add(step, 4, -1)
+
+        @pl.when(source_zlo > zlo)
+        def _():
+            state_ref[...] = before_ref[...]
 
 
 def join(lengths_ref, own_ref, other_ref, out_ref):
@@ -164,14 +171,7 @@
     with jax.named_scope("tokens_to_heads"):
         parts = lax.all_to_all(parts, ("y", "x"), 0, 0, tiled=True)
     with jax.named_scope("split"):
-        own, pairs = call(
-            split,
-            [
-                jax.ShapeDtypeStruct((4, ROWS, HD), bf16),
-                jax.ShapeDtypeStruct((4, 2 * ROWS, HD), bf16),
-            ],
-            [vmem],
-        )(parts)
+        own, keys, values = call(split, [jax.ShapeDtypeStruct((4, ROWS, HD), bf16)] * 3, [vmem])(parts)
 
     chips = 8
     place = [z % 2 * 4 + z // 2 for z in range(chips)]
@@ -185,10 +185,10 @@
         other = swap(own)
     state_shape = jax.ShapeDtypeStruct((4, STATE, 2 * ROWS), jnp.float32)
 
-    def step(arrivals, sources, state):
+    def step(keys, values, sources, state):
         first = state is None
-        operands = [lengths, own, other] + arrivals + ([] if first else [state])
-        count = sum(a.shape[0] for a in arrivals)
+        operands = [lengths, own, other] + keys + values + ([] if first else [state])
+        count = sum(a.shape[0] for a in keys)
         return call(
             functools.partial(attend, sources, first),
             state_shape,
@@ -198,21 +198,23 @@
             input_output_aliases={} if first else {len(operands) - 1: 0},
         )(*operands)
 
-    from_below, from_above = pairs, pairs
+    def hop(pair, distance):
+        below, above = pair
+        if distance == 4:
+            below, above = below[:2], above[2:]
+        return [lax.ppermute(below, RING, up), lax.ppermute(above, RING, down)]
+
     state = None
-    arrived = [pairs]
+    held = ([keys], [values])
+    moving = ([keys, keys], [values, values])
     sources = [(0, 0)]
     for distance in range(1, 6):
-        with jax.named_scope("ring"):
-            if distance < 4:
-                from_below = lax.ppermute(from_below, RING, up)
-                from_above = lax.ppermute(from_above, RING, down)
-            elif distance == 4:
-                from_below = lax.ppermute(from_below[:2], RING, up)
-                from_above = lax.ppermute(from_above[2:], RING, down)
+        if distance < 5:
+            with jax.named_scope("ring"):
+                moving = tuple(hop(pair, distance) for pair in moving)
         with jax.named_scope("attend"):
-            state = step(arrived, tuple(sources), state)
-        arrived = [from_below, from_above]
+            state = step(*held, tuple(sources), state)
+        held = moving
         sources = [(-distance, 0), (distance, 0 if distance < 4 else 2)]
     with jax.named_scope("swap_terms"):
         theirs = swap(state[:, :, ROWS:])

time: 96.5 us -> 93 us (0.964)
  waiting for transfers between devices: 30.1 us -> 5.66 us
  starting transfers between devices: 19.3 us -> 39.2 us
    ppermute x8 -> x16, waiting for transfers between devices: 28.4 us -> 4.03 us  [hop(): return [lax.ppermute(below, RING, up), lax.ppermute(above, RING, down)]]
    ppermute x8 -> x16, starting transfers between devices: 13.7 us -> 28.5 us  [hop(): return [lax.ppermute(below, RING, up), lax.ppermute(above, RING, down)]]
    ppermute x2, starting transfers between devices: 5.58 us -> 10.7 us  [swap(): return lax.ppermute(block, 'core', [(0, 1), (1, 0)])]
  transfers between devices with their start and end apart: 10 -> 18, of which waited for: 5 -> 4; matrix products, arithmetic and copies ran while one was open for 0% -> 0% of each run, Pallas kernels for 9% -> 10%
where the time goes in v3:
time: 93 us; the launch traced here: 91.9 us
  starting transfers between devices  39.2 us (42%)
  blocking collectives  31.6 us (34%)
  Pallas kernels  14 us (15%)
  waiting for transfers between devices  5.66 us (6%)
  local copies, waits for them, and re-layouts  1.22 us (1%)
    ppermute x16, starting transfers between devices, hop(): return [lax.ppermute(below, RING, up), lax.ppermute(above, RING, down)]  28.5 us
    all_to_all x1, blocking collectives, shards(): parts = lax.all_to_all(parts, ('y', 'x'), 0, 0, tiled=True)  20.9 us
    pallas_call x5, Pallas kernels, step(): call(functools.partial(attend, sources, first), state_shape, [smem] + [vm...  12.3 us
    all_to_all x1, blocking collectives, shards(): attended = lax.all_to_all(attended, ('y', 'x'), 0, 0, tiled=True)  10.7 us
    ppermute x2, starting transfers between devices, swap(): return lax.ppermute(block, 'core', [(0, 1), (1, 0)])  10.7 us
    ppermute x16, waiting for transfers between devices, hop(): return [lax.ppermute(below, RING, up), lax.ppermute(above, RING, down)]  4.03 us
  transfers between devices with their start and end apart: 18, of which 4 were waited for; matrix products, arithmetic and copies ran while one was open for 0% of the time, Pallas kernels for 10%

profile of v3, /device:TPU:1, one launch (start us, length us, event | category | flops | bytes accessed | tf_op | source)
XLA Modules:
  0.0 91.9 jit_solution(3424617991098983466)
XLA Ops:
  0.0 1.1 %copy-done = bf16[3,1,64,2048]{3,2,1,0:T(8,128)(2,1)S(1)} copy-done((bf16[3,1,64,2048]{3,2,1,0:T(8,128)(2,1)S(1)}, bf16[3,1,64,2048]{3,2,1,0:T(8,128)(2,1)}, u32[]{:S(2)}) %copy-start) | copy-done | bytes 786456
  1.1 0.1 pack.1
  1.3 0.0 copy-start.1
  1.3 20.9 %all_to_all.10.parts_ref = bf16[16,192,128]{2,1,0:T(8,128)(2,1)S(1)} all-to-all(bf16[16,192,128]{2,1,0:T(8,128)(2,1)S(1)} %pack.1), channel_id=1, replica_groups=mesh['zlo'=2,'y'=4,'core'=2,'x'=4,'zhi'=4] {'y','x'}, dimensions={0} | all-to-all | bytes 1572864 | tf_op jit(solution)/shard_map/tokens_to_heads/all_to_all | solution.py:172
  22.2 0.1 split.1
  22.3 1.7 %collective-permute-start.9 = (bf16[4,256,128]{2,1,0:T(8,128)(2,1)S(1)}, bf16[4,256,128]{2,1,0:T(8,128)(2,1)S(1)}, u32[]{:S(2)}, u32[]{:S(2)}) collective-permute-start(bf16[4,256,128]{2,1,0:T(8,128)(2,1)S(1)} %get-tuple-element.10.refs_4_), channel_id=1, source_target_pairs={{0,128},{128,1},{1,129},{129,2},{2,130},{130,3},{3,131},{131,0},{4... | collective-permute-start | bytes 786440 | tf_op jit(solution)/shard_map/ring/ppermute | solution.py:205
  24.0 4.0 %collective-permute-start.13 = (bf16[4,256,128]{2,1,0:T(8,128)(2,1)S(1)}, bf16[4,256,128]{2,1,0:T(8,128)(2,1)S(1)}, u32[]{:S(2)}, u32[]{:S(2)}) collective-permute-start(bf16[4,256,128]{2,1,0:T(8,128)(2,1)S(1)} %get-tuple-element.10.refs_4_), channel_id=1, source_target_pairs={{0,131},{128,0},{1,128},{129,1},{2,129},{130,2},{3,130},{131,3},{4... | collective-permute-start | bytes 786440 | tf_op jit(solution)/shard_map/ring/ppermute | solution.py:205
  28.0 0.0 collective-permute-start.1
  28.0 2.7 %collective-permute-start.5 = (bf16[4,256,128]{2,1,0:T(8,128)(2,1)S(1)}, bf16[4,256,128]{2,1,0:T(8,128)(2,1)S(1)}, u32[]{:S(2)}, u32[]{:S(2)}) collective-permute-start(bf16[4,256,128]{2,1,0:T(8,128)(2,1)S(1)} %get-tuple-element.9.refs_3_), channel_id=1, source_target_pairs={{0,131},{128,0},{1,128},{129,1},{2,129},{130,2},{3,130},{131,3},{4... | collective-permute-start | bytes 786440 | tf_op jit(solution)/shard_map/ring/ppermute | solution.py:205
  30.7 2.6 %collective-permute-start = (bf16[4,256,128]{2,1,0:T(8,128)(2,1)S(1)}, bf16[4,256,128]{2,1,0:T(8,128)(2,1)S(1)}, u32[]{:S(2)}, u32[]{:S(2)}) collective-permute-start(bf16[4,256,128]{2,1,0:T(8,128)(2,1)S(1)} %get-tuple-element.8.refs_1_), channel_id=1, source_target_pairs={{0,16},{16,0},{1,17},{17,1},{2,18},{18,2},{3,19},{19,3},{4,20},{20... | collective-permute-start | bytes 786440 | tf_op jit(solution)/shard_map/swap_queries/ppermute | solution.py:182
  33.4 0.0 collective-permute-done.9.refs_5_
  33.4 0.0 collective-permute-start.10
  33.4 0.0 collective-permute-done.13.refs_6_
  33.4 2.7 %collective-permute-start.14 = (bf16[4,256,128]{2,1,0:T(8,128)(2,1)S(1)}, bf16[4,256,128]{2,1,0:T(8,128)(2,1)S(1)}, u32[]{:S(2)}, u32[]{:S(2)}) collective-permute-start(bf16[4,256,128]{2,1,0:T(8,128)(2,1)S(1)} %collective-permute-done.13.refs_6_), channel_id=1, source_target_pairs={{0,131},{128,0},{1,128},{129,1},{2,129},{130,2},{3,130},{131,3},{4... | collective-permute-start | bytes 786440 | tf_op jit(solution)/shard_map/ring/ppermute | solution.py:205
  36.0 2.3 %collective-permute-done.1.refs_3_ = bf16[4,256,128]{2,1,0:T(8,128)(2,1)S(1)} collective-permute-done((bf16[4,256,128]{2,1,0:T(8,128)(2,1)S(1)}, bf16[4,256,128]{2,1,0:T(8,128)(2,1)S(1)}, u32[]{:S(2)}, u32[]{:S(2)}) %collective-permute-start.1) | collective-permute-done | bytes 262176 | tf_op jit(solution)/shard_map/ring/ppermute | solution.py:205
  38.4 0.0 collective-permute-start.2
  38.4 0.0 collective-permute-done.5.refs_4_
  38.4 2.7 %collective-permute-start.6 = (bf16[4,256,128]{2,1,0:T(8,128)(2,1)S(1)}, bf16[4,256,128]{2,1,0:T(8,128)(2,1)S(1)}, u32[]{:S(2)}, u32[]{:S(2)}) collective-permute-start(bf16[4,256,128]{2,1,0:T(8,128)(2,1)S(1)} %collective-permute-done.5.refs_4_), channel_id=1, source_target_pairs={{0,131},{128,0},{1,128},{129,1},{2,129},{130,2},{3,130},{131,3},{4... | collective-permute-start | bytes 786440 | tf_op jit(solution)/shard_map/ring/ppermute | solution.py:205
  41.1 0.0 collective-permute-done.refs_2_
  41.1 3.0 %attend.5.refs_7_ = f32[4,144,512]{2,1,0:T(8,128)S(1)} custom-call(s32[16]{0:T(128)S(1)} %copy-done.1, bf16[4,256,128]{2,1,0:T(8,128)(2,1)S(1)} %get-tuple-element.8.refs_1_, bf16[4,256,128]{2,1,0:T(8,128)(2,1)S(1)} %collective-permute-done.refs_2_, bf16[4,256,128]{2,1,0:T(8,128)(2,1)S(1)} %get-tuple-element.9.refs_3_, ...), custom_call_target="tpu_custom_call" | custom-call | flops 4294967296 | bytes 8388608 | tf_op jit(solution)/shard_map/attend/pallas_call | solution.py:192
  44.1 0.7 attend.6.refs_7_
  44.8 0.0 collective-permute-done.10.refs_5_
  44.8 5.0 %collective-permute-start.11 = (bf16[4,256,128]{2,1,0:T(8,128)(2,1)S(1)}, bf16[4,256,128]{2,1,0:T(8,128)(2,1)S(1)}, u32[]{:S(2)}, u32[]{:S(2)}) collective-permute-start(bf16[4,256,128]{2,1,0:T(8,128)(2,1)S(1)} %collective-permute-done.10.refs_5_), channel_id=1, source_target_pairs={{0,128},{128,1},{1,129},{129,2},{2,130},{130,3},{3,131},{131,0},{4... | collective-permute-start | bytes 786440 | tf_op jit(solution)/shard_map/ring/ppermute | solution.py:205
  49.8 0.0 collective-permute-done.14.refs_6_
  49.8 1.5 %collective-permute-start.15 = (bf16[4,256,128]{2,1,0:T(8,128)(2,1)S(1)}, bf16[4,256,128]{2,1,0:T(8,128)(2,1)S(1)}, u32[]{:S(2)}, u32[]{:S(2)}) collective-permute-start(bf16[4,256,128]{2,1,0:T(8,128)(2,1)S(1)} %collective-permute-done.14.refs_6_), channel_id=1, source_target_pairs={{0,131},{128,0},{1,128},{129,1},{2,129},{130,2},{3,130},{131,3},{4... | collective-permute-start | bytes 786440 | tf_op jit(solution)/shard_map/ring/ppermute | solution.py:205
  51.3 0.0 collective-permute-done.2.refs_3_
  51.3 0.0 collective-permute-start.3
  51.3 0.0 collective-permute-done.6.refs_4_
  51.3 2.7 %collective-permute-start.7 = (bf16[4,256,128]{2,1,0:T(8,128)(2,1)S(1)}, bf16[4,256,128]{2,1,0:T(8,128)(2,1)S(1)}, u32[]{:S(2)}, u32[]{:S(2)}) collective-permute-start(bf16[4,256,128]{2,1,0:T(8,128)(2,1)S(1)} %collective-permute-done.6.refs_4_), channel_id=1, source_target_pairs={{0,131},{128,0},{1,128},{129,1},{2,129},{130,2},{3,130},{131,3},{4... | collective-permute-start | bytes 786440 | tf_op jit(solution)/shard_map/ring/ppermute | solution.py:205
  54.0 4.7 %attend.7.refs_7_ = f32[4,144,512]{2,1,0:T(8,128)S(1)} custom-call(s32[16]{0:T(128)S(1)} %copy-done.1, bf16[4,256,128]{2,1,0:T(8,128)(2,1)S(1)} %get-tuple-element.8.refs_1_, bf16[4,256,128]{2,1,0:T(8,128)(2,1)S(1)} %collective-permute-done.refs_2_, bf16[4,256,128]{2,1,0:T(8,128)(2,1)S(1)} %collective-permute-done.2.refs_3_, ...), custom_call_target="tpu_custom_call", output_to_operand_aliasing={{}: (7, {})} | custom-call | flops 8589934592 | bytes 8388608 | tf_op jit(solution)/shard_map/attend/pallas_call | solution.py:192
  58.7 0.0 collective-permute-done.11.refs_5_
  58.8 0.1 collective-permute-start.12
  58.9 0.0 collective-permute-done.15.refs_6_
  58.9 2.7 %collective-permute-start.16 = (bf16[2,256,128]{2,1,0:T(8,128)(2,1)S(1)}, bf16[2,256,128]{2,1,0:T(8,128)(2,1)S(1)}, u32[]{:S(2)}, u32[]{:S(2)}) collective-permute-start(bf16[2,256,128]{2,1,0:T(8,128)(2,1)S(1)} %slice.23), channel_id=1, source_target_pairs={{0,131},{128,0},{1,128},{129,1},{2,129},{130,2},{3,130},{131,3},{4... | collective-permute-start | bytes 393224 | tf_op jit(solution)/shard_map/ring/ppermute | solution.py:205
  61.6 0.0 collective-permute-done.3.refs_3_
  61.6 0.1 collective-permute-start.4
  61.7 0.0 collective-permute-done.7.refs_4_
  61.8 2.7 %collective-permute-start.8 = (bf16[2,256,128]{2,1,0:T(8,128)(2,1)S(1)}, bf16[2,256,128]{2,1,0:T(8,128)(2,1)S(1)}, u32[]{:S(2)}, u32[]{:S(2)}) collective-permute-start(bf16[2,256,128]{2,1,0:T(8,128)(2,1)S(1)} %slice.21), channel_id=1, source_target_pairs={{0,131},{128,0},{1,128},{129,1},{2,129},{130,2},{3,130},{131,3},{4... | collective-permute-start | bytes 393224 | tf_op jit(solution)/shard_map/ring/ppermute | solution.py:205
  64.5 0.7 attend.8.refs_7_
  65.2 0.4 collective-permute-done.12.refs_5_
  65.6 1.2 %collective-permute-done.4.refs_3_ = bf16[2,256,128]{2,1,0:T(8,128)(2,1)S(1)} collective-permute-done((bf16[2,256,128]{2,1,0:T(8,128)(2,1)S(1)}, bf16[2,256,128]{2,1,0:T(8,128)(2,1)S(1)}, u32[]{:S(2)}, u32[]{:S(2)}) %collective-permute-start.4) | collective-permute-done | bytes 131104 | tf_op jit(solution)/shard_map/ring/ppermute | solution.py:205
  66.9 0.0 collective-permute-done.8.refs_4_
  66.9 3.1 %attend.9.own_ref = f32[4,144,512]{2,1,0:T(8,128)S(1)} custom-call(s32[16]{0:T(128)S(1)} %copy-done.1, bf16[4,256,128]{2,1,0:T(8,128)(2,1)S(1)} %get-tuple-element.8.refs_1_, bf16[4,256,128]{2,1,0:T(8,128)(2,1)S(1)} %collective-permute-done.refs_2_, bf16[2,256,128]{2,1,0:T(8,128)(2,1)S(1)} %collective-permute-done.4.refs_3_, ...), custom_call_target="tpu_custom_call", output_to_operand_aliasing={{}: (7, {})} | custom-call | flops 4294967296 | bytes 8388608 | tf_op jit(solution)/shard_map/attend/pallas_call | solution.py:192
  70.0 8.1 %collective-permute-start.17 = (f32[4,144,256]{2,1,0:T(8,128)S(1)}, f32[4,144,256]{2,1,0:T(8,128)S(1)}, u32[]{:S(2)}, u32[]{:S(2)}) collective-permute-start(f32[4,144,256]{2,1,0:T(8,128)S(1)} %slice.24), channel_id=1, source_target_pairs={{0,16},{16,0},{1,17},{17,1},{2,18},{18,2},{3,19},{19,3},{4,20},{20... | collective-permute-start | bytes 1769480 | tf_op jit(solution)/shard_map/swap_terms/ppermute | solution.py:182
  78.1 1.6 %collective-permute-done.17.other_ref = f32[4,144,256]{2,1,0:T(8,128)S(1)} collective-permute-done((f32[4,144,256]{2,1,0:T(8,128)S(1)}, f32[4,144,256]{2,1,0:T(8,128)S(1)}, u32[]{:S(2)}, u32[]{:S(2)}) %collective-permute-start.17) | collective-permute-done | bytes 589856 | tf_op jit(solution)/shard_map/swap_terms/ppermute | solution.py:182
  79.7 0.7 join.1
  80.4 10.7 %all_to_all.11.parts_ref = bf16[16,64,128]{2,1,0:T(8,128)(2,1)S(1)} all-to-all(bf16[16,64,128]{2,1,0:T(8,128)(2,1)S(1)} %join.1), channel_id=1, replica_groups=mesh['zlo'=2,'y'=4,'core'=2,'x'=4,'zhi'=4] {'y','x'}, dimensions={0} | all-to-all | bytes 524288 | tf_op jit(solution)/shard_map/heads_to_tokens/all_to_all | solution.py:228
  91.2 0.8 unpack.1
  (8 shorter events, 0.1 us)
Async XLA Ops:
  0.0 1.1 %copy-start = (bf16[3,1,64,2048]{3,2,1,0:T(8,128)(2,1)S(1)}, bf16[3,1,64,2048]{3,2,1,0:T(8,128)(2,1)}, u32[]{:S(2)}) copy-start(bf16[3,1,64,2048]{3,2,1,0:T(8,128)(2,1)} %param.2) | copy-start | bytes 2359300
  1.3 39.8 %copy-start.1 = (s32[16]{0:T(128)S(1)}, s32[16]{0:T(128)}, u32[]{:S(2)}) copy-start(s32[16]{0:T(128)} %lengths_ref.1) | copy-start | bytes 196
  22.3 11.1 %collective-permute-start.9 = (bf16[4,256,128]{2,1,0:T(8,128)(2,1)S(1)}, bf16[4,256,128]{2,1,0:T(8,128)(2,1)S(1)}, u32[]{:S(2)}, u32[]{:S(2)}) collective-permute-start(bf16[4,256,128]{2,1,0:T(8,128)(2,1)S(1)} %get-tuple-element.10.refs_4_), channel_id=1, source_target_pairs={{0,128},{128,1},{1,129},{129,2},{2,130},{130,3},{3,131},{131,0},{4... | collective-permute-start | bytes 786440 | tf_op jit(solution)/shard_map/ring/ppermute | solution.py:205
  24.0 9.4 %collective-permute-start.13 = (bf16[4,256,128]{2,1,0:T(8,128)(2,1)S(1)}, bf16[4,256,128]{2,1,0:T(8,128)(2,1)S(1)}, u32[]{:S(2)}, u32[]{:S(2)}) collective-permute-start(bf16[4,256,128]{2,1,0:T(8,128)(2,1)S(1)} %get-tuple-element.10.refs_4_), channel_id=1, source_target_pairs={{0,131},{128,0},{1,128},{129,1},{2,129},{130,2},{3,130},{131,3},{4... | collective-permute-start | bytes 786440 | tf_op jit(solution)/shard_map/ring/ppermute | solution.py:205
  28.0 10.3 %collective-permute-start.1 = (bf16[4,256,128]{2,1,0:T(8,128)(2,1)S(1)}, bf16[4,256,128]{2,1,0:T(8,128)(2,1)S(1)}, u32[]{:S(2)}, u32[]{:S(2)}) collective-permute-start(bf16[4,256,128]{2,1,0:T(8,128)(2,1)S(1)} %get-tuple-element.9.refs_3_), channel_id=1, source_target_pairs={{0,128},{128,1},{1,129},{129,2},{2,130},{130,3},{3,131},{131,0},{4... | collective-permute-start | bytes 786440 | tf_op jit(solution)/shard_map/ring/ppermute | solution.py:205
  28.0 10.4 %collective-permute-start.5 = (bf16[4,256,128]{2,1,0:T(8,128)(2,1)S(1)}, bf16[4,256,128]{2,1,0:T(8,128)(2,1)S(1)}, u32[]{:S(2)}, u32[]{:S(2)}) collective-permute-start(bf16[4,256,128]{2,1,0:T(8,128)(2,1)S(1)} %get-tuple-element.9.refs_3_), channel_id=1, source_target_pairs={{0,131},{128,0},{1,128},{129,1},{2,129},{130,2},{3,130},{131,3},{4... | collective-permute-start | bytes 786440 | tf_op jit(solution)/shard_map/ring/ppermute | solution.py:205
  30.7 10.4 %collective-permute-start = (bf16[4,256,128]{2,1,0:T(8,128)(2,1)S(1)}, bf16[4,256,128]{2,1,0:T(8,128)(2,1)S(1)}, u32[]{:S(2)}, u32[]{:S(2)}) collective-permute-start(bf16[4,256,128]{2,1,0:T(8,128)(2,1)S(1)} %get-tuple-element.8.refs_1_), channel_id=1, source_target_pairs={{0,16},{16,0},{1,17},{17,1},{2,18},{18,2},{3,19},{19,3},{4,20},{20... | collective-permute-start | bytes 786440 | tf_op jit(solution)/shard_map/swap_queries/ppermute | solution.py:182
  33.4 11.5 %collective-permute-start.10 = (bf16[4,256,128]{2,1,0:T(8,128)(2,1)S(1)}, bf16[4,256,128]{2,1,0:T(8,128)(2,1)S(1)}, u32[]{:S(2)}, u32[]{:S(2)}) collective-permute-start(bf16[4,256,128]{2,1,0:T(8,128)(2,1)S(1)} %collective-permute-done.9.refs_5_), channel_id=1, source_target_pairs={{0,128},{128,1},{1,129},{129,2},{2,130},{130,3},{3,131},{131,0},{4... | collective-permute-start | bytes 786440 | tf_op jit(solution)/shard_map/ring/ppermute | solution.py:205
  33.4 16.4 %collective-permute-start.14 = (bf16[4,256,128]{2,1,0:T(8,128)(2,1)S(1)}, bf16[4,256,128]{2,1,0:T(8,128)(2,1)S(1)}, u32[]{:S(2)}, u32[]{:S(2)}) collective-permute-start(bf16[4,256,128]{2,1,0:T(8,128)(2,1)S(1)} %collective-permute-done.13.refs_6_), channel_id=1, source_target_pairs={{0,131},{128,0},{1,128},{129,1},{2,129},{130,2},{3,130},{131,3},{4... | collective-permute-start | bytes 786440 | tf_op jit(solution)/shard_map/ring/ppermute | solution.py:205
  38.4 12.9 %collective-permute-start.2 = (bf16[4,256,128]{2,1,0:T(8,128)(2,1)S(1)}, bf16[4,256,128]{2,1,0:T(8,128)(2,1)S(1)}, u32[]{:S(2)}, u32[]{:S(2)}) collective-permute-start(bf16[4,256,128]{2,1,0:T(8,128)(2,1)S(1)} %collective-permute-done.1.refs_3_), channel_id=1, source_target_pairs={{0,128},{128,1},{1,129},{129,2},{2,130},{130,3},{3,131},{131,0},{4... | collective-permute-start | bytes 786440 | tf_op jit(solution)/shard_map/ring/ppermute | solution.py:205
  38.4 12.9 %collective-permute-start.6 = (bf16[4,256,128]{2,1,0:T(8,128)(2,1)S(1)}, bf16[4,256,128]{2,1,0:T(8,128)(2,1)S(1)}, u32[]{:S(2)}, u32[]{:S(2)}) collective-permute-start(bf16[4,256,128]{2,1,0:T(8,128)(2,1)S(1)} %collective-permute-done.5.refs_4_), channel_id=1, source_target_pairs={{0,131},{128,0},{1,128},{129,1},{2,129},{130,2},{3,130},{131,3},{4... | collective-permute-start | bytes 786440 | tf_op jit(solution)/shard_map/ring/ppermute | solution.py:205
  44.8 13.9 %collective-permute-start.11 = (bf16[4,256,128]{2,1,0:T(8,128)(2,1)S(1)}, bf16[4,256,128]{2,1,0:T(8,128)(2,1)S(1)}, u32[]{:S(2)}, u32[]{:S(2)}) collective-permute-start(bf16[4,256,128]{2,1,0:T(8,128)(2,1)S(1)} %collective-permute-done.10.refs_5_), channel_id=1, source_target_pairs={{0,128},{128,1},{1,129},{129,2},{2,130},{130,3},{3,131},{131,0},{4... | collective-permute-start | bytes 786440 | tf_op jit(solution)/shard_map/ring/ppermute | solution.py:205
  49.8 9.0 %collective-permute-start.15 = (bf16[4,256,128]{2,1,0:T(8,128)(2,1)S(1)}, bf16[4,256,128]{2,1,0:T(8,128)(2,1)S(1)}, u32[]{:S(2)}, u32[]{:S(2)}) collective-permute-start(bf16[4,256,128]{2,1,0:T(8,128)(2,1)S(1)} %collective-permute-done.14.refs_6_), channel_id=1, source_target_pairs={{0,131},{128,0},{1,128},{129,1},{2,129},{130,2},{3,130},{131,3},{4... | collective-permute-start | bytes 786440 | tf_op jit(solution)/shard_map/ring/ppermute | solution.py:205
  51.3 10.3 %collective-permute-start.3 = (bf16[4,256,128]{2,1,0:T(8,128)(2,1)S(1)}, bf16[4,256,128]{2,1,0:T(8,128)(2,1)S(1)}, u32[]{:S(2)}, u32[]{:S(2)}) collective-permute-start(bf16[4,256,128]{2,1,0:T(8,128)(2,1)S(1)} %collective-permute-done.2.refs_3_), channel_id=1, source_target_pairs={{0,128},{128,1},{1,129},{129,2},{2,130},{130,3},{3,131},{131,0},{4... | collective-permute-start | bytes 786440 | tf_op jit(solution)/shard_map/ring/ppermute | solution.py:205
  51.3 10.4 %collective-permute-start.7 = (bf16[4,256,128]{2,1,0:T(8,128)(2,1)S(1)}, bf16[4,256,128]{2,1,0:T(8,128)(2,1)S(1)}, u32[]{:S(2)}, u32[]{:S(2)}) collective-permute-start(bf16[4,256,128]{2,1,0:T(8,128)(2,1)S(1)} %collective-permute-done.6.refs_4_), channel_id=1, source_target_pairs={{0,131},{128,0},{1,128},{129,1},{2,129},{130,2},{3,130},{131,3},{4... | collective-permute-start | bytes 786440 | tf_op jit(solution)/shard_map/ring/ppermute | solution.py:205
  58.8 6.8 %collective-permute-start.12 = (bf16[2,256,128]{2,1,0:T(8,128)(2,1)S(1)}, bf16[2,256,128]{2,1,0:T(8,128)(2,1)S(1)}, u32[]{:S(2)}, u32[]{:S(2)}) collective-permute-start(bf16[2,256,128]{2,1,0:T(8,128)(2,1)S(1)} %slice.22), channel_id=1, source_target_pairs={{0,128},{128,1},{1,129},{129,2},{2,130},{130,3},{3,131},{131,0},{4... | collective-permute-start | bytes 393224 | tf_op jit(solution)/shard_map/ring/ppermute | solution.py:205
  58.9 6.7 %collective-permute-start.16 = (bf16[2,256,128]{2,1,0:T(8,128)(2,1)S(1)}, bf16[2,256,128]{2,1,0:T(8,128)(2,1)S(1)}, u32[]{:S(2)}, u32[]{:S(2)}) collective-permute-start(bf16[2,256,128]{2,1,0:T(8,128)(2,1)S(1)} %slice.23), channel_id=1, source_target_pairs={{0,131},{128,0},{1,128},{129,1},{2,129},{130,2},{3,130},{131,3},{4... | collective-permute-start | bytes 393224 | tf_op jit(solution)/shard_map/ring/ppermute | solution.py:205
  61.6 5.2 %collective-permute-start.4 = (bf16[2,256,128]{2,1,0:T(8,128)(2,1)S(1)}, bf16[2,256,128]{2,1,0:T(8,128)(2,1)S(1)}, u32[]{:S(2)}, u32[]{:S(2)}) collective-permute-start(bf16[2,256,128]{2,1,0:T(8,128)(2,1)S(1)} %slice.20), channel_id=1, source_target_pairs={{0,128},{128,1},{1,129},{129,2},{2,130},{130,3},{3,131},{131,0},{4... | collective-permute-start | bytes 393224 | tf_op jit(solution)/shard_map/ring/ppermute | solution.py:205
  61.8 5.1 %collective-permute-start.8 = (bf16[2,256,128]{2,1,0:T(8,128)(2,1)S(1)}, bf16[2,256,128]{2,1,0:T(8,128)(2,1)S(1)}, u32[]{:S(2)}, u32[]{:S(2)}) collective-permute-start(bf16[2,256,128]{2,1,0:T(8,128)(2,1)S(1)} %slice.21), channel_id=1, source_target_pairs={{0,131},{128,0},{1,128},{129,1},{2,129},{130,2},{3,130},{131,3},{4... | collective-permute-start | bytes 393224 | tf_op jit(solution)/shard_map/ring/ppermute | solution.py:205
  70.0 9.7 %collective-permute-start.17 = (f32[4,144,256]{2,1,0:T(8,128)S(1)}, f32[4,144,256]{2,1,0:T(8,128)S(1)}, u32[]{:S(2)}, u32[]{:S(2)}) collective-permute-start(f32[4,144,256]{2,1,0:T(8,128)S(1)} %slice.24), channel_id=1, source_target_pairs={{0,16},{16,0},{1,17},{17,1},{2,18},{18,2},{3,19},{19,3},{4,20},{20... | collective-permute-start | bytes 1769480 | tf_op jit(solution)/shard_map/swap_terms/ppermute | solution.py:182

commit v4 on v3

--- a/solution.py
+++ b/solution.py
@@ -31,21 +31,21 @@
         out_ref[:, head * HD : (head + 1) * HD] = parts_ref[head]
 
 
-def split(parts_ref, query_ref, key_ref, value_ref):
+def split(parts_ref, query_ref, *pair_refs):
     for span in range(4):
         block = parts_ref.at[4 * span : 4 * span + 4]
+        pair_ref = pair_refs[span // 2].at[span % 2]
         query_ref[span] = block[:, :SLICE, :].reshape(ROWS, HD)
-        key_ref[span] = block[:, SLICE : 2 * SLICE, :].reshape(ROWS, HD)
+        pair_ref[:ROWS] = block[:, SLICE : 2 * SLICE, :].reshape(ROWS, HD)
         turned = block[:, 2 * SLICE :, :].reshape(ROWS, HD).T
-        value_ref[span, :HD] = turned[:, :HD]
-        value_ref[span, HD:] = turned[:, HD:]
+        pair_ref[ROWS : ROWS + HD] = turned[:, :HD]
+        pair_ref[ROWS + HD :] = turned[:, HD:]
 
 
 def attend(sources, first, *refs):
     refs = list(refs)
     lengths_ref, own_ref, other_ref = refs[:3]
-    key_refs = refs[3 : 3 + len(sources)]
-    value_refs = refs[3 + len(sources) : 3 + 2 * len(sources)]
+    arrivals = refs[3 : 3 + len(sources)]
     before_ref = None if first else refs[-2]
     state_ref = refs[-1]
     core = lax.axis_index("core")
@@ -53,7 +53,7 @@
     zed = lax.axis_index("zhi") * 2 + zlo
     pieces = []
     for number, (distance, begin) in enumerate(sources):
-        for place in range(key_refs[number].shape[0]):
+        for place in range(arrivals[number].shape[0]):
             pieces.append((place + begin, number, place))
     pieces.sort()
     source_zed = [lax.rem(zed + 8 + distance, 8) for distance, _ in sources]
@@ -69,8 +69,9 @@
         for span, number, place in pieces:
             if span >= count:
                 continue
+            block = arrivals[number].at[place]
             score = lax.dot_general(
-                key_refs[number][place],
+                block[:ROWS, :],
                 queries,
                 (((1,), (1,)), ((), ())),
                 preferred_element_type=jnp.float32,
@@ -88,8 +89,7 @@
                 elif part >= 2:
                     rows = jnp.where(row < bound, rows, FILL)
                 scores.append(rows)
-            block = value_refs[number].at[place]
-            turned = jnp.concatenate([block[:HD, :], block[HD:, :]], axis=1)
+            turned = jnp.concatenate([block[ROWS : ROWS + HD, :], block[ROWS + HD :, :]], axis=1)
             values.append(jnp.concatenate([turned, ones], axis=0))
         scores = jnp.concatenate(scores, axis=0)
         peak = jnp.max(scores, axis=0, keepdims=True)
@@ -118,7 +118,7 @@
 
         @pl.when(source_zlo < zlo)
         def _():
-            @pl.loop(0, 4)
+            @pl.loop(0, 4, unroll=2)
             def _(step):
                 add(step, 4, -1)
 
@@ -171,7 +171,12 @@
     with jax.named_scope("tokens_to_heads"):
         parts = lax.all_to_all(parts, ("y", "x"), 0, 0, tiled=True)
     with jax.named_scope("split"):
-        own, keys, values = call(split, [jax.ShapeDtypeStruct((4, ROWS, HD), bf16)] * 3, [vmem])(parts)
+        own, *pairs = call(
+            split,
+            [jax.ShapeDtypeStruct((4, ROWS, HD), bf16)]
+            + [jax.ShapeDtypeStruct((2, 2 * ROWS, HD), bf16)] * 2,
+            [vmem],
+        )(parts)
 
     chips = 8
     place = [z % 2 * 4 + z // 2 for z in range(chips)]
@@ -185,10 +190,10 @@
         other = swap(own)
     state_shape = jax.ShapeDtypeStruct((4, STATE, 2 * ROWS), jnp.float32)
 
-    def step(keys, values, sources, state):
+    def step(arrivals, sources, state):
         first = state is None
-        operands = [lengths, own, other] + keys + values + ([] if first else [state])
-        count = sum(a.shape[0] for a in keys)
+        operands = [lengths, own, other] + arrivals + ([] if first else [state])
+        count = sum(a.shape[0] for a in arrivals)
         return call(
             functools.partial(attend, sources, first),
             state_shape,
@@ -198,24 +203,29 @@
             input_output_aliases={} if first else {len(operands) - 1: 0},
         )(*operands)
 
-    def hop(pair, distance):
-        below, above = pair
-        if distance == 4:
-            below, above = below[:2], above[2:]
-        return [lax.ppermute(below, RING, up), lax.ppermute(above, RING, down)]
-
-    state = None
-    held = ([keys], [values])
-    moving = ([keys, keys], [values, values])
-    sources = [(0, 0)]
-    for distance in range(1, 6):
-        if distance < 5:
-            with jax.named_scope("ring"):
-                moving = tuple(hop(pair, distance) for pair in moving)
+    def hop(below, above):
+        with jax.named_scope("ring"):
+            return (
+                [lax.ppermute(block, RING, up) for block in below],
+                [lax.ppermute(block, RING, down) for block in above],
+            )
+
+    below, above = hop(pairs, pairs)
+    with jax.named_scope("attend"):
+        state = step(pairs, ((0, 0), (0, 2)), None)
+    below[0], state = lax.optimization_barrier((below[0], state))
+    for distance in range(1, 5):
+        arrived = below + above
+        if distance < 4:
+            sources = ((-distance, 0), (-distance, 2), (distance, 0), (distance, 2))
+        else:
+            sources = ((-distance, 0), (distance, 2))
+        if distance < 3:
+            below, above = hop(below, above)
+        elif distance == 3:
+            below, above = hop(below[:1], above[1:])
         with jax.named_scope("attend"):
-            state = step(*held, tuple(sources), state)
-        held = moving
-        sources = [(-distance, 0), (distance, 0 if distance < 4 else 2)]
+            state = step(arrived, sources, state)
     with jax.named_scope("swap_terms"):
         theirs = swap(state[:, :, ROWS:])
     with jax.named_scope("join"):

time: 93 us -> 95.2 us (1.024)
  the two profiles are of different devices: /device:TPU:1 before, /device:TPU:96 now
where the time goes in v4:
time: 95.2 us; the launch traced here: 95 us
  blocking collectives  33.1 us (35%)
  Pallas kernels  25.6 us (27%)
  starting transfers between devices  20.9 us (22%)
  waiting for transfers between devices  14.1 us (15%)
  local copies, waits for them, and re-layouts  1.18 us (1%)
    pallas_call x5, Pallas kernels, step(): call(functools.partial(attend, sources, first), state_shape, [smem] + [vm...  23.8 us
    all_to_all x1, blocking collectives, shards(): parts = lax.all_to_all(parts, ('y', 'x'), 0, 0, tiled=True)  21.2 us
    ppermute x7, starting transfers between devices, hop(): lax.ppermute(block, RING, up)  20.7 us
    all_to_all x1, blocking collectives, shards(): attended = lax.all_to_all(attended, ('y', 'x'), 0, 0, tiled=True)  11.9 us
    ppermute x7, waiting for transfers between devices, hop(): lax.ppermute(block, RING, down)  9.87 us
    ppermute x7, waiting for transfers between devices, hop(): lax.ppermute(block, RING, up)  2.27 us
    ppermute x2, waiting for transfers between devices, swap(): return lax.ppermute(block, 'core', [(0, 1), (1, 0)])  1.99 us
  transfers between devices with their start and end apart: 16, of which 5 were waited for; matrix products, arithmetic and copies ran while one was open for 0% of the time, Pallas kernels for 22%

profile of v4, /device:TPU:96, one launch (start us, length us, event | category | flops | bytes accessed | tf_op | source)
XLA Modules:
  0.0 95.0 jit_solution(15957405386856839251)
XLA Ops:
  0.0 0.0 copy-start
  0.0 1.1 %copy-done = bf16[3,1,64,2048]{3,2,1,0:T(8,128)(2,1)S(1)} copy-done((bf16[3,1,64,2048]{3,2,1,0:T(8,128)(2,1)S(1)}, bf16[3,1,64,2048]{3,2,1,0:T(8,128)(2,1)}, u32[]{:S(2)}) %copy-start) | copy-done | bytes 786456
  1.1 0.1 pack.1
  1.3 0.0 copy-start.1
  1.3 21.2 %all_to_all.10.parts_ref = bf16[16,192,128]{2,1,0:T(8,128)(2,1)S(1)} all-to-all(bf16[16,192,128]{2,1,0:T(8,128)(2,1)S(1)} %pack.1), channel_id=1, replica_groups=mesh['zlo'=2,'y'=4,'core'=2,'x'=4,'zhi'=4] {'y','x'}, dimensions={0} | all-to-all | bytes 1572864 | tf_op jit(solution)/shard_map/tokens_to_heads/all_to_all | solution.py:172
  22.5 0.1 split.1
  22.6 0.1 collective-permute-start
  22.7 3.2 %collective-permute-start.1 = (bf16[2,512,128]{2,1,0:T(8,128)(2,1)S(1)}, bf16[2,512,128]{2,1,0:T(8,128)(2,1)S(1)}, u32[]{:S(2)}, u32[]{:S(2)}) collective-permute-start(bf16[2,512,128]{2,1,0:T(8,128)(2,1)S(1)} %get-tuple-element.11.refs_3_), channel_id=1, source_target_pairs={{0,128},{128,1},{1,129},{129,2},{2,130},{130,3},{3,131},{131,0},{4... | collective-permute-start | bytes 786440 | tf_op jit(solution)/shard_map/ring/ppermute | solution.py:209
  25.9 0.0 collective-permute-start.12
  25.9 0.0 collective-permute-start.5
  25.9 3.3 %collective-permute-start.9 = (bf16[2,512,128]{2,1,0:T(8,128)(2,1)S(1)}, bf16[2,512,128]{2,1,0:T(8,128)(2,1)S(1)}, u32[]{:S(2)}, u32[]{:S(2)}) collective-permute-start(bf16[2,512,128]{2,1,0:T(8,128)(2,1)S(1)} %get-tuple-element.12.refs_4_), channel_id=1, source_target_pairs={{0,128},{128,1},{1,129},{129,2},{2,130},{130,3},{3,131},{131,0},{4... | collective-permute-start | bytes 786440 | tf_op jit(solution)/shard_map/ring/ppermute | solution.py:209
  29.2 0.0 collective-permute-done.refs_2_
  29.2 0.0 copy-done.1
  29.2 3.0 %attend.5.refs_7_ = f32[4,144,512]{2,1,0:T(8,128)S(1)} custom-call(s32[16]{0:T(128)S(1)} %copy-done.1, bf16[4,256,128]{2,1,0:T(8,128)(2,1)S(1)} %get-tuple-element.10.refs_1_, bf16[4,256,128]{2,1,0:T(8,128)(2,1)S(1)} %collective-permute-done.refs_2_, bf16[2,512,128]{2,1,0:T(8,128)(2,1)S(1)} %get-tuple-element.11.refs_3_, ...), custom_call_target="tpu_custom_call" | custom-call | flops 4294967296 | bytes 8388608 | tf_op jit(solution)/shard_map/attend/pallas_call | solution.py:197
  32.2 0.3 collective-permute-done.1.refs_3_
  32.5 3.7 %collective-permute-start.2 = (bf16[2,512,128]{2,1,0:T(8,128)(2,1)S(1)}, bf16[2,512,128]{2,1,0:T(8,128)(2,1)S(1)}, u32[]{:S(2)}, u32[]{:S(2)}) collective-permute-start(bf16[2,512,128]{2,1,0:T(8,128)(2,1)S(1)} %collective-permute-done.1.refs_3_), channel_id=1, source_target_pairs={{0,128},{128,1},{1,129},{129,2},{2,130},{130,3},{3,131},{131,0},{4... | collective-permute-start | bytes 786440 | tf_op jit(solution)/shard_map/ring/ppermute | solution.py:209
  36.2 1.9 %collective-permute-done.9.refs_4_ = bf16[2,512,128]{2,1,0:T(8,128)(2,1)S(1)} collective-permute-done((bf16[2,512,128]{2,1,0:T(8,128)(2,1)S(1)}, bf16[2,512,128]{2,1,0:T(8,128)(2,1)S(1)}, u32[]{:S(2)}, u32[]{:S(2)}) %collective-permute-start.9) | collective-permute-done | bytes 262176 | tf_op jit(solution)/shard_map/ring/ppermute | solution.py:209
  38.1 3.7 %collective-permute-start.10 = (bf16[2,512,128]{2,1,0:T(8,128)(2,1)S(1)}, bf16[2,512,128]{2,1,0:T(8,128)(2,1)S(1)}, u32[]{:S(2)}, u32[]{:S(2)}) collective-permute-start(bf16[2,512,128]{2,1,0:T(8,128)(2,1)S(1)} %collective-permute-done.9.refs_4_), channel_id=1, source_target_pairs={{0,128},{128,1},{1,129},{129,2},{2,130},{130,3},{3,131},{131,0},{4... | collective-permute-start | bytes 786440 | tf_op jit(solution)/shard_map/ring/ppermute | solution.py:209
  41.8 0.0 collective-permute-done.12.refs_5_
  41.8 0.0 collective-permute-start.13
  41.8 0.0 collective-permute-done.5.refs_6_
  41.9 0.1 collective-permute-start.6
  41.9 6.4 %attend.6.refs_7_ = f32[4,144,512]{2,1,0:T(8,128)S(1)} custom-call(s32[16]{0:T(128)S(1)} %copy-done.1, bf16[4,256,128]{2,1,0:T(8,128)(2,1)S(1)} %get-tuple-element.10.refs_1_, bf16[4,256,128]{2,1,0:T(8,128)(2,1)S(1)} %collective-permute-done.refs_2_, bf16[2,512,128]{2,1,0:T(8,128)(2,1)S(1)} %collective-permute-done.1.refs_3_, ...), custom_call_target="tpu_custom_call", output_to_operand_aliasing={{}: (7, {})} | custom-call | flops 8589934592 | bytes 8388608 | tf_op jit(solution)/shard_map/attend/pallas_call | solution.py:197
  48.3 0.0 collective-permute-done.2.refs_3_
  48.4 0.3 collective-permute-start.3
  48.6 7.1 %collective-permute-done.6.refs_6_ = bf16[2,512,128]{2,1,0:T(8,128)(2,1)S(1)} collective-permute-done((bf16[2,512,128]{2,1,0:T(8,128)(2,1)S(1)}, bf16[2,512,128]{2,1,0:T(8,128)(2,1)S(1)}, u32[]{:S(2)}, u32[]{:S(2)}) %collective-permute-start.6) | collective-permute-done | bytes 262176 | tf_op jit(solution)/shard_map/ring/ppermute | solution.py:210
  55.8 0.0 collective-permute-start.7
  55.8 0.0 collective-permute-done.10.refs_4_
  55.8 3.2 %collective-permute-start.11 = (bf16[2,512,128]{2,1,0:T(8,128)(2,1)S(1)}, bf16[2,512,128]{2,1,0:T(8,128)(2,1)S(1)}, u32[]{:S(2)}, u32[]{:S(2)}) collective-permute-start(bf16[2,512,128]{2,1,0:T(8,128)(2,1)S(1)} %collective-permute-done.10.refs_4_), channel_id=1, source_target_pairs={{0,128},{128,1},{1,129},{129,2},{2,130},{130,3},{3,131},{131,0},{4... | collective-permute-start | bytes 786440 | tf_op jit(solution)/shard_map/ring/ppermute | solution.py:209
  59.0 0.0 collective-permute-done.13.refs_5_
  59.0 0.0 collective-permute-start.14
  59.0 4.7 %attend.7.refs_7_ = f32[4,144,512]{2,1,0:T(8,128)S(1)} custom-call(s32[16]{0:T(128)S(1)} %copy-done.1, bf16[4,256,128]{2,1,0:T(8,128)(2,1)S(1)} %get-tuple-element.10.refs_1_, bf16[4,256,128]{2,1,0:T(8,128)(2,1)S(1)} %collective-permute-done.refs_2_, bf16[2,512,128]{2,1,0:T(8,128)(2,1)S(1)} %collective-permute-done.2.refs_3_, ...), custom_call_target="tpu_custom_call", output_to_operand_aliasing={{}: (7, {})} | custom-call | flops 8589934592 | bytes 8388608 | tf_op jit(solution)/shard_map/attend/pallas_call | solution.py:197
  63.7 0.0 collective-permute-done.3.refs_3_
  63.8 3.3 %collective-permute-start.4 = (bf16[2,512,128]{2,1,0:T(8,128)(2,1)S(1)}, bf16[2,512,128]{2,1,0:T(8,128)(2,1)S(1)}, u32[]{:S(2)}, u32[]{:S(2)}) collective-permute-start(bf16[2,512,128]{2,1,0:T(8,128)(2,1)S(1)} %collective-permute-done.3.refs_3_), channel_id=1, source_target_pairs={{0,128},{128,1},{1,129},{129,2},{2,130},{130,3},{3,131},{131,0},{4... | collective-permute-start | bytes 786440 | tf_op jit(solution)/shard_map/ring/ppermute | solution.py:209
  67.1 0.0 collective-permute-done.7.refs_6_
  67.1 0.0 collective-permute-start.8
  67.1 0.0 collective-permute-done.11.refs_4_
  67.1 2.7 %collective-permute-done.14.refs_5_ = bf16[2,512,128]{2,1,0:T(8,128)(2,1)S(1)} collective-permute-done((bf16[2,512,128]{2,1,0:T(8,128)(2,1)S(1)}, bf16[2,512,128]{2,1,0:T(8,128)(2,1)S(1)}, u32[]{:S(2)}, u32[]{:S(2)}) %collective-permute-start.14) | collective-permute-done | bytes 262176 | tf_op jit(solution)/shard_map/ring/ppermute | solution.py:210
  69.8 6.6 %attend.8.refs_5_ = f32[4,144,512]{2,1,0:T(8,128)S(1)} custom-call(s32[16]{0:T(128)S(1)} %copy-done.1, bf16[4,256,128]{2,1,0:T(8,128)(2,1)S(1)} %get-tuple-element.10.refs_1_, bf16[4,256,128]{2,1,0:T(8,128)(2,1)S(1)} %collective-permute-done.refs_2_, bf16[2,512,128]{2,1,0:T(8,128)(2,1)S(1)} %collective-permute-done.3.refs_3_, ...), custom_call_target="tpu_custom_call", output_to_operand_aliasing={{}: (7, {})} | custom-call | flops 8589934592 | bytes 8388608 | tf_op jit(solution)/shard_map/attend/pallas_call | solution.py:197
  76.4 0.0 collective-permute-done.4.refs_3_
  76.4 0.0 collective-permute-done.8.refs_4_
  76.4 3.1 %attend.9.own_ref = f32[4,144,512]{2,1,0:T(8,128)S(1)} custom-call(s32[16]{0:T(128)S(1)} %copy-done.1, bf16[4,256,128]{2,1,0:T(8,128)(2,1)S(1)} %get-tuple-element.10.refs_1_, bf16[4,256,128]{2,1,0:T(8,128)(2,1)S(1)} %collective-permute-done.refs_2_, bf16[2,512,128]{2,1,0:T(8,128)(2,1)S(1)} %collective-permute-done.4.refs_3_, ...), custom_call_target="tpu_custom_call", output_to_operand_aliasing={{}: (5, {})} | custom-call | flops 4294967296 | bytes 8388608 | tf_op jit(solution)/shard_map/attend/pallas_call | solution.py:197
  79.6 0.1 collective-permute-start.15
  79.7 2.0 %collective-permute-done.15.other_ref = f32[4,144,256]{2,1,0:T(8,128)S(1)} collective-permute-done((f32[4,144,256]{2,1,0:T(8,128)S(1)}, f32[4,144,256]{2,1,0:T(8,128)S(1)}, u32[]{:S(2)}, u32[]{:S(2)}) %collective-permute-start.15) | collective-permute-done | bytes 589856 | tf_op jit(solution)/shard_map/swap_terms/ppermute | solution.py:187
  81.7 0.7 join.1
  82.4 11.9 %all_to_all.11.parts_ref = bf16[16,64,128]{2,1,0:T(8,128)(2,1)S(1)} all-to-all(bf16[16,64,128]{2,1,0:T(8,128)(2,1)S(1)} %join.1), channel_id=1, replica_groups=mesh['zlo'=2,'y'=4,'core'=2,'x'=4,'zhi'=4] {'y','x'}, dimensions={0} | all-to-all | bytes 524288 | tf_op jit(solution)/shard_map/heads_to_tokens/all_to_all | solution.py:238
  94.3 0.8 unpack.1
  (1 shorter events, 0.0 us)
Async XLA Ops:
  0.0 1.1 %copy-start = (bf16[3,1,64,2048]{3,2,1,0:T(8,128)(2,1)S(1)}, bf16[3,1,64,2048]{3,2,1,0:T(8,128)(2,1)}, u32[]{:S(2)}) copy-start(bf16[3,1,64,2048]{3,2,1,0:T(8,128)(2,1)} %param.2) | copy-start | bytes 2359300
  1.3 27.9 %copy-start.1 = (s32[16]{0:T(128)S(1)}, s32[16]{0:T(128)}, u32[]{:S(2)}) copy-start(s32[16]{0:T(128)} %lengths_ref.1) | copy-start | bytes 196
  22.6 6.6 %collective-permute-start = (bf16[4,256,128]{2,1,0:T(8,128)(2,1)S(1)}, bf16[4,256,128]{2,1,0:T(8,128)(2,1)S(1)}, u32[]{:S(2)}, u32[]{:S(2)}) collective-permute-start(bf16[4,256,128]{2,1,0:T(8,128)(2,1)S(1)} %get-tuple-element.10.refs_1_), channel_id=1, source_target_pairs={{0,16},{16,0},{1,17},{17,1},{2,18},{18,2},{3,19},{19,3},{4,20},{20... | collective-permute-start | bytes 786440 | tf_op jit(solution)/shard_map/swap_queries/ppermute | solution.py:187
  22.7 9.8 %collective-permute-start.1 = (bf16[2,512,128]{2,1,0:T(8,128)(2,1)S(1)}, bf16[2,512,128]{2,1,0:T(8,128)(2,1)S(1)}, u32[]{:S(2)}, u32[]{:S(2)}) collective-permute-start(bf16[2,512,128]{2,1,0:T(8,128)(2,1)S(1)} %get-tuple-element.11.refs_3_), channel_id=1, source_target_pairs={{0,128},{128,1},{1,129},{129,2},{2,130},{130,3},{3,131},{131,0},{4... | collective-permute-start | bytes 786440 | tf_op jit(solution)/shard_map/ring/ppermute | solution.py:209
  25.9 15.9 %collective-permute-start.12 = (bf16[2,512,128]{2,1,0:T(8,128)(2,1)S(1)}, bf16[2,512,128]{2,1,0:T(8,128)(2,1)S(1)}, u32[]{:S(2)}, u32[]{:S(2)}) collective-permute-start(bf16[2,512,128]{2,1,0:T(8,128)(2,1)S(1)} %get-tuple-element.11.refs_3_), channel_id=1, source_target_pairs={{0,131},{128,0},{1,128},{129,1},{2,129},{130,2},{3,130},{131,3},{4... | collective-permute-start | bytes 786440 | tf_op jit(solution)/shard_map/ring/ppermute | solution.py:210
  25.9 15.9 %collective-permute-start.5 = (bf16[2,512,128]{2,1,0:T(8,128)(2,1)S(1)}, bf16[2,512,128]{2,1,0:T(8,128)(2,1)S(1)}, u32[]{:S(2)}, u32[]{:S(2)}) collective-permute-start(bf16[2,512,128]{2,1,0:T(8,128)(2,1)S(1)} %get-tuple-element.12.refs_4_), channel_id=1, source_target_pairs={{0,131},{128,0},{1,128},{129,1},{2,129},{130,2},{3,130},{131,3},{4... | collective-permute-start | bytes 786440 | tf_op jit(solution)/shard_map/ring/ppermute | solution.py:210
  25.9 12.2 %collective-permute-start.9 = (bf16[2,512,128]{2,1,0:T(8,128)(2,1)S(1)}, bf16[2,512,128]{2,1,0:T(8,128)(2,1)S(1)}, u32[]{:S(2)}, u32[]{:S(2)}) collective-permute-start(bf16[2,512,128]{2,1,0:T(8,128)(2,1)S(1)} %get-tuple-element.12.refs_4_), channel_id=1, source_target_pairs={{0,128},{128,1},{1,129},{129,2},{2,130},{130,3},{3,131},{131,0},{4... | collective-permute-start | bytes 786440 | tf_op jit(solution)/shard_map/ring/ppermute | solution.py:209
  32.5 15.8 %collective-permute-start.2 = (bf16[2,512,128]{2,1,0:T(8,128)(2,1)S(1)}, bf16[2,512,128]{2,1,0:T(8,128)(2,1)S(1)}, u32[]{:S(2)}, u32[]{:S(2)}) collective-permute-start(bf16[2,512,128]{2,1,0:T(8,128)(2,1)S(1)} %collective-permute-done.1.refs_3_), channel_id=1, source_target_pairs={{0,128},{128,1},{1,129},{129,2},{2,130},{130,3},{3,131},{131,0},{4... | collective-permute-start | bytes 786440 | tf_op jit(solution)/shard_map/ring/ppermute | solution.py:209
  38.1 17.6 %collective-permute-start.10 = (bf16[2,512,128]{2,1,0:T(8,128)(2,1)S(1)}, bf16[2,512,128]{2,1,0:T(8,128)(2,1)S(1)}, u32[]{:S(2)}, u32[]{:S(2)}) collective-permute-start(bf16[2,512,128]{2,1,0:T(8,128)(2,1)S(1)} %collective-permute-done.9.refs_4_), channel_id=1, source_target_pairs={{0,128},{128,1},{1,129},{129,2},{2,130},{130,3},{3,131},{131,0},{4... | collective-permute-start | bytes 786440 | tf_op jit(solution)/shard_map/ring/ppermute | solution.py:209
  41.8 17.2 %collective-permute-start.13 = (bf16[2,512,128]{2,1,0:T(8,128)(2,1)S(1)}, bf16[2,512,128]{2,1,0:T(8,128)(2,1)S(1)}, u32[]{:S(2)}, u32[]{:S(2)}) collective-permute-start(bf16[2,512,128]{2,1,0:T(8,128)(2,1)S(1)} %collective-permute-done.12.refs_5_), channel_id=1, source_target_pairs={{0,131},{128,0},{1,128},{129,1},{2,129},{130,2},{3,130},{131,3},{4... | collective-permute-start | bytes 786440 | tf_op jit(solution)/shard_map/ring/ppermute | solution.py:210
  41.9 13.9 %collective-permute-start.6 = (bf16[2,512,128]{2,1,0:T(8,128)(2,1)S(1)}, bf16[2,512,128]{2,1,0:T(8,128)(2,1)S(1)}, u32[]{:S(2)}, u32[]{:S(2)}) collective-permute-start(bf16[2,512,128]{2,1,0:T(8,128)(2,1)S(1)} %collective-permute-done.5.refs_6_), channel_id=1, source_target_pairs={{0,131},{128,0},{1,128},{129,1},{2,129},{130,2},{3,130},{131,3},{4... | collective-permute-start | bytes 786440 | tf_op jit(solution)/shard_map/ring/ppermute | solution.py:210
  48.4 15.4 %collective-permute-start.3 = (bf16[2,512,128]{2,1,0:T(8,128)(2,1)S(1)}, bf16[2,512,128]{2,1,0:T(8,128)(2,1)S(1)}, u32[]{:S(2)}, u32[]{:S(2)}) collective-permute-start(bf16[2,512,128]{2,1,0:T(8,128)(2,1)S(1)} %collective-permute-done.2.refs_3_), channel_id=1, source_target_pairs={{0,128},{128,1},{1,129},{129,2},{2,130},{130,3},{3,131},{131,0},{4... | collective-permute-start | bytes 786440 | tf_op jit(solution)/shard_map/ring/ppermute | solution.py:209
  55.8 11.3 %collective-permute-start.7 = (bf16[2,512,128]{2,1,0:T(8,128)(2,1)S(1)}, bf16[2,512,128]{2,1,0:T(8,128)(2,1)S(1)}, u32[]{:S(2)}, u32[]{:S(2)}) collective-permute-start(bf16[2,512,128]{2,1,0:T(8,128)(2,1)S(1)} %collective-permute-done.6.refs_6_), channel_id=1, source_target_pairs={{0,131},{128,0},{1,128},{129,1},{2,129},{130,2},{3,130},{131,3},{4... | collective-permute-start | bytes 786440 | tf_op jit(solution)/shard_map/ring/ppermute | solution.py:210
  55.8 11.3 %collective-permute-start.11 = (bf16[2,512,128]{2,1,0:T(8,128)(2,1)S(1)}, bf16[2,512,128]{2,1,0:T(8,128)(2,1)S(1)}, u32[]{:S(2)}, u32[]{:S(2)}) collective-permute-start(bf16[2,512,128]{2,1,0:T(8,128)(2,1)S(1)} %collective-permute-done.10.refs_4_), channel_id=1, source_target_pairs={{0,128},{128,1},{1,129},{129,2},{2,130},{130,3},{3,131},{131,0},{4... | collective-permute-start | bytes 786440 | tf_op jit(solution)/shard_map/ring/ppermute | solution.py:209
  59.0 10.8 %collective-permute-start.14 = (bf16[2,512,128]{2,1,0:T(8,128)(2,1)S(1)}, bf16[2,512,128]{2,1,0:T(8,128)(2,1)S(1)}, u32[]{:S(2)}, u32[]{:S(2)}) collective-permute-start(bf16[2,512,128]{2,1,0:T(8,128)(2,1)S(1)} %collective-permute-done.13.refs_5_), channel_id=1, source_target_pairs={{0,131},{128,0},{1,128},{129,1},{2,129},{130,2},{3,130},{131,3},{4... | collective-permute-start | bytes 786440 | tf_op jit(solution)/shard_map/ring/ppermute | solution.py:210
  63.8 12.7 %collective-permute-start.4 = (bf16[2,512,128]{2,1,0:T(8,128)(2,1)S(1)}, bf16[2,512,128]{2,1,0:T(8,128)(2,1)S(1)}, u32[]{:S(2)}, u32[]{:S(2)}) collective-permute-start(bf16[2,512,128]{2,1,0:T(8,128)(2,1)S(1)} %collective-permute-done.3.refs_3_), channel_id=1, source_target_pairs={{0,128},{128,1},{1,129},{129,2},{2,130},{130,3},{3,131},{131,0},{4... | collective-permute-start | bytes 786440 | tf_op jit(solution)/shard_map/ring/ppermute | solution.py:209
  67.1 9.4 %collective-permute-start.8 = (bf16[2,512,128]{2,1,0:T(8,128)(2,1)S(1)}, bf16[2,512,128]{2,1,0:T(8,128)(2,1)S(1)}, u32[]{:S(2)}, u32[]{:S(2)}) collective-permute-start(bf16[2,512,128]{2,1,0:T(8,128)(2,1)S(1)} %collective-permute-done.7.refs_6_), channel_id=1, source_target_pairs={{0,131},{128,0},{1,128},{129,1},{2,129},{130,2},{3,130},{131,3},{4... | collective-permute-start | bytes 786440 | tf_op jit(solution)/shard_map/ring/ppermute | solution.py:210
  79.6 2.1 %collective-permute-start.15 = (f32[4,144,256]{2,1,0:T(8,128)S(1)}, f32[4,144,256]{2,1,0:T(8,128)S(1)}, u32[]{:S(2)}, u32[]{:S(2)}) collective-permute-start(f32[4,144,256]{2,1,0:T(8,128)S(1)} %slice.4), channel_id=1, source_target_pairs={{0,16},{16,0},{1,17},{17,1},{2,18},{18,2},{3,19},{19,3},{4,20},{20... | collective-permute-start | bytes 1769480 | tf_op jit(solution)/shard_map/swap_terms/ppermute | solution.py:187

commit v5 on v4

--- a/solution.py
+++ b/solution.py
@@ -16,7 +16,7 @@
 STATE = HD + 16
 SCALE = math.log2(math.e) / math.sqrt(HD)
 VMEM = pltpu.VMEM
-RING = ("zlo", "zhi")
+RING = ("zlo", "core", "zhi")
 
 
 def pack(qkv_ref, out_ref):
@@ -31,34 +31,31 @@
         out_ref[:, head * HD : (head + 1) * HD] = parts_ref[head]
 
 
-def split(parts_ref, query_ref, *pair_refs):
+def split(parts_ref, query_ref, pair_ref):
     for span in range(4):
         block = parts_ref.at[4 * span : 4 * span + 4]
-        pair_ref = pair_refs[span // 2].at[span % 2]
         query_ref[span] = block[:, :SLICE, :].reshape(ROWS, HD)
-        pair_ref[:ROWS] = block[:, SLICE : 2 * SLICE, :].reshape(ROWS, HD)
+        pair_ref[span, :ROWS] = block[:, SLICE : 2 * SLICE, :].reshape(ROWS, HD)
         turned = block[:, 2 * SLICE :, :].reshape(ROWS, HD).T
-        pair_ref[ROWS : ROWS + HD] = turned[:, :HD]
-        pair_ref[ROWS + HD :] = turned[:, HD:]
-
-
-def attend(sources, first, *refs):
+        pair_ref[span, ROWS : ROWS + HD] = turned[:, :HD]
+        pair_ref[span, ROWS + HD :] = turned[:, HD:]
+
+
+def attend(distance, first, *refs):
     refs = list(refs)
     lengths_ref, own_ref, other_ref = refs[:3]
-    arrivals = refs[3 : 3 + len(sources)]
+    arrivals = refs[3:-1] if first else refs[3:-2]
     before_ref = None if first else refs[-2]
     state_ref = refs[-1]
     core = lax.axis_index("core")
     zlo = lax.axis_index("zlo")
     zed = lax.axis_index("zhi") * 2 + zlo
-    pieces = []
-    for number, (distance, begin) in enumerate(sources):
-        for place in range(arrivals[number].shape[0]):
-            pieces.append((place + begin, number, place))
-    pieces.sort()
-    source_zed = [lax.rem(zed + 8 + distance, 8) for distance, _ in sources]
-    source_zlo = lax.rem(source_zed[0], 2)
-    aligned = sources[0][0] % 2 == 0
+    pieces = [(span, number) for span in range(4) for number in range(len(arrivals))]
+    source_zed = lax.rem(zed + 8 + jnp.where(core == 0, -distance, distance), 8)
+    source_zlo = lax.rem(source_zed, 2)
+    source_core = [core, 1 - core]
+    offset = (source_zed // 2) * SLICE
+    aligned = distance % 2 == 0
 
     ones = jnp.where(lax.broadcasted_iota(jnp.int32, (16, ROWS), 0) < 8, 1.0, 0.0)
     ones = ones.astype(jnp.bfloat16)
@@ -66,25 +63,26 @@
     def add(step, count, last):
         queries = jnp.concatenate([own_ref[step], other_ref[step]], axis=0)
         scores, values = [], []
-        for span, number, place in pieces:
+        for span, number in pieces:
             if span >= count:
                 continue
-            block = arrivals[number].at[place]
+            block = arrivals[number].at[span]
             score = lax.dot_general(
                 block[:ROWS, :],
                 queries,
                 (((1,), (1,)), ((), ())),
                 preferred_element_type=jnp.float32,
             )
-            live = lengths_ref[source_zlo * 8 + 2 * span + core]
-            offset = (source_zed[number] // 2) * SLICE
+            live = lengths_ref[source_zlo * 8 + 2 * span + source_core[number]]
             row = lax.broadcasted_iota(jnp.int32, (SLICE, 2 * ROWS), 0)
             other_half = lax.broadcasted_iota(jnp.int32, (SLICE, 2 * ROWS), 1) >= ROWS
             for part in range(4):
                 rows = score[part * SLICE : (part + 1) * SLICE]
                 bound = live - part * ROWS - offset
                 if span == last:
-                    bound = jnp.where(other_half, jnp.where(core == 1, 0, bound), bound)
+                    own_bound = jnp.where(source_core[number] <= core, bound, 0)
+                    other_bound = jnp.where(source_core[number] <= 1 - core, bound, 0)
+                    bound = jnp.where(other_half, other_bound, own_bound)
                     rows = jnp.where(row < bound, rows, FILL)
                 elif part >= 2:
                     rows = jnp.where(row < bound, rows, FILL)
@@ -171,61 +169,60 @@
     with jax.named_scope("tokens_to_heads"):
         parts = lax.all_to_all(parts, ("y", "x"), 0, 0, tiled=True)
     with jax.named_scope("split"):
-        own, *pairs = call(
+        own, pairs = call(
             split,
-            [jax.ShapeDtypeStruct((4, ROWS, HD), bf16)]
-            + [jax.ShapeDtypeStruct((2, 2 * ROWS, HD), bf16)] * 2,
+            [
+                jax.ShapeDtypeStruct((4, ROWS, HD), bf16),
+                jax.ShapeDtypeStruct((4, 2 * ROWS, HD), bf16),
+            ],
             [vmem],
         )(parts)
 
     chips = 8
-    place = [z % 2 * 4 + z // 2 for z in range(chips)]
-    up = [(place[z], place[(z + 1) % chips]) for z in range(chips)]
-    down = [(place[z], place[(z - 1) % chips]) for z in range(chips)]
+    place = [z % 2 * 8 + z // 2 for z in range(chips)]
+    route = [(place[z], place[(z + 1) % chips]) for z in range(chips)]
+    route += [(place[z] + 4, place[(z - 1) % chips] + 4) for z in range(chips)]
+
+    def hop(block):
+        with jax.named_scope("ring"):
+            return lax.ppermute(block, RING, route)
 
     def swap(block):
         return lax.ppermute(block, "core", [(0, 1), (1, 0)])
 
+    first_chain = hop(pairs)
     with jax.named_scope("swap_queries"):
         other = swap(own)
+    with jax.named_scope("swap_pairs"):
+        second = swap(pairs)
+    other, second = lax.optimization_barrier((other, second))
+    second_chain = hop(second)
     state_shape = jax.ShapeDtypeStruct((4, STATE, 2 * ROWS), jnp.float32)
 
-    def step(arrivals, sources, state):
+    def step(arrivals, distance, state):
         first = state is None
         operands = [lengths, own, other] + arrivals + ([] if first else [state])
-        count = sum(a.shape[0] for a in arrivals)
-        return call(
-            functools.partial(attend, sources, first),
-            state_shape,
-            [smem] + [vmem] * (len(operands) - 1),
-            flops=4 * HD * ROWS * ROWS * 8 * count * 4,
-            moved=8 * 2**20,
-            input_output_aliases={} if first else {len(operands) - 1: 0},
-        )(*operands)
-
-    def hop(below, above):
-        with jax.named_scope("ring"):
-            return (
-                [lax.ppermute(block, RING, up) for block in below],
-                [lax.ppermute(block, RING, down) for block in above],
-            )
-
-    below, above = hop(pairs, pairs)
-    with jax.named_scope("attend"):
-        state = step(pairs, ((0, 0), (0, 2)), None)
-    below[0], state = lax.optimization_barrier((below[0], state))
-    for distance in range(1, 5):
-        arrived = below + above
-        if distance < 4:
-            sources = ((-distance, 0), (-distance, 2), (distance, 0), (distance, 2))
-        else:
-            sources = ((-distance, 0), (distance, 2))
+        count = 4 * len(arrivals)
+        with jax.named_scope("attend"):
+            return call(
+                functools.partial(attend, distance, first),
+                state_shape,
+                [smem] + [vmem] * (len(operands) - 1),
+                flops=4 * HD * ROWS * ROWS * 8 * count * 4,
+                moved=8 * 2**20,
+                input_output_aliases={} if first else {len(operands) - 1: 0},
+            )(*operands)
+
+    state = step([pairs], 0, None)
+    for distance in range(1, 4):
+        first_chain, state = lax.optimization_barrier((first_chain, state))
+        second_chain, state = lax.optimization_barrier((second_chain, state))
+        arrived = [first_chain, second_chain]
+        first_chain = hop(first_chain)
         if distance < 3:
-            below, above = hop(below, above)
-        elif distance == 3:
-            below, above = hop(below[:1], above[1:])
-        with jax.named_scope("attend"):
-            state = step(arrived, sources, state)
+            second_chain = hop(second_chain)
+        state = step(arrived, distance, state)
+    state = step([first_chain], 4, state)
     with jax.named_scope("swap_terms"):
         theirs = swap(state[:, :, ROWS:])
     with jax.named_scope("join"):

time: 95.2 us -> 89 us (0.935)
  the two profiles are of different devices: /device:TPU:96 before, /device:TPU:1 now
where the time goes in v5:
time: 89 us; the launch traced here: 88.6 us
  blocking collectives  31.6 us (36%)
  starting transfers between devices  25.6 us (29%)
  waiting for transfers between devices  16.1 us (18%)
  Pallas kernels  14 us (16%)
  local copies, waits for them, and re-layouts  1.18 us (1%)
    ppermute x7, starting transfers between devices, hop(): return lax.ppermute(block, RING, route)  21.7 us
    all_to_all x1, blocking collectives, shards(): parts = lax.all_to_all(parts, ('y', 'x'), 0, 0, tiled=True)  20.9 us
    ppermute x7, waiting for transfers between devices, hop(): return lax.ppermute(block, RING, route)  14.5 us
    pallas_call x5, Pallas kernels, step(): call(functools.partial(attend, distance, first), state_shape, [smem] + [v...  12.3 us
    all_to_all x1, blocking collectives, shards(): attended = lax.all_to_all(attended, ('y', 'x'), 0, 0, tiled=True)  10.7 us
    ppermute x3, starting transfers between devices, swap(): return lax.ppermute(block, 'core', [(0, 1), (1, 0)])  3.91 us
  transfers between devices with their start and end apart: 10, of which 7 were waited for; matrix products, arithmetic and copies ran while one was open for 0% of the time, Pallas kernels for 10%

profile of v5, /device:TPU:1, one launch (start us, length us, event | category | flops | bytes accessed | tf_op | source)
XLA Modules:
  0.0 88.6 jit_solution(17100386221322689970)
XLA Ops:
  0.0 0.0 copy-start
  0.0 1.1 %copy-done = bf16[3,1,64,2048]{3,2,1,0:T(8,128)(2,1)S(1)} copy-done((bf16[3,1,64,2048]{3,2,1,0:T(8,128)(2,1)S(1)}, bf16[3,1,64,2048]{3,2,1,0:T(8,128)(2,1)}, u32[]{:S(2)}) %copy-start) | copy-done | bytes 786456
  1.1 0.1 pack.1
  1.3 0.0 copy-start.1
  1.3 20.9 %all_to_all.10.parts_ref = bf16[16,192,128]{2,1,0:T(8,128)(2,1)S(1)} all-to-all(bf16[16,192,128]{2,1,0:T(8,128)(2,1)S(1)} %pack.1), channel_id=1, replica_groups=mesh['zlo'=2,'y'=4,'core'=2,'x'=4,'zhi'=4] {'y','x'}, dimensions={0} | all-to-all | bytes 1572864 | tf_op jit(solution)/shard_map/tokens_to_heads/all_to_all | solution.py:170
  22.2 0.1 split.1
  22.3 1.9 %collective-permute-start.1 = (bf16[4,512,128]{2,1,0:T(8,128)(2,1)S(1)}, bf16[4,512,128]{2,1,0:T(8,128)(2,1)S(1)}, u32[]{:S(2)}, u32[]{:S(2)}) collective-permute-start(bf16[4,512,128]{2,1,0:T(8,128)(2,1)S(1)} %get-tuple-element.22.refs_3_), channel_id=1, source_target_pairs={{0,16},{16,0},{1,17},{17,1},{2,18},{18,2},{3,19},{19,3},{4,20},{20... | collective-permute-start | bytes 1572872 | tf_op jit(solution)/shard_map/swap_pairs/ppermute | solution.py:191
  24.2 0.1 collective-permute-start
  24.3 5.6 %collective-permute-start.2 = (bf16[4,512,128]{2,1,0:T(8,128)(2,1)S(1)}, bf16[4,512,128]{2,1,0:T(8,128)(2,1)S(1)}, u32[]{:S(2)}, u32[]{:S(2)}) collective-permute-start(bf16[4,512,128]{2,1,0:T(8,128)(2,1)S(1)} %get-tuple-element.22.refs_3_), channel_id=1, source_target_pairs={{0,128},{128,1},{1,129},{129,2},{2,130},{130,3},{3,131},{131,0},{1... | collective-permute-start | bytes 1572872 | tf_op jit(solution)/shard_map/ring/ppermute | solution.py:188
  29.9 0.0 collective-permute-done.refs_2_
  29.9 0.0 collective-permute-done.1
  29.9 1.8 %collective-permute-start.4 = (bf16[4,512,128]{2,1,0:T(8,128)(2,1)S(1)}, bf16[4,512,128]{2,1,0:T(8,128)(2,1)S(1)}, u32[]{:S(2)}, u32[]{:S(2)}) collective-permute-start(bf16[4,512,128]{2,1,0:T(8,128)(2,1)S(1)} %collective-permute-done.1), channel_id=1, source_target_pairs={{0,128},{128,1},{1,129},{129,2},{2,130},{130,3},{3,131},{131,0},{1... | collective-permute-start | bytes 1572872 | tf_op jit(solution)/shard_map/ring/ppermute | solution.py:188
  31.7 0.0 copy-done.1
  31.7 3.0 %attend.5.refs_5_ = f32[4,144,512]{2,1,0:T(8,128)S(1)} custom-call(s32[16]{0:T(128)S(1)} %copy-done.1, bf16[4,256,128]{2,1,0:T(8,128)(2,1)S(1)} %get-tuple-element.21.refs_1_, bf16[4,256,128]{2,1,0:T(8,128)(2,1)S(1)} %collective-permute-done.refs_2_, bf16[4,512,128]{2,1,0:T(8,128)(2,1)S(1)} %get-tuple-element.22.refs_3_), custom_call_target="tpu_custom_call" | custom-call | flops 4294967296 | bytes 8388608 | tf_op jit(solution)/shard_map/attend/pallas_call | solution.py:207
  34.7 1.3 %collective-permute-done.2.refs_3_ = bf16[4,512,128]{2,1,0:T(8,128)(2,1)S(1)} collective-permute-done((bf16[4,512,128]{2,1,0:T(8,128)(2,1)S(1)}, bf16[4,512,128]{2,1,0:T(8,128)(2,1)S(1)}, u32[]{:S(2)}, u32[]{:S(2)}) %collective-permute-start.2) | collective-permute-done | bytes 524320 | tf_op jit(solution)/shard_map/ring/ppermute | solution.py:188
  36.0 3.1 %collective-permute-start.3 = (bf16[4,512,128]{2,1,0:T(8,128)(2,1)S(1)}, bf16[4,512,128]{2,1,0:T(8,128)(2,1)S(1)}, u32[]{:S(2)}, u32[]{:S(2)}) collective-permute-start(bf16[4,512,128]{2,1,0:T(8,128)(2,1)S(1)} %collective-permute-done.2.refs_3_), channel_id=1, source_target_pairs={{0,128},{128,1},{1,129},{129,2},{2,130},{130,3},{3,131},{131,0},{1... | collective-permute-start | bytes 1572872 | tf_op jit(solution)/shard_map/ring/ppermute | solution.py:188
  39.1 2.5 %collective-permute-done.4.refs_4_ = bf16[4,512,128]{2,1,0:T(8,128)(2,1)S(1)} collective-permute-done((bf16[4,512,128]{2,1,0:T(8,128)(2,1)S(1)}, bf16[4,512,128]{2,1,0:T(8,128)(2,1)S(1)}, u32[]{:S(2)}, u32[]{:S(2)}) %collective-permute-start.4) | collective-permute-done | bytes 524320 | tf_op jit(solution)/shard_map/ring/ppermute | solution.py:188
  41.6 3.1 %collective-permute-start.6 = (bf16[4,512,128]{2,1,0:T(8,128)(2,1)S(1)}, bf16[4,512,128]{2,1,0:T(8,128)(2,1)S(1)}, u32[]{:S(2)}, u32[]{:S(2)}) collective-permute-start(bf16[4,512,128]{2,1,0:T(8,128)(2,1)S(1)} %collective-permute-done.4.refs_4_), channel_id=1, source_target_pairs={{0,128},{128,1},{1,129},{129,2},{2,130},{130,3},{3,131},{131,0},{1... | collective-permute-start | bytes 1572872 | tf_op jit(solution)/shard_map/ring/ppermute | solution.py:188
  44.7 0.7 attend.6.refs_5_
  45.4 1.8 %collective-permute-done.3.refs_3_ = bf16[4,512,128]{2,1,0:T(8,128)(2,1)S(1)} collective-permute-done((bf16[4,512,128]{2,1,0:T(8,128)(2,1)S(1)}, bf16[4,512,128]{2,1,0:T(8,128)(2,1)S(1)}, u32[]{:S(2)}, u32[]{:S(2)}) %collective-permute-start.3) | collective-permute-done | bytes 524320 | tf_op jit(solution)/shard_map/ring/ppermute | solution.py:188
  47.2 4.1 %collective-permute-start.5 = (bf16[4,512,128]{2,1,0:T(8,128)(2,1)S(1)}, bf16[4,512,128]{2,1,0:T(8,128)(2,1)S(1)}, u32[]{:S(2)}, u32[]{:S(2)}) collective-permute-start(bf16[4,512,128]{2,1,0:T(8,128)(2,1)S(1)} %collective-permute-done.3.refs_3_), channel_id=1, source_target_pairs={{0,128},{128,1},{1,129},{129,2},{2,130},{130,3},{3,131},{131,0},{1... | collective-permute-start | bytes 1572872 | tf_op jit(solution)/shard_map/ring/ppermute | solution.py:188
  51.3 1.5 %collective-permute-done.6.refs_4_ = bf16[4,512,128]{2,1,0:T(8,128)(2,1)S(1)} collective-permute-done((bf16[4,512,128]{2,1,0:T(8,128)(2,1)S(1)}, bf16[4,512,128]{2,1,0:T(8,128)(2,1)S(1)}, u32[]{:S(2)}, u32[]{:S(2)}) %collective-permute-start.6) | collective-permute-done | bytes 524320 | tf_op jit(solution)/shard_map/ring/ppermute | solution.py:188
  52.8 3.1 %collective-permute-start.8 = (bf16[4,512,128]{2,1,0:T(8,128)(2,1)S(1)}, bf16[4,512,128]{2,1,0:T(8,128)(2,1)S(1)}, u32[]{:S(2)}, u32[]{:S(2)}) collective-permute-start(bf16[4,512,128]{2,1,0:T(8,128)(2,1)S(1)} %collective-permute-done.6.refs_4_), channel_id=1, source_target_pairs={{0,128},{128,1},{1,129},{129,2},{2,130},{130,3},{3,131},{131,0},{1... | collective-permute-start | bytes 1572872 | tf_op jit(solution)/shard_map/ring/ppermute | solution.py:188
  56.0 4.7 %attend.7.refs_5_ = f32[4,144,512]{2,1,0:T(8,128)S(1)} custom-call(s32[16]{0:T(128)S(1)} %copy-done.1, bf16[4,256,128]{2,1,0:T(8,128)(2,1)S(1)} %get-tuple-element.21.refs_1_, bf16[4,256,128]{2,1,0:T(8,128)(2,1)S(1)} %collective-permute-done.refs_2_, bf16[4,512,128]{2,1,0:T(8,128)(2,1)S(1)} %collective-permute-done.3.refs_3_, ...), custom_call_target="tpu_custom_call", output_to_operand_aliasing={{}: (5, {})} | custom-call | flops 8589934592 | bytes 8388608 | tf_op jit(solution)/shard_map/attend/pallas_call | solution.py:207
  60.7 0.0 collective-permute-done.5.refs_3_
  60.7 0.9 collective-permute-start.7
  61.6 2.5 %collective-permute-done.8.refs_4_ = bf16[4,512,128]{2,1,0:T(8,128)(2,1)S(1)} collective-permute-done((bf16[4,512,128]{2,1,0:T(8,128)(2,1)S(1)}, bf16[4,512,128]{2,1,0:T(8,128)(2,1)S(1)}, u32[]{:S(2)}, u32[]{:S(2)}) %collective-permute-start.8) | collective-permute-done | bytes 524320 | tf_op jit(solution)/shard_map/ring/ppermute | solution.py:188
  64.1 0.7 attend.8.refs_4_
  64.8 4.9 %collective-permute-done.7.refs_3_ = bf16[4,512,128]{2,1,0:T(8,128)(2,1)S(1)} collective-permute-done((bf16[4,512,128]{2,1,0:T(8,128)(2,1)S(1)}, bf16[4,512,128]{2,1,0:T(8,128)(2,1)S(1)}, u32[]{:S(2)}, u32[]{:S(2)}) %collective-permute-start.7) | collective-permute-done | bytes 524320 | tf_op jit(solution)/shard_map/ring/ppermute | solution.py:188
  69.7 3.1 %attend.9.own_ref = f32[4,144,512]{2,1,0:T(8,128)S(1)} custom-call(s32[16]{0:T(128)S(1)} %copy-done.1, bf16[4,256,128]{2,1,0:T(8,128)(2,1)S(1)} %get-tuple-element.21.refs_1_, bf16[4,256,128]{2,1,0:T(8,128)(2,1)S(1)} %collective-permute-done.refs_2_, bf16[4,512,128]{2,1,0:T(8,128)(2,1)S(1)} %collective-permute-done.7.refs_3_, ...), custom_call_target="tpu_custom_call", output_to_operand_aliasing={{}: (4, {})} | custom-call | flops 4294967296 | bytes 8388608 | tf_op jit(solution)/shard_map/attend/pallas_call | solution.py:207
  72.8 1.9 %collective-permute-start.9 = (f32[4,144,256]{2,1,0:T(8,128)S(1)}, f32[4,144,256]{2,1,0:T(8,128)S(1)}, u32[]{:S(2)}, u32[]{:S(2)}) collective-permute-start(f32[4,144,256]{2,1,0:T(8,128)S(1)} %slice.4), channel_id=1, source_target_pairs={{0,16},{16,0},{1,17},{17,1},{2,18},{18,2},{3,19},{19,3},{4,20},{20... | collective-permute-start | bytes 1769480 | tf_op jit(solution)/shard_map/swap_terms/ppermute | solution.py:191
  74.8 1.6 %collective-permute-done.9.other_ref = f32[4,144,256]{2,1,0:T(8,128)S(1)} collective-permute-done((f32[4,144,256]{2,1,0:T(8,128)S(1)}, f32[4,144,256]{2,1,0:T(8,128)S(1)}, u32[]{:S(2)}, u32[]{:S(2)}) %collective-permute-start.9) | collective-permute-done | bytes 589856 | tf_op jit(solution)/shard_map/swap_terms/ppermute | solution.py:191
  76.4 0.7 join.1
  77.1 10.7 %all_to_all.11.parts_ref = bf16[16,64,128]{2,1,0:T(8,128)(2,1)S(1)} all-to-all(bf16[16,64,128]{2,1,0:T(8,128)(2,1)S(1)} %join.1), channel_id=1, replica_groups=mesh['zlo'=2,'y'=4,'core'=2,'x'=4,'zhi'=4] {'y','x'}, dimensions={0} | all-to-all | bytes 524288 | tf_op jit(solution)/shard_map/heads_to_tokens/all_to_all | solution.py:235
  87.8 0.8 unpack.1
  (1 shorter events, 0.0 us)
Async XLA Ops:
  0.0 1.1 %copy-start = (bf16[3,1,64,2048]{3,2,1,0:T(8,128)(2,1)S(1)}, bf16[3,1,64,2048]{3,2,1,0:T(8,128)(2,1)}, u32[]{:S(2)}) copy-start(bf16[3,1,64,2048]{3,2,1,0:T(8,128)(2,1)} %param.2) | copy-start | bytes 2359300
  1.3 30.4 %copy-start.1 = (s32[16]{0:T(128)S(1)}, s32[16]{0:T(128)}, u32[]{:S(2)}) copy-start(s32[16]{0:T(128)} %lengths_ref.1) | copy-start | bytes 196
  22.3 7.6 %collective-permute-start.1 = (bf16[4,512,128]{2,1,0:T(8,128)(2,1)S(1)}, bf16[4,512,128]{2,1,0:T(8,128)(2,1)S(1)}, u32[]{:S(2)}, u32[]{:S(2)}) collective-permute-start(bf16[4,512,128]{2,1,0:T(8,128)(2,1)S(1)} %get-tuple-element.22.refs_3_), channel_id=1, source_target_pairs={{0,16},{16,0},{1,17},{17,1},{2,18},{18,2},{3,19},{19,3},{4,20},{20... | collective-permute-start | bytes 1572872 | tf_op jit(solution)/shard_map/swap_pairs/ppermute | solution.py:191
  24.2 5.7 %collective-permute-start = (bf16[4,256,128]{2,1,0:T(8,128)(2,1)S(1)}, bf16[4,256,128]{2,1,0:T(8,128)(2,1)S(1)}, u32[]{:S(2)}, u32[]{:S(2)}) collective-permute-start(bf16[4,256,128]{2,1,0:T(8,128)(2,1)S(1)} %get-tuple-element.21.refs_1_), channel_id=1, source_target_pairs={{0,16},{16,0},{1,17},{17,1},{2,18},{18,2},{3,19},{19,3},{4,20},{20... | collective-permute-start | bytes 786440 | tf_op jit(solution)/shard_map/swap_queries/ppermute | solution.py:191
  24.3 11.7 %collective-permute-start.2 = (bf16[4,512,128]{2,1,0:T(8,128)(2,1)S(1)}, bf16[4,512,128]{2,1,0:T(8,128)(2,1)S(1)}, u32[]{:S(2)}, u32[]{:S(2)}) collective-permute-start(bf16[4,512,128]{2,1,0:T(8,128)(2,1)S(1)} %get-tuple-element.22.refs_3_), channel_id=1, source_target_pairs={{0,128},{128,1},{1,129},{129,2},{2,130},{130,3},{3,131},{131,0},{1... | collective-permute-start | bytes 1572872 | tf_op jit(solution)/shard_map/ring/ppermute | solution.py:188
  29.9 11.7 %collective-permute-start.4 = (bf16[4,512,128]{2,1,0:T(8,128)(2,1)S(1)}, bf16[4,512,128]{2,1,0:T(8,128)(2,1)S(1)}, u32[]{:S(2)}, u32[]{:S(2)}) collective-permute-start(bf16[4,512,128]{2,1,0:T(8,128)(2,1)S(1)} %collective-permute-done.1), channel_id=1, source_target_pairs={{0,128},{128,1},{1,129},{129,2},{2,130},{130,3},{3,131},{131,0},{1... | collective-permute-start | bytes 1572872 | tf_op jit(solution)/shard_map/ring/ppermute | solution.py:188
  36.0 11.2 %collective-permute-start.3 = (bf16[4,512,128]{2,1,0:T(8,128)(2,1)S(1)}, bf16[4,512,128]{2,1,0:T(8,128)(2,1)S(1)}, u32[]{:S(2)}, u32[]{:S(2)}) collective-permute-start(bf16[4,512,128]{2,1,0:T(8,128)(2,1)S(1)} %collective-permute-done.2.refs_3_), channel_id=1, source_target_pairs={{0,128},{128,1},{1,129},{129,2},{2,130},{130,3},{3,131},{131,0},{1... | collective-permute-start | bytes 1572872 | tf_op jit(solution)/shard_map/ring/ppermute | solution.py:188
  41.6 11.2 %collective-permute-start.6 = (bf16[4,512,128]{2,1,0:T(8,128)(2,1)S(1)}, bf16[4,512,128]{2,1,0:T(8,128)(2,1)S(1)}, u32[]{:S(2)}, u32[]{:S(2)}) collective-permute-start(bf16[4,512,128]{2,1,0:T(8,128)(2,1)S(1)} %collective-permute-done.4.refs_4_), channel_id=1, source_target_pairs={{0,128},{128,1},{1,129},{129,2},{2,130},{130,3},{3,131},{131,0},{1... | collective-permute-start | bytes 1572872 | tf_op jit(solution)/shard_map/ring/ppermute | solution.py:188
  47.2 13.5 %collective-permute-start.5 = (bf16[4,512,128]{2,1,0:T(8,128)(2,1)S(1)}, bf16[4,512,128]{2,1,0:T(8,128)(2,1)S(1)}, u32[]{:S(2)}, u32[]{:S(2)}) collective-permute-start(bf16[4,512,128]{2,1,0:T(8,128)(2,1)S(1)} %collective-permute-done.3.refs_3_), channel_id=1, source_target_pairs={{0,128},{128,1},{1,129},{129,2},{2,130},{130,3},{3,131},{131,0},{1... | collective-permute-start | bytes 1572872 | tf_op jit(solution)/shard_map/ring/ppermute | solution.py:188
  52.8 11.2 %collective-permute-start.8 = (bf16[4,512,128]{2,1,0:T(8,128)(2,1)S(1)}, bf16[4,512,128]{2,1,0:T(8,128)(2,1)S(1)}, u32[]{:S(2)}, u32[]{:S(2)}) collective-permute-start(bf16[4,512,128]{2,1,0:T(8,128)(2,1)S(1)} %collective-permute-done.6.refs_4_), channel_id=1, source_target_pairs={{0,128},{128,1},{1,129},{129,2},{2,130},{130,3},{3,131},{131,0},{1... | collective-permute-start | bytes 1572872 | tf_op jit(solution)/shard_map/ring/ppermute | solution.py:188
  60.7 9.0 %collective-permute-start.7 = (bf16[4,512,128]{2,1,0:T(8,128)(2,1)S(1)}, bf16[4,512,128]{2,1,0:T(8,128)(2,1)S(1)}, u32[]{:S(2)}, u32[]{:S(2)}) collective-permute-start(bf16[4,512,128]{2,1,0:T(8,128)(2,1)S(1)} %collective-permute-done.5.refs_3_), channel_id=1, source_target_pairs={{0,128},{128,1},{1,129},{129,2},{2,130},{130,3},{3,131},{131,0},{1... | collective-permute-start | bytes 1572872 | tf_op jit(solution)/shard_map/ring/ppermute | solution.py:188
  72.8 3.6 %collective-permute-start.9 = (f32[4,144,256]{2,1,0:T(8,128)S(1)}, f32[4,144,256]{2,1,0:T(8,128)S(1)}, u32[]{:S(2)}, u32[]{:S(2)}) collective-permute-start(f32[4,144,256]{2,1,0:T(8,128)S(1)} %slice.4), channel_id=1, source_target_pairs={{0,16},{16,0},{1,17},{17,1},{2,18},{18,2},{3,19},{19,3},{4,20},{20... | collective-permute-start | bytes 1769480 | tf_op jit(solution)/shard_map/swap_terms/ppermute | solution.py:191

commit v6 on v5

--- a/solution.py
+++ b/solution.py
@@ -41,7 +41,7 @@
         pair_ref[span, ROWS + HD :] = turned[:, HD:]
 
 
-def attend(distance, first, *refs):
+def attend(distance, parts, first, *refs):
     refs = list(refs)
     lengths_ref, own_ref, other_ref = refs[:3]
     arrivals = refs[3:-1] if first else refs[3:-2]
@@ -50,10 +50,14 @@
     core = lax.axis_index("core")
     zlo = lax.axis_index("zlo")
     zed = lax.axis_index("zhi") * 2 + zlo
-    pieces = [(span, number) for span in range(4) for number in range(len(arrivals))]
+    pieces = []
+    for number, (_, begin) in enumerate(parts):
+        for place in range(arrivals[number].shape[0]):
+            pieces.append((place + begin, number, place))
+    pieces.sort()
     source_zed = lax.rem(zed + 8 + jnp.where(core == 0, -distance, distance), 8)
     source_zlo = lax.rem(source_zed, 2)
-    source_core = [core, 1 - core]
+    source_core = [core if chain == 0 else 1 - core for chain, _ in parts]
     offset = (source_zed // 2) * SLICE
     aligned = distance % 2 == 0
 
@@ -63,10 +67,10 @@
     def add(step, count, last):
         queries = jnp.concatenate([own_ref[step], other_ref[step]], axis=0)
         scores, values = [], []
-        for span, number in pieces:
+        for span, number, place in pieces:
             if span >= count:
                 continue
-            block = arrivals[number].at[span]
+            block = arrivals[number].at[place]
             score = lax.dot_general(
                 block[:ROWS, :],
                 queries,
@@ -89,6 +93,9 @@
                 scores.append(rows)
             turned = jnp.concatenate([block[ROWS : ROWS + HD, :], block[ROWS + HD :, :]], axis=1)
             values.append(jnp.concatenate([turned, ones], axis=0))
+        if not scores:
+            state_ref[step] = before_ref[step]
+            return
         scores = jnp.concatenate(scores, axis=0)
         peak = jnp.max(scores, axis=0, keepdims=True)
         if not first:
@@ -190,22 +197,22 @@
     def swap(block):
         return lax.ppermute(block, "core", [(0, 1), (1, 0)])
 
-    first_chain = hop(pairs)
     with jax.named_scope("swap_queries"):
         other = swap(own)
     with jax.named_scope("swap_pairs"):
         second = swap(pairs)
+    first_chain = hop(pairs)
     other, second = lax.optimization_barrier((other, second))
     second_chain = hop(second)
     state_shape = jax.ShapeDtypeStruct((4, STATE, 2 * ROWS), jnp.float32)
 
-    def step(arrivals, distance, state):
+    def step(arrivals, distance, parts, state):
         first = state is None
         operands = [lengths, own, other] + arrivals + ([] if first else [state])
-        count = 4 * len(arrivals)
+        count = sum(a.shape[0] for a in arrivals)
         with jax.named_scope("attend"):
             return call(
-                functools.partial(attend, distance, first),
+                functools.partial(attend, distance, parts, first),
                 state_shape,
                 [smem] + [vmem] * (len(operands) - 1),
                 flops=4 * HD * ROWS * ROWS * 8 * count * 4,
@@ -213,16 +220,24 @@
                 input_output_aliases={} if first else {len(operands) - 1: 0},
             )(*operands)
 
-    state = step([pairs], 0, None)
-    for distance in range(1, 4):
-        first_chain, state = lax.optimization_barrier((first_chain, state))
-        second_chain, state = lax.optimization_barrier((second_chain, state))
+    def after(block, state):
+        return lax.optimization_barrier((block, state))
+
+    state = step([pairs], 0, ((0, 0),), None)
+    for distance in range(1, 3):
+        first_chain, state = after(first_chain, state)
+        second_chain, state = after(second_chain, state)
         arrived = [first_chain, second_chain]
-        first_chain = hop(first_chain)
-        if distance < 3:
-            second_chain = hop(second_chain)
-        state = step(arrived, distance, state)
-    state = step([first_chain], 4, state)
+        first_chain, second_chain = hop(first_chain), hop(second_chain)
+        state = step(arrived, distance, ((0, 0), (1, 0)), state)
+    first_chain, state = after(first_chain, state)
+    halves = [hop(first_chain[:2]), hop(first_chain[2:])]
+    state = step([first_chain], 3, ((0, 0),), state)
+    second_chain, state = after(second_chain, state)
+    state = step([second_chain], 3, ((1, 0),), state)
+    for number in range(2):
+        block, state = after(halves[number], state)
+        state = step([block], 4, ((0, 2 * number),), state)
     with jax.named_scope("swap_terms"):
         theirs = swap(state[:, :, ROWS:])
     with jax.named_scope("join"):

time: 89 us -> 90.3 us (1.015)
  the two profiles are of different devices: /device:TPU:1 before, /device:TPU:32 now
where the time goes in v6:
time: 90.3 us; the launch traced here: 90.1 us
  blocking collectives  33 us (37%)
  Pallas kernels  28.2 us (31%)
  starting transfers between devices  16.7 us (18%)
  waiting for transfers between devices  10.8 us (12%)
  local copies, waits for them, and re-layouts  1.22 us (1%)
    pallas_call x7, Pallas kernels, step(): call(functools.partial(attend, distance, parts, first), state_shape, [sme...  26.5 us
    all_to_all x1, blocking collectives, shards(): parts = lax.all_to_all(parts, ('y', 'x'), 0, 0, tiled=True)  21.2 us
    ppermute x8, starting transfers between devices, hop(): return lax.ppermute(block, RING, route)  16 us
    all_to_all x1, blocking collectives, shards(): attended = lax.all_to_all(attended, ('y', 'x'), 0, 0, tiled=True)  11.9 us
    ppermute x8, waiting for transfers between devices, hop(): return lax.ppermute(block, RING, route)  8.76 us
    ppermute x3, waiting for transfers between devices, swap(): return lax.ppermute(block, 'core', [(0, 1), (1, 0)])  2 us
  transfers between devices with their start and end apart: 11, of which 4 were waited for; matrix products, arithmetic and copies ran while one was open for 0% of the time, Pallas kernels for 28%

profile of v6, /device:TPU:32, one launch (start us, length us, event | category | flops | bytes accessed | tf_op | source)
XLA Modules:
  0.0 90.1 jit_solution(4714449419344640394)
XLA Ops:
  0.0 0.0 copy-start
  0.0 1.1 %copy-done = bf16[3,1,64,2048]{3,2,1,0:T(8,128)(2,1)S(1)} copy-done((bf16[3,1,64,2048]{3,2,1,0:T(8,128)(2,1)S(1)}, bf16[3,1,64,2048]{3,2,1,0:T(8,128)(2,1)}, u32[]{:S(2)}) %copy-start) | copy-done | bytes 786456
  1.1 0.1 pack.1
  1.3 0.0 copy-start.1
  1.3 21.2 %all_to_all.10.parts_ref = bf16[16,192,128]{2,1,0:T(8,128)(2,1)S(1)} all-to-all(bf16[16,192,128]{2,1,0:T(8,128)(2,1)S(1)} %pack.1), channel_id=1, replica_groups=mesh['zlo'=2,'y'=4,'core'=2,'x'=4,'zhi'=4] {'y','x'}, dimensions={0} | all-to-all | bytes 1572864 | tf_op jit(solution)/shard_map/tokens_to_heads/all_to_all | solution.py:177
  22.5 0.1 split.1
  22.6 0.1 collective-permute-start.1
  22.7 0.5 collective-permute-start
  23.2 1.9 %collective-permute-start.2 = (bf16[4,512,128]{2,1,0:T(8,128)(2,1)S(1)}, bf16[4,512,128]{2,1,0:T(8,128)(2,1)S(1)}, u32[]{:S(2)}, u32[]{:S(2)}) collective-permute-start(bf16[4,512,128]{2,1,0:T(8,128)(2,1)S(1)} %get-tuple-element.26.refs_3_), channel_id=1, source_target_pairs={{0,128},{128,1},{1,129},{129,2},{2,130},{130,3},{3,131},{131,0},{1... | collective-permute-start | bytes 1572872 | tf_op jit(solution)/shard_map/ring/ppermute | solution.py:195
  25.1 0.0 collective-permute-done.refs_2_
  25.1 0.0 collective-permute-done.1
  25.1 1.9 %collective-permute-start.4 = (bf16[4,512,128]{2,1,0:T(8,128)(2,1)S(1)}, bf16[4,512,128]{2,1,0:T(8,128)(2,1)S(1)}, u32[]{:S(2)}, u32[]{:S(2)}) collective-permute-start(bf16[4,512,128]{2,1,0:T(8,128)(2,1)S(1)} %collective-permute-done.1), channel_id=1, source_target_pairs={{0,128},{128,1},{1,129},{129,2},{2,130},{130,3},{3,131},{131,0},{1... | collective-permute-start | bytes 1572872 | tf_op jit(solution)/shard_map/ring/ppermute | solution.py:195
  27.0 0.0 copy-done.1
  27.0 3.0 %attend.7.refs_5_ = f32[4,144,512]{2,1,0:T(8,128)S(1)} custom-call(s32[16]{0:T(128)S(1)} %copy-done.1, bf16[4,256,128]{2,1,0:T(8,128)(2,1)S(1)} %get-tuple-element.25.refs_1_, bf16[4,256,128]{2,1,0:T(8,128)(2,1)S(1)} %collective-permute-done.refs_2_, bf16[4,512,128]{2,1,0:T(8,128)(2,1)S(1)} %get-tuple-element.26.refs_3_), custom_call_target="tpu_custom_call" | custom-call | flops 4294967296 | bytes 8388608 | tf_op jit(solution)/shard_map/attend/pallas_call | solution.py:214
  30.1 2.3 %collective-permute-done.2.refs_3_ = bf16[4,512,128]{2,1,0:T(8,128)(2,1)S(1)} collective-permute-done((bf16[4,512,128]{2,1,0:T(8,128)(2,1)S(1)}, bf16[4,512,128]{2,1,0:T(8,128)(2,1)S(1)}, u32[]{:S(2)}, u32[]{:S(2)}) %collective-permute-start.2) | collective-permute-done | bytes 524320 | tf_op jit(solution)/shard_map/ring/ppermute | solution.py:195
  32.4 1.9 %collective-permute-start.3 = (bf16[4,512,128]{2,1,0:T(8,128)(2,1)S(1)}, bf16[4,512,128]{2,1,0:T(8,128)(2,1)S(1)}, u32[]{:S(2)}, u32[]{:S(2)}) collective-permute-start(bf16[4,512,128]{2,1,0:T(8,128)(2,1)S(1)} %collective-permute-done.2.refs_3_), channel_id=1, source_target_pairs={{0,128},{128,1},{1,129},{129,2},{2,130},{130,3},{3,131},{131,0},{1... | collective-permute-start | bytes 1572872 | tf_op jit(solution)/shard_map/ring/ppermute | solution.py:195
  34.3 3.7 %collective-permute-done.4.refs_4_ = bf16[4,512,128]{2,1,0:T(8,128)(2,1)S(1)} collective-permute-done((bf16[4,512,128]{2,1,0:T(8,128)(2,1)S(1)}, bf16[4,512,128]{2,1,0:T(8,128)(2,1)S(1)}, u32[]{:S(2)}, u32[]{:S(2)}) %collective-permute-start.4) | collective-permute-done | bytes 524320 | tf_op jit(solution)/shard_map/ring/ppermute | solution.py:195
  38.0 1.9 %collective-permute-start.6 = (bf16[4,512,128]{2,1,0:T(8,128)(2,1)S(1)}, bf16[4,512,128]{2,1,0:T(8,128)(2,1)S(1)}, u32[]{:S(2)}, u32[]{:S(2)}) collective-permute-start(bf16[4,512,128]{2,1,0:T(8,128)(2,1)S(1)} %collective-permute-done.4.refs_4_), channel_id=1, source_target_pairs={{0,128},{128,1},{1,129},{129,2},{2,130},{130,3},{3,131},{131,0},{1... | collective-permute-start | bytes 1572872 | tf_op jit(solution)/shard_map/ring/ppermute | solution.py:195
  39.9 6.5 %attend.8.refs_5_ = f32[4,144,512]{2,1,0:T(8,128)S(1)} custom-call(s32[16]{0:T(128)S(1)} %copy-done.1, bf16[4,256,128]{2,1,0:T(8,128)(2,1)S(1)} %get-tuple-element.25.refs_1_, bf16[4,256,128]{2,1,0:T(8,128)(2,1)S(1)} %collective-permute-done.refs_2_, bf16[4,512,128]{2,1,0:T(8,128)(2,1)S(1)} %collective-permute-done.2.refs_3_, ...), custom_call_target="tpu_custom_call", output_to_operand_aliasing={{}: (5, {})} | custom-call | flops 8589934592 | bytes 8388608 | tf_op jit(solution)/shard_map/attend/pallas_call | solution.py:214
  46.4 0.0 collective-permute-done.3.refs_3_
  46.4 0.1 collective-permute-start.5
  46.5 2.7 %collective-permute-done.6.refs_4_ = bf16[4,512,128]{2,1,0:T(8,128)(2,1)S(1)} collective-permute-done((bf16[4,512,128]{2,1,0:T(8,128)(2,1)S(1)}, bf16[4,512,128]{2,1,0:T(8,128)(2,1)S(1)}, u32[]{:S(2)}, u32[]{:S(2)}) %collective-permute-start.6) | collective-permute-done | bytes 524320 | tf_op jit(solution)/shard_map/ring/ppermute | solution.py:195
  49.2 3.5 %collective-permute-start.9 = (bf16[4,512,128]{2,1,0:T(8,128)(2,1)S(1)}, bf16[4,512,128]{2,1,0:T(8,128)(2,1)S(1)}, u32[]{:S(2)}, u32[]{:S(2)}) collective-permute-start(bf16[4,512,128]{2,1,0:T(8,128)(2,1)S(1)} %collective-permute-done.6.refs_4_), channel_id=1, source_target_pairs={{0,128},{128,1},{1,129},{129,2},{2,130},{130,3},{3,131},{131,0},{1... | collective-permute-start | bytes 1572872 | tf_op jit(solution)/shard_map/ring/ppermute | solution.py:195
  52.7 4.7 %attend.9.refs_4_ = f32[4,144,512]{2,1,0:T(8,128)S(1)} custom-call(s32[16]{0:T(128)S(1)} %copy-done.1, bf16[4,256,128]{2,1,0:T(8,128)(2,1)S(1)} %get-tuple-element.25.refs_1_, bf16[4,256,128]{2,1,0:T(8,128)(2,1)S(1)} %collective-permute-done.refs_2_, bf16[4,512,128]{2,1,0:T(8,128)(2,1)S(1)} %collective-permute-done.3.refs_3_, ...), custom_call_target="tpu_custom_call", output_to_operand_aliasing={{}: (5, {})} | custom-call | flops 8589934592 | bytes 8388608 | tf_op jit(solution)/shard_map/attend/pallas_call | solution.py:214
  57.5 0.0 collective-permute-done.5.refs_3_
  57.5 2.0 %collective-permute-start.8 = (bf16[2,512,128]{2,1,0:T(8,128)(2,1)S(1)}, bf16[2,512,128]{2,1,0:T(8,128)(2,1)S(1)}, u32[]{:S(2)}, u32[]{:S(2)}) collective-permute-start(bf16[2,512,128]{2,1,0:T(8,128)(2,1)S(1)} %get-tuple-element.45), channel_id=1, source_target_pairs={{0,128},{128,1},{1,129},{129,2},{2,130},{130,3},{3,131},{131,0},{1... | collective-permute-start | bytes 786440 | tf_op jit(solution)/shard_map/ring/ppermute | solution.py:195
  59.5 2.7 %collective-permute-start.7 = (bf16[2,512,128]{2,1,0:T(8,128)(2,1)S(1)}, bf16[2,512,128]{2,1,0:T(8,128)(2,1)S(1)}, u32[]{:S(2)}, u32[]{:S(2)}) collective-permute-start(bf16[2,512,128]{2,1,0:T(8,128)(2,1)S(1)} %get-tuple-element.46), channel_id=1, source_target_pairs={{0,128},{128,1},{1,129},{129,2},{2,130},{130,3},{3,131},{131,0},{1... | collective-permute-start | bytes 786440 | tf_op jit(solution)/shard_map/ring/ppermute | solution.py:195
  62.3 4.0 %attend.10.refs_4_ = f32[4,144,512]{2,1,0:T(8,128)S(1)} custom-call(s32[16]{0:T(128)S(1)} %copy-done.1, bf16[4,256,128]{2,1,0:T(8,128)(2,1)S(1)} %get-tuple-element.25.refs_1_, bf16[4,256,128]{2,1,0:T(8,128)(2,1)S(1)} %collective-permute-done.refs_2_, bf16[4,512,128]{2,1,0:T(8,128)(2,1)S(1)} %collective-permute-done.5.refs_3_, ...), custom_call_target="tpu_custom_call", output_to_operand_aliasing={{}: (4, {})} | custom-call | flops 4294967296 | bytes 8388608 | tf_op jit(solution)/shard_map/attend/pallas_call | solution.py:214
  66.3 0.0 collective-permute-done.9.refs_3_
  66.3 4.0 %attend.11.refs_4_ = f32[4,144,512]{2,1,0:T(8,128)S(1)} custom-call(s32[16]{0:T(128)S(1)} %copy-done.1, bf16[4,256,128]{2,1,0:T(8,128)(2,1)S(1)} %get-tuple-element.25.refs_1_, bf16[4,256,128]{2,1,0:T(8,128)(2,1)S(1)} %collective-permute-done.refs_2_, bf16[4,512,128]{2,1,0:T(8,128)(2,1)S(1)} %collective-permute-done.9.refs_3_, ...), custom_call_target="tpu_custom_call", output_to_operand_aliasing={{}: (4, {})} | custom-call | flops 4294967296 | bytes 8388608 | tf_op jit(solution)/shard_map/attend/pallas_call | solution.py:214
  70.4 0.0 collective-permute-done.8.refs_3_
  70.4 2.6 %attend.12.refs_4_ = f32[4,144,512]{2,1,0:T(8,128)S(1)} custom-call(s32[16]{0:T(128)S(1)} %copy-done.1, bf16[4,256,128]{2,1,0:T(8,128)(2,1)S(1)} %get-tuple-element.25.refs_1_, bf16[4,256,128]{2,1,0:T(8,128)(2,1)S(1)} %collective-permute-done.refs_2_, bf16[2,512,128]{2,1,0:T(8,128)(2,1)S(1)} %collective-permute-done.8.refs_3_, ...), custom_call_target="tpu_custom_call", output_to_operand_aliasing={{}: (4, {})} | custom-call | flops 2147483648 | bytes 8388608 | tf_op jit(solution)/shard_map/attend/pallas_call | solution.py:214
  72.9 0.0 collective-permute-done.7.refs_3_
  73.0 1.6 %attend.13.own_ref = f32[4,144,512]{2,1,0:T(8,128)S(1)} custom-call(s32[16]{0:T(128)S(1)} %copy-done.1, bf16[4,256,128]{2,1,0:T(8,128)(2,1)S(1)} %get-tuple-element.25.refs_1_, bf16[4,256,128]{2,1,0:T(8,128)(2,1)S(1)} %collective-permute-done.refs_2_, bf16[2,512,128]{2,1,0:T(8,128)(2,1)S(1)} %collective-permute-done.7.refs_3_, ...), custom_call_target="tpu_custom_call", output_to_operand_aliasing={{}: (4, {})} | custom-call | flops 2147483648 | bytes 8388608 | tf_op jit(solution)/shard_map/attend/pallas_call | solution.py:214
  74.6 0.1 collective-permute-start.10
  74.7 2.0 %collective-permute-done.10.other_ref = f32[4,144,256]{2,1,0:T(8,128)S(1)} collective-permute-done((f32[4,144,256]{2,1,0:T(8,128)S(1)}, f32[4,144,256]{2,1,0:T(8,128)S(1)}, u32[]{:S(2)}, u32[]{:S(2)}) %collective-permute-start.10) | collective-permute-done | bytes 589856 | tf_op jit(solution)/shard_map/swap_terms/ppermute | solution.py:198
  76.7 0.7 join.1
  77.5 11.9 %all_to_all.11.parts_ref = bf16[16,64,128]{2,1,0:T(8,128)(2,1)S(1)} all-to-all(bf16[16,64,128]{2,1,0:T(8,128)(2,1)S(1)} %join.1), channel_id=1, replica_groups=mesh['zlo'=2,'y'=4,'core'=2,'x'=4,'zhi'=4] {'y','x'}, dimensions={0} | all-to-all | bytes 524288 | tf_op jit(solution)/shard_map/heads_to_tokens/all_to_all | solution.py:250
  89.3 0.8 unpack.1
  (2 shorter events, 0.1 us)
Async XLA Ops:
  0.0 1.1 %copy-start = (bf16[3,1,64,2048]{3,2,1,0:T(8,128)(2,1)S(1)}, bf16[3,1,64,2048]{3,2,1,0:T(8,128)(2,1)}, u32[]{:S(2)}) copy-start(bf16[3,1,64,2048]{3,2,1,0:T(8,128)(2,1)} %param.2) | copy-start | bytes 2359300
  1.3 25.8 %copy-start.1 = (s32[16]{0:T(128)S(1)}, s32[16]{0:T(128)}, u32[]{:S(2)}) copy-start(s32[16]{0:T(128)} %lengths_ref.1) | copy-start | bytes 196
  22.6 2.5 %collective-permute-start.1 = (bf16[4,512,128]{2,1,0:T(8,128)(2,1)S(1)}, bf16[4,512,128]{2,1,0:T(8,128)(2,1)S(1)}, u32[]{:S(2)}, u32[]{:S(2)}) collective-permute-start(bf16[4,512,128]{2,1,0:T(8,128)(2,1)S(1)} %get-tuple-element.26.refs_3_), channel_id=1, source_target_pairs={{0,16},{16,0},{1,17},{17,1},{2,18},{18,2},{3,19},{19,3},{4,20},{20... | collective-permute-start | bytes 1572872 | tf_op jit(solution)/shard_map/swap_pairs/ppermute | solution.py:198
  22.7 2.4 %collective-permute-start = (bf16[4,256,128]{2,1,0:T(8,128)(2,1)S(1)}, bf16[4,256,128]{2,1,0:T(8,128)(2,1)S(1)}, u32[]{:S(2)}, u32[]{:S(2)}) collective-permute-start(bf16[4,256,128]{2,1,0:T(8,128)(2,1)S(1)} %get-tuple-element.25.refs_1_), channel_id=1, source_target_pairs={{0,16},{16,0},{1,17},{17,1},{2,18},{18,2},{3,19},{19,3},{4,20},{20... | collective-permute-start | bytes 786440 | tf_op jit(solution)/shard_map/swap_queries/ppermute | solution.py:198
  23.2 9.2 %collective-permute-start.2 = (bf16[4,512,128]{2,1,0:T(8,128)(2,1)S(1)}, bf16[4,512,128]{2,1,0:T(8,128)(2,1)S(1)}, u32[]{:S(2)}, u32[]{:S(2)}) collective-permute-start(bf16[4,512,128]{2,1,0:T(8,128)(2,1)S(1)} %get-tuple-element.26.refs_3_), channel_id=1, source_target_pairs={{0,128},{128,1},{1,129},{129,2},{2,130},{130,3},{3,131},{131,0},{1... | collective-permute-start | bytes 1572872 | tf_op jit(solution)/shard_map/ring/ppermute | solution.py:195
  25.1 12.9 %collective-permute-start.4 = (bf16[4,512,128]{2,1,0:T(8,128)(2,1)S(1)}, bf16[4,512,128]{2,1,0:T(8,128)(2,1)S(1)}, u32[]{:S(2)}, u32[]{:S(2)}) collective-permute-start(bf16[4,512,128]{2,1,0:T(8,128)(2,1)S(1)} %collective-permute-done.1), channel_id=1, source_target_pairs={{0,128},{128,1},{1,129},{129,2},{2,130},{130,3},{3,131},{131,0},{1... | collective-permute-start | bytes 1572872 | tf_op jit(solution)/shard_map/ring/ppermute | solution.py:195
  32.4 14.0 %collective-permute-start.3 = (bf16[4,512,128]{2,1,0:T(8,128)(2,1)S(1)}, bf16[4,512,128]{2,1,0:T(8,128)(2,1)S(1)}, u32[]{:S(2)}, u32[]{:S(2)}) collective-permute-start(bf16[4,512,128]{2,1,0:T(8,128)(2,1)S(1)} %collective-permute-done.2.refs_3_), channel_id=1, source_target_pairs={{0,128},{128,1},{1,129},{129,2},{2,130},{130,3},{3,131},{131,0},{1... | collective-permute-start | bytes 1572872 | tf_op jit(solution)/shard_map/ring/ppermute | solution.py:195
  38.0 11.2 %collective-permute-start.6 = (bf16[4,512,128]{2,1,0:T(8,128)(2,1)S(1)}, bf16[4,512,128]{2,1,0:T(8,128)(2,1)S(1)}, u32[]{:S(2)}, u32[]{:S(2)}) collective-permute-start(bf16[4,512,128]{2,1,0:T(8,128)(2,1)S(1)} %collective-permute-done.4.refs_4_), channel_id=1, source_target_pairs={{0,128},{128,1},{1,129},{129,2},{2,130},{130,3},{3,131},{131,0},{1... | collective-permute-start | bytes 1572872 | tf_op jit(solution)/shard_map/ring/ppermute | solution.py:195
  46.4 11.1 %collective-permute-start.5 = (bf16[4,512,128]{2,1,0:T(8,128)(2,1)S(1)}, bf16[4,512,128]{2,1,0:T(8,128)(2,1)S(1)}, u32[]{:S(2)}, u32[]{:S(2)}) collective-permute-start(bf16[4,512,128]{2,1,0:T(8,128)(2,1)S(1)} %collective-permute-done.3.refs_3_), channel_id=1, source_target_pairs={{0,128},{128,1},{1,129},{129,2},{2,130},{130,3},{3,131},{131,0},{1... | collective-permute-start | bytes 1572872 | tf_op jit(solution)/shard_map/ring/ppermute | solution.py:195
  49.2 17.1 %collective-permute-start.9 = (bf16[4,512,128]{2,1,0:T(8,128)(2,1)S(1)}, bf16[4,512,128]{2,1,0:T(8,128)(2,1)S(1)}, u32[]{:S(2)}, u32[]{:S(2)}) collective-permute-start(bf16[4,512,128]{2,1,0:T(8,128)(2,1)S(1)} %collective-permute-done.6.refs_4_), channel_id=1, source_target_pairs={{0,128},{128,1},{1,129},{129,2},{2,130},{130,3},{3,131},{131,0},{1... | collective-permute-start | bytes 1572872 | tf_op jit(solution)/shard_map/ring/ppermute | solution.py:195
  57.5 12.8 %collective-permute-start.8 = (bf16[2,512,128]{2,1,0:T(8,128)(2,1)S(1)}, bf16[2,512,128]{2,1,0:T(8,128)(2,1)S(1)}, u32[]{:S(2)}, u32[]{:S(2)}) collective-permute-start(bf16[2,512,128]{2,1,0:T(8,128)(2,1)S(1)} %get-tuple-element.45), channel_id=1, source_target_pairs={{0,128},{128,1},{1,129},{129,2},{2,130},{130,3},{3,131},{131,0},{1... | collective-permute-start | bytes 786440 | tf_op jit(solution)/shard_map/ring/ppermute | solution.py:195
  59.5 13.4 %collective-permute-start.7 = (bf16[2,512,128]{2,1,0:T(8,128)(2,1)S(1)}, bf16[2,512,128]{2,1,0:T(8,128)(2,1)S(1)}, u32[]{:S(2)}, u32[]{:S(2)}) collective-permute-start(bf16[2,512,128]{2,1,0:T(8,128)(2,1)S(1)} %get-tuple-element.46), channel_id=1, source_target_pairs={{0,128},{128,1},{1,129},{129,2},{2,130},{130,3},{3,131},{131,0},{1... | collective-permute-start | bytes 786440 | tf_op jit(solution)/shard_map/ring/ppermute | solution.py:195
  74.6 2.1 %collective-permute-start.10 = (f32[4,144,256]{2,1,0:T(8,128)S(1)}, f32[4,144,256]{2,1,0:T(8,128)S(1)}, u32[]{:S(2)}, u32[]{:S(2)}) collective-permute-start(f32[4,144,256]{2,1,0:T(8,128)S(1)} %slice.12), channel_id=1, source_target_pairs={{0,16},{16,0},{1,17},{17,1},{2,18},{18,2},{3,19},{19,3},{4,20},{20... | collective-permute-start | bytes 1769480 | tf_op jit(solution)/shard_map/swap_terms/ppermute | solution.py:198

commit v7 on v5

--- a/solution.py
+++ b/solution.py
@@ -41,7 +41,7 @@
         pair_ref[span, ROWS + HD :] = turned[:, HD:]
 
 
-def attend(distance, first, *refs):
+def attend(distance, first, half, *refs):
     refs = list(refs)
     lengths_ref, own_ref, other_ref = refs[:3]
     arrivals = refs[3:-1] if first else refs[3:-2]
@@ -57,11 +57,17 @@
     offset = (source_zed // 2) * SLICE
     aligned = distance % 2 == 0
 
+    width = state_ref.shape[2]
+    columns = slice(ROWS if half == 1 else 0, ROWS if half == 0 else 2 * ROWS)
+
     ones = jnp.where(lax.broadcasted_iota(jnp.int32, (16, ROWS), 0) < 8, 1.0, 0.0)
     ones = ones.astype(jnp.bfloat16)
 
     def add(step, count, last):
-        queries = jnp.concatenate([own_ref[step], other_ref[step]], axis=0)
+        if half is None:
+            queries = jnp.concatenate([own_ref[step], other_ref[step]], axis=0)
+        else:
+            queries = (own_ref, other_ref)[half][step]
         scores, values = [], []
         for span, number in pieces:
             if span >= count:
@@ -74,15 +80,18 @@
                 preferred_element_type=jnp.float32,
             )
             live = lengths_ref[source_zlo * 8 + 2 * span + source_core[number]]
-            row = lax.broadcasted_iota(jnp.int32, (SLICE, 2 * ROWS), 0)
-            other_half = lax.broadcasted_iota(jnp.int32, (SLICE, 2 * ROWS), 1) >= ROWS
+            row = lax.broadcasted_iota(jnp.int32, (SLICE, width), 0)
+            other_half = lax.broadcasted_iota(jnp.int32, (SLICE, width), 1) >= ROWS
             for part in range(4):
                 rows = score[part * SLICE : (part + 1) * SLICE]
                 bound = live - part * ROWS - offset
                 if span == last:
                     own_bound = jnp.where(source_core[number] <= core, bound, 0)
                     other_bound = jnp.where(source_core[number] <= 1 - core, bound, 0)
-                    bound = jnp.where(other_half, other_bound, own_bound)
+                    if half is None:
+                        bound = jnp.where(other_half, other_bound, own_bound)
+                    else:
+                        bound = (own_bound, other_bound)[half]
                     rows = jnp.where(row < bound, rows, FILL)
                 elif part >= 2:
                     rows = jnp.where(row < bound, rows, FILL)
@@ -92,7 +101,7 @@
         scores = jnp.concatenate(scores, axis=0)
         peak = jnp.max(scores, axis=0, keepdims=True)
         if not first:
-            old_peak = before_ref[step, HD + 8 : HD + 9, :]
+            old_peak = before_ref[step, HD + 8 : HD + 9, columns]
             peak = jnp.maximum(old_peak, peak)
         shifted = (scores - peak) * SCALE
         weights = jnp.exp2(shifted)
@@ -105,9 +114,9 @@
         fresh = fresh[: HD + 8]
         if not first:
             keep = jnp.exp2((old_peak - peak) * SCALE)
-            fresh = before_ref[step, : HD + 8, :] * keep + fresh
+            fresh = before_ref[step, : HD + 8, columns] * keep + fresh
         state_ref[step, : HD + 8, :] = fresh
-        state_ref[step, HD + 8 :, :] = jnp.broadcast_to(peak, (8, 2 * ROWS))
+        state_ref[step, HD + 8 :, :] = jnp.broadcast_to(peak, (8, width))
 
     if aligned:
         for step in range(4):
@@ -131,13 +140,13 @@
     offset = lax.axis_index("zhi") * SLICE
     for step in range(4):
         live = lengths_ref[zlo * 8 + 2 * step + core]
-        first_peak = own_ref[step, HD + 8 : HD + 9, :ROWS]
+        first_peak = own_ref[step, HD + 8 : HD + 9, :]
         second_peak = other_ref[step, HD + 8 : HD + 9, :]
         peak = jnp.maximum(first_peak, second_peak)
         first = jnp.exp2((first_peak - peak) * SCALE)
         second = jnp.exp2((second_peak - peak) * SCALE)
-        total = own_ref[step, HD : HD + 1, :ROWS] * first + other_ref[step, HD : HD + 1, :] * second
-        numerator = own_ref[step, :HD, :ROWS] * first + other_ref[step, :HD, :] * second
+        total = own_ref[step, HD : HD + 1, :] * first + other_ref[step, HD : HD + 1, :] * second
+        numerator = own_ref[step, :HD, :] * first + other_ref[step, :HD, :] * second
         result = (numerator / total).T
         row = lax.broadcasted_iota(jnp.int32, (SLICE, HD), 0)
         for piece in range(4):
@@ -183,9 +192,12 @@
     route = [(place[z], place[(z + 1) % chips]) for z in range(chips)]
     route += [(place[z] + 4, place[(z - 1) % chips] + 4) for z in range(chips)]
 
-    def hop(block):
+    across = [(place[z] + 4, place[(z + 1) % chips]) for z in range(chips)]
+    across += [(place[z], place[(z - 1) % chips] + 4) for z in range(chips)]
+
+    def hop(block, pairs=route):
         with jax.named_scope("ring"):
-            return lax.ppermute(block, RING, route)
+            return lax.ppermute(block, RING, pairs)
 
     def swap(block):
         return lax.ppermute(block, "core", [(0, 1), (1, 0)])
@@ -193,24 +205,22 @@
     first_chain = hop(pairs)
     with jax.named_scope("swap_queries"):
         other = swap(own)
-    with jax.named_scope("swap_pairs"):
-        second = swap(pairs)
-    other, second = lax.optimization_barrier((other, second))
-    second_chain = hop(second)
-    state_shape = jax.ShapeDtypeStruct((4, STATE, 2 * ROWS), jnp.float32)
-
-    def step(arrivals, distance, state):
+    other, again = lax.optimization_barrier((other, pairs))
+    second_chain = hop(again, across)
+
+    def step(arrivals, distance, state, half=None):
         first = state is None
         operands = [lengths, own, other] + arrivals + ([] if first else [state])
         count = 4 * len(arrivals)
+        width = 2 * ROWS if half is None else ROWS
         with jax.named_scope("attend"):
             return call(
-                functools.partial(attend, distance, first),
-                state_shape,
+                functools.partial(attend, distance, first, half),
+                jax.ShapeDtypeStruct((4, STATE, width), jnp.float32),
                 [smem] + [vmem] * (len(operands) - 1),
-                flops=4 * HD * ROWS * ROWS * 8 * count * 4,
+                flops=16 * HD * ROWS * width * 4 * count,
                 moved=8 * 2**20,
-                input_output_aliases={} if first else {len(operands) - 1: 0},
+                input_output_aliases={} if first or half is not None else {len(operands) - 1: 0},
             )(*operands)
 
     state = step([pairs], 0, None)
@@ -222,15 +232,16 @@
         if distance < 3:
             second_chain = hop(second_chain)
         state = step(arrived, distance, state)
-    state = step([first_chain], 4, state)
+    theirs = step([first_chain], 4, state, 1)
     with jax.named_scope("swap_terms"):
-        theirs = swap(state[:, :, ROWS:])
+        theirs = swap(theirs)
+    mine = step([first_chain], 4, state, 0)
     with jax.named_scope("join"):
         attended = call(
             join,
             jax.ShapeDtypeStruct((heads, SLICE, HD), bf16),
             [smem, vmem, vmem],
-        )(lengths, state, theirs)
+        )(lengths, mine, theirs)
     with jax.named_scope("heads_to_tokens"):
         attended = lax.all_to_all(attended, ("y", "x"), 0, 0, tiled=True)
     with jax.named_scope("unpack"):

time: 89 us -> 91.8 us (1.031)
  waiting for transfers between devices: 16.1 us -> 20.4 us
  starting transfers between devices: 25.6 us -> 23 us
  Pallas kernels: 14 us -> 15 us
    ppermute x7, waiting for transfers between devices: 14.5 us -> 20.4 us  [hop(): return lax.ppermute(block, RING, pairs)]
    ppermute x7, starting transfers between devices: 21.7 us -> 17.6 us  [hop(): return lax.ppermute(block, RING, pairs)]
    ppermute x3 -> x2, waiting for transfers between devices: 1.64 us -> 0.01 us  [swap(): return lax.ppermute(block, 'core', [(0, 1), (1, 0)])]
    ppermute x3 -> x2, starting transfers between devices: 3.91 us -> 5.45 us  [swap(): return lax.ppermute(block, 'core', [(0, 1), (1, 0)])]
    pallas_call x5 -> x6, Pallas kernels: 12.3 us -> 13.2 us  [step(): call(functools.partial(attend, distance, first, half), jax.ShapeDtypeStru...]
  transfers between devices with their start and end apart: 10 -> 9, of which waited for: 7 -> 5; matrix products, arithmetic and copies ran while one was open for 0% -> 0% of each run, Pallas kernels for 10% -> 12%
where the time goes in v7:
time: 91.8 us; the launch traced here: 91.6 us
  blocking collectives  32 us (35%)
  starting transfers between devices  23 us (25%)
  waiting for transfers between devices  20.4 us (22%)
  Pallas kernels  15 us (16%)
  local copies, waits for them, and re-layouts  1.14 us (1%)
    all_to_all x1, blocking collectives, shards(): parts = lax.all_to_all(parts, ('y', 'x'), 0, 0, tiled=True)  20.9 us
    ppermute x7, waiting for transfers between devices, hop(): return lax.ppermute(block, RING, pairs)  20.4 us
    ppermute x7, starting transfers between devices, hop(): return lax.ppermute(block, RING, pairs)  17.6 us
    pallas_call x6, Pallas kernels, step(): call(functools.partial(attend, distance, first, half), jax.ShapeDtypeStru...  13.2 us
    all_to_all x1, blocking collectives, shards(): attended = lax.all_to_all(attended, ('y', 'x'), 0, 0, tiled=True)  11.1 us
    ppermute x2, starting transfers between devices, swap(): return lax.ppermute(block, 'core', [(0, 1), (1, 0)])  5.45 us
  transfers between devices with their start and end apart: 9, of which 5 were waited for; matrix products, arithmetic and copies ran while one was open for 0% of the time, Pallas kernels for 12%

profile of v7, /device:TPU:1, one launch (start us, length us, event | category | flops | bytes accessed | tf_op | source)
XLA Modules:
  0.0 91.6 jit_solution(16384695915719128592)
XLA Ops:
  0.0 0.0 copy-start
  0.0 1.1 %copy-done = bf16[3,1,64,2048]{3,2,1,0:T(8,128)(2,1)S(1)} copy-done((bf16[3,1,64,2048]{3,2,1,0:T(8,128)(2,1)S(1)}, bf16[3,1,64,2048]{3,2,1,0:T(8,128)(2,1)}, u32[]{:S(2)}) %copy-start) | copy-done | bytes 786456
  1.1 0.1 pack.1
  1.3 0.0 copy-start.1
  1.3 20.9 %all_to_all.10.parts_ref = bf16[16,192,128]{2,1,0:T(8,128)(2,1)S(1)} all-to-all(bf16[16,192,128]{2,1,0:T(8,128)(2,1)S(1)} %pack.1), channel_id=1, replica_groups=mesh['zlo'=2,'y'=4,'core'=2,'x'=4,'zhi'=4] {'y','x'}, dimensions={0} | all-to-all | bytes 1572864 | tf_op jit(solution)/shard_map/tokens_to_heads/all_to_all | solution.py:179
  22.2 0.1 split.1
  22.3 1.9 %collective-permute-start = (bf16[4,256,128]{2,1,0:T(8,128)(2,1)S(1)}, bf16[4,256,128]{2,1,0:T(8,128)(2,1)S(1)}, u32[]{:S(2)}, u32[]{:S(2)}) collective-permute-start(bf16[4,256,128]{2,1,0:T(8,128)(2,1)S(1)} %get-tuple-element.21.refs_1_), channel_id=1, source_target_pairs={{0,16},{16,0},{1,17},{17,1},{2,18},{18,2},{3,19},{19,3},{4,20},{20... | collective-permute-start | bytes 786440 | tf_op jit(solution)/shard_map/swap_queries/ppermute | solution.py:203
  24.2 5.6 %collective-permute-start.1 = (bf16[4,512,128]{2,1,0:T(8,128)(2,1)S(1)}, bf16[4,512,128]{2,1,0:T(8,128)(2,1)S(1)}, u32[]{:S(2)}, u32[]{:S(2)}) collective-permute-start(bf16[4,512,128]{2,1,0:T(8,128)(2,1)S(1)} %get-tuple-element.25.refs_3_), channel_id=1, source_target_pairs={{0,128},{128,1},{1,129},{129,2},{2,130},{130,3},{3,131},{131,0},{1... | collective-permute-start | bytes 1572872 | tf_op jit(solution)/shard_map/ring/ppermute | solution.py:200
  29.8 0.0 collective-permute-done.refs_2_
  29.8 0.0 collective-permute-start.3
  29.8 0.0 copy-done.1
  29.8 3.0 %attend.6.refs_5_ = f32[4,144,512]{2,1,0:T(8,128)S(1)} custom-call(s32[16]{0:T(128)S(1)} %copy-done.1, bf16[4,256,128]{2,1,0:T(8,128)(2,1)S(1)} %get-tuple-element.21.refs_1_, bf16[4,256,128]{2,1,0:T(8,128)(2,1)S(1)} %collective-permute-done.refs_2_, bf16[4,512,128]{2,1,0:T(8,128)(2,1)S(1)} %get-tuple-element.25.refs_3_), custom_call_target="tpu_custom_call" | custom-call | flops 4294967296 | bytes 8388608 | tf_op jit(solution)/shard_map/attend/pallas_call | solution.py:217
  32.8 6.9 %collective-permute-done.1.refs_3_ = bf16[4,512,128]{2,1,0:T(8,128)(2,1)S(1)} collective-permute-done((bf16[4,512,128]{2,1,0:T(8,128)(2,1)S(1)}, bf16[4,512,128]{2,1,0:T(8,128)(2,1)S(1)}, u32[]{:S(2)}, u32[]{:S(2)}) %collective-permute-start.1) | collective-permute-done | bytes 524320 | tf_op jit(solution)/shard_map/ring/ppermute | solution.py:200
  39.7 3.1 %collective-permute-start.2 = (bf16[4,512,128]{2,1,0:T(8,128)(2,1)S(1)}, bf16[4,512,128]{2,1,0:T(8,128)(2,1)S(1)}, u32[]{:S(2)}, u32[]{:S(2)}) collective-permute-start(bf16[4,512,128]{2,1,0:T(8,128)(2,1)S(1)} %collective-permute-done.1.refs_3_), channel_id=1, source_target_pairs={{0,128},{128,1},{1,129},{129,2},{2,130},{130,3},{3,131},{131,0},{1... | collective-permute-start | bytes 1572872 | tf_op jit(solution)/shard_map/ring/ppermute | solution.py:200
  42.8 0.0 collective-permute-done.3.refs_4_
  42.8 1.8 %collective-permute-start.5 = (bf16[4,512,128]{2,1,0:T(8,128)(2,1)S(1)}, bf16[4,512,128]{2,1,0:T(8,128)(2,1)S(1)}, u32[]{:S(2)}, u32[]{:S(2)}) collective-permute-start(bf16[4,512,128]{2,1,0:T(8,128)(2,1)S(1)} %collective-permute-done.3.refs_4_), channel_id=1, source_target_pairs={{0,128},{128,1},{1,129},{129,2},{2,130},{130,3},{3,131},{131,0},{1... | collective-permute-start | bytes 1572872 | tf_op jit(solution)/shard_map/ring/ppermute | solution.py:200
  44.6 0.7 attend.7.refs_5_
  45.3 3.6 %collective-permute-done.2.refs_3_ = bf16[4,512,128]{2,1,0:T(8,128)(2,1)S(1)} collective-permute-done((bf16[4,512,128]{2,1,0:T(8,128)(2,1)S(1)}, bf16[4,512,128]{2,1,0:T(8,128)(2,1)S(1)}, u32[]{:S(2)}, u32[]{:S(2)}) %collective-permute-start.2) | collective-permute-done | bytes 524320 | tf_op jit(solution)/shard_map/ring/ppermute | solution.py:200
  48.9 3.1 %collective-permute-start.4 = (bf16[4,512,128]{2,1,0:T(8,128)(2,1)S(1)}, bf16[4,512,128]{2,1,0:T(8,128)(2,1)S(1)}, u32[]{:S(2)}, u32[]{:S(2)}) collective-permute-start(bf16[4,512,128]{2,1,0:T(8,128)(2,1)S(1)} %collective-permute-done.2.refs_3_), channel_id=1, source_target_pairs={{0,128},{128,1},{1,129},{129,2},{2,130},{130,3},{3,131},{131,0},{1... | collective-permute-start | bytes 1572872 | tf_op jit(solution)/shard_map/ring/ppermute | solution.py:200
  52.1 2.5 %collective-permute-done.5.refs_4_ = bf16[4,512,128]{2,1,0:T(8,128)(2,1)S(1)} collective-permute-done((bf16[4,512,128]{2,1,0:T(8,128)(2,1)S(1)}, bf16[4,512,128]{2,1,0:T(8,128)(2,1)S(1)}, u32[]{:S(2)}, u32[]{:S(2)}) %collective-permute-start.5) | collective-permute-done | bytes 524320 | tf_op jit(solution)/shard_map/ring/ppermute | solution.py:200
  54.6 3.1 %collective-permute-start.7 = (bf16[4,512,128]{2,1,0:T(8,128)(2,1)S(1)}, bf16[4,512,128]{2,1,0:T(8,128)(2,1)S(1)}, u32[]{:S(2)}, u32[]{:S(2)}) collective-permute-start(bf16[4,512,128]{2,1,0:T(8,128)(2,1)S(1)} %collective-permute-done.5.refs_4_), channel_id=1, source_target_pairs={{0,128},{128,1},{1,129},{129,2},{2,130},{130,3},{3,131},{131,0},{1... | collective-permute-start | bytes 1572872 | tf_op jit(solution)/shard_map/ring/ppermute | solution.py:200
  57.7 4.8 %attend.8.refs_5_ = f32[4,144,512]{2,1,0:T(8,128)S(1)} custom-call(s32[16]{0:T(128)S(1)} %copy-done.1, bf16[4,256,128]{2,1,0:T(8,128)(2,1)S(1)} %get-tuple-element.21.refs_1_, bf16[4,256,128]{2,1,0:T(8,128)(2,1)S(1)} %collective-permute-done.refs_2_, bf16[4,512,128]{2,1,0:T(8,128)(2,1)S(1)} %collective-permute-done.2.refs_3_, ...), custom_call_target="tpu_custom_call", output_to_operand_aliasing={{}: (5, {})} | custom-call | flops 8589934592 | bytes 8388608 | tf_op jit(solution)/shard_map/attend/pallas_call | solution.py:217
  62.4 0.0 collective-permute-done.4.refs_3_
  62.5 0.8 collective-permute-start.6
  63.3 2.5 %collective-permute-done.7.refs_4_ = bf16[4,512,128]{2,1,0:T(8,128)(2,1)S(1)} collective-permute-done((bf16[4,512,128]{2,1,0:T(8,128)(2,1)S(1)}, bf16[4,512,128]{2,1,0:T(8,128)(2,1)S(1)}, u32[]{:S(2)}, u32[]{:S(2)}) %collective-permute-start.7) | collective-permute-done | bytes 524320 | tf_op jit(solution)/shard_map/ring/ppermute | solution.py:200
  65.8 0.7 attend.9.refs_4_
  66.5 4.9 %collective-permute-done.6.refs_3_ = bf16[4,512,128]{2,1,0:T(8,128)(2,1)S(1)} collective-permute-done((bf16[4,512,128]{2,1,0:T(8,128)(2,1)S(1)}, bf16[4,512,128]{2,1,0:T(8,128)(2,1)S(1)}, u32[]{:S(2)}, u32[]{:S(2)}) %collective-permute-start.6) | collective-permute-done | bytes 524320 | tf_op jit(solution)/shard_map/ring/ppermute | solution.py:200
  71.4 2.0 %attend.11 = f32[4,144,256]{2,1,0:T(8,128)S(1)} custom-call(s32[16]{0:T(128)S(1)} %copy-done.1, bf16[4,256,128]{2,1,0:T(8,128)(2,1)S(1)} %get-tuple-element.21.refs_1_, bf16[4,256,128]{2,1,0:T(8,128)(2,1)S(1)} %collective-permute-done.refs_2_, bf16[4,512,128]{2,1,0:T(8,128)(2,1)S(1)} %collective-permute-done.6.refs_3_, f32[4,144,512]{2,1,0:T(8,128)S(1)} %attend.9.refs_4_), custom_call_target="tpu_custom_call" | custom-call | flops 2147483648 | bytes 8388608 | tf_op jit(solution)/shard_map/attend/pallas_call | solution.py:217
  73.4 3.6 %collective-permute-start.8 = (f32[4,144,256]{2,1,0:T(8,128)S(1)}, f32[4,144,256]{2,1,0:T(8,128)S(1)}, u32[]{:S(2)}, u32[]{:S(2)}) collective-permute-start(f32[4,144,256]{2,1,0:T(8,128)S(1)} %attend.11), channel_id=1, source_target_pairs={{0,16},{16,0},{1,17},{17,1},{2,18},{18,2},{3,19},{19,3},{4,20},{20... | collective-permute-start | bytes 1769480 | tf_op jit(solution)/shard_map/swap_terms/ppermute | solution.py:203
  77.0 2.0 %attend.10.own_ref = f32[4,144,256]{2,1,0:T(8,128)S(1)} custom-call(s32[16]{0:T(128)S(1)} %copy-done.1, bf16[4,256,128]{2,1,0:T(8,128)(2,1)S(1)} %get-tuple-element.21.refs_1_, bf16[4,256,128]{2,1,0:T(8,128)(2,1)S(1)} %collective-permute-done.refs_2_, bf16[4,512,128]{2,1,0:T(8,128)(2,1)S(1)} %collective-permute-done.6.refs_3_, f32[4,144,512]{2,1,0:T(8,128)S(1)} %attend.9.refs_4_), custom_call_target="tpu_custom_call" | custom-call | flops 2147483648 | bytes 8388608 | tf_op jit(solution)/shard_map/attend/pallas_call | solution.py:217
  79.0 0.0 collective-permute-done.8.other_ref
  79.0 0.7 join.1
  79.7 11.1 %all_to_all.11.parts_ref = bf16[16,64,128]{2,1,0:T(8,128)(2,1)S(1)} all-to-all(bf16[16,64,128]{2,1,0:T(8,128)(2,1)S(1)} %join.1), channel_id=1, replica_groups=mesh['zlo'=2,'y'=4,'core'=2,'x'=4,'zhi'=4] {'y','x'}, dimensions={0} | all-to-all | bytes 524288 | tf_op jit(solution)/shard_map/heads_to_tokens/all_to_all | solution.py:246
  90.9 0.8 unpack.1
Async XLA Ops:
  0.0 1.1 %copy-start = (bf16[3,1,64,2048]{3,2,1,0:T(8,128)(2,1)S(1)}, bf16[3,1,64,2048]{3,2,1,0:T(8,128)(2,1)}, u32[]{:S(2)}) copy-start(bf16[3,1,64,2048]{3,2,1,0:T(8,128)(2,1)} %param.2) | copy-start | bytes 2359300
  1.3 28.5 %copy-start.1 = (s32[16]{0:T(128)S(1)}, s32[16]{0:T(128)}, u32[]{:S(2)}) copy-start(s32[16]{0:T(128)} %lengths_ref.1) | copy-start | bytes 196
  22.3 7.5 %collective-permute-start = (bf16[4,256,128]{2,1,0:T(8,128)(2,1)S(1)}, bf16[4,256,128]{2,1,0:T(8,128)(2,1)S(1)}, u32[]{:S(2)}, u32[]{:S(2)}) collective-permute-start(bf16[4,256,128]{2,1,0:T(8,128)(2,1)S(1)} %get-tuple-element.21.refs_1_), channel_id=1, source_target_pairs={{0,16},{16,0},{1,17},{17,1},{2,18},{18,2},{3,19},{19,3},{4,20},{20... | collective-permute-start | bytes 786440 | tf_op jit(solution)/shard_map/swap_queries/ppermute | solution.py:203
  24.2 15.5 %collective-permute-start.1 = (bf16[4,512,128]{2,1,0:T(8,128)(2,1)S(1)}, bf16[4,512,128]{2,1,0:T(8,128)(2,1)S(1)}, u32[]{:S(2)}, u32[]{:S(2)}) collective-permute-start(bf16[4,512,128]{2,1,0:T(8,128)(2,1)S(1)} %get-tuple-element.25.refs_3_), channel_id=1, source_target_pairs={{0,128},{128,1},{1,129},{129,2},{2,130},{130,3},{3,131},{131,0},{1... | collective-permute-start | bytes 1572872 | tf_op jit(solution)/shard_map/ring/ppermute | solution.py:200
  29.8 13.1 %collective-permute-start.3 = (bf16[4,512,128]{2,1,0:T(8,128)(2,1)S(1)}, bf16[4,512,128]{2,1,0:T(8,128)(2,1)S(1)}, u32[]{:S(2)}, u32[]{:S(2)}) collective-permute-start(bf16[4,512,128]{2,1,0:T(8,128)(2,1)S(1)} %get-tuple-element.25.refs_3_), channel_id=1, source_target_pairs={{16,128},{144,1},{17,129},{145,2},{18,130},{146,3},{19,131},{147,0... | collective-permute-start | bytes 1572872 | tf_op jit(solution)/shard_map/ring/ppermute | solution.py:200
  39.7 9.2 %collective-permute-start.2 = (bf16[4,512,128]{2,1,0:T(8,128)(2,1)S(1)}, bf16[4,512,128]{2,1,0:T(8,128)(2,1)S(1)}, u32[]{:S(2)}, u32[]{:S(2)}) collective-permute-start(bf16[4,512,128]{2,1,0:T(8,128)(2,1)S(1)} %collective-permute-done.1.refs_3_), channel_id=1, source_target_pairs={{0,128},{128,1},{1,129},{129,2},{2,130},{130,3},{3,131},{131,0},{1... | collective-permute-start | bytes 1572872 | tf_op jit(solution)/shard_map/ring/ppermute | solution.py:200
  42.8 11.7 %collective-permute-start.5 = (bf16[4,512,128]{2,1,0:T(8,128)(2,1)S(1)}, bf16[4,512,128]{2,1,0:T(8,128)(2,1)S(1)}, u32[]{:S(2)}, u32[]{:S(2)}) collective-permute-start(bf16[4,512,128]{2,1,0:T(8,128)(2,1)S(1)} %collective-permute-done.3.refs_4_), channel_id=1, source_target_pairs={{0,128},{128,1},{1,129},{129,2},{2,130},{130,3},{3,131},{131,0},{1... | collective-permute-start | bytes 1572872 | tf_op jit(solution)/shard_map/ring/ppermute | solution.py:200
  48.9 13.5 %collective-permute-start.4 = (bf16[4,512,128]{2,1,0:T(8,128)(2,1)S(1)}, bf16[4,512,128]{2,1,0:T(8,128)(2,1)S(1)}, u32[]{:S(2)}, u32[]{:S(2)}) collective-permute-start(bf16[4,512,128]{2,1,0:T(8,128)(2,1)S(1)} %collective-permute-done.2.refs_3_), channel_id=1, source_target_pairs={{0,128},{128,1},{1,129},{129,2},{2,130},{130,3},{3,131},{131,0},{1... | collective-permute-start | bytes 1572872 | tf_op jit(solution)/shard_map/ring/ppermute | solution.py:200
  54.6 11.2 %collective-permute-start.7 = (bf16[4,512,128]{2,1,0:T(8,128)(2,1)S(1)}, bf16[4,512,128]{2,1,0:T(8,128)(2,1)S(1)}, u32[]{:S(2)}, u32[]{:S(2)}) collective-permute-start(bf16[4,512,128]{2,1,0:T(8,128)(2,1)S(1)} %collective-permute-done.5.refs_4_), channel_id=1, source_target_pairs={{0,128},{128,1},{1,129},{129,2},{2,130},{130,3},{3,131},{131,0},{1... | collective-permute-start | bytes 1572872 | tf_op jit(solution)/shard_map/ring/ppermute | solution.py:200
  62.5 9.0 %collective-permute-start.6 = (bf16[4,512,128]{2,1,0:T(8,128)(2,1)S(1)}, bf16[4,512,128]{2,1,0:T(8,128)(2,1)S(1)}, u32[]{:S(2)}, u32[]{:S(2)}) collective-permute-start(bf16[4,512,128]{2,1,0:T(8,128)(2,1)S(1)} %collective-permute-done.4.refs_3_), channel_id=1, source_target_pairs={{0,128},{128,1},{1,129},{129,2},{2,130},{130,3},{3,131},{131,0},{1... | collective-permute-start | bytes 1572872 | tf_op jit(solution)/shard_map/ring/ppermute | solution.py:200
  73.4 5.6 %collective-permute-start.8 = (f32[4,144,256]{2,1,0:T(8,128)S(1)}, f32[4,144,256]{2,1,0:T(8,128)S(1)}, u32[]{:S(2)}, u32[]{:S(2)}) collective-permute-start(f32[4,144,256]{2,1,0:T(8,128)S(1)} %attend.11), channel_id=1, source_target_pairs={{0,16},{16,0},{1,17},{17,1},{2,18},{18,2},{3,19},{19,3},{4,20},{20... | collective-permute-start | bytes 1769480 | tf_op jit(solution)/shard_map/swap_terms/ppermute | solution.py:203

commit v8 on v7

--- a/solution.py
+++ b/solution.py
@@ -192,12 +192,9 @@
     route = [(place[z], place[(z + 1) % chips]) for z in range(chips)]
     route += [(place[z] + 4, place[(z - 1) % chips] + 4) for z in range(chips)]
 
-    across = [(place[z] + 4, place[(z + 1) % chips]) for z in range(chips)]
-    across += [(place[z], place[(z - 1) % chips] + 4) for z in range(chips)]
-
-    def hop(block, pairs=route):
+    def hop(block):
         with jax.named_scope("ring"):
-            return lax.ppermute(block, RING, pairs)
+            return lax.ppermute(block, RING, route)
 
     def swap(block):
         return lax.ppermute(block, "core", [(0, 1), (1, 0)])
@@ -205,8 +202,10 @@
     first_chain = hop(pairs)
     with jax.named_scope("swap_queries"):
         other = swap(own)
-    other, again = lax.optimization_barrier((other, pairs))
-    second_chain = hop(again, across)
+    with jax.named_scope("swap_pairs"):
+        second = swap(pairs)
+    other, second = lax.optimization_barrier((other, second))
+    second_chain = hop(second)
 
     def step(arrivals, distance, state, half=None):
         first = state is None

time: 91.8 us -> 88.5 us (0.964)
  waiting for transfers between devices: 20.4 us -> 14.5 us
  starting transfers between devices: 23 us -> 25.5 us
    ppermute x7, waiting for transfers between devices: 20.4 us -> 14.5 us  [hop(): return lax.ppermute(block, RING, route)]
    ppermute x7, starting transfers between devices: 17.6 us -> 21.6 us  [hop(): return lax.ppermute(block, RING, route)]
    ppermute x2 -> x3, starting transfers between devices: 5.45 us -> 3.9 us  [swap(): return lax.ppermute(block, 'core', [(0, 1), (1, 0)])]
  transfers between devices with their start and end apart: 9 -> 10, of which waited for: 5 -> 6; matrix products, arithmetic and copies ran while one was open for 0% -> 0% of each run, Pallas kernels for 12% -> 13%
where the time goes in v8:
time: 88.5 us; the launch traced here: 88.3 us
  blocking collectives  32 us (36%)
  starting transfers between devices  25.5 us (29%)
  Pallas kernels  14.9 us (17%)
  waiting for transfers between devices  14.5 us (16%)
  local copies, waits for them, and re-layouts  1.14 us (1%)
    ppermute x7, starting transfers between devices, hop(): return lax.ppermute(block, RING, route)  21.6 us
    all_to_all x1, blocking collectives, shards(): parts = lax.all_to_all(parts, ('y', 'x'), 0, 0, tiled=True)  20.9 us
    ppermute x7, waiting for transfers between devices, hop(): return lax.ppermute(block, RING, route)  14.5 us
    pallas_call x6, Pallas kernels, step(): call(functools.partial(attend, distance, first, half), jax.ShapeDtypeStru...  13.2 us
    all_to_all x1, blocking collectives, shards(): attended = lax.all_to_all(attended, ('y', 'x'), 0, 0, tiled=True)  11.1 us
    ppermute x3, starting transfers between devices, swap(): return lax.ppermute(block, 'core', [(0, 1), (1, 0)])  3.9 us
  transfers between devices with their start and end apart: 10, of which 6 were waited for; matrix products, arithmetic and copies ran while one was open for 0% of the time, Pallas kernels for 13%

profile of v8, /device:TPU:1, one launch (start us, length us, event | category | flops | bytes accessed | tf_op | source)
XLA Modules:
  0.0 88.3 jit_solution(11483348657755421289)
XLA Ops:
  0.0 0.0 copy-start
  0.0 1.1 %copy-done = bf16[3,1,64,2048]{3,2,1,0:T(8,128)(2,1)S(1)} copy-done((bf16[3,1,64,2048]{3,2,1,0:T(8,128)(2,1)S(1)}, bf16[3,1,64,2048]{3,2,1,0:T(8,128)(2,1)}, u32[]{:S(2)}) %copy-start) | copy-done | bytes 786456
  1.1 0.1 pack.1
  1.3 0.0 copy-start.1
  1.3 20.9 %all_to_all.10.parts_ref = bf16[16,192,128]{2,1,0:T(8,128)(2,1)S(1)} all-to-all(bf16[16,192,128]{2,1,0:T(8,128)(2,1)S(1)} %pack.1), channel_id=1, replica_groups=mesh['zlo'=2,'y'=4,'core'=2,'x'=4,'zhi'=4] {'y','x'}, dimensions={0} | all-to-all | bytes 1572864 | tf_op jit(solution)/shard_map/tokens_to_heads/all_to_all | solution.py:179
  22.2 0.1 split.1
  22.3 1.9 %collective-permute-start.1 = (bf16[4,512,128]{2,1,0:T(8,128)(2,1)S(1)}, bf16[4,512,128]{2,1,0:T(8,128)(2,1)S(1)}, u32[]{:S(2)}, u32[]{:S(2)}) collective-permute-start(bf16[4,512,128]{2,1,0:T(8,128)(2,1)S(1)} %get-tuple-element.22.refs_3_), channel_id=1, source_target_pairs={{0,16},{16,0},{1,17},{17,1},{2,18},{18,2},{3,19},{19,3},{4,20},{20... | collective-permute-start | bytes 1572872 | tf_op jit(solution)/shard_map/swap_pairs/ppermute | solution.py:200
  24.2 0.1 collective-permute-start
  24.3 5.6 %collective-permute-start.2 = (bf16[4,512,128]{2,1,0:T(8,128)(2,1)S(1)}, bf16[4,512,128]{2,1,0:T(8,128)(2,1)S(1)}, u32[]{:S(2)}, u32[]{:S(2)}) collective-permute-start(bf16[4,512,128]{2,1,0:T(8,128)(2,1)S(1)} %get-tuple-element.22.refs_3_), channel_id=1, source_target_pairs={{0,128},{128,1},{1,129},{129,2},{2,130},{130,3},{3,131},{131,0},{1... | collective-permute-start | bytes 1572872 | tf_op jit(solution)/shard_map/ring/ppermute | solution.py:197
  29.9 0.0 collective-permute-done.refs_2_
  29.9 0.0 collective-permute-done.1
  29.9 1.8 %collective-permute-start.4 = (bf16[4,512,128]{2,1,0:T(8,128)(2,1)S(1)}, bf16[4,512,128]{2,1,0:T(8,128)(2,1)S(1)}, u32[]{:S(2)}, u32[]{:S(2)}) collective-permute-start(bf16[4,512,128]{2,1,0:T(8,128)(2,1)S(1)} %collective-permute-done.1), channel_id=1, source_target_pairs={{0,128},{128,1},{1,129},{129,2},{2,130},{130,3},{3,131},{131,0},{1... | collective-permute-start | bytes 1572872 | tf_op jit(solution)/shard_map/ring/ppermute | solution.py:197
  31.7 0.0 copy-done.1
  31.7 3.0 %attend.6.refs_5_ = f32[4,144,512]{2,1,0:T(8,128)S(1)} custom-call(s32[16]{0:T(128)S(1)} %copy-done.1, bf16[4,256,128]{2,1,0:T(8,128)(2,1)S(1)} %get-tuple-element.21.refs_1_, bf16[4,256,128]{2,1,0:T(8,128)(2,1)S(1)} %collective-permute-done.refs_2_, bf16[4,512,128]{2,1,0:T(8,128)(2,1)S(1)} %get-tuple-element.22.refs_3_), custom_call_target="tpu_custom_call" | custom-call | flops 4294967296 | bytes 8388608 | tf_op jit(solution)/shard_map/attend/pallas_call | solution.py:216
  34.7 1.3 %collective-permute-done.2.refs_3_ = bf16[4,512,128]{2,1,0:T(8,128)(2,1)S(1)} collective-permute-done((bf16[4,512,128]{2,1,0:T(8,128)(2,1)S(1)}, bf16[4,512,128]{2,1,0:T(8,128)(2,1)S(1)}, u32[]{:S(2)}, u32[]{:S(2)}) %collective-permute-start.2) | collective-permute-done | bytes 524320 | tf_op jit(solution)/shard_map/ring/ppermute | solution.py:197
  36.0 3.1 %collective-permute-start.3 = (bf16[4,512,128]{2,1,0:T(8,128)(2,1)S(1)}, bf16[4,512,128]{2,1,0:T(8,128)(2,1)S(1)}, u32[]{:S(2)}, u32[]{:S(2)}) collective-permute-start(bf16[4,512,128]{2,1,0:T(8,128)(2,1)S(1)} %collective-permute-done.2.refs_3_), channel_id=1, source_target_pairs={{0,128},{128,1},{1,129},{129,2},{2,130},{130,3},{3,131},{131,0},{1... | collective-permute-start | bytes 1572872 | tf_op jit(solution)/shard_map/ring/ppermute | solution.py:197
  39.1 2.5 %collective-permute-done.4.refs_4_ = bf16[4,512,128]{2,1,0:T(8,128)(2,1)S(1)} collective-permute-done((bf16[4,512,128]{2,1,0:T(8,128)(2,1)S(1)}, bf16[4,512,128]{2,1,0:T(8,128)(2,1)S(1)}, u32[]{:S(2)}, u32[]{:S(2)}) %collective-permute-start.4) | collective-permute-done | bytes 524320 | tf_op jit(solution)/shard_map/ring/ppermute | solution.py:197
  41.6 3.1 %collective-permute-start.6 = (bf16[4,512,128]{2,1,0:T(8,128)(2,1)S(1)}, bf16[4,512,128]{2,1,0:T(8,128)(2,1)S(1)}, u32[]{:S(2)}, u32[]{:S(2)}) collective-permute-start(bf16[4,512,128]{2,1,0:T(8,128)(2,1)S(1)} %collective-permute-done.4.refs_4_), channel_id=1, source_target_pairs={{0,128},{128,1},{1,129},{129,2},{2,130},{130,3},{3,131},{131,0},{1... | collective-permute-start | bytes 1572872 | tf_op jit(solution)/shard_map/ring/ppermute | solution.py:197
  44.7 0.7 attend.7.refs_5_
  45.4 1.8 %collective-permute-done.3.refs_3_ = bf16[4,512,128]{2,1,0:T(8,128)(2,1)S(1)} collective-permute-done((bf16[4,512,128]{2,1,0:T(8,128)(2,1)S(1)}, bf16[4,512,128]{2,1,0:T(8,128)(2,1)S(1)}, u32[]{:S(2)}, u32[]{:S(2)}) %collective-permute-start.3) | collective-permute-done | bytes 524320 | tf_op jit(solution)/shard_map/ring/ppermute | solution.py:197
  47.2 4.1 %collective-permute-start.5 = (bf16[4,512,128]{2,1,0:T(8,128)(2,1)S(1)}, bf16[4,512,128]{2,1,0:T(8,128)(2,1)S(1)}, u32[]{:S(2)}, u32[]{:S(2)}) collective-permute-start(bf16[4,512,128]{2,1,0:T(8,128)(2,1)S(1)} %collective-permute-done.3.refs_3_), channel_id=1, source_target_pairs={{0,128},{128,1},{1,129},{129,2},{2,130},{130,3},{3,131},{131,0},{1... | collective-permute-start | bytes 1572872 | tf_op jit(solution)/shard_map/ring/ppermute | solution.py:197
  51.3 1.6 %collective-permute-done.6.refs_4_ = bf16[4,512,128]{2,1,0:T(8,128)(2,1)S(1)} collective-permute-done((bf16[4,512,128]{2,1,0:T(8,128)(2,1)S(1)}, bf16[4,512,128]{2,1,0:T(8,128)(2,1)S(1)}, u32[]{:S(2)}, u32[]{:S(2)}) %collective-permute-start.6) | collective-permute-done | bytes 524320 | tf_op jit(solution)/shard_map/ring/ppermute | solution.py:197
  52.8 3.1 %collective-permute-start.8 = (bf16[4,512,128]{2,1,0:T(8,128)(2,1)S(1)}, bf16[4,512,128]{2,1,0:T(8,128)(2,1)S(1)}, u32[]{:S(2)}, u32[]{:S(2)}) collective-permute-start(bf16[4,512,128]{2,1,0:T(8,128)(2,1)S(1)} %collective-permute-done.6.refs_4_), channel_id=1, source_target_pairs={{0,128},{128,1},{1,129},{129,2},{2,130},{130,3},{3,131},{131,0},{1... | collective-permute-start | bytes 1572872 | tf_op jit(solution)/shard_map/ring/ppermute | solution.py:197
  56.0 4.8 %attend.8.refs_5_ = f32[4,144,512]{2,1,0:T(8,128)S(1)} custom-call(s32[16]{0:T(128)S(1)} %copy-done.1, bf16[4,256,128]{2,1,0:T(8,128)(2,1)S(1)} %get-tuple-element.21.refs_1_, bf16[4,256,128]{2,1,0:T(8,128)(2,1)S(1)} %collective-permute-done.refs_2_, bf16[4,512,128]{2,1,0:T(8,128)(2,1)S(1)} %collective-permute-done.3.refs_3_, ...), custom_call_target="tpu_custom_call", output_to_operand_aliasing={{}: (5, {})} | custom-call | flops 8589934592 | bytes 8388608 | tf_op jit(solution)/shard_map/attend/pallas_call | solution.py:216
  60.7 0.0 collective-permute-done.5.refs_3_
  60.7 0.8 collective-permute-start.7
  61.6 2.5 %collective-permute-done.8.refs_4_ = bf16[4,512,128]{2,1,0:T(8,128)(2,1)S(1)} collective-permute-done((bf16[4,512,128]{2,1,0:T(8,128)(2,1)S(1)}, bf16[4,512,128]{2,1,0:T(8,128)(2,1)S(1)}, u32[]{:S(2)}, u32[]{:S(2)}) %collective-permute-start.8) | collective-permute-done | bytes 524320 | tf_op jit(solution)/shard_map/ring/ppermute | solution.py:197
  64.1 0.7 attend.9.refs_4_
  64.8 4.9 %collective-permute-done.7.refs_3_ = bf16[4,512,128]{2,1,0:T(8,128)(2,1)S(1)} collective-permute-done((bf16[4,512,128]{2,1,0:T(8,128)(2,1)S(1)}, bf16[4,512,128]{2,1,0:T(8,128)(2,1)S(1)}, u32[]{:S(2)}, u32[]{:S(2)}) %collective-permute-start.7) | collective-permute-done | bytes 524320 | tf_op jit(solution)/shard_map/ring/ppermute | solution.py:197
  69.7 2.0 %attend.11 = f32[4,144,256]{2,1,0:T(8,128)S(1)} custom-call(s32[16]{0:T(128)S(1)} %copy-done.1, bf16[4,256,128]{2,1,0:T(8,128)(2,1)S(1)} %get-tuple-element.21.refs_1_, bf16[4,256,128]{2,1,0:T(8,128)(2,1)S(1)} %collective-permute-done.refs_2_, bf16[4,512,128]{2,1,0:T(8,128)(2,1)S(1)} %collective-permute-done.7.refs_3_, f32[4,144,512]{2,1,0:T(8,128)S(1)} %attend.9.refs_4_), custom_call_target="tpu_custom_call" | custom-call | flops 2147483648 | bytes 8388608 | tf_op jit(solution)/shard_map/attend/pallas_call | solution.py:216
  71.7 1.9 %collective-permute-start.9 = (f32[4,144,256]{2,1,0:T(8,128)S(1)}, f32[4,144,256]{2,1,0:T(8,128)S(1)}, u32[]{:S(2)}, u32[]{:S(2)}) collective-permute-start(f32[4,144,256]{2,1,0:T(8,128)S(1)} %attend.11), channel_id=1, source_target_pairs={{0,16},{16,0},{1,17},{17,1},{2,18},{18,2},{3,19},{19,3},{4,20},{20... | collective-permute-start | bytes 1769480 | tf_op jit(solution)/shard_map/swap_terms/ppermute | solution.py:200
  73.6 2.0 %attend.10.own_ref = f32[4,144,256]{2,1,0:T(8,128)S(1)} custom-call(s32[16]{0:T(128)S(1)} %copy-done.1, bf16[4,256,128]{2,1,0:T(8,128)(2,1)S(1)} %get-tuple-element.21.refs_1_, bf16[4,256,128]{2,1,0:T(8,128)(2,1)S(1)} %collective-permute-done.refs_2_, bf16[4,512,128]{2,1,0:T(8,128)(2,1)S(1)} %collective-permute-done.7.refs_3_, f32[4,144,512]{2,1,0:T(8,128)S(1)} %attend.9.refs_4_), custom_call_target="tpu_custom_call" | custom-call | flops 2147483648 | bytes 8388608 | tf_op jit(solution)/shard_map/attend/pallas_call | solution.py:216
  75.6 0.0 collective-permute-done.9.other_ref
  75.7 0.7 join.1
  76.4 11.1 %all_to_all.11.parts_ref = bf16[16,64,128]{2,1,0:T(8,128)(2,1)S(1)} all-to-all(bf16[16,64,128]{2,1,0:T(8,128)(2,1)S(1)} %join.1), channel_id=1, replica_groups=mesh['zlo'=2,'y'=4,'core'=2,'x'=4,'zhi'=4] {'y','x'}, dimensions={0} | all-to-all | bytes 524288 | tf_op jit(solution)/shard_map/heads_to_tokens/all_to_all | solution.py:245
  87.5 0.8 unpack.1
Async XLA Ops:
  0.0 1.1 %copy-start = (bf16[3,1,64,2048]{3,2,1,0:T(8,128)(2,1)S(1)}, bf16[3,1,64,2048]{3,2,1,0:T(8,128)(2,1)}, u32[]{:S(2)}) copy-start(bf16[3,1,64,2048]{3,2,1,0:T(8,128)(2,1)} %param.2) | copy-start | bytes 2359300
  1.3 30.4 %copy-start.1 = (s32[16]{0:T(128)S(1)}, s32[16]{0:T(128)}, u32[]{:S(2)}) copy-start(s32[16]{0:T(128)} %lengths_ref.1) | copy-start | bytes 196
  22.3 7.6 %collective-permute-start.1 = (bf16[4,512,128]{2,1,0:T(8,128)(2,1)S(1)}, bf16[4,512,128]{2,1,0:T(8,128)(2,1)S(1)}, u32[]{:S(2)}, u32[]{:S(2)}) collective-permute-start(bf16[4,512,128]{2,1,0:T(8,128)(2,1)S(1)} %get-tuple-element.22.refs_3_), channel_id=1, source_target_pairs={{0,16},{16,0},{1,17},{17,1},{2,18},{18,2},{3,19},{19,3},{4,20},{20... | collective-permute-start | bytes 1572872 | tf_op jit(solution)/shard_map/swap_pairs/ppermute | solution.py:200
  24.2 5.7 %collective-permute-start = (bf16[4,256,128]{2,1,0:T(8,128)(2,1)S(1)}, bf16[4,256,128]{2,1,0:T(8,128)(2,1)S(1)}, u32[]{:S(2)}, u32[]{:S(2)}) collective-permute-start(bf16[4,256,128]{2,1,0:T(8,128)(2,1)S(1)} %get-tuple-element.21.refs_1_), channel_id=1, source_target_pairs={{0,16},{16,0},{1,17},{17,1},{2,18},{18,2},{3,19},{19,3},{4,20},{20... | collective-permute-start | bytes 786440 | tf_op jit(solution)/shard_map/swap_queries/ppermute | solution.py:200
  24.3 11.7 %collective-permute-start.2 = (bf16[4,512,128]{2,1,0:T(8,128)(2,1)S(1)}, bf16[4,512,128]{2,1,0:T(8,128)(2,1)S(1)}, u32[]{:S(2)}, u32[]{:S(2)}) collective-permute-start(bf16[4,512,128]{2,1,0:T(8,128)(2,1)S(1)} %get-tuple-element.22.refs_3_), channel_id=1, source_target_pairs={{0,128},{128,1},{1,129},{129,2},{2,130},{130,3},{3,131},{131,0},{1... | collective-permute-start | bytes 1572872 | tf_op jit(solution)/shard_map/ring/ppermute | solution.py:197
  29.9 11.7 %collective-permute-start.4 = (bf16[4,512,128]{2,1,0:T(8,128)(2,1)S(1)}, bf16[4,512,128]{2,1,0:T(8,128)(2,1)S(1)}, u32[]{:S(2)}, u32[]{:S(2)}) collective-permute-start(bf16[4,512,128]{2,1,0:T(8,128)(2,1)S(1)} %collective-permute-done.1), channel_id=1, source_target_pairs={{0,128},{128,1},{1,129},{129,2},{2,130},{130,3},{3,131},{131,0},{1... | collective-permute-start | bytes 1572872 | tf_op jit(solution)/shard_map/ring/ppermute | solution.py:197
  36.0 11.2 %collective-permute-start.3 = (bf16[4,512,128]{2,1,0:T(8,128)(2,1)S(1)}, bf16[4,512,128]{2,1,0:T(8,128)(2,1)S(1)}, u32[]{:S(2)}, u32[]{:S(2)}) collective-permute-start(bf16[4,512,128]{2,1,0:T(8,128)(2,1)S(1)} %collective-permute-done.2.refs_3_), channel_id=1, source_target_pairs={{0,128},{128,1},{1,129},{129,2},{2,130},{130,3},{3,131},{131,0},{1... | collective-permute-start | bytes 1572872 | tf_op jit(solution)/shard_map/ring/ppermute | solution.py:197
  41.6 11.2 %collective-permute-start.6 = (bf16[4,512,128]{2,1,0:T(8,128)(2,1)S(1)}, bf16[4,512,128]{2,1,0:T(8,128)(2,1)S(1)}, u32[]{:S(2)}, u32[]{:S(2)}) collective-permute-start(bf16[4,512,128]{2,1,0:T(8,128)(2,1)S(1)} %collective-permute-done.4.refs_4_), channel_id=1, source_target_pairs={{0,128},{128,1},{1,129},{129,2},{2,130},{130,3},{3,131},{131,0},{1... | collective-permute-start | bytes 1572872 | tf_op jit(solution)/shard_map/ring/ppermute | solution.py:197
  47.2 13.5 %collective-permute-start.5 = (bf16[4,512,128]{2,1,0:T(8,128)(2,1)S(1)}, bf16[4,512,128]{2,1,0:T(8,128)(2,1)S(1)}, u32[]{:S(2)}, u32[]{:S(2)}) collective-permute-start(bf16[4,512,128]{2,1,0:T(8,128)(2,1)S(1)} %collective-permute-done.3.refs_3_), channel_id=1, source_target_pairs={{0,128},{128,1},{1,129},{129,2},{2,130},{130,3},{3,131},{131,0},{1... | collective-permute-start | bytes 1572872 | tf_op jit(solution)/shard_map/ring/ppermute | solution.py:197
  52.8 11.2 %collective-permute-start.8 = (bf16[4,512,128]{2,1,0:T(8,128)(2,1)S(1)}, bf16[4,512,128]{2,1,0:T(8,128)(2,1)S(1)}, u32[]{:S(2)}, u32[]{:S(2)}) collective-permute-start(bf16[4,512,128]{2,1,0:T(8,128)(2,1)S(1)} %collective-permute-done.6.refs_4_), channel_id=1, source_target_pairs={{0,128},{128,1},{1,129},{129,2},{2,130},{130,3},{3,131},{131,0},{1... | collective-permute-start | bytes 1572872 | tf_op jit(solution)/shard_map/ring/ppermute | solution.py:197
  60.7 9.0 %collective-permute-start.7 = (bf16[4,512,128]{2,1,0:T(8,128)(2,1)S(1)}, bf16[4,512,128]{2,1,0:T(8,128)(2,1)S(1)}, u32[]{:S(2)}, u32[]{:S(2)}) collective-permute-start(bf16[4,512,128]{2,1,0:T(8,128)(2,1)S(1)} %collective-permute-done.5.refs_3_), channel_id=1, source_target_pairs={{0,128},{128,1},{1,129},{129,2},{2,130},{130,3},{3,131},{131,0},{1... | collective-permute-start | bytes 1572872 | tf_op jit(solution)/shard_map/ring/ppermute | solution.py:197
  71.7 3.9 %collective-permute-start.9 = (f32[4,144,256]{2,1,0:T(8,128)S(1)}, f32[4,144,256]{2,1,0:T(8,128)S(1)}, u32[]{:S(2)}, u32[]{:S(2)}) collective-permute-start(f32[4,144,256]{2,1,0:T(8,128)S(1)} %attend.11), channel_id=1, source_target_pairs={{0,16},{16,0},{1,17},{17,1},{2,18},{18,2},{3,19},{19,3},{4,20},{20... | collective-permute-start | bytes 1769480 | tf_op jit(solution)/shard_map/swap_terms/ppermute | solution.py:200

commit v9 on v8

--- a/solution.py
+++ b/solution.py
@@ -63,25 +63,24 @@
     ones = jnp.where(lax.broadcasted_iota(jnp.int32, (16, ROWS), 0) < 8, 1.0, 0.0)
     ones = ones.astype(jnp.bfloat16)
 
-    def add(step, count, last):
+    def scores_of(step, count, last):
         if half is None:
             queries = jnp.concatenate([own_ref[step], other_ref[step]], axis=0)
         else:
             queries = (own_ref, other_ref)[half][step]
-        scores, values = [], []
+        row = lax.broadcasted_iota(jnp.int32, (SLICE, width), 0)
+        other_half = lax.broadcasted_iota(jnp.int32, (SLICE, width), 1) >= ROWS
+        scores = []
         for span, number in pieces:
             if span >= count:
                 continue
-            block = arrivals[number].at[span]
             score = lax.dot_general(
-                block[:ROWS, :],
+                arrivals[number][span, :ROWS, :],
                 queries,
                 (((1,), (1,)), ((), ())),
                 preferred_element_type=jnp.float32,
             )
             live = lengths_ref[source_zlo * 8 + 2 * span + source_core[number]]
-            row = lax.broadcasted_iota(jnp.int32, (SLICE, width), 0)
-            other_half = lax.broadcasted_iota(jnp.int32, (SLICE, width), 1) >= ROWS
             for part in range(4):
                 rows = score[part * SLICE : (part + 1) * SLICE]
                 bound = live - part * ROWS - offset
@@ -96,38 +95,50 @@
                 elif part >= 2:
                     rows = jnp.where(row < bound, rows, FILL)
                 scores.append(rows)
-            turned = jnp.concatenate([block[ROWS : ROWS + HD, :], block[ROWS + HD :, :]], axis=1)
-            values.append(jnp.concatenate([turned, ones], axis=0))
-        scores = jnp.concatenate(scores, axis=0)
-        peak = jnp.max(scores, axis=0, keepdims=True)
-        if not first:
-            old_peak = before_ref[step, HD + 8 : HD + 9, columns]
-            peak = jnp.maximum(old_peak, peak)
-        shifted = (scores - peak) * SCALE
-        weights = jnp.exp2(shifted)
-        if last == 0:
-            weights = jnp.where(scores > FILL, weights, 0.0)
-        weights = weights.astype(jnp.bfloat16)
-        fresh = jnp.dot(
-            jnp.concatenate(values, axis=1), weights, preferred_element_type=jnp.float32
-        )
-        fresh = fresh[: HD + 8]
-        if not first:
-            keep = jnp.exp2((old_peak - peak) * SCALE)
-            fresh = before_ref[step, : HD + 8, columns] * keep + fresh
-        state_ref[step, : HD + 8, :] = fresh
-        state_ref[step, HD + 8 :, :] = jnp.broadcast_to(peak, (8, width))
+        return jnp.concatenate(scores, axis=0)
+
+    def values_of(count):
+        values = []
+        for span, number in pieces:
+            if span < count:
+                block = arrivals[number].at[span]
+                turned = jnp.concatenate([block[ROWS : ROWS + HD, :], block[ROWS + HD :, :]], axis=1)
+                values.append(jnp.concatenate([turned, ones], axis=0))
+        return jnp.concatenate(values, axis=1)
+
+    def add(steps):
+        scores = [scores_of(*step) for step in steps]
+        olds = [None if first else before_ref[step, HD + 8 : HD + 9, columns] for step, _, _ in steps]
+        peaks = []
+        for old, score in zip(olds, scores):
+            peak = jnp.max(score, axis=0, keepdims=True)
+            peaks.append(peak if first else jnp.maximum(old, peak))
+        weights = []
+        for (_, _, last), score, peak in zip(steps, scores, peaks):
+            weight = jnp.exp2((score - peak) * SCALE)
+            if last == 0:
+                weight = jnp.where(score > FILL, weight, 0.0)
+            weights.append(weight.astype(jnp.bfloat16))
+        fresh = [
+            jnp.dot(values_of(count), weight, preferred_element_type=jnp.float32)[: HD + 8]
+            for (_, count, _), weight in zip(steps, weights)
+        ]
+        for (step, _, _), old, peak, term in zip(steps, olds, peaks, fresh):
+            if not first:
+                keep = jnp.exp2((old - peak) * SCALE)
+                term = before_ref[step, : HD + 8, columns] * keep + term
+            state_ref[step, : HD + 8, :] = term
+            state_ref[step, HD + 8 :, :] = jnp.broadcast_to(peak, (8, width))
 
     if aligned:
-        for step in range(4):
-            add(step, step + 1, step)
+        add([(step, step + 1, step) for step in range(4)])
     else:
 
         @pl.when(source_zlo < zlo)
         def _():
-            @pl.loop(0, 4, unroll=2)
-            def _(step):
-                add(step, 4, -1)
+            @pl.loop(0, 2)
+            def _(pair):
+                add([(2 * pair, 4, -1), (2 * pair + 1, 4, -1)])
 
         @pl.when(source_zlo > zlo)
         def _():

time: 88.5 us -> 87.2 us (0.985)
  Pallas kernels: 14.9 us -> 13.2 us
    pallas_call x6, Pallas kernels: 13.2 us -> 11.5 us  [step(): call(functools.partial(attend, distance, first, half), jax.ShapeDtypeStru...]
  transfers between devices with their start and end apart: 10 -> 10, of which waited for: 6 -> 6; matrix products, arithmetic and copies ran while one was open for 0% -> 0% of each run, Pallas kernels for 13% -> 11%
where the time goes in v9:
time: 87.2 us; the launch traced here: 87.1 us
  blocking collectives  31.7 us (36%)
  starting transfers between devices  25.6 us (29%)
  waiting for transfers between devices  15.3 us (18%)
  Pallas kernels  13.2 us (15%)
  local copies, waits for them, and re-layouts  1.14 us (1%)
    ppermute x7, starting transfers between devices, hop(): return lax.ppermute(block, RING, route)  21.8 us
    all_to_all x1, blocking collectives, shards(): parts = lax.all_to_all(parts, ('y', 'x'), 0, 0, tiled=True)  20.9 us
    ppermute x7, waiting for transfers between devices, hop(): return lax.ppermute(block, RING, route)  15.3 us
    pallas_call x6, Pallas kernels, step(): call(functools.partial(attend, distance, first, half), jax.ShapeDtypeStru...  11.5 us
    all_to_all x1, blocking collectives, shards(): attended = lax.all_to_all(attended, ('y', 'x'), 0, 0, tiled=True)  10.8 us
    ppermute x3, starting transfers between devices, swap(): return lax.ppermute(block, 'core', [(0, 1), (1, 0)])  3.79 us
  transfers between devices with their start and end apart: 10, of which 6 were waited for; matrix products, arithmetic and copies ran while one was open for 0% of the time, Pallas kernels for 11%

profile of v9, /device:TPU:1, one launch (start us, length us, event | category | flops | bytes accessed | tf_op | source)
XLA Modules:
  0.0 87.1 jit_solution(7149601346655532678)
XLA Ops:
  0.0 0.0 copy-start
  0.0 1.1 %copy-done = bf16[3,1,64,2048]{3,2,1,0:T(8,128)(2,1)S(1)} copy-done((bf16[3,1,64,2048]{3,2,1,0:T(8,128)(2,1)S(1)}, bf16[3,1,64,2048]{3,2,1,0:T(8,128)(2,1)}, u32[]{:S(2)}) %copy-start) | copy-done | bytes 786456
  1.1 0.1 pack.1
  1.3 0.0 copy-start.1
  1.3 20.9 %all_to_all.10.parts_ref = bf16[16,192,128]{2,1,0:T(8,128)(2,1)S(1)} all-to-all(bf16[16,192,128]{2,1,0:T(8,128)(2,1)S(1)} %pack.1), channel_id=1, replica_groups=mesh['zlo'=2,'y'=4,'core'=2,'x'=4,'zhi'=4] {'y','x'}, dimensions={0} | all-to-all | bytes 1572864 | tf_op jit(solution)/shard_map/tokens_to_heads/all_to_all | solution.py:190
  22.2 0.1 split.1
  22.3 1.9 %collective-permute-start.1 = (bf16[4,512,128]{2,1,0:T(8,128)(2,1)S(1)}, bf16[4,512,128]{2,1,0:T(8,128)(2,1)S(1)}, u32[]{:S(2)}, u32[]{:S(2)}) collective-permute-start(bf16[4,512,128]{2,1,0:T(8,128)(2,1)S(1)} %get-tuple-element.22.refs_3_), channel_id=1, source_target_pairs={{0,16},{16,0},{1,17},{17,1},{2,18},{18,2},{3,19},{19,3},{4,20},{20... | collective-permute-start | bytes 1572872 | tf_op jit(solution)/shard_map/swap_pairs/ppermute | solution.py:211
  24.2 0.1 collective-permute-start
  24.3 5.6 %collective-permute-start.2 = (bf16[4,512,128]{2,1,0:T(8,128)(2,1)S(1)}, bf16[4,512,128]{2,1,0:T(8,128)(2,1)S(1)}, u32[]{:S(2)}, u32[]{:S(2)}) collective-permute-start(bf16[4,512,128]{2,1,0:T(8,128)(2,1)S(1)} %get-tuple-element.22.refs_3_), channel_id=1, source_target_pairs={{0,128},{128,1},{1,129},{129,2},{2,130},{130,3},{3,131},{131,0},{1... | collective-permute-start | bytes 1572872 | tf_op jit(solution)/shard_map/ring/ppermute | solution.py:208
  29.9 0.0 collective-permute-done.refs_2_
  29.9 0.0 collective-permute-done.1
  29.9 1.8 %collective-permute-start.4 = (bf16[4,512,128]{2,1,0:T(8,128)(2,1)S(1)}, bf16[4,512,128]{2,1,0:T(8,128)(2,1)S(1)}, u32[]{:S(2)}, u32[]{:S(2)}) collective-permute-start(bf16[4,512,128]{2,1,0:T(8,128)(2,1)S(1)} %collective-permute-done.1), channel_id=1, source_target_pairs={{0,128},{128,1},{1,129},{129,2},{2,130},{130,3},{3,131},{131,0},{1... | collective-permute-start | bytes 1572872 | tf_op jit(solution)/shard_map/ring/ppermute | solution.py:208
  31.7 0.0 copy-done.1
  31.7 2.4 %attend.6.refs_5_ = f32[4,144,512]{2,1,0:T(8,128)S(1)} custom-call(s32[16]{0:T(128)S(1)} %copy-done.1, bf16[4,256,128]{2,1,0:T(8,128)(2,1)S(1)} %get-tuple-element.21.refs_1_, bf16[4,256,128]{2,1,0:T(8,128)(2,1)S(1)} %collective-permute-done.refs_2_, bf16[4,512,128]{2,1,0:T(8,128)(2,1)S(1)} %get-tuple-element.22.refs_3_), custom_call_target="tpu_custom_call" | custom-call | flops 4294967296 | bytes 8388608 | tf_op jit(solution)/shard_map/attend/pallas_call | solution.py:227
  34.1 1.9 %collective-permute-done.2.refs_3_ = bf16[4,512,128]{2,1,0:T(8,128)(2,1)S(1)} collective-permute-done((bf16[4,512,128]{2,1,0:T(8,128)(2,1)S(1)}, bf16[4,512,128]{2,1,0:T(8,128)(2,1)S(1)}, u32[]{:S(2)}, u32[]{:S(2)}) %collective-permute-start.2) | collective-permute-done | bytes 524320 | tf_op jit(solution)/shard_map/ring/ppermute | solution.py:208
  36.0 3.1 %collective-permute-start.3 = (bf16[4,512,128]{2,1,0:T(8,128)(2,1)S(1)}, bf16[4,512,128]{2,1,0:T(8,128)(2,1)S(1)}, u32[]{:S(2)}, u32[]{:S(2)}) collective-permute-start(bf16[4,512,128]{2,1,0:T(8,128)(2,1)S(1)} %collective-permute-done.2.refs_3_), channel_id=1, source_target_pairs={{0,128},{128,1},{1,129},{129,2},{2,130},{130,3},{3,131},{131,0},{1... | collective-permute-start | bytes 1572872 | tf_op jit(solution)/shard_map/ring/ppermute | solution.py:208
  39.1 2.5 %collective-permute-done.4.refs_4_ = bf16[4,512,128]{2,1,0:T(8,128)(2,1)S(1)} collective-permute-done((bf16[4,512,128]{2,1,0:T(8,128)(2,1)S(1)}, bf16[4,512,128]{2,1,0:T(8,128)(2,1)S(1)}, u32[]{:S(2)}, u32[]{:S(2)}) %collective-permute-start.4) | collective-permute-done | bytes 524320 | tf_op jit(solution)/shard_map/ring/ppermute | solution.py:208
  41.6 3.1 %collective-permute-start.6 = (bf16[4,512,128]{2,1,0:T(8,128)(2,1)S(1)}, bf16[4,512,128]{2,1,0:T(8,128)(2,1)S(1)}, u32[]{:S(2)}, u32[]{:S(2)}) collective-permute-start(bf16[4,512,128]{2,1,0:T(8,128)(2,1)S(1)} %collective-permute-done.4.refs_4_), channel_id=1, source_target_pairs={{0,128},{128,1},{1,129},{129,2},{2,130},{130,3},{3,131},{131,0},{1... | collective-permute-start | bytes 1572872 | tf_op jit(solution)/shard_map/ring/ppermute | solution.py:208
  44.7 0.7 attend.7.refs_5_
  45.4 1.8 %collective-permute-done.3.refs_3_ = bf16[4,512,128]{2,1,0:T(8,128)(2,1)S(1)} collective-permute-done((bf16[4,512,128]{2,1,0:T(8,128)(2,1)S(1)}, bf16[4,512,128]{2,1,0:T(8,128)(2,1)S(1)}, u32[]{:S(2)}, u32[]{:S(2)}) %collective-permute-start.3) | collective-permute-done | bytes 524320 | tf_op jit(solution)/shard_map/ring/ppermute | solution.py:208
  47.2 3.8 %collective-permute-start.5 = (bf16[4,512,128]{2,1,0:T(8,128)(2,1)S(1)}, bf16[4,512,128]{2,1,0:T(8,128)(2,1)S(1)}, u32[]{:S(2)}, u32[]{:S(2)}) collective-permute-start(bf16[4,512,128]{2,1,0:T(8,128)(2,1)S(1)} %collective-permute-done.3.refs_3_), channel_id=1, source_target_pairs={{0,128},{128,1},{1,129},{129,2},{2,130},{130,3},{3,131},{131,0},{1... | collective-permute-start | bytes 1572872 | tf_op jit(solution)/shard_map/ring/ppermute | solution.py:208
  51.1 1.8 %collective-permute-done.6.refs_4_ = bf16[4,512,128]{2,1,0:T(8,128)(2,1)S(1)} collective-permute-done((bf16[4,512,128]{2,1,0:T(8,128)(2,1)S(1)}, bf16[4,512,128]{2,1,0:T(8,128)(2,1)S(1)}, u32[]{:S(2)}, u32[]{:S(2)}) %collective-permute-start.6) | collective-permute-done | bytes 524320 | tf_op jit(solution)/shard_map/ring/ppermute | solution.py:208
  52.8 3.1 %collective-permute-start.8 = (bf16[4,512,128]{2,1,0:T(8,128)(2,1)S(1)}, bf16[4,512,128]{2,1,0:T(8,128)(2,1)S(1)}, u32[]{:S(2)}, u32[]{:S(2)}) collective-permute-start(bf16[4,512,128]{2,1,0:T(8,128)(2,1)S(1)} %collective-permute-done.6.refs_4_), channel_id=1, source_target_pairs={{0,128},{128,1},{1,129},{129,2},{2,130},{130,3},{3,131},{131,0},{1... | collective-permute-start | bytes 1572872 | tf_op jit(solution)/shard_map/ring/ppermute | solution.py:208
  56.0 4.4 %attend.8.refs_5_ = f32[4,144,512]{2,1,0:T(8,128)S(1)} custom-call(s32[16]{0:T(128)S(1)} %copy-done.1, bf16[4,256,128]{2,1,0:T(8,128)(2,1)S(1)} %get-tuple-element.21.refs_1_, bf16[4,256,128]{2,1,0:T(8,128)(2,1)S(1)} %collective-permute-done.refs_2_, bf16[4,512,128]{2,1,0:T(8,128)(2,1)S(1)} %collective-permute-done.3.refs_3_, ...), custom_call_target="tpu_custom_call", output_to_operand_aliasing={{}: (5, {})} | custom-call | flops 8589934592 | bytes 8388608 | tf_op jit(solution)/shard_map/attend/pallas_call | solution.py:227
  60.3 0.0 collective-permute-done.5.refs_3_
  60.3 1.2 %collective-permute-start.7 = (bf16[4,512,128]{2,1,0:T(8,128)(2,1)S(1)}, bf16[4,512,128]{2,1,0:T(8,128)(2,1)S(1)}, u32[]{:S(2)}, u32[]{:S(2)}) collective-permute-start(bf16[4,512,128]{2,1,0:T(8,128)(2,1)S(1)} %collective-permute-done.5.refs_3_), channel_id=1, source_target_pairs={{0,128},{128,1},{1,129},{129,2},{2,130},{130,3},{3,131},{131,0},{1... | collective-permute-start | bytes 1572872 | tf_op jit(solution)/shard_map/ring/ppermute | solution.py:208
  61.6 2.5 %collective-permute-done.8.refs_4_ = bf16[4,512,128]{2,1,0:T(8,128)(2,1)S(1)} collective-permute-done((bf16[4,512,128]{2,1,0:T(8,128)(2,1)S(1)}, bf16[4,512,128]{2,1,0:T(8,128)(2,1)S(1)}, u32[]{:S(2)}, u32[]{:S(2)}) %collective-permute-start.8) | collective-permute-done | bytes 524320 | tf_op jit(solution)/shard_map/ring/ppermute | solution.py:208
  64.1 0.7 attend.9.refs_4_
  64.8 4.9 %collective-permute-done.7.refs_3_ = bf16[4,512,128]{2,1,0:T(8,128)(2,1)S(1)} collective-permute-done((bf16[4,512,128]{2,1,0:T(8,128)(2,1)S(1)}, bf16[4,512,128]{2,1,0:T(8,128)(2,1)S(1)}, u32[]{:S(2)}, u32[]{:S(2)}) %collective-permute-start.7) | collective-permute-done | bytes 524320 | tf_op jit(solution)/shard_map/ring/ppermute | solution.py:208
  69.7 1.6 %attend.11 = f32[4,144,256]{2,1,0:T(8,128)S(1)} custom-call(s32[16]{0:T(128)S(1)} %copy-done.1, bf16[4,256,128]{2,1,0:T(8,128)(2,1)S(1)} %get-tuple-element.21.refs_1_, bf16[4,256,128]{2,1,0:T(8,128)(2,1)S(1)} %collective-permute-done.refs_2_, bf16[4,512,128]{2,1,0:T(8,128)(2,1)S(1)} %collective-permute-done.7.refs_3_, f32[4,144,512]{2,1,0:T(8,128)S(1)} %attend.9.refs_4_), custom_call_target="tpu_custom_call" | custom-call | flops 2147483648 | bytes 8388608 | tf_op jit(solution)/shard_map/attend/pallas_call | solution.py:227
  71.3 1.8 %collective-permute-start.9 = (f32[4,144,256]{2,1,0:T(8,128)S(1)}, f32[4,144,256]{2,1,0:T(8,128)S(1)}, u32[]{:S(2)}, u32[]{:S(2)}) collective-permute-start(f32[4,144,256]{2,1,0:T(8,128)S(1)} %attend.11), channel_id=1, source_target_pairs={{0,16},{16,0},{1,17},{17,1},{2,18},{18,2},{3,19},{19,3},{4,20},{20... | collective-permute-start | bytes 1769480 | tf_op jit(solution)/shard_map/swap_terms/ppermute | solution.py:211
  73.2 1.6 %attend.10.own_ref = f32[4,144,256]{2,1,0:T(8,128)S(1)} custom-call(s32[16]{0:T(128)S(1)} %copy-done.1, bf16[4,256,128]{2,1,0:T(8,128)(2,1)S(1)} %get-tuple-element.21.refs_1_, bf16[4,256,128]{2,1,0:T(8,128)(2,1)S(1)} %collective-permute-done.refs_2_, bf16[4,512,128]{2,1,0:T(8,128)(2,1)S(1)} %collective-permute-done.7.refs_3_, f32[4,144,512]{2,1,0:T(8,128)S(1)} %attend.9.refs_4_), custom_call_target="tpu_custom_call" | custom-call | flops 2147483648 | bytes 8388608 | tf_op jit(solution)/shard_map/attend/pallas_call | solution.py:227
  74.8 0.0 collective-permute-done.9.other_ref
  74.8 0.7 join.1
  75.5 10.8 %all_to_all.11.parts_ref = bf16[16,64,128]{2,1,0:T(8,128)(2,1)S(1)} all-to-all(bf16[16,64,128]{2,1,0:T(8,128)(2,1)S(1)} %join.1), channel_id=1, replica_groups=mesh['zlo'=2,'y'=4,'core'=2,'x'=4,'zhi'=4] {'y','x'}, dimensions={0} | all-to-all | bytes 524288 | tf_op jit(solution)/shard_map/heads_to_tokens/all_to_all | solution.py:256
  86.3 0.8 unpack.1
Async XLA Ops:
  0.0 1.1 %copy-start = (bf16[3,1,64,2048]{3,2,1,0:T(8,128)(2,1)S(1)}, bf16[3,1,64,2048]{3,2,1,0:T(8,128)(2,1)}, u32[]{:S(2)}) copy-start(bf16[3,1,64,2048]{3,2,1,0:T(8,128)(2,1)} %param.2) | copy-start | bytes 2359300
  1.3 30.4 %copy-start.1 = (s32[16]{0:T(128)S(1)}, s32[16]{0:T(128)}, u32[]{:S(2)}) copy-start(s32[16]{0:T(128)} %lengths_ref.1) | copy-start | bytes 196
  22.3 7.6 %collective-permute-start.1 = (bf16[4,512,128]{2,1,0:T(8,128)(2,1)S(1)}, bf16[4,512,128]{2,1,0:T(8,128)(2,1)S(1)}, u32[]{:S(2)}, u32[]{:S(2)}) collective-permute-start(bf16[4,512,128]{2,1,0:T(8,128)(2,1)S(1)} %get-tuple-element.22.refs_3_), channel_id=1, source_target_pairs={{0,16},{16,0},{1,17},{17,1},{2,18},{18,2},{3,19},{19,3},{4,20},{20... | collective-permute-start | bytes 1572872 | tf_op jit(solution)/shard_map/swap_pairs/ppermute | solution.py:211
  24.2 5.7 %collective-permute-start = (bf16[4,256,128]{2,1,0:T(8,128)(2,1)S(1)}, bf16[4,256,128]{2,1,0:T(8,128)(2,1)S(1)}, u32[]{:S(2)}, u32[]{:S(2)}) collective-permute-start(bf16[4,256,128]{2,1,0:T(8,128)(2,1)S(1)} %get-tuple-element.21.refs_1_), channel_id=1, source_target_pairs={{0,16},{16,0},{1,17},{17,1},{2,18},{18,2},{3,19},{19,3},{4,20},{20... | collective-permute-start | bytes 786440 | tf_op jit(solution)/shard_map/swap_queries/ppermute | solution.py:211
  24.3 11.7 %collective-permute-start.2 = (bf16[4,512,128]{2,1,0:T(8,128)(2,1)S(1)}, bf16[4,512,128]{2,1,0:T(8,128)(2,1)S(1)}, u32[]{:S(2)}, u32[]{:S(2)}) collective-permute-start(bf16[4,512,128]{2,1,0:T(8,128)(2,1)S(1)} %get-tuple-element.22.refs_3_), channel_id=1, source_target_pairs={{0,128},{128,1},{1,129},{129,2},{2,130},{130,3},{3,131},{131,0},{1... | collective-permute-start | bytes 1572872 | tf_op jit(solution)/shard_map/ring/ppermute | solution.py:208
  29.9 11.7 %collective-permute-start.4 = (bf16[4,512,128]{2,1,0:T(8,128)(2,1)S(1)}, bf16[4,512,128]{2,1,0:T(8,128)(2,1)S(1)}, u32[]{:S(2)}, u32[]{:S(2)}) collective-permute-start(bf16[4,512,128]{2,1,0:T(8,128)(2,1)S(1)} %collective-permute-done.1), channel_id=1, source_target_pairs={{0,128},{128,1},{1,129},{129,2},{2,130},{130,3},{3,131},{131,0},{1... | collective-permute-start | bytes 1572872 | tf_op jit(solution)/shard_map/ring/ppermute | solution.py:208
  36.0 11.2 %collective-permute-start.3 = (bf16[4,512,128]{2,1,0:T(8,128)(2,1)S(1)}, bf16[4,512,128]{2,1,0:T(8,128)(2,1)S(1)}, u32[]{:S(2)}, u32[]{:S(2)}) collective-permute-start(bf16[4,512,128]{2,1,0:T(8,128)(2,1)S(1)} %collective-permute-done.2.refs_3_), channel_id=1, source_target_pairs={{0,128},{128,1},{1,129},{129,2},{2,130},{130,3},{3,131},{131,0},{1... | collective-permute-start | bytes 1572872 | tf_op jit(solution)/shard_map/ring/ppermute | solution.py:208
  41.6 11.2 %collective-permute-start.6 = (bf16[4,512,128]{2,1,0:T(8,128)(2,1)S(1)}, bf16[4,512,128]{2,1,0:T(8,128)(2,1)S(1)}, u32[]{:S(2)}, u32[]{:S(2)}) collective-permute-start(bf16[4,512,128]{2,1,0:T(8,128)(2,1)S(1)} %collective-permute-done.4.refs_4_), channel_id=1, source_target_pairs={{0,128},{128,1},{1,129},{129,2},{2,130},{130,3},{3,131},{131,0},{1... | collective-permute-start | bytes 1572872 | tf_op jit(solution)/shard_map/ring/ppermute | solution.py:208
  47.2 13.1 %collective-permute-start.5 = (bf16[4,512,128]{2,1,0:T(8,128)(2,1)S(1)}, bf16[4,512,128]{2,1,0:T(8,128)(2,1)S(1)}, u32[]{:S(2)}, u32[]{:S(2)}) collective-permute-start(bf16[4,512,128]{2,1,0:T(8,128)(2,1)S(1)} %collective-permute-done.3.refs_3_), channel_id=1, source_target_pairs={{0,128},{128,1},{1,129},{129,2},{2,130},{130,3},{3,131},{131,0},{1... | collective-permute-start | bytes 1572872 | tf_op jit(solution)/shard_map/ring/ppermute | solution.py:208
  52.8 11.2 %collective-permute-start.8 = (bf16[4,512,128]{2,1,0:T(8,128)(2,1)S(1)}, bf16[4,512,128]{2,1,0:T(8,128)(2,1)S(1)}, u32[]{:S(2)}, u32[]{:S(2)}) collective-permute-start(bf16[4,512,128]{2,1,0:T(8,128)(2,1)S(1)} %collective-permute-done.6.refs_4_), channel_id=1, source_target_pairs={{0,128},{128,1},{1,129},{129,2},{2,130},{130,3},{3,131},{131,0},{1... | collective-permute-start | bytes 1572872 | tf_op jit(solution)/shard_map/ring/ppermute | solution.py:208
  60.3 9.4 %collective-permute-start.7 = (bf16[4,512,128]{2,1,0:T(8,128)(2,1)S(1)}, bf16[4,512,128]{2,1,0:T(8,128)(2,1)S(1)}, u32[]{:S(2)}, u32[]{:S(2)}) collective-permute-start(bf16[4,512,128]{2,1,0:T(8,128)(2,1)S(1)} %collective-permute-done.5.refs_3_), channel_id=1, source_target_pairs={{0,128},{128,1},{1,129},{129,2},{2,130},{130,3},{3,131},{131,0},{1... | collective-permute-start | bytes 1572872 | tf_op jit(solution)/shard_map/ring/ppermute | solution.py:208
  71.3 3.5 %collective-permute-start.9 = (f32[4,144,256]{2,1,0:T(8,128)S(1)}, f32[4,144,256]{2,1,0:T(8,128)S(1)}, u32[]{:S(2)}, u32[]{:S(2)}) collective-permute-start(f32[4,144,256]{2,1,0:T(8,128)S(1)} %attend.11), channel_id=1, source_target_pairs={{0,16},{16,0},{1,17},{17,1},{2,18},{18,2},{3,19},{19,3},{4,20},{20... | collective-permute-start | bytes 1769480 | tf_op jit(solution)/shard_map/swap_terms/ppermute | solution.py:211

commit v10 on v9

--- a/solution.py
+++ b/solution.py
@@ -41,7 +41,7 @@
         pair_ref[span, ROWS + HD :] = turned[:, HD:]
 
 
-def attend(distance, first, half, *refs):
+def attend(distance, chains, first, half, *refs):
     refs = list(refs)
     lengths_ref, own_ref, other_ref = refs[:3]
     arrivals = refs[3:-1] if first else refs[3:-2]
@@ -53,7 +53,7 @@
     pieces = [(span, number) for span in range(4) for number in range(len(arrivals))]
     source_zed = lax.rem(zed + 8 + jnp.where(core == 0, -distance, distance), 8)
     source_zlo = lax.rem(source_zed, 2)
-    source_core = [core, 1 - core]
+    source_core = [core if chain == 0 else 1 - core for chain in chains]
     offset = (source_zed // 2) * SLICE
     aligned = distance % 2 == 0
 
@@ -136,9 +136,11 @@
 
         @pl.when(source_zlo < zlo)
         def _():
-            @pl.loop(0, 2)
-            def _(pair):
-                add([(2 * pair, 4, -1), (2 * pair + 1, 4, -1)])
+            together = 4 // len(arrivals)
+
+            @pl.loop(0, len(arrivals))
+            def _(group):
+                add([(together * group + member, 4, -1) for member in range(together)])
 
         @pl.when(source_zlo > zlo)
         def _():
@@ -218,14 +220,14 @@
     other, second = lax.optimization_barrier((other, second))
     second_chain = hop(second)
 
-    def step(arrivals, distance, state, half=None):
+    def step(arrivals, distance, state, half=None, chains=(0, 1)):
         first = state is None
         operands = [lengths, own, other] + arrivals + ([] if first else [state])
         count = 4 * len(arrivals)
         width = 2 * ROWS if half is None else ROWS
         with jax.named_scope("attend"):
             return call(
-                functools.partial(attend, distance, first, half),
+                functools.partial(attend, distance, chains[: len(arrivals)], first, half),
                 jax.ShapeDtypeStruct((4, STATE, width), jnp.float32),
                 [smem] + [vmem] * (len(operands) - 1),
                 flops=16 * HD * ROWS * width * 4 * count,
@@ -234,14 +236,20 @@
             )(*operands)
 
     state = step([pairs], 0, None)
-    for distance in range(1, 4):
-        first_chain, state = lax.optimization_barrier((first_chain, state))
-        second_chain, state = lax.optimization_barrier((second_chain, state))
+    def after(block, state):
+        return lax.optimization_barrier((block, state))
+
+    for distance in range(1, 3):
+        first_chain, state = after(first_chain, state)
+        second_chain, state = after(second_chain, state)
         arrived = [first_chain, second_chain]
-        first_chain = hop(first_chain)
-        if distance < 3:
-            second_chain = hop(second_chain)
+        first_chain, second_chain = hop(first_chain), hop(second_chain)
         state = step(arrived, distance, state)
+    arrived, state = after(first_chain, state)
+    first_chain = hop(arrived)
+    state = step([arrived], 3, state)
+    second_chain, state = after(second_chain, state)
+    state = step([second_chain], 3, state, chains=(1,))
     theirs = step([first_chain], 4, state, 1)
     with jax.named_scope("swap_terms"):
         theirs = swap(theirs)

time: 87.2 us -> 87.2 us (level)
    pallas_call x6 -> x7, Pallas kernels: 11.5 us -> 12.2 us  [step(): call(functools.partial(attend, distance, chains[:len(arrivals)], first, h...]
  transfers between devices with their start and end apart: 10 -> 10, of which waited for: 6 -> 6; matrix products, arithmetic and copies ran while one was open for 0% -> 0% of each run, Pallas kernels for 11% -> 12%
where the time goes in v10:
time: 87.2 us; the launch traced here: 87.1 us
  blocking collectives  31.7 us (36%)
  starting transfers between devices  25.6 us (29%)
  waiting for transfers between devices  14.6 us (17%)
  Pallas kernels  13.9 us (16%)
  local copies, waits for them, and re-layouts  1.14 us (1%)
    ppermute x7, starting transfers between devices, hop(): return lax.ppermute(block, RING, route)  21.8 us
    all_to_all x1, blocking collectives, shards(): parts = lax.all_to_all(parts, ('y', 'x'), 0, 0, tiled=True)  20.9 us
    ppermute x7, waiting for transfers between devices, hop(): return lax.ppermute(block, RING, route)  14.6 us
    pallas_call x7, Pallas kernels, step(): call(functools.partial(attend, distance, chains[:len(arrivals)], first, h...  12.2 us
    all_to_all x1, blocking collectives, shards(): attended = lax.all_to_all(attended, ('y', 'x'), 0, 0, tiled=True)  10.8 us
    ppermute x3, starting transfers between devices, swap(): return lax.ppermute(block, 'core', [(0, 1), (1, 0)])  3.79 us
  transfers between devices with their start and end apart: 10, of which 6 were waited for; matrix products, arithmetic and copies ran while one was open for 0% of the time, Pallas kernels for 12%

profile of v10, /device:TPU:1, one launch (start us, length us, event | category | flops | bytes accessed | tf_op | source)
XLA Modules:
  0.0 87.1 jit_solution(12334155814303321396)
XLA Ops:
  0.0 0.0 copy-start
  0.0 1.1 %copy-done = bf16[3,1,64,2048]{3,2,1,0:T(8,128)(2,1)S(1)} copy-done((bf16[3,1,64,2048]{3,2,1,0:T(8,128)(2,1)S(1)}, bf16[3,1,64,2048]{3,2,1,0:T(8,128)(2,1)}, u32[]{:S(2)}) %copy-start) | copy-done | bytes 786456
  1.1 0.1 pack.1
  1.3 0.0 copy-start.1
  1.3 20.9 %all_to_all.10.parts_ref = bf16[16,192,128]{2,1,0:T(8,128)(2,1)S(1)} all-to-all(bf16[16,192,128]{2,1,0:T(8,128)(2,1)S(1)} %pack.1), channel_id=1, replica_groups=mesh['zlo'=2,'y'=4,'core'=2,'x'=4,'zhi'=4] {'y','x'}, dimensions={0} | all-to-all | bytes 1572864 | tf_op jit(solution)/shard_map/tokens_to_heads/all_to_all | solution.py:192
  22.2 0.1 split.1
  22.3 1.9 %collective-permute-start.1 = (bf16[4,512,128]{2,1,0:T(8,128)(2,1)S(1)}, bf16[4,512,128]{2,1,0:T(8,128)(2,1)S(1)}, u32[]{:S(2)}, u32[]{:S(2)}) collective-permute-start(bf16[4,512,128]{2,1,0:T(8,128)(2,1)S(1)} %get-tuple-element.22.refs_3_), channel_id=1, source_target_pairs={{0,16},{16,0},{1,17},{17,1},{2,18},{18,2},{3,19},{19,3},{4,20},{20... | collective-permute-start | bytes 1572872 | tf_op jit(solution)/shard_map/swap_pairs/ppermute | solution.py:213
  24.2 0.1 collective-permute-start
  24.3 5.6 %collective-permute-start.2 = (bf16[4,512,128]{2,1,0:T(8,128)(2,1)S(1)}, bf16[4,512,128]{2,1,0:T(8,128)(2,1)S(1)}, u32[]{:S(2)}, u32[]{:S(2)}) collective-permute-start(bf16[4,512,128]{2,1,0:T(8,128)(2,1)S(1)} %get-tuple-element.22.refs_3_), channel_id=1, source_target_pairs={{0,128},{128,1},{1,129},{129,2},{2,130},{130,3},{3,131},{131,0},{1... | collective-permute-start | bytes 1572872 | tf_op jit(solution)/shard_map/ring/ppermute | solution.py:210
  29.9 0.0 collective-permute-done.refs_2_
  29.9 0.0 collective-permute-done.1
  29.9 1.8 %collective-permute-start.4 = (bf16[4,512,128]{2,1,0:T(8,128)(2,1)S(1)}, bf16[4,512,128]{2,1,0:T(8,128)(2,1)S(1)}, u32[]{:S(2)}, u32[]{:S(2)}) collective-permute-start(bf16[4,512,128]{2,1,0:T(8,128)(2,1)S(1)} %collective-permute-done.1), channel_id=1, source_target_pairs={{0,128},{128,1},{1,129},{129,2},{2,130},{130,3},{3,131},{131,0},{1... | collective-permute-start | bytes 1572872 | tf_op jit(solution)/shard_map/ring/ppermute | solution.py:210
  31.7 0.0 copy-done.1
  31.7 2.4 %attend.7.refs_5_ = f32[4,144,512]{2,1,0:T(8,128)S(1)} custom-call(s32[16]{0:T(128)S(1)} %copy-done.1, bf16[4,256,128]{2,1,0:T(8,128)(2,1)S(1)} %get-tuple-element.21.refs_1_, bf16[4,256,128]{2,1,0:T(8,128)(2,1)S(1)} %collective-permute-done.refs_2_, bf16[4,512,128]{2,1,0:T(8,128)(2,1)S(1)} %get-tuple-element.22.refs_3_), custom_call_target="tpu_custom_call" | custom-call | flops 4294967296 | bytes 8388608 | tf_op jit(solution)/shard_map/attend/pallas_call | solution.py:229
  34.1 1.9 %collective-permute-done.2.refs_3_ = bf16[4,512,128]{2,1,0:T(8,128)(2,1)S(1)} collective-permute-done((bf16[4,512,128]{2,1,0:T(8,128)(2,1)S(1)}, bf16[4,512,128]{2,1,0:T(8,128)(2,1)S(1)}, u32[]{:S(2)}, u32[]{:S(2)}) %collective-permute-start.2) | collective-permute-done | bytes 524320 | tf_op jit(solution)/shard_map/ring/ppermute | solution.py:210
  36.0 3.1 %collective-permute-start.3 = (bf16[4,512,128]{2,1,0:T(8,128)(2,1)S(1)}, bf16[4,512,128]{2,1,0:T(8,128)(2,1)S(1)}, u32[]{:S(2)}, u32[]{:S(2)}) collective-permute-start(bf16[4,512,128]{2,1,0:T(8,128)(2,1)S(1)} %collective-permute-done.2.refs_3_), channel_id=1, source_target_pairs={{0,128},{128,1},{1,129},{129,2},{2,130},{130,3},{3,131},{131,0},{1... | collective-permute-start | bytes 1572872 | tf_op jit(solution)/shard_map/ring/ppermute | solution.py:210
  39.1 2.5 %collective-permute-done.4.refs_4_ = bf16[4,512,128]{2,1,0:T(8,128)(2,1)S(1)} collective-permute-done((bf16[4,512,128]{2,1,0:T(8,128)(2,1)S(1)}, bf16[4,512,128]{2,1,0:T(8,128)(2,1)S(1)}, u32[]{:S(2)}, u32[]{:S(2)}) %collective-permute-start.4) | collective-permute-done | bytes 524320 | tf_op jit(solution)/shard_map/ring/ppermute | solution.py:210
  41.6 3.1 %collective-permute-start.6 = (bf16[4,512,128]{2,1,0:T(8,128)(2,1)S(1)}, bf16[4,512,128]{2,1,0:T(8,128)(2,1)S(1)}, u32[]{:S(2)}, u32[]{:S(2)}) collective-permute-start(bf16[4,512,128]{2,1,0:T(8,128)(2,1)S(1)} %collective-permute-done.4.refs_4_), channel_id=1, source_target_pairs={{0,128},{128,1},{1,129},{129,2},{2,130},{130,3},{3,131},{131,0},{1... | collective-permute-start | bytes 1572872 | tf_op jit(solution)/shard_map/ring/ppermute | solution.py:210
  44.7 0.7 attend.8.refs_5_
  45.4 1.8 %collective-permute-done.3.refs_3_ = bf16[4,512,128]{2,1,0:T(8,128)(2,1)S(1)} collective-permute-done((bf16[4,512,128]{2,1,0:T(8,128)(2,1)S(1)}, bf16[4,512,128]{2,1,0:T(8,128)(2,1)S(1)}, u32[]{:S(2)}, u32[]{:S(2)}) %collective-permute-start.3) | collective-permute-done | bytes 524320 | tf_op jit(solution)/shard_map/ring/ppermute | solution.py:210
  47.2 3.8 %collective-permute-start.5 = (bf16[4,512,128]{2,1,0:T(8,128)(2,1)S(1)}, bf16[4,512,128]{2,1,0:T(8,128)(2,1)S(1)}, u32[]{:S(2)}, u32[]{:S(2)}) collective-permute-start(bf16[4,512,128]{2,1,0:T(8,128)(2,1)S(1)} %collective-permute-done.3.refs_3_), channel_id=1, source_target_pairs={{0,128},{128,1},{1,129},{129,2},{2,130},{130,3},{3,131},{131,0},{1... | collective-permute-start | bytes 1572872 | tf_op jit(solution)/shard_map/ring/ppermute | solution.py:210
  51.0 1.8 %collective-permute-done.6.refs_4_ = bf16[4,512,128]{2,1,0:T(8,128)(2,1)S(1)} collective-permute-done((bf16[4,512,128]{2,1,0:T(8,128)(2,1)S(1)}, bf16[4,512,128]{2,1,0:T(8,128)(2,1)S(1)}, u32[]{:S(2)}, u32[]{:S(2)}) %collective-permute-start.6) | collective-permute-done | bytes 524320 | tf_op jit(solution)/shard_map/ring/ppermute | solution.py:210
  52.8 3.1 %collective-permute-start.8 = (bf16[4,512,128]{2,1,0:T(8,128)(2,1)S(1)}, bf16[4,512,128]{2,1,0:T(8,128)(2,1)S(1)}, u32[]{:S(2)}, u32[]{:S(2)}) collective-permute-start(bf16[4,512,128]{2,1,0:T(8,128)(2,1)S(1)} %collective-permute-done.6.refs_4_), channel_id=1, source_target_pairs={{0,128},{128,1},{1,129},{129,2},{2,130},{130,3},{3,131},{131,0},{1... | collective-permute-start | bytes 1572872 | tf_op jit(solution)/shard_map/ring/ppermute | solution.py:210
  56.0 4.4 %attend.9.refs_4_ = f32[4,144,512]{2,1,0:T(8,128)S(1)} custom-call(s32[16]{0:T(128)S(1)} %copy-done.1, bf16[4,256,128]{2,1,0:T(8,128)(2,1)S(1)} %get-tuple-element.21.refs_1_, bf16[4,256,128]{2,1,0:T(8,128)(2,1)S(1)} %collective-permute-done.refs_2_, bf16[4,512,128]{2,1,0:T(8,128)(2,1)S(1)} %collective-permute-done.3.refs_3_, ...), custom_call_target="tpu_custom_call", output_to_operand_aliasing={{}: (5, {})} | custom-call | flops 8589934592 | bytes 8388608 | tf_op jit(solution)/shard_map/attend/pallas_call | solution.py:229
  60.3 0.0 collective-permute-done.5.refs_3_
  60.3 1.2 %collective-permute-start.7 = (bf16[4,512,128]{2,1,0:T(8,128)(2,1)S(1)}, bf16[4,512,128]{2,1,0:T(8,128)(2,1)S(1)}, u32[]{:S(2)}, u32[]{:S(2)}) collective-permute-start(bf16[4,512,128]{2,1,0:T(8,128)(2,1)S(1)} %collective-permute-done.5.refs_3_), channel_id=1, source_target_pairs={{0,128},{128,1},{1,129},{129,2},{2,130},{130,3},{3,131},{131,0},{1... | collective-permute-start | bytes 1572872 | tf_op jit(solution)/shard_map/ring/ppermute | solution.py:210
  61.6 0.7 attend.10.refs_4_
  62.3 1.8 %collective-permute-done.8.refs_3_ = bf16[4,512,128]{2,1,0:T(8,128)(2,1)S(1)} collective-permute-done((bf16[4,512,128]{2,1,0:T(8,128)(2,1)S(1)}, bf16[4,512,128]{2,1,0:T(8,128)(2,1)S(1)}, u32[]{:S(2)}, u32[]{:S(2)}) %collective-permute-start.8) | collective-permute-done | bytes 524320 | tf_op jit(solution)/shard_map/ring/ppermute | solution.py:210
  64.1 0.7 attend.11.refs_4_
  64.8 4.9 %collective-permute-done.7.refs_3_ = bf16[4,512,128]{2,1,0:T(8,128)(2,1)S(1)} collective-permute-done((bf16[4,512,128]{2,1,0:T(8,128)(2,1)S(1)}, bf16[4,512,128]{2,1,0:T(8,128)(2,1)S(1)}, u32[]{:S(2)}, u32[]{:S(2)}) %collective-permute-start.7) | collective-permute-done | bytes 524320 | tf_op jit(solution)/shard_map/ring/ppermute | solution.py:210
  69.7 1.6 %attend.13 = f32[4,144,256]{2,1,0:T(8,128)S(1)} custom-call(s32[16]{0:T(128)S(1)} %copy-done.1, bf16[4,256,128]{2,1,0:T(8,128)(2,1)S(1)} %get-tuple-element.21.refs_1_, bf16[4,256,128]{2,1,0:T(8,128)(2,1)S(1)} %collective-permute-done.refs_2_, bf16[4,512,128]{2,1,0:T(8,128)(2,1)S(1)} %collective-permute-done.7.refs_3_, f32[4,144,512]{2,1,0:T(8,128)S(1)} %attend.11.refs_4_), custom_call_target="tpu_custom_call" | custom-call | flops 2147483648 | bytes 8388608 | tf_op jit(solution)/shard_map/attend/pallas_call | solution.py:229
  71.3 1.8 %collective-permute-start.9 = (f32[4,144,256]{2,1,0:T(8,128)S(1)}, f32[4,144,256]{2,1,0:T(8,128)S(1)}, u32[]{:S(2)}, u32[]{:S(2)}) collective-permute-start(f32[4,144,256]{2,1,0:T(8,128)S(1)} %attend.13), channel_id=1, source_target_pairs={{0,16},{16,0},{1,17},{17,1},{2,18},{18,2},{3,19},{19,3},{4,20},{20... | collective-permute-start | bytes 1769480 | tf_op jit(solution)/shard_map/swap_terms/ppermute | solution.py:213
  73.2 1.6 %attend.12.own_ref = f32[4,144,256]{2,1,0:T(8,128)S(1)} custom-call(s32[16]{0:T(128)S(1)} %copy-done.1, bf16[4,256,128]{2,1,0:T(8,128)(2,1)S(1)} %get-tuple-element.21.refs_1_, bf16[4,256,128]{2,1,0:T(8,128)(2,1)S(1)} %collective-permute-done.refs_2_, bf16[4,512,128]{2,1,0:T(8,128)(2,1)S(1)} %collective-permute-done.7.refs_3_, f32[4,144,512]{2,1,0:T(8,128)S(1)} %attend.11.refs_4_), custom_call_target="tpu_custom_call" | custom-call | flops 2147483648 | bytes 8388608 | tf_op jit(solution)/shard_map/attend/pallas_call | solution.py:229
  74.8 0.0 collective-permute-done.9.other_ref
  74.8 0.7 join.1
  75.5 10.8 %all_to_all.11.parts_ref = bf16[16,64,128]{2,1,0:T(8,128)(2,1)S(1)} all-to-all(bf16[16,64,128]{2,1,0:T(8,128)(2,1)S(1)} %join.1), channel_id=1, replica_groups=mesh['zlo'=2,'y'=4,'core'=2,'x'=4,'zhi'=4] {'y','x'}, dimensions={0} | all-to-all | bytes 524288 | tf_op jit(solution)/shard_map/heads_to_tokens/all_to_all | solution.py:264
  86.3 0.8 unpack.1
Async XLA Ops:
  0.0 1.1 %copy-start = (bf16[3,1,64,2048]{3,2,1,0:T(8,128)(2,1)S(1)}, bf16[3,1,64,2048]{3,2,1,0:T(8,128)(2,1)}, u32[]{:S(2)}) copy-start(bf16[3,1,64,2048]{3,2,1,0:T(8,128)(2,1)} %param.2) | copy-start | bytes 2359300
  1.3 30.4 %copy-start.1 = (s32[16]{0:T(128)S(1)}, s32[16]{0:T(128)}, u32[]{:S(2)}) copy-start(s32[16]{0:T(128)} %lengths_ref.1) | copy-start | bytes 196
  22.3 7.6 %collective-permute-start.1 = (bf16[4,512,128]{2,1,0:T(8,128)(2,1)S(1)}, bf16[4,512,128]{2,1,0:T(8,128)(2,1)S(1)}, u32[]{:S(2)}, u32[]{:S(2)}) collective-permute-start(bf16[4,512,128]{2,1,0:T(8,128)(2,1)S(1)} %get-tuple-element.22.refs_3_), channel_id=1, source_target_pairs={{0,16},{16,0},{1,17},{17,1},{2,18},{18,2},{3,19},{19,3},{4,20},{20... | collective-permute-start | bytes 1572872 | tf_op jit(solution)/shard_map/swap_pairs/ppermute | solution.py:213
  24.2 5.7 %collective-permute-start = (bf16[4,256,128]{2,1,0:T(8,128)(2,1)S(1)}, bf16[4,256,128]{2,1,0:T(8,128)(2,1)S(1)}, u32[]{:S(2)}, u32[]{:S(2)}) collective-permute-start(bf16[4,256,128]{2,1,0:T(8,128)(2,1)S(1)} %get-tuple-element.21.refs_1_), channel_id=1, source_target_pairs={{0,16},{16,0},{1,17},{17,1},{2,18},{18,2},{3,19},{19,3},{4,20},{20... | collective-permute-start | bytes 786440 | tf_op jit(solution)/shard_map/swap_queries/ppermute | solution.py:213
  24.3 11.7 %collective-permute-start.2 = (bf16[4,512,128]{2,1,0:T(8,128)(2,1)S(1)}, bf16[4,512,128]{2,1,0:T(8,128)(2,1)S(1)}, u32[]{:S(2)}, u32[]{:S(2)}) collective-permute-start(bf16[4,512,128]{2,1,0:T(8,128)(2,1)S(1)} %get-tuple-element.22.refs_3_), channel_id=1, source_target_pairs={{0,128},{128,1},{1,129},{129,2},{2,130},{130,3},{3,131},{131,0},{1... | collective-permute-start | bytes 1572872 | tf_op jit(solution)/shard_map/ring/ppermute | solution.py:210
  29.9 11.7 %collective-permute-start.4 = (bf16[4,512,128]{2,1,0:T(8,128)(2,1)S(1)}, bf16[4,512,128]{2,1,0:T(8,128)(2,1)S(1)}, u32[]{:S(2)}, u32[]{:S(2)}) collective-permute-start(bf16[4,512,128]{2,1,0:T(8,128)(2,1)S(1)} %collective-permute-done.1), channel_id=1, source_target_pairs={{0,128},{128,1},{1,129},{129,2},{2,130},{130,3},{3,131},{131,0},{1... | collective-permute-start | bytes 1572872 | tf_op jit(solution)/shard_map/ring/ppermute | solution.py:210
  36.0 11.2 %collective-permute-start.3 = (bf16[4,512,128]{2,1,0:T(8,128)(2,1)S(1)}, bf16[4,512,128]{2,1,0:T(8,128)(2,1)S(1)}, u32[]{:S(2)}, u32[]{:S(2)}) collective-permute-start(bf16[4,512,128]{2,1,0:T(8,128)(2,1)S(1)} %collective-permute-done.2.refs_3_), channel_id=1, source_target_pairs={{0,128},{128,1},{1,129},{129,2},{2,130},{130,3},{3,131},{131,0},{1... | collective-permute-start | bytes 1572872 | tf_op jit(solution)/shard_map/ring/ppermute | solution.py:210
  41.6 11.2 %collective-permute-start.6 = (bf16[4,512,128]{2,1,0:T(8,128)(2,1)S(1)}, bf16[4,512,128]{2,1,0:T(8,128)(2,1)S(1)}, u32[]{:S(2)}, u32[]{:S(2)}) collective-permute-start(bf16[4,512,128]{2,1,0:T(8,128)(2,1)S(1)} %collective-permute-done.4.refs_4_), channel_id=1, source_target_pairs={{0,128},{128,1},{1,129},{129,2},{2,130},{130,3},{3,131},{131,0},{1... | collective-permute-start | bytes 1572872 | tf_op jit(solution)/shard_map/ring/ppermute | solution.py:210
  47.2 13.1 %collective-permute-start.5 = (bf16[4,512,128]{2,1,0:T(8,128)(2,1)S(1)}, bf16[4,512,128]{2,1,0:T(8,128)(2,1)S(1)}, u32[]{:S(2)}, u32[]{:S(2)}) collective-permute-start(bf16[4,512,128]{2,1,0:T(8,128)(2,1)S(1)} %collective-permute-done.3.refs_3_), channel_id=1, source_target_pairs={{0,128},{128,1},{1,129},{129,2},{2,130},{130,3},{3,131},{131,0},{1... | collective-permute-start | bytes 1572872 | tf_op jit(solution)/shard_map/ring/ppermute | solution.py:210
  52.8 11.2 %collective-permute-start.8 = (bf16[4,512,128]{2,1,0:T(8,128)(2,1)S(1)}, bf16[4,512,128]{2,1,0:T(8,128)(2,1)S(1)}, u32[]{:S(2)}, u32[]{:S(2)}) collective-permute-start(bf16[4,512,128]{2,1,0:T(8,128)(2,1)S(1)} %collective-permute-done.6.refs_4_), channel_id=1, source_target_pairs={{0,128},{128,1},{1,129},{129,2},{2,130},{130,3},{3,131},{131,0},{1... | collective-permute-start | bytes 1572872 | tf_op jit(solution)/shard_map/ring/ppermute | solution.py:210
  60.3 9.4 %collective-permute-start.7 = (bf16[4,512,128]{2,1,0:T(8,128)(2,1)S(1)}, bf16[4,512,128]{2,1,0:T(8,128)(2,1)S(1)}, u32[]{:S(2)}, u32[]{:S(2)}) collective-permute-start(bf16[4,512,128]{2,1,0:T(8,128)(2,1)S(1)} %collective-permute-done.5.refs_3_), channel_id=1, source_target_pairs={{0,128},{128,1},{1,129},{129,2},{2,130},{130,3},{3,131},{131,0},{1... | collective-permute-start | bytes 1572872 | tf_op jit(solution)/shard_map/ring/ppermute | solution.py:210
  71.3 3.5 %collective-permute-start.9 = (f32[4,144,256]{2,1,0:T(8,128)S(1)}, f32[4,144,256]{2,1,0:T(8,128)S(1)}, u32[]{:S(2)}, u32[]{:S(2)}) collective-permute-start(f32[4,144,256]{2,1,0:T(8,128)S(1)} %attend.13), channel_id=1, source_target_pairs={{0,16},{16,0},{1,17},{17,1},{2,18},{18,2},{3,19},{19,3},{4,20},{20... | collective-permute-start | bytes 1769480 | tf_op jit(solution)/shard_map/swap_terms/ppermute | solution.py:213

commit v11 on v10

--- a/solution.py
+++ b/solution.py
@@ -41,7 +41,7 @@
         pair_ref[span, ROWS + HD :] = turned[:, HD:]
 
 
-def attend(distance, chains, first, half, *refs):
+def attend(distance, chains, begin, steps, first, half, *refs):
     refs = list(refs)
     lengths_ref, own_ref, other_ref = refs[:3]
     arrivals = refs[3:-1] if first else refs[3:-2]
@@ -50,7 +50,8 @@
     core = lax.axis_index("core")
     zlo = lax.axis_index("zlo")
     zed = lax.axis_index("zhi") * 2 + zlo
-    pieces = [(span, number) for span in range(4) for number in range(len(arrivals))]
+    end = begin + arrivals[0].shape[0]
+    pieces = [(span, number) for span in range(begin, end) for number in range(len(arrivals))]
     source_zed = lax.rem(zed + 8 + jnp.where(core == 0, -distance, distance), 8)
     source_zlo = lax.rem(source_zed, 2)
     source_core = [core if chain == 0 else 1 - core for chain in chains]
@@ -75,7 +76,7 @@
             if span >= count:
                 continue
             score = lax.dot_general(
-                arrivals[number][span, :ROWS, :],
+                arrivals[number][span - begin, :ROWS, :],
                 queries,
                 (((1,), (1,)), ((), ())),
                 preferred_element_type=jnp.float32,
@@ -101,37 +102,38 @@
         values = []
         for span, number in pieces:
             if span < count:
-                block = arrivals[number].at[span]
+                block = arrivals[number].at[span - begin]
                 turned = jnp.concatenate([block[ROWS : ROWS + HD, :], block[ROWS + HD :, :]], axis=1)
                 values.append(jnp.concatenate([turned, ones], axis=0))
         return jnp.concatenate(values, axis=1)
 
-    def add(steps):
-        scores = [scores_of(*step) for step in steps]
-        olds = [None if first else before_ref[step, HD + 8 : HD + 9, columns] for step, _, _ in steps]
+    def add(work):
+        scores = [scores_of(*step) for step in work]
+        olds = [None if first else before_ref[step, HD + 8 : HD + 9, columns] for step, _, _ in work]
         peaks = []
         for old, score in zip(olds, scores):
             peak = jnp.max(score, axis=0, keepdims=True)
             peaks.append(peak if first else jnp.maximum(old, peak))
         weights = []
-        for (_, _, last), score, peak in zip(steps, scores, peaks):
+        for (_, _, last), score, peak in zip(work, scores, peaks):
             weight = jnp.exp2((score - peak) * SCALE)
             if last == 0:
                 weight = jnp.where(score > FILL, weight, 0.0)
             weights.append(weight.astype(jnp.bfloat16))
         fresh = [
             jnp.dot(values_of(count), weight, preferred_element_type=jnp.float32)[: HD + 8]
-            for (_, count, _), weight in zip(steps, weights)
+            for (_, count, _), weight in zip(work, weights)
         ]
-        for (step, _, _), old, peak, term in zip(steps, olds, peaks, fresh):
+        for (step, _, _), old, peak, term in zip(work, olds, peaks, fresh):
             if not first:
                 keep = jnp.exp2((old - peak) * SCALE)
                 term = before_ref[step, : HD + 8, columns] * keep + term
-            state_ref[step, : HD + 8, :] = term
-            state_ref[step, HD + 8 :, :] = jnp.broadcast_to(peak, (8, width))
+            place = step - steps[0]
+            state_ref[place, : HD + 8, :] = term
+            state_ref[place, HD + 8 :, :] = jnp.broadcast_to(peak, (8, width))
 
     if aligned:
-        add([(step, step + 1, step) for step in range(4)])
+        add([(step, step + 1, step) for step in steps])
     else:
 
         @pl.when(source_zlo < zlo)
@@ -147,19 +149,21 @@
             state_ref[...] = before_ref[...]
 
 
-def join(lengths_ref, own_ref, other_ref, out_ref):
+def join(lengths_ref, state_ref, mine_ref, early_ref, late_ref, out_ref):
     core = lax.axis_index("core")
     zlo = lax.axis_index("zlo")
     offset = lax.axis_index("zhi") * SLICE
     for step in range(4):
         live = lengths_ref[zlo * 8 + 2 * step + core]
-        first_peak = own_ref[step, HD + 8 : HD + 9, :]
-        second_peak = other_ref[step, HD + 8 : HD + 9, :]
+        own = state_ref.at[step] if step < 2 else mine_ref.at[step - 2]
+        other = early_ref.at[step] if step < 2 else late_ref.at[step - 2]
+        first_peak = own[HD + 8 : HD + 9, :ROWS]
+        second_peak = other[HD + 8 : HD + 9, :]
         peak = jnp.maximum(first_peak, second_peak)
         first = jnp.exp2((first_peak - peak) * SCALE)
         second = jnp.exp2((second_peak - peak) * SCALE)
-        total = own_ref[step, HD : HD + 1, :] * first + other_ref[step, HD : HD + 1, :] * second
-        numerator = own_ref[step, :HD, :] * first + other_ref[step, :HD, :] * second
+        total = own[HD : HD + 1, :ROWS] * first + other[HD : HD + 1, :] * second
+        numerator = own[:HD, :ROWS] * first + other[:HD, :] * second
         result = (numerator / total).T
         row = lax.broadcasted_iota(jnp.int32, (SLICE, HD), 0)
         for piece in range(4):
@@ -220,17 +224,20 @@
     other, second = lax.optimization_barrier((other, second))
     second_chain = hop(second)
 
-    def step(arrivals, distance, state, half=None, chains=(0, 1)):
+    def step(arrivals, distance, state, half=None, chains=(0, 1), begin=0, steps=(0, 1, 2, 3)):
         first = state is None
         operands = [lengths, own, other] + arrivals + ([] if first else [state])
-        count = 4 * len(arrivals)
+        count = sum(a.shape[0] for a in arrivals)
         width = 2 * ROWS if half is None else ROWS
+        kernel = functools.partial(
+            attend, distance, chains[: len(arrivals)], begin, steps, first, half
+        )
         with jax.named_scope("attend"):
             return call(
-                functools.partial(attend, distance, chains[: len(arrivals)], first, half),
-                jax.ShapeDtypeStruct((4, STATE, width), jnp.float32),
+                kernel,
+                jax.ShapeDtypeStruct((len(steps), STATE, width), jnp.float32),
                 [smem] + [vmem] * (len(operands) - 1),
-                flops=16 * HD * ROWS * width * 4 * count,
+                flops=4 * HD * ROWS * width * len(steps) * 4 * count,
                 moved=8 * 2**20,
                 input_output_aliases={} if first or half is not None else {len(operands) - 1: 0},
             )(*operands)
@@ -246,20 +253,25 @@
         first_chain, second_chain = hop(first_chain), hop(second_chain)
         state = step(arrived, distance, state)
     arrived, state = after(first_chain, state)
-    first_chain = hop(arrived)
+    halves = [hop(arrived[:2]), hop(arrived[2:])]
     state = step([arrived], 3, state)
     second_chain, state = after(second_chain, state)
     state = step([second_chain], 3, state, chains=(1,))
-    theirs = step([first_chain], 4, state, 1)
+    block, state = after(halves[0], state)
+    state = step([block], 4, state)
     with jax.named_scope("swap_terms"):
-        theirs = swap(theirs)
-    mine = step([first_chain], 4, state, 0)
+        early = swap(state[:2, :, ROWS:])
+    block, state, early = lax.optimization_barrier((halves[1], state, early))
+    late = step([block], 4, state, 1, begin=2, steps=(2, 3))
+    with jax.named_scope("swap_terms"):
+        late = swap(late)
+    mine = step([block], 4, state, 0, begin=2, steps=(2, 3))
     with jax.named_scope("join"):
         attended = call(
             join,
             jax.ShapeDtypeStruct((heads, SLICE, HD), bf16),
-            [smem, vmem, vmem],
-        )(lengths, mine, theirs)
+            [smem, vmem, vmem, vmem, vmem],
+        )(lengths, state, mine, early, late)
     with jax.named_scope("heads_to_tokens"):
         attended = lax.all_to_all(attended, ("y", "x"), 0, 0, tiled=True)
     with jax.named_scope("unpack"):

time: 87.2 us -> 93.4 us (1.071)
  starting transfers between devices: 25.6 us -> 30.1 us
  Pallas kernels: 13.9 us -> 15 us
    ppermute x7 -> x8, starting transfers between devices: 21.8 us -> 24.3 us  [hop(): return lax.ppermute(block, RING, route)]
    ppermute x3 -> x4, starting transfers between devices: 3.79 us -> 5.75 us  [swap(): return lax.ppermute(block, 'core', [(0, 1), (1, 0)])]
    pallas_call x7 -> x8, Pallas kernels: 12.2 us -> 13.3 us  [step(): call(kernel, jax.ShapeDtypeStruct((len(steps), STATE, width), jnp.float32...]
    ppermute x7 -> x8, waiting for transfers between devices: 14.6 us -> 15 us  [hop(): return lax.ppermute(block, RING, route)]
  transfers between devices with their start and end apart: 10 -> 12, of which waited for: 6 -> 8; matrix products, arithmetic and copies ran while one was open for 0% -> 0% of each run, Pallas kernels for 12% -> 11%
where the time goes in v11:
time: 93.4 us; the launch traced here: 93.2 us
  blocking collectives  31.6 us (34%)
  starting transfers between devices  30.1 us (32%)
  waiting for transfers between devices  15.1 us (16%)
  Pallas kernels  15 us (16%)
  local copies, waits for them, and re-layouts  1.2 us (1%)
    ppermute x8, starting transfers between devices, hop(): return lax.ppermute(block, RING, route)  24.3 us
    all_to_all x1, blocking collectives, shards(): parts = lax.all_to_all(parts, ('y', 'x'), 0, 0, tiled=True)  20.9 us
    ppermute x8, waiting for transfers between devices, hop(): return lax.ppermute(block, RING, route)  15 us
    pallas_call x8, Pallas kernels, step(): call(kernel, jax.ShapeDtypeStruct((len(steps), STATE, width), jnp.float32...  13.3 us
    all_to_all x1, blocking collectives, shards(): attended = lax.all_to_all(attended, ('y', 'x'), 0, 0, tiled=True)  10.7 us
    ppermute x4, starting transfers between devices, swap(): return lax.ppermute(block, 'core', [(0, 1), (1, 0)])  5.75 us
  transfers between devices with their start and end apart: 12, of which 8 were waited for; matrix products, arithmetic and copies ran while one was open for 0% of the time, Pallas kernels for 11%

profile of v11, /device:TPU:1, one launch (start us, length us, event | category | flops | bytes accessed | tf_op | source)
XLA Modules:
  0.0 93.2 jit_solution(825464812462611229)
XLA Ops:
  0.0 0.0 copy-start
  0.0 1.1 %copy-done = bf16[3,1,64,2048]{3,2,1,0:T(8,128)(2,1)S(1)} copy-done((bf16[3,1,64,2048]{3,2,1,0:T(8,128)(2,1)S(1)}, bf16[3,1,64,2048]{3,2,1,0:T(8,128)(2,1)}, u32[]{:S(2)}) %copy-start) | copy-done | bytes 786456
  1.1 0.1 pack.1
  1.3 0.0 copy-start.1
  1.3 20.9 %all_to_all.10.parts_ref = bf16[16,192,128]{2,1,0:T(8,128)(2,1)S(1)} all-to-all(bf16[16,192,128]{2,1,0:T(8,128)(2,1)S(1)} %pack.1), channel_id=1, replica_groups=mesh['zlo'=2,'y'=4,'core'=2,'x'=4,'zhi'=4] {'y','x'}, dimensions={0} | all-to-all | bytes 1572864 | tf_op jit(solution)/shard_map/tokens_to_heads/all_to_all | solution.py:196
  22.2 0.1 split.1
  22.3 1.9 %collective-permute-start.2 = (bf16[4,512,128]{2,1,0:T(8,128)(2,1)S(1)}, bf16[4,512,128]{2,1,0:T(8,128)(2,1)S(1)}, u32[]{:S(2)}, u32[]{:S(2)}) collective-permute-start(bf16[4,512,128]{2,1,0:T(8,128)(2,1)S(1)} %get-tuple-element.26.refs_3_), channel_id=1, source_target_pairs={{0,16},{16,0},{1,17},{17,1},{2,18},{18,2},{3,19},{19,3},{4,20},{20... | collective-permute-start | bytes 1572872 | tf_op jit(solution)/shard_map/swap_pairs/ppermute | solution.py:217
  24.2 0.1 collective-permute-start.1
  24.3 5.6 %collective-permute-start = (bf16[4,512,128]{2,1,0:T(8,128)(2,1)S(1)}, bf16[4,512,128]{2,1,0:T(8,128)(2,1)S(1)}, u32[]{:S(2)}, u32[]{:S(2)}) collective-permute-start(bf16[4,512,128]{2,1,0:T(8,128)(2,1)S(1)} %get-tuple-element.26.refs_3_), channel_id=1, source_target_pairs={{0,128},{128,1},{1,129},{129,2},{2,130},{130,3},{3,131},{131,0},{1... | collective-permute-start | bytes 1572872 | tf_op jit(solution)/shard_map/ring/ppermute | solution.py:214
  29.9 0.0 collective-permute-done.1.refs_2_
  29.9 0.0 collective-permute-done.2
  29.9 1.8 %collective-permute-start.4 = (bf16[4,512,128]{2,1,0:T(8,128)(2,1)S(1)}, bf16[4,512,128]{2,1,0:T(8,128)(2,1)S(1)}, u32[]{:S(2)}, u32[]{:S(2)}) collective-permute-start(bf16[4,512,128]{2,1,0:T(8,128)(2,1)S(1)} %collective-permute-done.2), channel_id=1, source_target_pairs={{0,128},{128,1},{1,129},{129,2},{2,130},{130,3},{3,131},{131,0},{1... | collective-permute-start | bytes 1572872 | tf_op jit(solution)/shard_map/ring/ppermute | solution.py:214
  31.7 0.0 copy-done.1
  31.7 2.4 %attend.8.refs_5_ = f32[4,144,512]{2,1,0:T(8,128)S(1)} custom-call(s32[16]{0:T(128)S(1)} %copy-done.1, bf16[4,256,128]{2,1,0:T(8,128)(2,1)S(1)} %get-tuple-element.27.refs_1_, bf16[4,256,128]{2,1,0:T(8,128)(2,1)S(1)} %collective-permute-done.1.refs_2_, bf16[4,512,128]{2,1,0:T(8,128)(2,1)S(1)} %get-tuple-element.26.refs_3_), custom_call_target="tpu_custom_call" | custom-call | flops 4294967296 | bytes 8388608 | tf_op jit(solution)/shard_map/attend/pallas_call | solution.py:236
  34.1 1.9 %collective-permute-done.refs_3_ = bf16[4,512,128]{2,1,0:T(8,128)(2,1)S(1)} collective-permute-done((bf16[4,512,128]{2,1,0:T(8,128)(2,1)S(1)}, bf16[4,512,128]{2,1,0:T(8,128)(2,1)S(1)}, u32[]{:S(2)}, u32[]{:S(2)}) %collective-permute-start) | collective-permute-done | bytes 524320 | tf_op jit(solution)/shard_map/ring/ppermute | solution.py:214
  36.0 3.1 %collective-permute-start.3 = (bf16[4,512,128]{2,1,0:T(8,128)(2,1)S(1)}, bf16[4,512,128]{2,1,0:T(8,128)(2,1)S(1)}, u32[]{:S(2)}, u32[]{:S(2)}) collective-permute-start(bf16[4,512,128]{2,1,0:T(8,128)(2,1)S(1)} %collective-permute-done.refs_3_), channel_id=1, source_target_pairs={{0,128},{128,1},{1,129},{129,2},{2,130},{130,3},{3,131},{131,0},{1... | collective-permute-start | bytes 1572872 | tf_op jit(solution)/shard_map/ring/ppermute | solution.py:214
  39.1 2.5 %collective-permute-done.4.refs_4_ = bf16[4,512,128]{2,1,0:T(8,128)(2,1)S(1)} collective-permute-done((bf16[4,512,128]{2,1,0:T(8,128)(2,1)S(1)}, bf16[4,512,128]{2,1,0:T(8,128)(2,1)S(1)}, u32[]{:S(2)}, u32[]{:S(2)}) %collective-permute-start.4) | collective-permute-done | bytes 524320 | tf_op jit(solution)/shard_map/ring/ppermute | solution.py:214
  41.6 3.1 %collective-permute-start.6 = (bf16[4,512,128]{2,1,0:T(8,128)(2,1)S(1)}, bf16[4,512,128]{2,1,0:T(8,128)(2,1)S(1)}, u32[]{:S(2)}, u32[]{:S(2)}) collective-permute-start(bf16[4,512,128]{2,1,0:T(8,128)(2,1)S(1)} %collective-permute-done.4.refs_4_), channel_id=1, source_target_pairs={{0,128},{128,1},{1,129},{129,2},{2,130},{130,3},{3,131},{131,0},{1... | collective-permute-start | bytes 1572872 | tf_op jit(solution)/shard_map/ring/ppermute | solution.py:214
  44.7 0.7 attend.9.refs_5_
  45.4 1.8 %collective-permute-done.3.refs_3_ = bf16[4,512,128]{2,1,0:T(8,128)(2,1)S(1)} collective-permute-done((bf16[4,512,128]{2,1,0:T(8,128)(2,1)S(1)}, bf16[4,512,128]{2,1,0:T(8,128)(2,1)S(1)}, u32[]{:S(2)}, u32[]{:S(2)}) %collective-permute-start.3) | collective-permute-done | bytes 524320 | tf_op jit(solution)/shard_map/ring/ppermute | solution.py:214
  47.2 3.8 %collective-permute-start.5 = (bf16[4,512,128]{2,1,0:T(8,128)(2,1)S(1)}, bf16[4,512,128]{2,1,0:T(8,128)(2,1)S(1)}, u32[]{:S(2)}, u32[]{:S(2)}) collective-permute-start(bf16[4,512,128]{2,1,0:T(8,128)(2,1)S(1)} %collective-permute-done.3.refs_3_), channel_id=1, source_target_pairs={{0,128},{128,1},{1,129},{129,2},{2,130},{130,3},{3,131},{131,0},{1... | collective-permute-start | bytes 1572872 | tf_op jit(solution)/shard_map/ring/ppermute | solution.py:214
  51.0 1.8 %collective-permute-done.6.refs_4_ = bf16[4,512,128]{2,1,0:T(8,128)(2,1)S(1)} collective-permute-done((bf16[4,512,128]{2,1,0:T(8,128)(2,1)S(1)}, bf16[4,512,128]{2,1,0:T(8,128)(2,1)S(1)}, u32[]{:S(2)}, u32[]{:S(2)}) %collective-permute-start.6) | collective-permute-done | bytes 524320 | tf_op jit(solution)/shard_map/ring/ppermute | solution.py:214
  52.8 3.1 %collective-permute-start.9 = (bf16[4,512,128]{2,1,0:T(8,128)(2,1)S(1)}, bf16[4,512,128]{2,1,0:T(8,128)(2,1)S(1)}, u32[]{:S(2)}, u32[]{:S(2)}) collective-permute-start(bf16[4,512,128]{2,1,0:T(8,128)(2,1)S(1)} %collective-permute-done.6.refs_4_), channel_id=1, source_target_pairs={{0,128},{128,1},{1,129},{129,2},{2,130},{130,3},{3,131},{131,0},{1... | collective-permute-start | bytes 1572872 | tf_op jit(solution)/shard_map/ring/ppermute | solution.py:214
  56.0 4.3 %attend.10.refs_4_ = f32[4,144,512]{2,1,0:T(8,128)S(1)} custom-call(s32[16]{0:T(128)S(1)} %copy-done.1, bf16[4,256,128]{2,1,0:T(8,128)(2,1)S(1)} %get-tuple-element.27.refs_1_, bf16[4,256,128]{2,1,0:T(8,128)(2,1)S(1)} %collective-permute-done.1.refs_2_, bf16[4,512,128]{2,1,0:T(8,128)(2,1)S(1)} %collective-permute-done.3.refs_3_, ...), custom_call_target="tpu_custom_call", output_to_operand_aliasing={{}: (5, {})} | custom-call | flops 8589934592 | bytes 8388608 | tf_op jit(solution)/shard_map/attend/pallas_call | solution.py:236
  60.3 0.0 collective-permute-done.5.refs_3_
  60.4 1.3 %collective-permute-start.8 = (bf16[2,512,128]{2,1,0:T(8,128)(2,1)S(1)}, bf16[2,512,128]{2,1,0:T(8,128)(2,1)S(1)}, u32[]{:S(2)}, u32[]{:S(2)}) collective-permute-start(bf16[2,512,128]{2,1,0:T(8,128)(2,1)S(1)} %get-tuple-element.47), channel_id=1, source_target_pairs={{0,128},{128,1},{1,129},{129,2},{2,130},{130,3},{3,131},{131,0},{1... | collective-permute-start | bytes 786440 | tf_op jit(solution)/shard_map/ring/ppermute | solution.py:214
  61.7 0.7 attend.11.refs_4_
  62.4 1.7 %collective-permute-done.9.refs_3_ = bf16[4,512,128]{2,1,0:T(8,128)(2,1)S(1)} collective-permute-done((bf16[4,512,128]{2,1,0:T(8,128)(2,1)S(1)}, bf16[4,512,128]{2,1,0:T(8,128)(2,1)S(1)}, u32[]{:S(2)}, u32[]{:S(2)}) %collective-permute-start.9) | collective-permute-done | bytes 524320 | tf_op jit(solution)/shard_map/ring/ppermute | solution.py:214
  64.1 0.7 attend.12.refs_4_
  64.8 2.1 %collective-permute-done.8.refs_3_ = bf16[2,512,128]{2,1,0:T(8,128)(2,1)S(1)} collective-permute-done((bf16[2,512,128]{2,1,0:T(8,128)(2,1)S(1)}, bf16[2,512,128]{2,1,0:T(8,128)(2,1)S(1)}, u32[]{:S(2)}, u32[]{:S(2)}) %collective-permute-start.8) | collective-permute-done | bytes 262176 | tf_op jit(solution)/shard_map/ring/ppermute | solution.py:214
  66.9 2.2 %attend.13.refs_4_.state_ref = f32[4,144,512]{2,1,0:T(8,128)S(1)} custom-call(s32[16]{0:T(128)S(1)} %copy-done.1, bf16[4,256,128]{2,1,0:T(8,128)(2,1)S(1)} %get-tuple-element.27.refs_1_, bf16[4,256,128]{2,1,0:T(8,128)(2,1)S(1)} %collective-permute-done.1.refs_2_, ...), custom_call_target="tpu_custom_call", output_to_operand_aliasing={{}: (4, {})} | custom-call | flops 2147483648 | bytes 8388608 | tf_op jit(solution)/shard_map/attend/pallas_call | solution.py:236
  69.1 1.8 %collective-permute-start.10 = (f32[2,144,256]{2,1,0:T(8,128)S(1)}, f32[2,144,256]{2,1,0:T(8,128)S(1)}, u32[]{:S(2)}, u32[]{:S(2)}) collective-permute-start(f32[2,144,256]{2,1,0:T(8,128)S(1)} %slice.12), channel_id=1, source_target_pairs={{0,16},{16,0},{1,17},{17,1},{2,18},{18,2},{3,19},{19,3},{4,20},{20... | collective-permute-start | bytes 884744 | tf_op jit(solution)/shard_map/swap_terms/ppermute | solution.py:217
  70.9 2.5 %collective-permute-start.7 = (bf16[2,512,128]{2,1,0:T(8,128)(2,1)S(1)}, bf16[2,512,128]{2,1,0:T(8,128)(2,1)S(1)}, u32[]{:S(2)}, u32[]{:S(2)}) collective-permute-start(bf16[2,512,128]{2,1,0:T(8,128)(2,1)S(1)} %get-tuple-element.48), channel_id=1, source_target_pairs={{0,128},{128,1},{1,129},{129,2},{2,130},{130,3},{3,131},{131,0},{1... | collective-permute-start | bytes 786440 | tf_op jit(solution)/shard_map/ring/ppermute | solution.py:214
  73.4 3.3 %collective-permute-done.7.refs_3_ = bf16[2,512,128]{2,1,0:T(8,128)(2,1)S(1)} collective-permute-done((bf16[2,512,128]{2,1,0:T(8,128)(2,1)S(1)}, bf16[2,512,128]{2,1,0:T(8,128)(2,1)S(1)}, u32[]{:S(2)}, u32[]{:S(2)}) %collective-permute-start.7) | collective-permute-done | bytes 262176 | tf_op jit(solution)/shard_map/ring/ppermute | solution.py:214
  76.7 0.0 collective-permute-done.10.early_ref
  76.7 1.1 %attend.15 = f32[2,144,256]{2,1,0:T(8,128)S(1)} custom-call(s32[16]{0:T(128)S(1)} %copy-done.1, bf16[4,256,128]{2,1,0:T(8,128)(2,1)S(1)} %get-tuple-element.27.refs_1_, bf16[4,256,128]{2,1,0:T(8,128)(2,1)S(1)} %collective-permute-done.1.refs_2_, bf16[2,512,128]{2,1,0:T(8,128)(2,1)S(1)} %collective-permute-done.7.refs_3_, ...), custom_call_target="tpu_custom_call" | custom-call | flops 536870912 | bytes 8388608 | tf_op jit(solution)/shard_map/attend/pallas_call | solution.py:236
  77.8 2.0 %collective-permute-start.11 = (f32[2,144,256]{2,1,0:T(8,128)S(1)}, f32[2,144,256]{2,1,0:T(8,128)S(1)}, u32[]{:S(2)}, u32[]{:S(2)}) collective-permute-start(f32[2,144,256]{2,1,0:T(8,128)S(1)} %attend.15), channel_id=1, source_target_pairs={{0,16},{16,0},{1,17},{17,1},{2,18},{18,2},{3,19},{19,3},{4,20},{20... | collective-permute-start | bytes 884744 | tf_op jit(solution)/shard_map/swap_terms/ppermute | solution.py:217
  79.8 1.1 %attend.14.mine_ref = f32[2,144,256]{2,1,0:T(8,128)S(1)} custom-call(s32[16]{0:T(128)S(1)} %copy-done.1, bf16[4,256,128]{2,1,0:T(8,128)(2,1)S(1)} %get-tuple-element.27.refs_1_, bf16[4,256,128]{2,1,0:T(8,128)(2,1)S(1)} %collective-permute-done.1.refs_2_, bf16[2,512,128]{2,1,0:T(8,128)(2,1)S(1)} %collective-permute-done.7.refs_3_, ...), custom_call_target="tpu_custom_call" | custom-call | flops 536870912 | bytes 8388608 | tf_op jit(solution)/shard_map/attend/pallas_call | solution.py:236
  80.9 0.1 collective-permute-done.11.late_ref
  81.0 0.7 join.1
  81.7 10.7 %all_to_all.11.parts_ref = bf16[16,64,128]{2,1,0:T(8,128)(2,1)S(1)} all-to-all(bf16[16,64,128]{2,1,0:T(8,128)(2,1)S(1)} %join.1), channel_id=1, replica_groups=mesh['zlo'=2,'y'=4,'core'=2,'x'=4,'zhi'=4] {'y','x'}, dimensions={0} | all-to-all | bytes 524288 | tf_op jit(solution)/shard_map/heads_to_tokens/all_to_all | solution.py:276
  92.4 0.8 unpack.1
  (2 shorter events, 0.1 us)
Async XLA Ops:
  0.0 1.1 %copy-start = (bf16[3,1,64,2048]{3,2,1,0:T(8,128)(2,1)S(1)}, bf16[3,1,64,2048]{3,2,1,0:T(8,128)(2,1)}, u32[]{:S(2)}) copy-start(bf16[3,1,64,2048]{3,2,1,0:T(8,128)(2,1)} %param.2) | copy-start | bytes 2359300
  1.3 30.4 %copy-start.1 = (s32[16]{0:T(128)S(1)}, s32[16]{0:T(128)}, u32[]{:S(2)}) copy-start(s32[16]{0:T(128)} %lengths_ref.1) | copy-start | bytes 196
  22.3 7.6 %collective-permute-start.2 = (bf16[4,512,128]{2,1,0:T(8,128)(2,1)S(1)}, bf16[4,512,128]{2,1,0:T(8,128)(2,1)S(1)}, u32[]{:S(2)}, u32[]{:S(2)}) collective-permute-start(bf16[4,512,128]{2,1,0:T(8,128)(2,1)S(1)} %get-tuple-element.26.refs_3_), channel_id=1, source_target_pairs={{0,16},{16,0},{1,17},{17,1},{2,18},{18,2},{3,19},{19,3},{4,20},{20... | collective-permute-start | bytes 1572872 | tf_op jit(solution)/shard_map/swap_pairs/ppermute | solution.py:217
  24.2 5.7 %collective-permute-start.1 = (bf16[4,256,128]{2,1,0:T(8,128)(2,1)S(1)}, bf16[4,256,128]{2,1,0:T(8,128)(2,1)S(1)}, u32[]{:S(2)}, u32[]{:S(2)}) collective-permute-start(bf16[4,256,128]{2,1,0:T(8,128)(2,1)S(1)} %get-tuple-element.27.refs_1_), channel_id=1, source_target_pairs={{0,16},{16,0},{1,17},{17,1},{2,18},{18,2},{3,19},{19,3},{4,20},{20... | collective-permute-start | bytes 786440 | tf_op jit(solution)/shard_map/swap_queries/ppermute | solution.py:217
  24.3 11.7 %collective-permute-start = (bf16[4,512,128]{2,1,0:T(8,128)(2,1)S(1)}, bf16[4,512,128]{2,1,0:T(8,128)(2,1)S(1)}, u32[]{:S(2)}, u32[]{:S(2)}) collective-permute-start(bf16[4,512,128]{2,1,0:T(8,128)(2,1)S(1)} %get-tuple-element.26.refs_3_), channel_id=1, source_target_pairs={{0,128},{128,1},{1,129},{129,2},{2,130},{130,3},{3,131},{131,0},{1... | collective-permute-start | bytes 1572872 | tf_op jit(solution)/shard_map/ring/ppermute | solution.py:214
  29.9 11.7 %collective-permute-start.4 = (bf16[4,512,128]{2,1,0:T(8,128)(2,1)S(1)}, bf16[4,512,128]{2,1,0:T(8,128)(2,1)S(1)}, u32[]{:S(2)}, u32[]{:S(2)}) collective-permute-start(bf16[4,512,128]{2,1,0:T(8,128)(2,1)S(1)} %collective-permute-done.2), channel_id=1, source_target_pairs={{0,128},{128,1},{1,129},{129,2},{2,130},{130,3},{3,131},{131,0},{1... | collective-permute-start | bytes 1572872 | tf_op jit(solution)/shard_map/ring/ppermute | solution.py:214
  36.0 11.2 %collective-permute-start.3 = (bf16[4,512,128]{2,1,0:T(8,128)(2,1)S(1)}, bf16[4,512,128]{2,1,0:T(8,128)(2,1)S(1)}, u32[]{:S(2)}, u32[]{:S(2)}) collective-permute-start(bf16[4,512,128]{2,1,0:T(8,128)(2,1)S(1)} %collective-permute-done.refs_3_), channel_id=1, source_target_pairs={{0,128},{128,1},{1,129},{129,2},{2,130},{130,3},{3,131},{131,0},{1... | collective-permute-start | bytes 1572872 | tf_op jit(solution)/shard_map/ring/ppermute | solution.py:214
  41.6 11.2 %collective-permute-start.6 = (bf16[4,512,128]{2,1,0:T(8,128)(2,1)S(1)}, bf16[4,512,128]{2,1,0:T(8,128)(2,1)S(1)}, u32[]{:S(2)}, u32[]{:S(2)}) collective-permute-start(bf16[4,512,128]{2,1,0:T(8,128)(2,1)S(1)} %collective-permute-done.4.refs_4_), channel_id=1, source_target_pairs={{0,128},{128,1},{1,129},{129,2},{2,130},{130,3},{3,131},{131,0},{1... | collective-permute-start | bytes 1572872 | tf_op jit(solution)/shard_map/ring/ppermute | solution.py:214
  47.2 13.1 %collective-permute-start.5 = (bf16[4,512,128]{2,1,0:T(8,128)(2,1)S(1)}, bf16[4,512,128]{2,1,0:T(8,128)(2,1)S(1)}, u32[]{:S(2)}, u32[]{:S(2)}) collective-permute-start(bf16[4,512,128]{2,1,0:T(8,128)(2,1)S(1)} %collective-permute-done.3.refs_3_), channel_id=1, source_target_pairs={{0,128},{128,1},{1,129},{129,2},{2,130},{130,3},{3,131},{131,0},{1... | collective-permute-start | bytes 1572872 | tf_op jit(solution)/shard_map/ring/ppermute | solution.py:214
  52.8 11.2 %collective-permute-start.9 = (bf16[4,512,128]{2,1,0:T(8,128)(2,1)S(1)}, bf16[4,512,128]{2,1,0:T(8,128)(2,1)S(1)}, u32[]{:S(2)}, u32[]{:S(2)}) collective-permute-start(bf16[4,512,128]{2,1,0:T(8,128)(2,1)S(1)} %collective-permute-done.6.refs_4_), channel_id=1, source_target_pairs={{0,128},{128,1},{1,129},{129,2},{2,130},{130,3},{3,131},{131,0},{1... | collective-permute-start | bytes 1572872 | tf_op jit(solution)/shard_map/ring/ppermute | solution.py:214
  60.4 6.5 %collective-permute-start.8 = (bf16[2,512,128]{2,1,0:T(8,128)(2,1)S(1)}, bf16[2,512,128]{2,1,0:T(8,128)(2,1)S(1)}, u32[]{:S(2)}, u32[]{:S(2)}) collective-permute-start(bf16[2,512,128]{2,1,0:T(8,128)(2,1)S(1)} %get-tuple-element.47), channel_id=1, source_target_pairs={{0,128},{128,1},{1,129},{129,2},{2,130},{130,3},{3,131},{131,0},{1... | collective-permute-start | bytes 786440 | tf_op jit(solution)/shard_map/ring/ppermute | solution.py:214
  69.1 7.6 %collective-permute-start.10 = (f32[2,144,256]{2,1,0:T(8,128)S(1)}, f32[2,144,256]{2,1,0:T(8,128)S(1)}, u32[]{:S(2)}, u32[]{:S(2)}) collective-permute-start(f32[2,144,256]{2,1,0:T(8,128)S(1)} %slice.12), channel_id=1, source_target_pairs={{0,16},{16,0},{1,17},{17,1},{2,18},{18,2},{3,19},{19,3},{4,20},{20... | collective-permute-start | bytes 884744 | tf_op jit(solution)/shard_map/swap_terms/ppermute | solution.py:217
  70.9 5.8 %collective-permute-start.7 = (bf16[2,512,128]{2,1,0:T(8,128)(2,1)S(1)}, bf16[2,512,128]{2,1,0:T(8,128)(2,1)S(1)}, u32[]{:S(2)}, u32[]{:S(2)}) collective-permute-start(bf16[2,512,128]{2,1,0:T(8,128)(2,1)S(1)} %get-tuple-element.48), channel_id=1, source_target_pairs={{0,128},{128,1},{1,129},{129,2},{2,130},{130,3},{3,131},{131,0},{1... | collective-permute-start | bytes 786440 | tf_op jit(solution)/shard_map/ring/ppermute | solution.py:214
  77.8 3.2 %collective-permute-start.11 = (f32[2,144,256]{2,1,0:T(8,128)S(1)}, f32[2,144,256]{2,1,0:T(8,128)S(1)}, u32[]{:S(2)}, u32[]{:S(2)}) collective-permute-start(f32[2,144,256]{2,1,0:T(8,128)S(1)} %attend.15), channel_id=1, source_target_pairs={{0,16},{16,0},{1,17},{17,1},{2,18},{18,2},{3,19},{19,3},{4,20},{20... | collective-permute-start | bytes 884744 | tf_op jit(solution)/shard_map/swap_terms/ppermute | solution.py:217

commit v12 on v11

--- a/solution.py
+++ b/solution.py
@@ -261,7 +261,7 @@
     state = step([block], 4, state)
     with jax.named_scope("swap_terms"):
         early = swap(state[:2, :, ROWS:])
-    block, state, early = lax.optimization_barrier((halves[1], state, early))
+    block, state = after(halves[1], state)
     late = step([block], 4, state, 1, begin=2, steps=(2, 3))
     with jax.named_scope("swap_terms"):
         late = swap(late)

time: 93.4 us -> 88 us (0.942); the launches traced: 93.2 us -> 86.6 us
  starting transfers between devices: 30.1 us -> 25.7 us
  waiting for transfers between devices: 15.1 us -> 12.7 us
    ppermute x8, waiting for transfers between devices: 15 us -> 12.3 us  [hop(): return lax.ppermute(block, RING, route)]
    ppermute x8, starting transfers between devices: 24.3 us -> 21.9 us  [hop(): return lax.ppermute(block, RING, route)]
    ppermute x4, starting transfers between devices: 5.75 us -> 3.8 us  [swap(): return lax.ppermute(block, 'core', [(0, 1), (1, 0)])]
  transfers between devices with their start and end apart: 12 -> 12, of which waited for: 8 -> 8; matrix products, arithmetic and copies ran while one was open for 0% -> 0% of each run, Pallas kernels for 11% -> 15%
where the time goes in v12:
time: 88 us; the launch traced here: 86.6 us
  blocking collectives  31.9 us (36%)
  starting transfers between devices  25.7 us (29%)
  Pallas kernels  15 us (17%)
  waiting for transfers between devices  12.7 us (14%)
  local copies, waits for them, and re-layouts  1.2 us (1%)
    ppermute x8, starting transfers between devices, hop(): return lax.ppermute(block, RING, route)  21.9 us
    all_to_all x1, blocking collectives, shards(): parts = lax.all_to_all(parts, ('y', 'x'), 0, 0, tiled=True)  20.9 us
    pallas_call x8, Pallas kernels, step(): call(kernel, jax.ShapeDtypeStruct((len(steps), STATE, width), jnp.float32...  13.3 us
    ppermute x8, waiting for transfers between devices, hop(): return lax.ppermute(block, RING, route)  12.3 us
    all_to_all x1, blocking collectives, shards(): attended = lax.all_to_all(attended, ('y', 'x'), 0, 0, tiled=True)  11 us
    ppermute x4, starting transfers between devices, swap(): return lax.ppermute(block, 'core', [(0, 1), (1, 0)])  3.8 us
  transfers between devices with their start and end apart: 12, of which 8 were waited for; matrix products, arithmetic and copies ran while one was open for 0% of the time, Pallas kernels for 15%

profile of v12, /device:TPU:1, one launch (start us, length us, event | category | flops | bytes accessed | tf_op | source)
XLA Modules:
  0.0 86.6 jit_solution(13846931224308599098)
XLA Ops:
  0.0 0.0 copy-start
  0.0 1.1 %copy-done = bf16[3,1,64,2048]{3,2,1,0:T(8,128)(2,1)S(1)} copy-done((bf16[3,1,64,2048]{3,2,1,0:T(8,128)(2,1)S(1)}, bf16[3,1,64,2048]{3,2,1,0:T(8,128)(2,1)}, u32[]{:S(2)}) %copy-start) | copy-done | bytes 786456
  1.1 0.1 pack.1
  1.3 0.0 copy-start.1
  1.3 20.9 %all_to_all.10.parts_ref = bf16[16,192,128]{2,1,0:T(8,128)(2,1)S(1)} all-to-all(bf16[16,192,128]{2,1,0:T(8,128)(2,1)S(1)} %pack.1), channel_id=1, replica_groups=mesh['zlo'=2,'y'=4,'core'=2,'x'=4,'zhi'=4] {'y','x'}, dimensions={0} | all-to-all | bytes 1572864 | tf_op jit(solution)/shard_map/tokens_to_heads/all_to_all | solution.py:196
  22.2 0.1 split.1
  22.3 1.9 %collective-permute-start.2 = (bf16[4,512,128]{2,1,0:T(8,128)(2,1)S(1)}, bf16[4,512,128]{2,1,0:T(8,128)(2,1)S(1)}, u32[]{:S(2)}, u32[]{:S(2)}) collective-permute-start(bf16[4,512,128]{2,1,0:T(8,128)(2,1)S(1)} %get-tuple-element.25.refs_3_), channel_id=1, source_target_pairs={{0,16},{16,0},{1,17},{17,1},{2,18},{18,2},{3,19},{19,3},{4,20},{20... | collective-permute-start | bytes 1572872 | tf_op jit(solution)/shard_map/swap_pairs/ppermute | solution.py:217
  24.2 0.1 collective-permute-start.1
  24.3 5.6 %collective-permute-start = (bf16[4,512,128]{2,1,0:T(8,128)(2,1)S(1)}, bf16[4,512,128]{2,1,0:T(8,128)(2,1)S(1)}, u32[]{:S(2)}, u32[]{:S(2)}) collective-permute-start(bf16[4,512,128]{2,1,0:T(8,128)(2,1)S(1)} %get-tuple-element.25.refs_3_), channel_id=1, source_target_pairs={{0,128},{128,1},{1,129},{129,2},{2,130},{130,3},{3,131},{131,0},{1... | collective-permute-start | bytes 1572872 | tf_op jit(solution)/shard_map/ring/ppermute | solution.py:214
  29.9 0.0 collective-permute-done.1.refs_2_
  29.9 0.0 collective-permute-done.2
  29.9 1.8 %collective-permute-start.4 = (bf16[4,512,128]{2,1,0:T(8,128)(2,1)S(1)}, bf16[4,512,128]{2,1,0:T(8,128)(2,1)S(1)}, u32[]{:S(2)}, u32[]{:S(2)}) collective-permute-start(bf16[4,512,128]{2,1,0:T(8,128)(2,1)S(1)} %collective-permute-done.2), channel_id=1, source_target_pairs={{0,128},{128,1},{1,129},{129,2},{2,130},{130,3},{3,131},{131,0},{1... | collective-permute-start | bytes 1572872 | tf_op jit(solution)/shard_map/ring/ppermute | solution.py:214
  31.7 0.0 copy-done.1
  31.7 2.4 %attend.8.refs_5_ = f32[4,144,512]{2,1,0:T(8,128)S(1)} custom-call(s32[16]{0:T(128)S(1)} %copy-done.1, bf16[4,256,128]{2,1,0:T(8,128)(2,1)S(1)} %get-tuple-element.26.refs_1_, bf16[4,256,128]{2,1,0:T(8,128)(2,1)S(1)} %collective-permute-done.1.refs_2_, bf16[4,512,128]{2,1,0:T(8,128)(2,1)S(1)} %get-tuple-element.25.refs_3_), custom_call_target="tpu_custom_call" | custom-call | flops 4294967296 | bytes 8388608 | tf_op jit(solution)/shard_map/attend/pallas_call | solution.py:236
  34.1 1.9 %collective-permute-done.refs_3_ = bf16[4,512,128]{2,1,0:T(8,128)(2,1)S(1)} collective-permute-done((bf16[4,512,128]{2,1,0:T(8,128)(2,1)S(1)}, bf16[4,512,128]{2,1,0:T(8,128)(2,1)S(1)}, u32[]{:S(2)}, u32[]{:S(2)}) %collective-permute-start) | collective-permute-done | bytes 524320 | tf_op jit(solution)/shard_map/ring/ppermute | solution.py:214
  36.0 3.1 %collective-permute-start.3 = (bf16[4,512,128]{2,1,0:T(8,128)(2,1)S(1)}, bf16[4,512,128]{2,1,0:T(8,128)(2,1)S(1)}, u32[]{:S(2)}, u32[]{:S(2)}) collective-permute-start(bf16[4,512,128]{2,1,0:T(8,128)(2,1)S(1)} %collective-permute-done.refs_3_), channel_id=1, source_target_pairs={{0,128},{128,1},{1,129},{129,2},{2,130},{130,3},{3,131},{131,0},{1... | collective-permute-start | bytes 1572872 | tf_op jit(solution)/shard_map/ring/ppermute | solution.py:214
  39.1 2.5 %collective-permute-done.4.refs_4_ = bf16[4,512,128]{2,1,0:T(8,128)(2,1)S(1)} collective-permute-done((bf16[4,512,128]{2,1,0:T(8,128)(2,1)S(1)}, bf16[4,512,128]{2,1,0:T(8,128)(2,1)S(1)}, u32[]{:S(2)}, u32[]{:S(2)}) %collective-permute-start.4) | collective-permute-done | bytes 524320 | tf_op jit(solution)/shard_map/ring/ppermute | solution.py:214
  41.6 3.1 %collective-permute-start.6 = (bf16[4,512,128]{2,1,0:T(8,128)(2,1)S(1)}, bf16[4,512,128]{2,1,0:T(8,128)(2,1)S(1)}, u32[]{:S(2)}, u32[]{:S(2)}) collective-permute-start(bf16[4,512,128]{2,1,0:T(8,128)(2,1)S(1)} %collective-permute-done.4.refs_4_), channel_id=1, source_target_pairs={{0,128},{128,1},{1,129},{129,2},{2,130},{130,3},{3,131},{131,0},{1... | collective-permute-start | bytes 1572872 | tf_op jit(solution)/shard_map/ring/ppermute | solution.py:214
  44.7 0.7 attend.9.refs_5_
  45.4 1.8 %collective-permute-done.3.refs_3_ = bf16[4,512,128]{2,1,0:T(8,128)(2,1)S(1)} collective-permute-done((bf16[4,512,128]{2,1,0:T(8,128)(2,1)S(1)}, bf16[4,512,128]{2,1,0:T(8,128)(2,1)S(1)}, u32[]{:S(2)}, u32[]{:S(2)}) %collective-permute-start.3) | collective-permute-done | bytes 524320 | tf_op jit(solution)/shard_map/ring/ppermute | solution.py:214
  47.2 3.7 %collective-permute-start.5 = (bf16[4,512,128]{2,1,0:T(8,128)(2,1)S(1)}, bf16[4,512,128]{2,1,0:T(8,128)(2,1)S(1)}, u32[]{:S(2)}, u32[]{:S(2)}) collective-permute-start(bf16[4,512,128]{2,1,0:T(8,128)(2,1)S(1)} %collective-permute-done.3.refs_3_), channel_id=1, source_target_pairs={{0,128},{128,1},{1,129},{129,2},{2,130},{130,3},{3,131},{131,0},{1... | collective-permute-start | bytes 1572872 | tf_op jit(solution)/shard_map/ring/ppermute | solution.py:214
  51.0 1.9 %collective-permute-done.6.refs_4_ = bf16[4,512,128]{2,1,0:T(8,128)(2,1)S(1)} collective-permute-done((bf16[4,512,128]{2,1,0:T(8,128)(2,1)S(1)}, bf16[4,512,128]{2,1,0:T(8,128)(2,1)S(1)}, u32[]{:S(2)}, u32[]{:S(2)}) %collective-permute-start.6) | collective-permute-done | bytes 524320 | tf_op jit(solution)/shard_map/ring/ppermute | solution.py:214
  52.8 3.1 %collective-permute-start.9 = (bf16[4,512,128]{2,1,0:T(8,128)(2,1)S(1)}, bf16[4,512,128]{2,1,0:T(8,128)(2,1)S(1)}, u32[]{:S(2)}, u32[]{:S(2)}) collective-permute-start(bf16[4,512,128]{2,1,0:T(8,128)(2,1)S(1)} %collective-permute-done.6.refs_4_), channel_id=1, source_target_pairs={{0,128},{128,1},{1,129},{129,2},{2,130},{130,3},{3,131},{131,0},{1... | collective-permute-start | bytes 1572872 | tf_op jit(solution)/shard_map/ring/ppermute | solution.py:214
  56.0 4.3 %attend.10.refs_4_ = f32[4,144,512]{2,1,0:T(8,128)S(1)} custom-call(s32[16]{0:T(128)S(1)} %copy-done.1, bf16[4,256,128]{2,1,0:T(8,128)(2,1)S(1)} %get-tuple-element.26.refs_1_, bf16[4,256,128]{2,1,0:T(8,128)(2,1)S(1)} %collective-permute-done.1.refs_2_, bf16[4,512,128]{2,1,0:T(8,128)(2,1)S(1)} %collective-permute-done.3.refs_3_, ...), custom_call_target="tpu_custom_call", output_to_operand_aliasing={{}: (5, {})} | custom-call | flops 8589934592 | bytes 8388608 | tf_op jit(solution)/shard_map/attend/pallas_call | solution.py:236
  60.3 0.0 collective-permute-done.5.refs_3_
  60.4 1.3 %collective-permute-start.8 = (bf16[2,512,128]{2,1,0:T(8,128)(2,1)S(1)}, bf16[2,512,128]{2,1,0:T(8,128)(2,1)S(1)}, u32[]{:S(2)}, u32[]{:S(2)}) collective-permute-start(bf16[2,512,128]{2,1,0:T(8,128)(2,1)S(1)} %get-tuple-element.45), channel_id=1, source_target_pairs={{0,128},{128,1},{1,129},{129,2},{2,130},{130,3},{3,131},{131,0},{1... | collective-permute-start | bytes 786440 | tf_op jit(solution)/shard_map/ring/ppermute | solution.py:214
  61.7 0.1 collective-permute-start.7
  61.8 0.7 attend.11.refs_4_
  62.5 1.6 %collective-permute-done.9.refs_3_ = bf16[4,512,128]{2,1,0:T(8,128)(2,1)S(1)} collective-permute-done((bf16[4,512,128]{2,1,0:T(8,128)(2,1)S(1)}, bf16[4,512,128]{2,1,0:T(8,128)(2,1)S(1)}, u32[]{:S(2)}, u32[]{:S(2)}) %collective-permute-start.9) | collective-permute-done | bytes 524320 | tf_op jit(solution)/shard_map/ring/ppermute | solution.py:214
  64.1 0.7 attend.12.refs_4_
  64.8 2.1 %collective-permute-done.8.refs_3_ = bf16[2,512,128]{2,1,0:T(8,128)(2,1)S(1)} collective-permute-done((bf16[2,512,128]{2,1,0:T(8,128)(2,1)S(1)}, bf16[2,512,128]{2,1,0:T(8,128)(2,1)S(1)}, u32[]{:S(2)}, u32[]{:S(2)}) %collective-permute-start.8) | collective-permute-done | bytes 262176 | tf_op jit(solution)/shard_map/ring/ppermute | solution.py:214
  66.9 2.2 %attend.13.refs_4_.state_ref = f32[4,144,512]{2,1,0:T(8,128)S(1)} custom-call(s32[16]{0:T(128)S(1)} %copy-done.1, bf16[4,256,128]{2,1,0:T(8,128)(2,1)S(1)} %get-tuple-element.26.refs_1_, bf16[4,256,128]{2,1,0:T(8,128)(2,1)S(1)} %collective-permute-done.1.refs_2_, ...), custom_call_target="tpu_custom_call", output_to_operand_aliasing={{}: (4, {})} | custom-call | flops 2147483648 | bytes 8388608 | tf_op jit(solution)/shard_map/attend/pallas_call | solution.py:236
  69.1 0.6 collective-permute-done.7.refs_3_
  69.7 1.7 %collective-permute-start.10 = (f32[2,144,256]{2,1,0:T(8,128)S(1)}, f32[2,144,256]{2,1,0:T(8,128)S(1)}, u32[]{:S(2)}, u32[]{:S(2)}) collective-permute-start(f32[2,144,256]{2,1,0:T(8,128)S(1)} %slice.12), channel_id=1, source_target_pairs={{0,16},{16,0},{1,17},{17,1},{2,18},{18,2},{3,19},{19,3},{4,20},{20... | collective-permute-start | bytes 884744 | tf_op jit(solution)/shard_map/swap_terms/ppermute | solution.py:217
  71.4 1.1 %attend.15 = f32[2,144,256]{2,1,0:T(8,128)S(1)} custom-call(s32[16]{0:T(128)S(1)} %copy-done.1, bf16[4,256,128]{2,1,0:T(8,128)(2,1)S(1)} %get-tuple-element.26.refs_1_, bf16[4,256,128]{2,1,0:T(8,128)(2,1)S(1)} %collective-permute-done.1.refs_2_, bf16[2,512,128]{2,1,0:T(8,128)(2,1)S(1)} %collective-permute-done.7.refs_3_, ...), custom_call_target="tpu_custom_call" | custom-call | flops 536870912 | bytes 8388608 | tf_op jit(solution)/shard_map/attend/pallas_call | solution.py:236
  72.5 0.1 collective-permute-start.11
  72.6 1.1 %attend.14.mine_ref = f32[2,144,256]{2,1,0:T(8,128)S(1)} custom-call(s32[16]{0:T(128)S(1)} %copy-done.1, bf16[4,256,128]{2,1,0:T(8,128)(2,1)S(1)} %get-tuple-element.26.refs_1_, bf16[4,256,128]{2,1,0:T(8,128)(2,1)S(1)} %collective-permute-done.1.refs_2_, bf16[2,512,128]{2,1,0:T(8,128)(2,1)S(1)} %collective-permute-done.7.refs_3_, ...), custom_call_target="tpu_custom_call" | custom-call | flops 536870912 | bytes 8388608 | tf_op jit(solution)/shard_map/attend/pallas_call | solution.py:236
  73.7 0.0 collective-permute-done.10.early_ref
  73.8 0.4 collective-permute-done.11.late_ref
  74.2 0.7 join.1
  74.9 11.0 %all_to_all.11.parts_ref = bf16[16,64,128]{2,1,0:T(8,128)(2,1)S(1)} all-to-all(bf16[16,64,128]{2,1,0:T(8,128)(2,1)S(1)} %join.1), channel_id=1, replica_groups=mesh['zlo'=2,'y'=4,'core'=2,'x'=4,'zhi'=4] {'y','x'}, dimensions={0} | all-to-all | bytes 524288 | tf_op jit(solution)/shard_map/heads_to_tokens/all_to_all | solution.py:276
  85.9 0.8 unpack.1
  (2 shorter events, 0.1 us)
Async XLA Ops:
  0.0 1.1 %copy-start = (bf16[3,1,64,2048]{3,2,1,0:T(8,128)(2,1)S(1)}, bf16[3,1,64,2048]{3,2,1,0:T(8,128)(2,1)}, u32[]{:S(2)}) copy-start(bf16[3,1,64,2048]{3,2,1,0:T(8,128)(2,1)} %param.2) | copy-start | bytes 2359300
  1.3 30.4 %copy-start.1 = (s32[16]{0:T(128)S(1)}, s32[16]{0:T(128)}, u32[]{:S(2)}) copy-start(s32[16]{0:T(128)} %lengths_ref.1) | copy-start | bytes 196
  22.3 7.6 %collective-permute-start.2 = (bf16[4,512,128]{2,1,0:T(8,128)(2,1)S(1)}, bf16[4,512,128]{2,1,0:T(8,128)(2,1)S(1)}, u32[]{:S(2)}, u32[]{:S(2)}) collective-permute-start(bf16[4,512,128]{2,1,0:T(8,128)(2,1)S(1)} %get-tuple-element.25.refs_3_), channel_id=1, source_target_pairs={{0,16},{16,0},{1,17},{17,1},{2,18},{18,2},{3,19},{19,3},{4,20},{20... | collective-permute-start | bytes 1572872 | tf_op jit(solution)/shard_map/swap_pairs/ppermute | solution.py:217
  24.2 5.7 %collective-permute-start.1 = (bf16[4,256,128]{2,1,0:T(8,128)(2,1)S(1)}, bf16[4,256,128]{2,1,0:T(8,128)(2,1)S(1)}, u32[]{:S(2)}, u32[]{:S(2)}) collective-permute-start(bf16[4,256,128]{2,1,0:T(8,128)(2,1)S(1)} %get-tuple-element.26.refs_1_), channel_id=1, source_target_pairs={{0,16},{16,0},{1,17},{17,1},{2,18},{18,2},{3,19},{19,3},{4,20},{20... | collective-permute-start | bytes 786440 | tf_op jit(solution)/shard_map/swap_queries/ppermute | solution.py:217
  24.3 11.7 %collective-permute-start = (bf16[4,512,128]{2,1,0:T(8,128)(2,1)S(1)}, bf16[4,512,128]{2,1,0:T(8,128)(2,1)S(1)}, u32[]{:S(2)}, u32[]{:S(2)}) collective-permute-start(bf16[4,512,128]{2,1,0:T(8,128)(2,1)S(1)} %get-tuple-element.25.refs_3_), channel_id=1, source_target_pairs={{0,128},{128,1},{1,129},{129,2},{2,130},{130,3},{3,131},{131,0},{1... | collective-permute-start | bytes 1572872 | tf_op jit(solution)/shard_map/ring/ppermute | solution.py:214
  29.9 11.7 %collective-permute-start.4 = (bf16[4,512,128]{2,1,0:T(8,128)(2,1)S(1)}, bf16[4,512,128]{2,1,0:T(8,128)(2,1)S(1)}, u32[]{:S(2)}, u32[]{:S(2)}) collective-permute-start(bf16[4,512,128]{2,1,0:T(8,128)(2,1)S(1)} %collective-permute-done.2), channel_id=1, source_target_pairs={{0,128},{128,1},{1,129},{129,2},{2,130},{130,3},{3,131},{131,0},{1... | collective-permute-start | bytes 1572872 | tf_op jit(solution)/shard_map/ring/ppermute | solution.py:214
  36.0 11.2 %collective-permute-start.3 = (bf16[4,512,128]{2,1,0:T(8,128)(2,1)S(1)}, bf16[4,512,128]{2,1,0:T(8,128)(2,1)S(1)}, u32[]{:S(2)}, u32[]{:S(2)}) collective-permute-start(bf16[4,512,128]{2,1,0:T(8,128)(2,1)S(1)} %collective-permute-done.refs_3_), channel_id=1, source_target_pairs={{0,128},{128,1},{1,129},{129,2},{2,130},{130,3},{3,131},{131,0},{1... | collective-permute-start | bytes 1572872 | tf_op jit(solution)/shard_map/ring/ppermute | solution.py:214
  41.6 11.2 %collective-permute-start.6 = (bf16[4,512,128]{2,1,0:T(8,128)(2,1)S(1)}, bf16[4,512,128]{2,1,0:T(8,128)(2,1)S(1)}, u32[]{:S(2)}, u32[]{:S(2)}) collective-permute-start(bf16[4,512,128]{2,1,0:T(8,128)(2,1)S(1)} %collective-permute-done.4.refs_4_), channel_id=1, source_target_pairs={{0,128},{128,1},{1,129},{129,2},{2,130},{130,3},{3,131},{131,0},{1... | collective-permute-start | bytes 1572872 | tf_op jit(solution)/shard_map/ring/ppermute | solution.py:214
  47.2 13.1 %collective-permute-start.5 = (bf16[4,512,128]{2,1,0:T(8,128)(2,1)S(1)}, bf16[4,512,128]{2,1,0:T(8,128)(2,1)S(1)}, u32[]{:S(2)}, u32[]{:S(2)}) collective-permute-start(bf16[4,512,128]{2,1,0:T(8,128)(2,1)S(1)} %collective-permute-done.3.refs_3_), channel_id=1, source_target_pairs={{0,128},{128,1},{1,129},{129,2},{2,130},{130,3},{3,131},{131,0},{1... | collective-permute-start | bytes 1572872 | tf_op jit(solution)/shard_map/ring/ppermute | solution.py:214
  52.8 11.2 %collective-permute-start.9 = (bf16[4,512,128]{2,1,0:T(8,128)(2,1)S(1)}, bf16[4,512,128]{2,1,0:T(8,128)(2,1)S(1)}, u32[]{:S(2)}, u32[]{:S(2)}) collective-permute-start(bf16[4,512,128]{2,1,0:T(8,128)(2,1)S(1)} %collective-permute-done.6.refs_4_), channel_id=1, source_target_pairs={{0,128},{128,1},{1,129},{129,2},{2,130},{130,3},{3,131},{131,0},{1... | collective-permute-start | bytes 1572872 | tf_op jit(solution)/shard_map/ring/ppermute | solution.py:214
  60.4 6.5 %collective-permute-start.8 = (bf16[2,512,128]{2,1,0:T(8,128)(2,1)S(1)}, bf16[2,512,128]{2,1,0:T(8,128)(2,1)S(1)}, u32[]{:S(2)}, u32[]{:S(2)}) collective-permute-start(bf16[2,512,128]{2,1,0:T(8,128)(2,1)S(1)} %get-tuple-element.45), channel_id=1, source_target_pairs={{0,128},{128,1},{1,129},{129,2},{2,130},{130,3},{3,131},{131,0},{1... | collective-permute-start | bytes 786440 | tf_op jit(solution)/shard_map/ring/ppermute | solution.py:214
  61.7 8.0 %collective-permute-start.7 = (bf16[2,512,128]{2,1,0:T(8,128)(2,1)S(1)}, bf16[2,512,128]{2,1,0:T(8,128)(2,1)S(1)}, u32[]{:S(2)}, u32[]{:S(2)}) collective-permute-start(bf16[2,512,128]{2,1,0:T(8,128)(2,1)S(1)} %get-tuple-element.46), channel_id=1, source_target_pairs={{0,128},{128,1},{1,129},{129,2},{2,130},{130,3},{3,131},{131,0},{1... | collective-permute-start | bytes 786440 | tf_op jit(solution)/shard_map/ring/ppermute | solution.py:214
  69.7 4.1 %collective-permute-start.10 = (f32[2,144,256]{2,1,0:T(8,128)S(1)}, f32[2,144,256]{2,1,0:T(8,128)S(1)}, u32[]{:S(2)}, u32[]{:S(2)}) collective-permute-start(f32[2,144,256]{2,1,0:T(8,128)S(1)} %slice.12), channel_id=1, source_target_pairs={{0,16},{16,0},{1,17},{17,1},{2,18},{18,2},{3,19},{19,3},{4,20},{20... | collective-permute-start | bytes 884744 | tf_op jit(solution)/shard_map/swap_terms/ppermute | solution.py:217
  72.5 1.7 %collective-permute-start.11 = (f32[2,144,256]{2,1,0:T(8,128)S(1)}, f32[2,144,256]{2,1,0:T(8,128)S(1)}, u32[]{:S(2)}, u32[]{:S(2)}) collective-permute-start(f32[2,144,256]{2,1,0:T(8,128)S(1)} %attend.15), channel_id=1, source_target_pairs={{0,16},{16,0},{1,17},{17,1},{2,18},{18,2},{3,19},{19,3},{4,20},{20... | collective-permute-start | bytes 884744 | tf_op jit(solution)/shard_map/swap_terms/ppermute | solution.py:217

commit v13 on v9

--- a/solution.py
+++ b/solution.py
@@ -188,16 +188,6 @@
         parts = call(pack, jax.ShapeDtypeStruct((heads, 3 * SLICE, HD), bf16), [vmem])(qkv[:, 0])
     with jax.named_scope("tokens_to_heads"):
         parts = lax.all_to_all(parts, ("y", "x"), 0, 0, tiled=True)
-    with jax.named_scope("split"):
-        own, pairs = call(
-            split,
-            [
-                jax.ShapeDtypeStruct((4, ROWS, HD), bf16),
-                jax.ShapeDtypeStruct((4, 2 * ROWS, HD), bf16),
-            ],
-            [vmem],
-        )(parts)
-
     chips = 8
     place = [z % 2 * 8 + z // 2 for z in range(chips)]
     route = [(place[z], place[(z + 1) % chips]) for z in range(chips)]
@@ -210,12 +200,22 @@
     def swap(block):
         return lax.ppermute(block, "core", [(0, 1), (1, 0)])
 
+    def divide(parts):
+        with jax.named_scope("split"):
+            return call(
+                split,
+                [
+                    jax.ShapeDtypeStruct((4, ROWS, HD), bf16),
+                    jax.ShapeDtypeStruct((4, 2 * ROWS, HD), bf16),
+                ],
+                [vmem],
+            )(parts)
+
+    with jax.named_scope("swap_parts"):
+        other_parts = swap(parts)
+    own, pairs = divide(parts)
     first_chain = hop(pairs)
-    with jax.named_scope("swap_queries"):
-        other = swap(own)
-    with jax.named_scope("swap_pairs"):
-        second = swap(pairs)
-    other, second = lax.optimization_barrier((other, second))
+    other, second = divide(other_parts)
     second_chain = hop(second)
 
     def step(arrivals, distance, state, half=None):

time: 87.2 us -> 86.7 us (level)
    ppermute x3 -> x2, starting transfers between devices: 3.79 us -> 3.2 us  [swap(): return lax.ppermute(block, 'core', [(0, 1), (1, 0)])]
  transfers between devices with their start and end apart: 10 -> 9, of which waited for: 6 -> 6; matrix products, arithmetic and copies ran while one was open for 0% -> 0% of each run, Pallas kernels for 11% -> 12%
where the time goes in v13:
time: 86.7 us; the launch traced here: 86.5 us
  blocking collectives  31.6 us (36%)
  starting transfers between devices  25 us (29%)
  waiting for transfers between devices  15.3 us (18%)
  Pallas kernels  13.3 us (15%)
  local copies, waits for them, and re-layouts  1.14 us (1%)
    ppermute x7, starting transfers between devices, hop(): return lax.ppermute(block, RING, route)  21.8 us
    all_to_all x1, blocking collectives, shards(): parts = lax.all_to_all(parts, ('y', 'x'), 0, 0, tiled=True)  20.9 us
    ppermute x7, waiting for transfers between devices, hop(): return lax.ppermute(block, RING, route)  15.3 us
    pallas_call x6, Pallas kernels, step(): call(functools.partial(attend, distance, first, half), jax.ShapeDtypeStru...  11.5 us
    all_to_all x1, blocking collectives, shards(): attended = lax.all_to_all(attended, ('y', 'x'), 0, 0, tiled=True)  10.8 us
    ppermute x2, starting transfers between devices, swap(): return lax.ppermute(block, 'core', [(0, 1), (1, 0)])  3.2 us
  transfers between devices with their start and end apart: 9, of which 6 were waited for; matrix products, arithmetic and copies ran while one was open for 0% of the time, Pallas kernels for 12%

profile of v13, /device:TPU:1, one launch (start us, length us, event | category | flops | bytes accessed | tf_op | source)
XLA Modules:
  0.0 86.5 jit_solution(13496037834847606086)
XLA Ops:
  0.0 0.0 copy-start
  0.0 1.1 %copy-done = bf16[3,1,64,2048]{3,2,1,0:T(8,128)(2,1)S(1)} copy-done((bf16[3,1,64,2048]{3,2,1,0:T(8,128)(2,1)S(1)}, bf16[3,1,64,2048]{3,2,1,0:T(8,128)(2,1)}, u32[]{:S(2)}) %copy-start) | copy-done | bytes 786456
  1.1 0.1 pack.1
  1.3 20.9 %all_to_all.10.parts_ref = bf16[16,192,128]{2,1,0:T(8,128)(2,1)S(1)} all-to-all(bf16[16,192,128]{2,1,0:T(8,128)(2,1)S(1)} %pack.1), channel_id=1, replica_groups=mesh['zlo'=2,'y'=4,'core'=2,'x'=4,'zhi'=4] {'y','x'}, dimensions={0} | all-to-all | bytes 1572864 | tf_op jit(solution)/shard_map/tokens_to_heads/all_to_all | solution.py:190
  22.2 0.0 copy-start.1
  22.2 1.8 %collective-permute-start = (bf16[16,192,128]{2,1,0:T(8,128)(2,1)S(1)}, bf16[16,192,128]{2,1,0:T(8,128)(2,1)S(1)}, u32[]{:S(2)}, u32[]{:S(2)}) collective-permute-start(bf16[16,192,128]{2,1,0:T(8,128)(2,1)S(1)} %all_to_all.10.parts_ref), channel_id=1, source_target_pairs={{0,16},{16,0},{1,17},{17,1},{2,18},{18,2},{3,19},{19,3},{4,20},{20... | collective-permute-start | bytes 2359304 | tf_op jit(solution)/shard_map/swap_parts/ppermute | solution.py:201
  24.0 0.1 split.2
  24.1 5.7 %collective-permute-start.1 = (bf16[4,512,128]{2,1,0:T(8,128)(2,1)S(1)}, bf16[4,512,128]{2,1,0:T(8,128)(2,1)S(1)}, u32[]{:S(2)}, u32[]{:S(2)}) collective-permute-start(bf16[4,512,128]{2,1,0:T(8,128)(2,1)S(1)} %get-tuple-element.23.refs_3_), channel_id=1, source_target_pairs={{0,128},{128,1},{1,129},{129,2},{2,130},{130,3},{3,131},{131,0},{1... | collective-permute-start | bytes 1572872 | tf_op jit(solution)/shard_map/ring/ppermute | solution.py:198
  29.7 0.0 collective-permute-done.parts_ref
  29.7 0.1 split.3
  29.9 1.8 %collective-permute-start.3 = (bf16[4,512,128]{2,1,0:T(8,128)(2,1)S(1)}, bf16[4,512,128]{2,1,0:T(8,128)(2,1)S(1)}, u32[]{:S(2)}, u32[]{:S(2)}) collective-permute-start(bf16[4,512,128]{2,1,0:T(8,128)(2,1)S(1)} %get-tuple-element.25), channel_id=1, source_target_pairs={{0,128},{128,1},{1,129},{129,2},{2,130},{130,3},{3,131},{131,0},{1... | collective-permute-start | bytes 1572872 | tf_op jit(solution)/shard_map/ring/ppermute | solution.py:198
  31.7 0.0 copy-done.1
  31.7 2.4 %attend.6.refs_5_ = f32[4,144,512]{2,1,0:T(8,128)S(1)} custom-call(s32[16]{0:T(128)S(1)} %copy-done.1, bf16[4,256,128]{2,1,0:T(8,128)(2,1)S(1)} %get-tuple-element.21.refs_1_, bf16[4,256,128]{2,1,0:T(8,128)(2,1)S(1)} %get-tuple-element.22.refs_2_, bf16[4,512,128]{2,1,0:T(8,128)(2,1)S(1)} %get-tuple-element.23.refs_3_), custom_call_target="tpu_custom_call" | custom-call | flops 4294967296 | bytes 8388608 | tf_op jit(solution)/shard_map/attend/pallas_call | solution.py:227
  34.1 1.8 %collective-permute-done.1.refs_3_ = bf16[4,512,128]{2,1,0:T(8,128)(2,1)S(1)} collective-permute-done((bf16[4,512,128]{2,1,0:T(8,128)(2,1)S(1)}, bf16[4,512,128]{2,1,0:T(8,128)(2,1)S(1)}, u32[]{:S(2)}, u32[]{:S(2)}) %collective-permute-start.1) | collective-permute-done | bytes 524320 | tf_op jit(solution)/shard_map/ring/ppermute | solution.py:198
  35.9 3.1 %collective-permute-start.2 = (bf16[4,512,128]{2,1,0:T(8,128)(2,1)S(1)}, bf16[4,512,128]{2,1,0:T(8,128)(2,1)S(1)}, u32[]{:S(2)}, u32[]{:S(2)}) collective-permute-start(bf16[4,512,128]{2,1,0:T(8,128)(2,1)S(1)} %collective-permute-done.1.refs_3_), channel_id=1, source_target_pairs={{0,128},{128,1},{1,129},{129,2},{2,130},{130,3},{3,131},{131,0},{1... | collective-permute-start | bytes 1572872 | tf_op jit(solution)/shard_map/ring/ppermute | solution.py:198
  39.0 2.5 %collective-permute-done.3.refs_4_ = bf16[4,512,128]{2,1,0:T(8,128)(2,1)S(1)} collective-permute-done((bf16[4,512,128]{2,1,0:T(8,128)(2,1)S(1)}, bf16[4,512,128]{2,1,0:T(8,128)(2,1)S(1)}, u32[]{:S(2)}, u32[]{:S(2)}) %collective-permute-start.3) | collective-permute-done | bytes 524320 | tf_op jit(solution)/shard_map/ring/ppermute | solution.py:198
  41.5 3.1 %collective-permute-start.5 = (bf16[4,512,128]{2,1,0:T(8,128)(2,1)S(1)}, bf16[4,512,128]{2,1,0:T(8,128)(2,1)S(1)}, u32[]{:S(2)}, u32[]{:S(2)}) collective-permute-start(bf16[4,512,128]{2,1,0:T(8,128)(2,1)S(1)} %collective-permute-done.3.refs_4_), channel_id=1, source_target_pairs={{0,128},{128,1},{1,129},{129,2},{2,130},{130,3},{3,131},{131,0},{1... | collective-permute-start | bytes 1572872 | tf_op jit(solution)/shard_map/ring/ppermute | solution.py:198
  44.6 0.7 attend.7.refs_5_
  45.3 1.8 %collective-permute-done.2.refs_3_ = bf16[4,512,128]{2,1,0:T(8,128)(2,1)S(1)} collective-permute-done((bf16[4,512,128]{2,1,0:T(8,128)(2,1)S(1)}, bf16[4,512,128]{2,1,0:T(8,128)(2,1)S(1)}, u32[]{:S(2)}, u32[]{:S(2)}) %collective-permute-start.2) | collective-permute-done | bytes 524320 | tf_op jit(solution)/shard_map/ring/ppermute | solution.py:198
  47.1 3.8 %collective-permute-start.4 = (bf16[4,512,128]{2,1,0:T(8,128)(2,1)S(1)}, bf16[4,512,128]{2,1,0:T(8,128)(2,1)S(1)}, u32[]{:S(2)}, u32[]{:S(2)}) collective-permute-start(bf16[4,512,128]{2,1,0:T(8,128)(2,1)S(1)} %collective-permute-done.2.refs_3_), channel_id=1, source_target_pairs={{0,128},{128,1},{1,129},{129,2},{2,130},{130,3},{3,131},{131,0},{1... | collective-permute-start | bytes 1572872 | tf_op jit(solution)/shard_map/ring/ppermute | solution.py:198
  50.9 1.8 %collective-permute-done.5.refs_4_ = bf16[4,512,128]{2,1,0:T(8,128)(2,1)S(1)} collective-permute-done((bf16[4,512,128]{2,1,0:T(8,128)(2,1)S(1)}, bf16[4,512,128]{2,1,0:T(8,128)(2,1)S(1)}, u32[]{:S(2)}, u32[]{:S(2)}) %collective-permute-start.5) | collective-permute-done | bytes 524320 | tf_op jit(solution)/shard_map/ring/ppermute | solution.py:198
  52.7 3.1 %collective-permute-start.7 = (bf16[4,512,128]{2,1,0:T(8,128)(2,1)S(1)}, bf16[4,512,128]{2,1,0:T(8,128)(2,1)S(1)}, u32[]{:S(2)}, u32[]{:S(2)}) collective-permute-start(bf16[4,512,128]{2,1,0:T(8,128)(2,1)S(1)} %collective-permute-done.5.refs_4_), channel_id=1, source_target_pairs={{0,128},{128,1},{1,129},{129,2},{2,130},{130,3},{3,131},{131,0},{1... | collective-permute-start | bytes 1572872 | tf_op jit(solution)/shard_map/ring/ppermute | solution.py:198
  55.8 4.4 %attend.8.refs_5_ = f32[4,144,512]{2,1,0:T(8,128)S(1)} custom-call(s32[16]{0:T(128)S(1)} %copy-done.1, bf16[4,256,128]{2,1,0:T(8,128)(2,1)S(1)} %get-tuple-element.21.refs_1_, bf16[4,256,128]{2,1,0:T(8,128)(2,1)S(1)} %get-tuple-element.22.refs_2_, bf16[4,512,128]{2,1,0:T(8,128)(2,1)S(1)} %collective-permute-done.2.refs_3_, ...), custom_call_target="tpu_custom_call", output_to_operand_aliasing={{}: (5, {})} | custom-call | flops 8589934592 | bytes 8388608 | tf_op jit(solution)/shard_map/attend/pallas_call | solution.py:227
  60.2 0.0 collective-permute-done.4.refs_3_
  60.2 1.2 %collective-permute-start.6 = (bf16[4,512,128]{2,1,0:T(8,128)(2,1)S(1)}, bf16[4,512,128]{2,1,0:T(8,128)(2,1)S(1)}, u32[]{:S(2)}, u32[]{:S(2)}) collective-permute-start(bf16[4,512,128]{2,1,0:T(8,128)(2,1)S(1)} %collective-permute-done.4.refs_3_), channel_id=1, source_target_pairs={{0,128},{128,1},{1,129},{129,2},{2,130},{130,3},{3,131},{131,0},{1... | collective-permute-start | bytes 1572872 | tf_op jit(solution)/shard_map/ring/ppermute | solution.py:198
  61.5 2.5 %collective-permute-done.7.refs_4_ = bf16[4,512,128]{2,1,0:T(8,128)(2,1)S(1)} collective-permute-done((bf16[4,512,128]{2,1,0:T(8,128)(2,1)S(1)}, bf16[4,512,128]{2,1,0:T(8,128)(2,1)S(1)}, u32[]{:S(2)}, u32[]{:S(2)}) %collective-permute-start.7) | collective-permute-done | bytes 524320 | tf_op jit(solution)/shard_map/ring/ppermute | solution.py:198
  64.0 0.7 attend.9.refs_4_
  64.7 4.9 %collective-permute-done.6.refs_3_ = bf16[4,512,128]{2,1,0:T(8,128)(2,1)S(1)} collective-permute-done((bf16[4,512,128]{2,1,0:T(8,128)(2,1)S(1)}, bf16[4,512,128]{2,1,0:T(8,128)(2,1)S(1)}, u32[]{:S(2)}, u32[]{:S(2)}) %collective-permute-start.6) | collective-permute-done | bytes 524320 | tf_op jit(solution)/shard_map/ring/ppermute | solution.py:198
  69.6 1.6 %attend.11 = f32[4,144,256]{2,1,0:T(8,128)S(1)} custom-call(s32[16]{0:T(128)S(1)} %copy-done.1, bf16[4,256,128]{2,1,0:T(8,128)(2,1)S(1)} %get-tuple-element.21.refs_1_, bf16[4,256,128]{2,1,0:T(8,128)(2,1)S(1)} %get-tuple-element.22.refs_2_, bf16[4,512,128]{2,1,0:T(8,128)(2,1)S(1)} %collective-permute-done.6.refs_3_, f32[4,144,512]{2,1,0:T(8,128)S(1)} %attend.9.refs_4_), custom_call_target="tpu_custom_call" | custom-call | flops 2147483648 | bytes 8388608 | tf_op jit(solution)/shard_map/attend/pallas_call | solution.py:227
  71.2 1.4 %collective-permute-start.8 = (f32[4,144,256]{2,1,0:T(8,128)S(1)}, f32[4,144,256]{2,1,0:T(8,128)S(1)}, u32[]{:S(2)}, u32[]{:S(2)}) collective-permute-start(f32[4,144,256]{2,1,0:T(8,128)S(1)} %attend.11), channel_id=1, source_target_pairs={{0,16},{16,0},{1,17},{17,1},{2,18},{18,2},{3,19},{19,3},{4,20},{20... | collective-permute-start | bytes 1769480 | tf_op jit(solution)/shard_map/swap_terms/ppermute | solution.py:201
  72.6 1.6 %attend.10.own_ref = f32[4,144,256]{2,1,0:T(8,128)S(1)} custom-call(s32[16]{0:T(128)S(1)} %copy-done.1, bf16[4,256,128]{2,1,0:T(8,128)(2,1)S(1)} %get-tuple-element.21.refs_1_, bf16[4,256,128]{2,1,0:T(8,128)(2,1)S(1)} %get-tuple-element.22.refs_2_, bf16[4,512,128]{2,1,0:T(8,128)(2,1)S(1)} %collective-permute-done.6.refs_3_, f32[4,144,512]{2,1,0:T(8,128)S(1)} %attend.9.refs_4_), custom_call_target="tpu_custom_call" | custom-call | flops 2147483648 | bytes 8388608 | tf_op jit(solution)/shard_map/attend/pallas_call | solution.py:227
  74.3 0.0 collective-permute-done.8.other_ref
  74.3 0.7 join.1
  75.0 10.8 %all_to_all.11.parts_ref = bf16[16,64,128]{2,1,0:T(8,128)(2,1)S(1)} all-to-all(bf16[16,64,128]{2,1,0:T(8,128)(2,1)S(1)} %join.1), channel_id=1, replica_groups=mesh['zlo'=2,'y'=4,'core'=2,'x'=4,'zhi'=4] {'y','x'}, dimensions={0} | all-to-all | bytes 524288 | tf_op jit(solution)/shard_map/heads_to_tokens/all_to_all | solution.py:256
  85.8 0.8 unpack.1
Async XLA Ops:
  0.0 1.1 %copy-start = (bf16[3,1,64,2048]{3,2,1,0:T(8,128)(2,1)S(1)}, bf16[3,1,64,2048]{3,2,1,0:T(8,128)(2,1)}, u32[]{:S(2)}) copy-start(bf16[3,1,64,2048]{3,2,1,0:T(8,128)(2,1)} %param.2) | copy-start | bytes 2359300
  22.2 9.5 %copy-start.1 = (s32[16]{0:T(128)S(1)}, s32[16]{0:T(128)}, u32[]{:S(2)}) copy-start(s32[16]{0:T(128)} %lengths_ref.1) | copy-start | bytes 196
  22.2 7.6 %collective-permute-start = (bf16[16,192,128]{2,1,0:T(8,128)(2,1)S(1)}, bf16[16,192,128]{2,1,0:T(8,128)(2,1)S(1)}, u32[]{:S(2)}, u32[]{:S(2)}) collective-permute-start(bf16[16,192,128]{2,1,0:T(8,128)(2,1)S(1)} %all_to_all.10.parts_ref), channel_id=1, source_target_pairs={{0,16},{16,0},{1,17},{17,1},{2,18},{18,2},{3,19},{19,3},{4,20},{20... | collective-permute-start | bytes 2359304 | tf_op jit(solution)/shard_map/swap_parts/ppermute | solution.py:201
  24.1 11.8 %collective-permute-start.1 = (bf16[4,512,128]{2,1,0:T(8,128)(2,1)S(1)}, bf16[4,512,128]{2,1,0:T(8,128)(2,1)S(1)}, u32[]{:S(2)}, u32[]{:S(2)}) collective-permute-start(bf16[4,512,128]{2,1,0:T(8,128)(2,1)S(1)} %get-tuple-element.23.refs_3_), channel_id=1, source_target_pairs={{0,128},{128,1},{1,129},{129,2},{2,130},{130,3},{3,131},{131,0},{1... | collective-permute-start | bytes 1572872 | tf_op jit(solution)/shard_map/ring/ppermute | solution.py:198
  29.9 11.6 %collective-permute-start.3 = (bf16[4,512,128]{2,1,0:T(8,128)(2,1)S(1)}, bf16[4,512,128]{2,1,0:T(8,128)(2,1)S(1)}, u32[]{:S(2)}, u32[]{:S(2)}) collective-permute-start(bf16[4,512,128]{2,1,0:T(8,128)(2,1)S(1)} %get-tuple-element.25), channel_id=1, source_target_pairs={{0,128},{128,1},{1,129},{129,2},{2,130},{130,3},{3,131},{131,0},{1... | collective-permute-start | bytes 1572872 | tf_op jit(solution)/shard_map/ring/ppermute | solution.py:198
  35.9 11.2 %collective-permute-start.2 = (bf16[4,512,128]{2,1,0:T(8,128)(2,1)S(1)}, bf16[4,512,128]{2,1,0:T(8,128)(2,1)S(1)}, u32[]{:S(2)}, u32[]{:S(2)}) collective-permute-start(bf16[4,512,128]{2,1,0:T(8,128)(2,1)S(1)} %collective-permute-done.1.refs_3_), channel_id=1, source_target_pairs={{0,128},{128,1},{1,129},{129,2},{2,130},{130,3},{3,131},{131,0},{1... | collective-permute-start | bytes 1572872 | tf_op jit(solution)/shard_map/ring/ppermute | solution.py:198
  41.5 11.2 %collective-permute-start.5 = (bf16[4,512,128]{2,1,0:T(8,128)(2,1)S(1)}, bf16[4,512,128]{2,1,0:T(8,128)(2,1)S(1)}, u32[]{:S(2)}, u32[]{:S(2)}) collective-permute-start(bf16[4,512,128]{2,1,0:T(8,128)(2,1)S(1)} %collective-permute-done.3.refs_4_), channel_id=1, source_target_pairs={{0,128},{128,1},{1,129},{129,2},{2,130},{130,3},{3,131},{131,0},{1... | collective-permute-start | bytes 1572872 | tf_op jit(solution)/shard_map/ring/ppermute | solution.py:198
  47.1 13.1 %collective-permute-start.4 = (bf16[4,512,128]{2,1,0:T(8,128)(2,1)S(1)}, bf16[4,512,128]{2,1,0:T(8,128)(2,1)S(1)}, u32[]{:S(2)}, u32[]{:S(2)}) collective-permute-start(bf16[4,512,128]{2,1,0:T(8,128)(2,1)S(1)} %collective-permute-done.2.refs_3_), channel_id=1, source_target_pairs={{0,128},{128,1},{1,129},{129,2},{2,130},{130,3},{3,131},{131,0},{1... | collective-permute-start | bytes 1572872 | tf_op jit(solution)/shard_map/ring/ppermute | solution.py:198
  52.7 11.2 %collective-permute-start.7 = (bf16[4,512,128]{2,1,0:T(8,128)(2,1)S(1)}, bf16[4,512,128]{2,1,0:T(8,128)(2,1)S(1)}, u32[]{:S(2)}, u32[]{:S(2)}) collective-permute-start(bf16[4,512,128]{2,1,0:T(8,128)(2,1)S(1)} %collective-permute-done.5.refs_4_), channel_id=1, source_target_pairs={{0,128},{128,1},{1,129},{129,2},{2,130},{130,3},{3,131},{131,0},{1... | collective-permute-start | bytes 1572872 | tf_op jit(solution)/shard_map/ring/ppermute | solution.py:198
  60.2 9.4 %collective-permute-start.6 = (bf16[4,512,128]{2,1,0:T(8,128)(2,1)S(1)}, bf16[4,512,128]{2,1,0:T(8,128)(2,1)S(1)}, u32[]{:S(2)}, u32[]{:S(2)}) collective-permute-start(bf16[4,512,128]{2,1,0:T(8,128)(2,1)S(1)} %collective-permute-done.4.refs_3_), channel_id=1, source_target_pairs={{0,128},{128,1},{1,129},{129,2},{2,130},{130,3},{3,131},{131,0},{1... | collective-permute-start | bytes 1572872 | tf_op jit(solution)/shard_map/ring/ppermute | solution.py:198
  71.2 3.1 %collective-permute-start.8 = (f32[4,144,256]{2,1,0:T(8,128)S(1)}, f32[4,144,256]{2,1,0:T(8,128)S(1)}, u32[]{:S(2)}, u32[]{:S(2)}) collective-permute-start(f32[4,144,256]{2,1,0:T(8,128)S(1)} %attend.11), channel_id=1, source_target_pairs={{0,16},{16,0},{1,17},{17,1},{2,18},{18,2},{3,19},{19,3},{4,20},{20... | collective-permute-start | bytes 1769480 | tf_op jit(solution)/shard_map/swap_terms/ppermute | solution.py:201

commit v14 on v10

--- a/solution.py
+++ b/solution.py
@@ -190,16 +190,6 @@
         parts = call(pack, jax.ShapeDtypeStruct((heads, 3 * SLICE, HD), bf16), [vmem])(qkv[:, 0])
     with jax.named_scope("tokens_to_heads"):
         parts = lax.all_to_all(parts, ("y", "x"), 0, 0, tiled=True)
-    with jax.named_scope("split"):
-        own, pairs = call(
-            split,
-            [
-                jax.ShapeDtypeStruct((4, ROWS, HD), bf16),
-                jax.ShapeDtypeStruct((4, 2 * ROWS, HD), bf16),
-            ],
-            [vmem],
-        )(parts)
-
     chips = 8
     place = [z % 2 * 8 + z // 2 for z in range(chips)]
     route = [(place[z], place[(z + 1) % chips]) for z in range(chips)]
@@ -212,12 +202,22 @@
     def swap(block):
         return lax.ppermute(block, "core", [(0, 1), (1, 0)])
 
+    def divide(parts):
+        with jax.named_scope("split"):
+            return call(
+                split,
+                [
+                    jax.ShapeDtypeStruct((4, ROWS, HD), bf16),
+                    jax.ShapeDtypeStruct((4, 2 * ROWS, HD), bf16),
+                ],
+                [vmem],
+            )(parts)
+
+    with jax.named_scope("swap_parts"):
+        other_parts = swap(parts)
+    own, pairs = divide(parts)
     first_chain = hop(pairs)
-    with jax.named_scope("swap_queries"):
-        other = swap(own)
-    with jax.named_scope("swap_pairs"):
-        second = swap(pairs)
-    other, second = lax.optimization_barrier((other, second))
+    other, second = divide(other_parts)
     second_chain = hop(second)
 
     def step(arrivals, distance, state, half=None, chains=(0, 1)):

time: 87.2 us -> 86.7 us (level)
    ppermute x3 -> x2, starting transfers between devices: 3.79 us -> 3.2 us  [swap(): return lax.ppermute(block, 'core', [(0, 1), (1, 0)])]
  transfers between devices with their start and end apart: 10 -> 9, of which waited for: 6 -> 6; matrix products, arithmetic and copies ran while one was open for 0% -> 0% of each run, Pallas kernels for 12% -> 12%
where the time goes in v14:
time: 86.7 us; the launch traced here: 86.5 us
  blocking collectives  31.6 us (36%)
  starting transfers between devices  25 us (29%)
  waiting for transfers between devices  14.6 us (17%)
  Pallas kernels  14 us (16%)
  local copies, waits for them, and re-layouts  1.14 us (1%)
    ppermute x7, starting transfers between devices, hop(): return lax.ppermute(block, RING, route)  21.8 us
    all_to_all x1, blocking collectives, shards(): parts = lax.all_to_all(parts, ('y', 'x'), 0, 0, tiled=True)  20.9 us
    ppermute x7, waiting for transfers between devices, hop(): return lax.ppermute(block, RING, route)  14.6 us
    pallas_call x7, Pallas kernels, step(): call(functools.partial(attend, distance, chains[:len(arrivals)], first, h...  12.2 us
    all_to_all x1, blocking collectives, shards(): attended = lax.all_to_all(attended, ('y', 'x'), 0, 0, tiled=True)  10.8 us
    ppermute x2, starting transfers between devices, swap(): return lax.ppermute(block, 'core', [(0, 1), (1, 0)])  3.2 us
  transfers between devices with their start and end apart: 9, of which 6 were waited for; matrix products, arithmetic and copies ran while one was open for 0% of the time, Pallas kernels for 12%

profile of v14, /device:TPU:1, one launch (start us, length us, event | category | flops | bytes accessed | tf_op | source)
XLA Modules:
  0.0 86.5 jit_solution(9659316351809354272)
XLA Ops:
  0.0 0.0 copy-start
  0.0 1.1 %copy-done = bf16[3,1,64,2048]{3,2,1,0:T(8,128)(2,1)S(1)} copy-done((bf16[3,1,64,2048]{3,2,1,0:T(8,128)(2,1)S(1)}, bf16[3,1,64,2048]{3,2,1,0:T(8,128)(2,1)}, u32[]{:S(2)}) %copy-start) | copy-done | bytes 786456
  1.1 0.1 pack.1
  1.3 20.9 %all_to_all.10.parts_ref = bf16[16,192,128]{2,1,0:T(8,128)(2,1)S(1)} all-to-all(bf16[16,192,128]{2,1,0:T(8,128)(2,1)S(1)} %pack.1), channel_id=1, replica_groups=mesh['zlo'=2,'y'=4,'core'=2,'x'=4,'zhi'=4] {'y','x'}, dimensions={0} | all-to-all | bytes 1572864 | tf_op jit(solution)/shard_map/tokens_to_heads/all_to_all | solution.py:192
  22.2 0.0 copy-start.1
  22.2 1.8 %collective-permute-start = (bf16[16,192,128]{2,1,0:T(8,128)(2,1)S(1)}, bf16[16,192,128]{2,1,0:T(8,128)(2,1)S(1)}, u32[]{:S(2)}, u32[]{:S(2)}) collective-permute-start(bf16[16,192,128]{2,1,0:T(8,128)(2,1)S(1)} %all_to_all.10.parts_ref), channel_id=1, source_target_pairs={{0,16},{16,0},{1,17},{17,1},{2,18},{18,2},{3,19},{19,3},{4,20},{20... | collective-permute-start | bytes 2359304 | tf_op jit(solution)/shard_map/swap_parts/ppermute | solution.py:203
  24.0 0.1 split.2
  24.1 5.7 %collective-permute-start.1 = (bf16[4,512,128]{2,1,0:T(8,128)(2,1)S(1)}, bf16[4,512,128]{2,1,0:T(8,128)(2,1)S(1)}, u32[]{:S(2)}, u32[]{:S(2)}) collective-permute-start(bf16[4,512,128]{2,1,0:T(8,128)(2,1)S(1)} %get-tuple-element.23.refs_3_), channel_id=1, source_target_pairs={{0,128},{128,1},{1,129},{129,2},{2,130},{130,3},{3,131},{131,0},{1... | collective-permute-start | bytes 1572872 | tf_op jit(solution)/shard_map/ring/ppermute | solution.py:200
  29.7 0.0 collective-permute-done.parts_ref
  29.7 0.1 split.3
  29.9 1.8 %collective-permute-start.3 = (bf16[4,512,128]{2,1,0:T(8,128)(2,1)S(1)}, bf16[4,512,128]{2,1,0:T(8,128)(2,1)S(1)}, u32[]{:S(2)}, u32[]{:S(2)}) collective-permute-start(bf16[4,512,128]{2,1,0:T(8,128)(2,1)S(1)} %get-tuple-element.25), channel_id=1, source_target_pairs={{0,128},{128,1},{1,129},{129,2},{2,130},{130,3},{3,131},{131,0},{1... | collective-permute-start | bytes 1572872 | tf_op jit(solution)/shard_map/ring/ppermute | solution.py:200
  31.7 0.0 copy-done.1
  31.7 2.4 %attend.7.refs_5_ = f32[4,144,512]{2,1,0:T(8,128)S(1)} custom-call(s32[16]{0:T(128)S(1)} %copy-done.1, bf16[4,256,128]{2,1,0:T(8,128)(2,1)S(1)} %get-tuple-element.21.refs_1_, bf16[4,256,128]{2,1,0:T(8,128)(2,1)S(1)} %get-tuple-element.22.refs_2_, bf16[4,512,128]{2,1,0:T(8,128)(2,1)S(1)} %get-tuple-element.23.refs_3_), custom_call_target="tpu_custom_call" | custom-call | flops 4294967296 | bytes 8388608 | tf_op jit(solution)/shard_map/attend/pallas_call | solution.py:229
  34.1 1.8 %collective-permute-done.1.refs_3_ = bf16[4,512,128]{2,1,0:T(8,128)(2,1)S(1)} collective-permute-done((bf16[4,512,128]{2,1,0:T(8,128)(2,1)S(1)}, bf16[4,512,128]{2,1,0:T(8,128)(2,1)S(1)}, u32[]{:S(2)}, u32[]{:S(2)}) %collective-permute-start.1) | collective-permute-done | bytes 524320 | tf_op jit(solution)/shard_map/ring/ppermute | solution.py:200
  35.9 3.1 %collective-permute-start.2 = (bf16[4,512,128]{2,1,0:T(8,128)(2,1)S(1)}, bf16[4,512,128]{2,1,0:T(8,128)(2,1)S(1)}, u32[]{:S(2)}, u32[]{:S(2)}) collective-permute-start(bf16[4,512,128]{2,1,0:T(8,128)(2,1)S(1)} %collective-permute-done.1.refs_3_), channel_id=1, source_target_pairs={{0,128},{128,1},{1,129},{129,2},{2,130},{130,3},{3,131},{131,0},{1... | collective-permute-start | bytes 1572872 | tf_op jit(solution)/shard_map/ring/ppermute | solution.py:200
  39.0 2.5 %collective-permute-done.3.refs_4_ = bf16[4,512,128]{2,1,0:T(8,128)(2,1)S(1)} collective-permute-done((bf16[4,512,128]{2,1,0:T(8,128)(2,1)S(1)}, bf16[4,512,128]{2,1,0:T(8,128)(2,1)S(1)}, u32[]{:S(2)}, u32[]{:S(2)}) %collective-permute-start.3) | collective-permute-done | bytes 524320 | tf_op jit(solution)/shard_map/ring/ppermute | solution.py:200
  41.5 3.1 %collective-permute-start.5 = (bf16[4,512,128]{2,1,0:T(8,128)(2,1)S(1)}, bf16[4,512,128]{2,1,0:T(8,128)(2,1)S(1)}, u32[]{:S(2)}, u32[]{:S(2)}) collective-permute-start(bf16[4,512,128]{2,1,0:T(8,128)(2,1)S(1)} %collective-permute-done.3.refs_4_), channel_id=1, source_target_pairs={{0,128},{128,1},{1,129},{129,2},{2,130},{130,3},{3,131},{131,0},{1... | collective-permute-start | bytes 1572872 | tf_op jit(solution)/shard_map/ring/ppermute | solution.py:200
  44.6 0.7 attend.8.refs_5_
  45.3 1.8 %collective-permute-done.2.refs_3_ = bf16[4,512,128]{2,1,0:T(8,128)(2,1)S(1)} collective-permute-done((bf16[4,512,128]{2,1,0:T(8,128)(2,1)S(1)}, bf16[4,512,128]{2,1,0:T(8,128)(2,1)S(1)}, u32[]{:S(2)}, u32[]{:S(2)}) %collective-permute-start.2) | collective-permute-done | bytes 524320 | tf_op jit(solution)/shard_map/ring/ppermute | solution.py:200
  47.1 3.8 %collective-permute-start.4 = (bf16[4,512,128]{2,1,0:T(8,128)(2,1)S(1)}, bf16[4,512,128]{2,1,0:T(8,128)(2,1)S(1)}, u32[]{:S(2)}, u32[]{:S(2)}) collective-permute-start(bf16[4,512,128]{2,1,0:T(8,128)(2,1)S(1)} %collective-permute-done.2.refs_3_), channel_id=1, source_target_pairs={{0,128},{128,1},{1,129},{129,2},{2,130},{130,3},{3,131},{131,0},{1... | collective-permute-start | bytes 1572872 | tf_op jit(solution)/shard_map/ring/ppermute | solution.py:200
  50.9 1.8 %collective-permute-done.5.refs_4_ = bf16[4,512,128]{2,1,0:T(8,128)(2,1)S(1)} collective-permute-done((bf16[4,512,128]{2,1,0:T(8,128)(2,1)S(1)}, bf16[4,512,128]{2,1,0:T(8,128)(2,1)S(1)}, u32[]{:S(2)}, u32[]{:S(2)}) %collective-permute-start.5) | collective-permute-done | bytes 524320 | tf_op jit(solution)/shard_map/ring/ppermute | solution.py:200
  52.7 3.1 %collective-permute-start.7 = (bf16[4,512,128]{2,1,0:T(8,128)(2,1)S(1)}, bf16[4,512,128]{2,1,0:T(8,128)(2,1)S(1)}, u32[]{:S(2)}, u32[]{:S(2)}) collective-permute-start(bf16[4,512,128]{2,1,0:T(8,128)(2,1)S(1)} %collective-permute-done.5.refs_4_), channel_id=1, source_target_pairs={{0,128},{128,1},{1,129},{129,2},{2,130},{130,3},{3,131},{131,0},{1... | collective-permute-start | bytes 1572872 | tf_op jit(solution)/shard_map/ring/ppermute | solution.py:200
  55.8 4.3 %attend.9.refs_4_ = f32[4,144,512]{2,1,0:T(8,128)S(1)} custom-call(s32[16]{0:T(128)S(1)} %copy-done.1, bf16[4,256,128]{2,1,0:T(8,128)(2,1)S(1)} %get-tuple-element.21.refs_1_, bf16[4,256,128]{2,1,0:T(8,128)(2,1)S(1)} %get-tuple-element.22.refs_2_, bf16[4,512,128]{2,1,0:T(8,128)(2,1)S(1)} %collective-permute-done.2.refs_3_, ...), custom_call_target="tpu_custom_call", output_to_operand_aliasing={{}: (5, {})} | custom-call | flops 8589934592 | bytes 8388608 | tf_op jit(solution)/shard_map/attend/pallas_call | solution.py:229
  60.2 0.0 collective-permute-done.4.refs_3_
  60.2 1.3 %collective-permute-start.6 = (bf16[4,512,128]{2,1,0:T(8,128)(2,1)S(1)}, bf16[4,512,128]{2,1,0:T(8,128)(2,1)S(1)}, u32[]{:S(2)}, u32[]{:S(2)}) collective-permute-start(bf16[4,512,128]{2,1,0:T(8,128)(2,1)S(1)} %collective-permute-done.4.refs_3_), channel_id=1, source_target_pairs={{0,128},{128,1},{1,129},{129,2},{2,130},{130,3},{3,131},{131,0},{1... | collective-permute-start | bytes 1572872 | tf_op jit(solution)/shard_map/ring/ppermute | solution.py:200
  61.5 0.7 attend.10.refs_4_
  62.2 1.8 %collective-permute-done.7.refs_3_ = bf16[4,512,128]{2,1,0:T(8,128)(2,1)S(1)} collective-permute-done((bf16[4,512,128]{2,1,0:T(8,128)(2,1)S(1)}, bf16[4,512,128]{2,1,0:T(8,128)(2,1)S(1)}, u32[]{:S(2)}, u32[]{:S(2)}) %collective-permute-start.7) | collective-permute-done | bytes 524320 | tf_op jit(solution)/shard_map/ring/ppermute | solution.py:200
  64.0 0.7 attend.11.refs_4_
  64.7 4.9 %collective-permute-done.6.refs_3_ = bf16[4,512,128]{2,1,0:T(8,128)(2,1)S(1)} collective-permute-done((bf16[4,512,128]{2,1,0:T(8,128)(2,1)S(1)}, bf16[4,512,128]{2,1,0:T(8,128)(2,1)S(1)}, u32[]{:S(2)}, u32[]{:S(2)}) %collective-permute-start.6) | collective-permute-done | bytes 524320 | tf_op jit(solution)/shard_map/ring/ppermute | solution.py:200
  69.6 1.6 %attend.13 = f32[4,144,256]{2,1,0:T(8,128)S(1)} custom-call(s32[16]{0:T(128)S(1)} %copy-done.1, bf16[4,256,128]{2,1,0:T(8,128)(2,1)S(1)} %get-tuple-element.21.refs_1_, bf16[4,256,128]{2,1,0:T(8,128)(2,1)S(1)} %get-tuple-element.22.refs_2_, bf16[4,512,128]{2,1,0:T(8,128)(2,1)S(1)} %collective-permute-done.6.refs_3_, f32[4,144,512]{2,1,0:T(8,128)S(1)} %attend.11.refs_4_), custom_call_target="tpu_custom_call" | custom-call | flops 2147483648 | bytes 8388608 | tf_op jit(solution)/shard_map/attend/pallas_call | solution.py:229
  71.2 1.4 %collective-permute-start.8 = (f32[4,144,256]{2,1,0:T(8,128)S(1)}, f32[4,144,256]{2,1,0:T(8,128)S(1)}, u32[]{:S(2)}, u32[]{:S(2)}) collective-permute-start(f32[4,144,256]{2,1,0:T(8,128)S(1)} %attend.13), channel_id=1, source_target_pairs={{0,16},{16,0},{1,17},{17,1},{2,18},{18,2},{3,19},{19,3},{4,20},{20... | collective-permute-start | bytes 1769480 | tf_op jit(solution)/shard_map/swap_terms/ppermute | solution.py:203
  72.6 1.6 %attend.12.own_ref = f32[4,144,256]{2,1,0:T(8,128)S(1)} custom-call(s32[16]{0:T(128)S(1)} %copy-done.1, bf16[4,256,128]{2,1,0:T(8,128)(2,1)S(1)} %get-tuple-element.21.refs_1_, bf16[4,256,128]{2,1,0:T(8,128)(2,1)S(1)} %get-tuple-element.22.refs_2_, bf16[4,512,128]{2,1,0:T(8,128)(2,1)S(1)} %collective-permute-done.6.refs_3_, f32[4,144,512]{2,1,0:T(8,128)S(1)} %attend.11.refs_4_), custom_call_target="tpu_custom_call" | custom-call | flops 2147483648 | bytes 8388608 | tf_op jit(solution)/shard_map/attend/pallas_call | solution.py:229
  74.3 0.0 collective-permute-done.8.other_ref
  74.3 0.7 join.1
  75.0 10.8 %all_to_all.11.parts_ref = bf16[16,64,128]{2,1,0:T(8,128)(2,1)S(1)} all-to-all(bf16[16,64,128]{2,1,0:T(8,128)(2,1)S(1)} %join.1), channel_id=1, replica_groups=mesh['zlo'=2,'y'=4,'core'=2,'x'=4,'zhi'=4] {'y','x'}, dimensions={0} | all-to-all | bytes 524288 | tf_op jit(solution)/shard_map/heads_to_tokens/all_to_all | solution.py:264
  85.8 0.8 unpack.1
Async XLA Ops:
  0.0 1.1 %copy-start = (bf16[3,1,64,2048]{3,2,1,0:T(8,128)(2,1)S(1)}, bf16[3,1,64,2048]{3,2,1,0:T(8,128)(2,1)}, u32[]{:S(2)}) copy-start(bf16[3,1,64,2048]{3,2,1,0:T(8,128)(2,1)} %param.2) | copy-start | bytes 2359300
  22.2 9.5 %copy-start.1 = (s32[16]{0:T(128)S(1)}, s32[16]{0:T(128)}, u32[]{:S(2)}) copy-start(s32[16]{0:T(128)} %lengths_ref.1) | copy-start | bytes 196
  22.2 7.6 %collective-permute-start = (bf16[16,192,128]{2,1,0:T(8,128)(2,1)S(1)}, bf16[16,192,128]{2,1,0:T(8,128)(2,1)S(1)}, u32[]{:S(2)}, u32[]{:S(2)}) collective-permute-start(bf16[16,192,128]{2,1,0:T(8,128)(2,1)S(1)} %all_to_all.10.parts_ref), channel_id=1, source_target_pairs={{0,16},{16,0},{1,17},{17,1},{2,18},{18,2},{3,19},{19,3},{4,20},{20... | collective-permute-start | bytes 2359304 | tf_op jit(solution)/shard_map/swap_parts/ppermute | solution.py:203
  24.1 11.8 %collective-permute-start.1 = (bf16[4,512,128]{2,1,0:T(8,128)(2,1)S(1)}, bf16[4,512,128]{2,1,0:T(8,128)(2,1)S(1)}, u32[]{:S(2)}, u32[]{:S(2)}) collective-permute-start(bf16[4,512,128]{2,1,0:T(8,128)(2,1)S(1)} %get-tuple-element.23.refs_3_), channel_id=1, source_target_pairs={{0,128},{128,1},{1,129},{129,2},{2,130},{130,3},{3,131},{131,0},{1... | collective-permute-start | bytes 1572872 | tf_op jit(solution)/shard_map/ring/ppermute | solution.py:200
  29.9 11.6 %collective-permute-start.3 = (bf16[4,512,128]{2,1,0:T(8,128)(2,1)S(1)}, bf16[4,512,128]{2,1,0:T(8,128)(2,1)S(1)}, u32[]{:S(2)}, u32[]{:S(2)}) collective-permute-start(bf16[4,512,128]{2,1,0:T(8,128)(2,1)S(1)} %get-tuple-element.25), channel_id=1, source_target_pairs={{0,128},{128,1},{1,129},{129,2},{2,130},{130,3},{3,131},{131,0},{1... | collective-permute-start | bytes 1572872 | tf_op jit(solution)/shard_map/ring/ppermute | solution.py:200
  35.9 11.2 %collective-permute-start.2 = (bf16[4,512,128]{2,1,0:T(8,128)(2,1)S(1)}, bf16[4,512,128]{2,1,0:T(8,128)(2,1)S(1)}, u32[]{:S(2)}, u32[]{:S(2)}) collective-permute-start(bf16[4,512,128]{2,1,0:T(8,128)(2,1)S(1)} %collective-permute-done.1.refs_3_), channel_id=1, source_target_pairs={{0,128},{128,1},{1,129},{129,2},{2,130},{130,3},{3,131},{131,0},{1... | collective-permute-start | bytes 1572872 | tf_op jit(solution)/shard_map/ring/ppermute | solution.py:200
  41.5 11.2 %collective-permute-start.5 = (bf16[4,512,128]{2,1,0:T(8,128)(2,1)S(1)}, bf16[4,512,128]{2,1,0:T(8,128)(2,1)S(1)}, u32[]{:S(2)}, u32[]{:S(2)}) collective-permute-start(bf16[4,512,128]{2,1,0:T(8,128)(2,1)S(1)} %collective-permute-done.3.refs_4_), channel_id=1, source_target_pairs={{0,128},{128,1},{1,129},{129,2},{2,130},{130,3},{3,131},{131,0},{1... | collective-permute-start | bytes 1572872 | tf_op jit(solution)/shard_map/ring/ppermute | solution.py:200
  47.1 13.1 %collective-permute-start.4 = (bf16[4,512,128]{2,1,0:T(8,128)(2,1)S(1)}, bf16[4,512,128]{2,1,0:T(8,128)(2,1)S(1)}, u32[]{:S(2)}, u32[]{:S(2)}) collective-permute-start(bf16[4,512,128]{2,1,0:T(8,128)(2,1)S(1)} %collective-permute-done.2.refs_3_), channel_id=1, source_target_pairs={{0,128},{128,1},{1,129},{129,2},{2,130},{130,3},{3,131},{131,0},{1... | collective-permute-start | bytes 1572872 | tf_op jit(solution)/shard_map/ring/ppermute | solution.py:200
  52.7 11.2 %collective-permute-start.7 = (bf16[4,512,128]{2,1,0:T(8,128)(2,1)S(1)}, bf16[4,512,128]{2,1,0:T(8,128)(2,1)S(1)}, u32[]{:S(2)}, u32[]{:S(2)}) collective-permute-start(bf16[4,512,128]{2,1,0:T(8,128)(2,1)S(1)} %collective-permute-done.5.refs_4_), channel_id=1, source_target_pairs={{0,128},{128,1},{1,129},{129,2},{2,130},{130,3},{3,131},{131,0},{1... | collective-permute-start | bytes 1572872 | tf_op jit(solution)/shard_map/ring/ppermute | solution.py:200
  60.2 9.4 %collective-permute-start.6 = (bf16[4,512,128]{2,1,0:T(8,128)(2,1)S(1)}, bf16[4,512,128]{2,1,0:T(8,128)(2,1)S(1)}, u32[]{:S(2)}, u32[]{:S(2)}) collective-permute-start(bf16[4,512,128]{2,1,0:T(8,128)(2,1)S(1)} %collective-permute-done.4.refs_3_), channel_id=1, source_target_pairs={{0,128},{128,1},{1,129},{129,2},{2,130},{130,3},{3,131},{131,0},{1... | collective-permute-start | bytes 1572872 | tf_op jit(solution)/shard_map/ring/ppermute | solution.py:200
  71.2 3.1 %collective-permute-start.8 = (f32[4,144,256]{2,1,0:T(8,128)S(1)}, f32[4,144,256]{2,1,0:T(8,128)S(1)}, u32[]{:S(2)}, u32[]{:S(2)}) collective-permute-start(f32[4,144,256]{2,1,0:T(8,128)S(1)} %attend.13), channel_id=1, source_target_pairs={{0,16},{16,0},{1,17},{17,1},{2,18},{18,2},{3,19},{19,3},{4,20},{20... | collective-permute-start | bytes 1769480 | tf_op jit(solution)/shard_map/swap_terms/ppermute | solution.py:203
